TPU v7x, 32 devices: a whole 2x2x4 slice. The times are simulated.
32 devices in a mesh: seq: 8 (over z, y), head: 4 (over x, core).
Axes of the slice: x: 2, y: 2, z: 4, core: 2. Of those that a mesh axis runs over, the one named last changes fastest.
Arguments:
- tokens: bfloat16 [8192, 1024], P('seq', 'head'), may hold values from -6 to 6
- lengths: int32 [4], replicated, may hold values from 128 to 7680, as said below
- pad_mask: int32 [8192], P('seq'), may hold values from 0 to 1, as said below
- ln1_gain: float32 [1024], replicated, may hold values from 0.5 to 1.5
- ln1_bias: float32 [1024], replicated, may hold values from -4 to 4
- ln2_gain: float32 [1024], replicated, may hold values from 0.5 to 1.5
- ln2_bias: float32 [1024], replicated, may hold values from -4 to 4
- w_qkv: bfloat16 [3, 1024, 1024], P(None, None, 'head'), may hold values from -0.1875 to 0.1875
- b_qkv: float32 [3, 1024], P(None, 'head'), may hold values from -4 to 4
- feat_weight: float32 [16, 64], P('head'), may hold values from 0.3 to 3
- w_out: bfloat16 [1024, 1024], P('head'), may hold values from -0.75 to 0.75
- b_out: float32 [1024], replicated, may hold values from -4 to 4
- w_in: bfloat16 [1024, 4096], P(None, 'head'), may hold values from -0.1875 to 0.1875
- b_in: float32 [4096], P('head'), may hold values from -4 to 4
- w_down: bfloat16 [4096, 1024], P('head'), may hold values from -0.09375 to 0.09375
- b_down: float32 [1024], replicated, may hold values from -4 to 4
- grad_out: bfloat16 [8192, 1024], P('seq', 'head'), may hold values from -6 to 6
Outputs:
- mixed: bfloat16 [8192, 1024], P('seq', 'head')
- grad_input: float32 [8192, 1024], P('seq', 'head')
- grad_ln1_gain: float32 [1024], P('head')
- grad_ln1_bias: float32 [1024], P('head')
- grad_ln2_gain: float32 [1024], P('head')
- grad_ln2_bias: float32 [1024], P('head')
- grad_w_qkv: float32 [3, 1024, 1024], P(None, None, 'head')
- grad_b_qkv: float32 [3, 1024], P(None, 'head')
- grad_feat_weight: float32 [16, 64], P('head')
- grad_w_out: float32 [1024, 1024], P('head')
- grad_b_out: float32 [1024], P('head')
- grad_w_in: float32 [1024, 4096], P(None, 'head')
- grad_b_in: float32 [4096], P('head')
- grad_w_down: float32 [4096, 1024], P('head')
- grad_b_down: float32 [1024], P('head')
Inputs may be any that keep to these rules, and one draw needn't show every extreme that they name: `lengths`: sequences are laid end to end and fill the stream; one of them, which one drawn from the seed, starts within the first 1024 tokens and ends within the last 1024; each other one holds 128 or 256 tokens. `pad_mask`: each sequence is real tokens followed by 0 to 32 padding tokens.
All inputs are finite; a program needn't handle non-finite values.
Results may differ from a plain program's by a relative error of at most 0.015.
Values may be sent and summed in bfloat16 or wider, within the bound.
No kernel may reach another device: no remote copies, remote signals or barrier semaphores. Data moves between devices by JAX's collectives and lax.ppermute only.
A program may use at most 192 MiB of HBM per device.

v0:
```python
import math

import jax
import jax.numpy as jnp
from jax import lax
from jax.sharding import PartitionSpec as P

ROT = 16


eps_norm = 1e-05
rope_base = 10000.0
feature_scale = 0.5
highest = lax.Precision.HIGHEST


def from_behind(block, axis, distance):
    devices = range(lax.axis_size(axis))
    route = [(i - distance, i) for i in devices if i - distance in devices]
    return lax.ppermute(block, axis, route)


def feature_table(feat_count, head_size):
    row_ids = jnp.arange(feat_count).astype(jnp.float32)
    col_ids = jnp.arange(head_size).astype(jnp.float32)
    cosines = jnp.cos(math.pi * (col_ids[None, :] + 0.5) * row_ids[:, None] / head_size)
    scaling = jnp.where(row_ids == 0, math.sqrt(1.0 / head_size), math.sqrt(2.0 / head_size))
    points = math.sqrt(2.0) * lax.erf_inv(2.0 * (row_ids + 0.5) / feat_count - 1.0)
    return feature_scale * (points * scaling)[:, None] * cosines


def rope_tables(position, rot_dims):
    half_dims = rot_dims // 2
    inverse = jnp.power(rope_base, -2.0 * jnp.arange(half_dims).astype(jnp.float32) / rot_dims)
    angles = position.astype(jnp.float32)[:, None] * inverse[None, :]
    return (jnp.cos(angles)[:, None, :], jnp.sin(angles)[:, None, :])


def rotate(values, cosine, sine):
    half_dims = cosine.shape[-1]
    first = values[..., :half_dims]
    second = values[..., half_dims : 2 * half_dims]
    return jnp.concatenate(
        [
            first * cosine - second * sine,
            second * cosine + first * sine,
            values[..., 2 * half_dims :],
        ],
        -1,
    )


def rotate_back(grads, cosine, sine):
    half_dims = cosine.shape[-1]
    first = grads[..., :half_dims]
    second = grads[..., half_dims : 2 * half_dims]
    return jnp.concatenate(
        [
            first * cosine + second * sine,
            second * cosine - first * sine,
            grads[..., 2 * half_dims :],
        ],
        -1,
    )


def positions(lengths, index_all):
    seq_ends = jnp.cumsum(lengths)
    starts = seq_ends - lengths
    segment = jnp.sum((index_all[:, None] >= seq_ends[None, :]).astype(jnp.int32), 1)
    picked = segment[:, None] == jnp.arange(lengths.shape[0])[None, :]
    position = index_all - jnp.sum(jnp.where(picked, starts[None, :], 0), 1)
    return (segment, position)


def gelu_slope(values):
    return 0.5 * (1.0 + lax.erf(values * (1.0 / math.sqrt(2.0)))) + values * jnp.exp(
        -0.5 * values * values
    ) * (1.0 / math.sqrt(2.0 * math.pi))


def combine(earlier, later):
    state_early, norm_early, label_early = earlier
    state_late, norm_late, label_late = later
    empty = label_late[0] < 0
    joins = (label_early[0] == label_late[0]).astype(jnp.float32)
    state_new = jnp.where(empty, state_early, state_late + joins * state_early)
    norm_new = jnp.where(empty, norm_early, norm_late + joins * norm_early)
    label_new = jnp.where(empty, label_early, label_late)
    return (state_new, norm_new, label_new)


def body(
    tokens,
    lengths,
    pad_mask,
    ln1_gain,
    ln1_bias,
    ln2_gain,
    ln2_bias,
    w_qkv,
    b_qkv,
    feat_weight,
    w_out,
    b_out,
    w_in,
    b_in,
    w_down,
    b_down,
    grad_out,
):
    row_count = tokens.shape[0]
    share_cols = tokens.shape[1]
    head_local = feat_weight.shape[0]
    head_size = w_qkv.shape[2] // head_local
    feat_count = feat_weight.shape[1]
    offset = lax.axis_index("head") * share_cols
    full_tokens, full_grad = (
        lax.all_gather(tokens, "head", axis=1, tiled=True),
        lax.all_gather(grad_out, "head", axis=1, tiled=True),
    )
    index_all = lax.axis_index("seq") * row_count + jnp.arange(row_count)
    segment, position = positions(lengths, index_all)
    seg_float = segment.astype(jnp.float32)
    valid_keys = pad_mask.astype(jnp.float32)
    x_float = full_tokens.astype(jnp.float32)
    centered = x_float - jnp.mean(x_float, -1, keepdims=True)
    inv_std = lax.rsqrt(jnp.mean(centered * centered, -1, keepdims=True) + eps_norm)
    normed = centered * inv_std
    ln1_out = (normed * ln1_gain + ln1_bias).astype(jnp.bfloat16)
    ln2_out = (normed * ln2_gain + ln2_bias).astype(jnp.bfloat16)
    qkv_all = (
        jnp.einsum("td,cde->cte", ln1_out, w_qkv, preferred_element_type=jnp.float32)
        + b_qkv[:, None, :]
    )
    cosine, sine = rope_tables(position, ROT)
    queries = rotate(qkv_all[0].reshape(row_count, head_local, head_size), cosine, sine)
    keys_rot = rotate(qkv_all[1].reshape(row_count, head_local, head_size), cosine, sine)
    values_low = qkv_all[2].reshape(row_count, head_local, head_size).astype(jnp.bfloat16)
    feat_table = feature_table(feat_count, head_size)
    query_expo = jnp.exp(jnp.einsum("thd,fd->thf", queries, feat_table, precision=highest))
    key_expo = (
        jnp.exp(jnp.einsum("thd,fd->thf", keys_rot, feat_table, precision=highest))
        * valid_keys[:, None, None]
    )
    query_feat = (feat_weight[None] * query_expo).astype(jnp.bfloat16)
    key_feat = (feat_weight[None] * key_expo).astype(jnp.bfloat16)
    last_label = seg_float[-1]
    tail_all = (seg_float == last_label).astype(jnp.float32)
    own_state = jnp.einsum(
        "thf,thd->hfd",
        key_feat * tail_all.astype(jnp.bfloat16)[:, None, None],
        values_low,
        preferred_element_type=jnp.float32,
    )
    own_norm = jnp.sum(key_feat.astype(jnp.float32) * tail_all[:, None, None], 0)
    own_part = (own_state, own_norm, jnp.reshape(last_label, (1,)))
    zero_carry = (jnp.zeros_like(own_state), jnp.zeros_like(own_norm), jnp.zeros((1,), jnp.float32))

    def forward_turn(step_index, incoming):
        return from_behind(combine(incoming, own_part), "seq", 1)

    carried = lax.fori_loop(0, lax.axis_size("seq") - 1, forward_turn, zero_carry)
    block_rows = min(512, row_count)
    block_count = row_count // block_rows
    row_ids = jnp.arange(block_rows)
    causal = row_ids[:, None] >= row_ids[None, :]

    def blocks(array):
        return array.reshape((block_count, block_rows) + array.shape[1:])

    def forward_block(carry_in, inputs):
        state_in, norm_in, label_in = carry_in
        query_blk, key_blk, value_blk, seg_blk = inputs
        joined = ((seg_blk[:, None] == seg_blk[None, :]) & causal).astype(jnp.float32)
        scores_low = (
            jnp.einsum("thf,shf->hts", query_blk, key_blk, preferred_element_type=jnp.float32)
            * joined[None]
        ).astype(jnp.bfloat16)
        enters = (seg_blk == label_in[0]).astype(jnp.float32)
        query_float = query_blk.astype(jnp.float32)
        numerator = jnp.einsum(
            "hts,shd->thd", scores_low, value_blk, preferred_element_type=jnp.float32
        ) + enters[:, None, None] * jnp.einsum(
            "thf,hfd->thd", query_float, state_in, precision=highest
        )
        denominator = jnp.sum(scores_low.astype(jnp.float32), -1).T + enters[:, None] * jnp.einsum(
            "thf,hf->th", query_float, norm_in, precision=highest
        )
        last_here = seg_blk[-1]
        tail_rows = (seg_blk == last_here).astype(jnp.float32)
        linked = (label_in[0] == last_here).astype(jnp.float32)
        state_out = linked * state_in + jnp.einsum(
            "thf,thd->hfd",
            key_blk * tail_rows.astype(jnp.bfloat16)[:, None, None],
            value_blk,
            preferred_element_type=jnp.float32,
        )
        norm_out = linked * norm_in + jnp.sum(
            key_blk.astype(jnp.float32) * tail_rows[:, None, None], 0
        )
        return (
            (state_out, norm_out, jnp.reshape(last_here, (1,))),
            (numerator / denominator[:, :, None], denominator, state_in, norm_in, label_in),
        )

    final_carry, kept = lax.scan(
        forward_block,
        carried,
        (blocks(query_feat), blocks(key_feat), blocks(values_low), blocks(seg_float)),
    )
    attn_blocks, denom_blocks, state_ins, norm_ins, label_ins = kept
    attn_float = attn_blocks.reshape(row_count, head_local, head_size)
    denominator = denom_blocks.reshape(row_count, head_local)
    attn_low = attn_float.reshape(row_count, share_cols).astype(jnp.bfloat16)
    pre_act = jnp.dot(ln2_out, w_in, preferred_element_type=jnp.float32) + b_in
    hidden_low = jax.nn.gelu(pre_act, approximate=False).astype(jnp.bfloat16)
    partial_value = jnp.dot(attn_low, w_out, preferred_element_type=jnp.float32) + jnp.dot(
        hidden_low, w_down, preferred_element_type=jnp.float32
    )
    mixed_share = lax.psum_scatter(partial_value, "head", scatter_dimension=1, tiled=True)
    bias_share = lax.dynamic_slice_in_dim(b_out, offset, share_cols) + lax.dynamic_slice_in_dim(
        b_down, offset, share_cols
    )
    mixed = (tokens.astype(jnp.float32) + mixed_share + bias_share).astype(jnp.bfloat16)
    grad_w_out = jnp.einsum("ti,tj->ij", attn_low, full_grad, preferred_element_type=jnp.float32)
    grad_w_down = jnp.einsum("tf,tj->fj", hidden_low, full_grad, preferred_element_type=jnp.float32)
    d_hidden = jnp.einsum("tj,fj->tf", full_grad, w_down, preferred_element_type=jnp.float32)
    d_pre = d_hidden * gelu_slope(pre_act)
    grad_b_in = jnp.sum(d_pre, 0)
    d_pre_low = d_pre.astype(jnp.bfloat16)
    grad_w_in = jnp.einsum("td,tf->df", ln2_out, d_pre_low, preferred_element_type=jnp.float32)
    d_ln2 = jnp.einsum("tf,df->td", d_pre_low, w_in, preferred_element_type=jnp.float32)
    d_attn = jnp.einsum("tj,ij->ti", full_grad, w_out, preferred_element_type=jnp.float32).reshape(
        row_count, head_local, head_size
    )
    d_num = d_attn / denominator[:, :, None]
    d_den = -jnp.sum(d_attn * attn_float, -1) / denominator
    d_num_low = d_num.astype(jnp.bfloat16)
    lead_rows = (seg_float == seg_float[0]).astype(jnp.float32)[:, None, None]
    query_lead = query_feat.astype(jnp.float32) * lead_rows
    own_grad = (
        jnp.einsum("thf,thd->hfd", query_lead, d_num, precision=highest),
        jnp.einsum("thf,th->hf", query_lead, d_den, precision=highest),
        jnp.reshape(seg_float[0], (1,)),
    )

    def backward_turn(step_index, incoming):
        return from_behind(combine(incoming, own_grad), "seq", -1)

    from_later = lax.fori_loop(0, lax.axis_size("seq") - 1, backward_turn, zero_carry)
    from_state, from_norm, from_label = from_later
    start_gate = (from_label[0] == last_label).astype(jnp.float32)

    def backward_block(carry_in, inputs):
        grad_state, grad_norm = carry_in
        (
            query_blk,
            key_blk,
            value_blk,
            seg_blk,
            dnum_blk,
            dnum_low_blk,
            dden_blk,
            state_in,
            norm_in,
            label_in,
        ) = inputs
        joined = ((seg_blk[:, None] == seg_blk[None, :]) & causal).astype(jnp.float32)
        query_float = query_blk.astype(jnp.float32)
        key_float = key_blk.astype(jnp.float32)
        value_float = value_blk.astype(jnp.float32)
        scores_low = (
            jnp.einsum("thf,shf->hts", query_blk, key_blk, preferred_element_type=jnp.float32)
            * joined[None]
        ).astype(jnp.bfloat16)
        d_scores = (
            (
                jnp.einsum(
                    "thd,shd->hts", dnum_low_blk, value_blk, preferred_element_type=jnp.float32
                )
                + dden_blk.T[:, :, None]
            )
            * joined[None]
        ).astype(jnp.bfloat16)
        enters = (seg_blk == label_in[0]).astype(jnp.float32)[:, None, None]
        d_query = jnp.einsum(
            "hts,shf->thf", d_scores, key_blk, preferred_element_type=jnp.float32
        ) + enters * (
            jnp.einsum("hfd,thd->thf", state_in, dnum_blk, precision=highest)
            + jnp.einsum("hf,th->thf", norm_in, dden_blk, precision=highest)
        )
        last_here = seg_blk[-1]
        tail_rows = (seg_blk == last_here).astype(jnp.float32)[:, None, None]
        linked = (label_in[0] == last_here).astype(jnp.float32)
        d_key = jnp.einsum(
            "hts,thf->shf", d_scores, query_blk, preferred_element_type=jnp.float32
        ) + tail_rows * (
            jnp.einsum("hfd,thd->thf", grad_state, value_float, precision=highest) + grad_norm[None]
        )
        d_value = jnp.einsum(
            "hts,thd->shd", scores_low, dnum_low_blk, preferred_element_type=jnp.float32
        ) + tail_rows * jnp.einsum("hfd,thf->thd", grad_state, key_float, precision=highest)
        back_state = (
            jnp.einsum("thf,thd->hfd", query_float * enters, dnum_blk, precision=highest)
            + linked * grad_state
        )
        back_norm = (
            jnp.einsum("thf,th->hf", query_float * enters, dden_blk, precision=highest)
            + linked * grad_norm
        )
        return ((back_state, back_norm), (d_query, d_key, d_value))

    final_grad, pieces = lax.scan(
        backward_block,
        (start_gate * from_state, start_gate * from_norm),
        (
            blocks(query_feat),
            blocks(key_feat),
            blocks(values_low),
            blocks(seg_float),
            blocks(d_num),
            blocks(d_num_low),
            blocks(d_den),
            state_ins,
            norm_ins,
            label_ins,
        ),
        reverse=True,
    )
    d_qf = pieces[0].reshape(row_count, head_local, feat_count)
    d_kf = pieces[1].reshape(row_count, head_local, feat_count)
    d_val = pieces[2].reshape(row_count, head_local, head_size)
    grad_feat = jnp.sum(d_qf * query_expo + d_kf * key_expo, 0)
    d_queries = jnp.einsum(
        "thf,fd->thd", d_qf * feat_weight[None] * query_expo, feat_table, precision=highest
    )
    d_keys = jnp.einsum(
        "thf,fd->thd", d_kf * feat_weight[None] * key_expo, feat_table, precision=highest
    )
    d_queries = rotate_back(d_queries, cosine, sine)
    d_keys = rotate_back(d_keys, cosine, sine)
    d_qkv = jnp.stack(
        [
            d_queries.reshape(row_count, share_cols),
            d_keys.reshape(row_count, share_cols),
            d_val.reshape(row_count, share_cols),
        ]
    )
    grad_b_qkv = jnp.sum(d_qkv, 1)
    d_qkv_low = d_qkv.astype(jnp.bfloat16)
    grad_w_qkv = jnp.einsum("td,cte->cde", ln1_out, d_qkv_low, preferred_element_type=jnp.float32)
    d_ln1 = jnp.einsum("cte,cde->td", d_qkv_low, w_qkv, preferred_element_type=jnp.float32)
    gain_part = jnp.stack(
        [
            jnp.sum(d_ln1 * normed, 0),
            jnp.sum(d_ln1, 0),
            jnp.sum(d_ln2 * normed, 0),
            jnp.sum(d_ln2, 0),
        ]
    )
    mixed_grad = ln1_gain * d_ln1 + ln2_gain * d_ln2
    normed_share = lax.dynamic_slice_in_dim(normed, offset, share_cols, 1)
    grad_total, gains_total = lax.psum((mixed_grad, gain_part), "head")
    mean_one = jnp.mean(grad_total, -1, keepdims=True)
    mean_two = jnp.mean(grad_total * normed, -1, keepdims=True)
    grad_share = lax.dynamic_slice_in_dim(grad_total, offset, share_cols, 1)
    gains_share = lax.dynamic_slice_in_dim(gains_total, offset, share_cols, 1)
    grad_input = grad_out.astype(jnp.float32) + inv_std * (
        grad_share - mean_one - normed_share * mean_two
    )
    grad_bias_out = jnp.sum(grad_out.astype(jnp.float32), 0)
    summed = lax.psum(
        (
            grad_w_qkv,
            grad_b_qkv,
            grad_feat,
            grad_w_out,
            grad_w_in,
            grad_b_in,
            grad_w_down,
            gains_share,
            grad_bias_out,
        ),
        "seq",
    )
    return (
        mixed,
        grad_input,
        summed[7][0],
        summed[7][1],
        summed[7][2],
        summed[7][3],
        summed[0],
        summed[1],
        summed[2],
        summed[3],
        summed[8],
        summed[4],
        summed[5],
        summed[6],
        summed[8],
    )


def solution(mesh):
    in_specs = (
        P("seq", "head"),
        P(),
        P("seq"),
        P(),
        P(),
        P(),
        P(),
        P(None, None, "head"),
        P(None, "head"),
        P("head", None),
        P("head", None),
        P(),
        P(None, "head"),
        P("head"),
        P("head", None),
        P(),
        P("seq", "head"),
    )
    out_specs = (
        P("seq", "head"),
        P("seq", "head"),
        P("head"),
        P("head"),
        P("head"),
        P("head"),
        P(None, None, "head"),
        P(None, "head"),
        P("head", None),
        P("head", None),
        P("head"),
        P(None, "head"),
        P("head"),
        P("head", None),
        P("head"),
    )
    return jax.shard_map(body, mesh=mesh, in_specs=in_specs, out_specs=out_specs, check_vma=False)
```

profile of v0, /device:TPU:8, one launch (start us, length us, event | category | flops | bytes accessed | tf_op | source)
XLA Modules:
  0.0 1003.3 jit_solution(16234372849047927526)
XLA Ops:
  14.7 18.9 %all-gather.3.cloned.1.call-done = bf16[1024,1024]{1,0:T(8,128)(2,1)} async-done(((bf16[1024,256]{1,0:T(8,128)(2,1)}), bf16[1024,1024]{1,0:T(8,128)(2,1)}) %all-gather.3.cloned.1.call-update) | async-done | bytes 2097168 | tf_op jit(solution)/shard_map/all_gather | solution.py:119
  51.9 93.9 %while.78 = (s32[]{:T(128)}, f32[4,64,64]{2,1,0:T(8,128)S(1)}, f32[4,64]{1,0:T(4,128)S(1)}, f32[1]{0:T(128)}, pred[]{:T(512)}, /*index=5*/f32[1]{0:T(128)}, f32[...) while((s32[]{:T(128)}, f32[4,64,64]{2,1,0:T(8,128)S(1)}, f32[4,64]{1,0:T(4,128)S(1)}, f32[1]{0:T(128)}, ...), condition=%wide.region_7.8_spmd, body=%wide.region_6.7_spmd.sunk | while | flops 49925 | bytes 466186 | solution.py:163
  53.0 3.4 collective-permute-start
  56.4 3.4 collective-permute-start.1
  60.4 4.7 collective-permute-start.2
  70.7 4.3 collective-permute-start.1
  75.7 3.8 collective-permute-start.2
  85.4 3.4 collective-permute-start.1
  89.4 3.2 collective-permute-start.2
  92.6 3.2 collective-permute-done.2
  101.7 3.2 collective-permute-start.2
  104.9 3.2 collective-permute-done.2
  114.0 3.2 collective-permute-start.2
  117.2 3.2 collective-permute-done.2
  126.3 3.2 collective-permute-start.2
  129.5 3.3 collective-permute-done.2
  138.7 3.2 collective-permute-start.2
  141.9 3.2 collective-permute-done.2
  146.8 29.0 %while.80 = (s32[]{:T(128)}, f32[4,64,64]{2,1,0:T(8,128)S(1)}, f32[4,64]{1,0:T(4,128)S(1)}, f32[1]{0:T(128)}, f32[2,512,4,64]{1,3,2,0:T(8,128)}, /*index=5*/f32[...) while((s32[]{:T(128)}, f32[4,64,64]{2,1,0:T(8,128)S(1)}, ...), condition=%wide.region_11.12_spmd.clone, body=%wide.region_8.11_spmd.clone.sunk | while | flops 393650944 | bytes 18851640 | solution.py:207
  178.2 2.8 multiply_reduce_fusion.3
  186.8 87.2 %while.79 = (s32[]{:T(128)}, f32[4,64,64]{2,1,0:T(8,128)S(1)}, f32[4,64]{1,0:T(4,128)S(1)}, f32[1]{0:T(128)}, pred[]{:T(512)}, /*index=5*/f32[1]{0:T(128)}, f32[...) while((s32[]{:T(128)}, f32[4,64,64]{2,1,0:T(8,128)S(1)}, f32[4,64]{1,0:T(4,128)S(1)}, f32[1]{0:T(128)}, ...), condition=%wide.region_15.16_spmd, body=%wide.region_14.15_spmd.sunk | while | flops 49925 | bytes 466186 | solution.py:251
  187.5 3.9 collective-permute-start.3
  194.0 3.2 collective-permute-start.5
  200.9 2.8 collective-permute-start.3
  206.3 3.2 collective-permute-start.5
  213.2 2.8 collective-permute-start.3
  218.6 3.2 collective-permute-start.5
  225.5 2.8 collective-permute-start.3
  230.9 3.2 collective-permute-start.5
  237.8 2.8 collective-permute-start.3
  243.2 3.2 collective-permute-start.5
  250.1 2.8 collective-permute-start.3
  255.5 3.2 collective-permute-start.5
  262.4 2.8 collective-permute-start.3
  267.8 3.2 collective-permute-start.5
  281.5 98.2 %while.81 = (s32[]{:T(128)}, f32[4,64,64]{2,1,0:T(8,128)S(1)}, f32[4,64]{1,0:T(4,128)S(1)}, f32[2,512,4,64]{1,0,3,2:T(2,128)}, f32[2,512,4,64]{1,0,3,2:T(2,128)}...) while((s32[]{:T(128)}, f32[4,64,64]{2,1,0:T(8,128)S(1)}, ...), condition=%wide.region_17.18_spmd.clone, body=%wide.region_16.17_spmd.clone.sunk | while | flops 1083345408 | bytes 31150916 | solution.py:314
  303.1 10.4 %dynamic_update_slice.74 = f32[2,512,4,64]{1,0,3,2:T(2,128)} dynamic-update-slice(f32[2,512,4,64]{1,0,3,2:T(2,128)} %get-tuple-element.1358, f32[1,512,4,64]{1,0,3,2:T(1,128)} %copy.162, s32[]{:T(128)S(6)} %sub.121, s32[]{:T(128)} %constant.94.clone.1..sunk.1, s32[]{:T(128)} %constant.94.clone.1..sunk.1, s32[]{:T(128)} %constant.94.clone.1..sunk.1) | dynamic-update-slice | bytes 1048580 | tf_op jit(solution)/shard_map/while/body/jit(dynamic_update_index_in_dim)/dynamic_update_slice | solution.py:207
  317.1 10.4 %dynamic_update_slice.75 = f32[2,512,4,64]{1,0,3,2:T(2,128)} dynamic-update-slice(f32[2,512,4,64]{1,0,3,2:T(2,128)} %get-tuple-element.1359, f32[1,512,4,64]{1,0,3,2:T(1,128)} %copy.163, s32[]{:T(128)S(6)} %sub.121, s32[]{:T(128)} %constant.94.clone.1..sunk.1, s32[]{:T(128)} %constant.94.clone.1..sunk.1, s32[]{:T(128)} %constant.94.clone.1..sunk.1) | dynamic-update-slice | bytes 1048580 | tf_op jit(solution)/shard_map/while/body/jit(dynamic_update_index_in_dim)/dynamic_update_slice | solution.py:207
  327.5 3.2 fusion.304
  352.1 10.4 %dynamic_update_slice.74 = f32[2,512,4,64]{1,0,3,2:T(2,128)} dynamic-update-slice(f32[2,512,4,64]{1,0,3,2:T(2,128)} %get-tuple-element.1358, f32[1,512,4,64]{1,0,3,2:T(1,128)} %copy.162, s32[]{:T(128)S(6)} %sub.121, s32[]{:T(128)} %constant.94.clone.1..sunk.1, s32[]{:T(128)} %constant.94.clone.1..sunk.1, s32[]{:T(128)} %constant.94.clone.1..sunk.1) | dynamic-update-slice | bytes 1048580 | tf_op jit(solution)/shard_map/while/body/jit(dynamic_update_index_in_dim)/dynamic_update_slice | solution.py:207
  366.1 10.4 %dynamic_update_slice.75 = f32[2,512,4,64]{1,0,3,2:T(2,128)} dynamic-update-slice(f32[2,512,4,64]{1,0,3,2:T(2,128)} %get-tuple-element.1359, f32[1,512,4,64]{1,0,3,2:T(1,128)} %copy.163, s32[]{:T(128)S(6)} %sub.121, s32[]{:T(128)} %constant.94.clone.1..sunk.1, s32[]{:T(128)} %constant.94.clone.1..sunk.1, s32[]{:T(128)} %constant.94.clone.1..sunk.1) | dynamic-update-slice | bytes 1048580 | tf_op jit(solution)/shard_map/while/body/jit(dynamic_update_index_in_dim)/dynamic_update_slice | solution.py:207
  376.5 3.2 fusion.304
  379.7 3.2 reshape.412
  382.9 2.9 fusion.134
  387.8 3.1 reshape.411
  396.4 14.0 %fusion.101 = (bf16[1024,1024]{1,0:T(8,128)(2,1)}, f32[1024,1024]{1,0:T(8,128)S(1)}) fusion(f32[1024]{0:T(1024)} %param.38, bf16[1024,1024]{1,0:T(8,128)(2,1)S(1)} %copy-done, bf16[1024,1024]{1,0:T(8,128)(2,1)S(1)} %copy-done.3, f32[1024]{0:T(1024)} %param.31, f32[1024]{0:T(1024)} %param.30, f32[1024]{0:T(1024)S(1)} %add_rsqrt_fusion, f32[1024]{0:T(1024)S(1)} %copy-done.28), kind=kOutput, calls=%fused_computation.136 | convolution fusion | flops 2222981120 | bytes 10506240 | tf_op jit(solution)/shard_map/dot_general | solution.py:216
  410.4 4.6 fusion.197
  415.0 4.5 fusion.132
  422.1 3.2 reshape.426
  435.0 8.8 fusion.107
  446.0 4.7 fusion.198
  450.8 2.9 convolution_add_fusion.4
  453.8 3.5 fusion.199
  457.3 6.6 convolution_bitcast_fusion.3
  463.9 4.4 fusion.200
  468.3 4.8 fusion.130
  478.0 54.4 %all-reduce.5.cloned.1.call-done = f32[1024,1024]{1,0:T(8,128)} async-done(((f32[1024,1024]{1,0:T(8,128)}), f32[1024,1024]{1,0:T(8,128)}) %all-reduce.5.cloned.1.call-update) | async-done | bytes 4194320 | tf_op jit(solution)/shard_map/psum | solution.py:364
  532.5 7.9 fusion.189
  540.4 10.4 %psum.78 = f32[4,1024]{1,0:T(4,128)S(1)} all-reduce(f32[4,1024]{1,0:T(4,128)S(1)} %pad_maximum_fusion.3), channel_id=1, replica_groups=mesh['seq'=8,'head'=4] {'head'}, use_global_device_ids=true, to_apply=%region_25.26 | all-reduce | flops 4096 | bytes 32768 | tf_op jit(solution)/shard_map/psum | solution.py:364
  550.8 3.0 convert_reduce_fusion.2
  553.8 34.3 %all-reduce = (f32[4,256]{1,0:T(4,128)S(1)}, f32[3,256]{1,0:T(4,128)}, f32[4,64]{1,0:T(4,128)}, f32[256]{0:T(256)S(1)}, f32[1024]{0:T(1024)}) all-reduce(f32[4,256]{1,0:T(4,128)S(1)} %constant_dynamic-slice_fusion.4, f32[3,256]{1,0:T(4,128)S(1)} %fusion.116, ...), channel_id=1, replica_groups=mesh['seq'=8,'head'=4] {'seq'}, use_global_device_ids=true, to_apply=%region_26.27 | all-reduce | flops 3328 | bytes 26624 | tf_op jit(solution)/shard_map/psum | solution.py:373
  590.9 393.3 %all-reduce.7.cloned.1.call-done = (f32[3,1024,256]{1,2,0:T(8,128)}, f32[256,1024]{1,0:T(8,128)}, f32[1024,1024]{1,0:T(8,128)}, f32[1024,1024]{1,0:T(8,128)}) async-done(((f32[3,1024,256]{1,2,0:T(8,128)}, f32[256,1024]{1,0:T(8,128)}, f32[1024,1024]{1,0:T(8,128)}, f32[1024,1024]{1,0:T(8,128)}), (f32[3,1024,256]{1,2,0:T(8,128)}, f32[256,1024]{1,0:T(8,128)}, f32[1024,1024]{1,0:T(8,128)}, ...) | async-done | bytes 12582928 | tf_op jit(solution)/shard_map/psum | solution.py:373
  984.2 3.6 copy.97
  989.4 4.9 copy.253
  (347 shorter events, 201.4 us)
Async XLA Ops:
  7.2 389.2 %copy-start = (bf16[1024,1024]{1,0:T(8,128)(2,1)S(1)}, bf16[1024,1024]{1,0:T(8,128)(2,1)}, u32[]{:S(2)}) copy-start(bf16[1024,1024]{1,0:T(8,128)(2,1)} %param.37) | copy-start | bytes 6291460
  7.2 30.9 %copy-start.43 = (f32[3,256]{1,0:T(4,128)S(1)}, f32[3,256]{1,0:T(4,128)}, u32[]{:S(2)}) copy-start(f32[3,256]{1,0:T(4,128)} %param.33) | copy-start | bytes 9220
  7.2 30.9 %copy-start.45 = (f32[1024]{0:T(1024)S(1)}, f32[1024]{0:T(1024)}, u32[]{:S(2)}) copy-start(f32[1024]{0:T(1024)} %param.29) | copy-start | bytes 12292
  7.2 30.9 %copy-start.38 = (f32[1024]{0:T(1024)S(1)}, f32[1024]{0:T(1024)}, u32[]{:S(2)}) copy-start(f32[1024]{0:T(1024)} %param.28) | copy-start | bytes 12292
  7.2 26.4 %all-gather.3.cloned.1.call-start = ((), (), s32[]{:S(2)}) async-start(), calls=%async_computation.1 | async-start | bytes 2621440 | tf_op jit(solution)/shard_map/all_gather | solution.py:119
  8.0 170.2 %all-gather.5.cloned.1.call-start = ((), (), s32[]{:S(2)}) async-start(), calls=%async_computation.3 | async-start | bytes 2621440 | tf_op jit(solution)/shard_map/all_gather | solution.py:120
  8.7 523.7 %all-reduce.5.cloned.1.call-start = ((), (), s32[]{:S(2)}) async-start(), calls=%async_computation.4 | async-start | bytes 8388608 | tf_op jit(solution)/shard_map/psum | solution.py:364
  8.8 33.4 %copy-start.31 = (f32[64]{0:T(128)}, f32[64]{0:T(128)S(1)}, u32[]{:S(2)}) copy-start(f32[64]{0:T(128)S(1)} %iota_convert_fusion) | copy-start | bytes 772
  8.8 33.3 %copy-start.33 = (f32[64]{0:T(128)}, f32[64]{0:T(128)S(1)}, u32[]{:S(2)}) copy-start(f32[64]{0:T(128)S(1)} %get-tuple-element.938) | copy-start | bytes 772
  8.9 33.3 %copy-start.35 = (f32[64]{0:T(128)}, f32[64]{0:T(128)S(1)}, u32[]{:S(2)}) copy-start(f32[64]{0:T(128)S(1)} %get-tuple-element.939) | copy-start | bytes 772
  14.7 26.1 %copy-start.22 = (f32[1024,8]{0,1:T(8,128)}, f32[1024,8]{0,1:T(8,128)S(1)}, u32[]{:S(2)}) copy-start(f32[1024,8]{0,1:T(8,128)S(1)} %get-tuple-element.919) | copy-start | bytes 98308
  14.7 26.1 %copy-start.23 = (f32[1024,8]{0,1:T(8,128)}, f32[1024,8]{0,1:T(8,128)S(1)}, u32[]{:S(2)}) copy-start(f32[1024,8]{0,1:T(8,128)S(1)} %get-tuple-element.920) | copy-start | bytes 98308
  53.0 13.9 %collective-permute-start = (f32[4,64,64]{2,1,0:T(8,128)S(1)}, f32[4,64,64]{2,1,0:T(8,128)S(1)}, u32[]{:S(2)}, u32[]{:S(2)}) collective-permute-start(f32[4,64,64]{2,1,0:T(8,128)S(1)} %add_select_fusion.8), channel_id=1, source_target_pairs={{0,4},{4,8},{8,12},{12,16},{16,20},{20,24},{24,28},{1,5},{5,9},{9,... | collective-permute-start | bytes 196616 | tf_op jit(solution)/shard_map/while/body/eval_jaxpr/ppermute | solution.py:20
  56.4 10.5 %collective-permute-start.1 = (f32[4,64]{1,0:T(4,128)S(1)}, f32[4,64]{1,0:T(4,128)S(1)}, u32[]{:S(2)}, u32[]{:S(2)}) collective-permute-start(f32[4,64]{1,0:T(4,128)S(1)} %add_select_fusion.9), channel_id=1, source_target_pairs={{0,4},{4,8},{8,12},{12,16},{16,20},{20,24},{24,28},{1,5},{5,9},{9,... | collective-permute-start | bytes 3080 | tf_op jit(solution)/shard_map/while/body/eval_jaxpr/ppermute | solution.py:20
  60.4 6.4 collective-permute-start.2
  68.2 13.9 %collective-permute-start = (f32[4,64,64]{2,1,0:T(8,128)S(1)}, f32[4,64,64]{2,1,0:T(8,128)S(1)}, u32[]{:S(2)}, u32[]{:S(2)}) collective-permute-start(f32[4,64,64]{2,1,0:T(8,128)S(1)} %add_select_fusion.8), channel_id=1, source_target_pairs={{0,4},{4,8},{8,12},{12,16},{16,20},{20,24},{24,28},{1,5},{5,9},{9,... | collective-permute-start | bytes 196616 | tf_op jit(solution)/shard_map/while/body/eval_jaxpr/ppermute | solution.py:20
  70.7 11.4 %collective-permute-start.1 = (f32[4,64]{1,0:T(4,128)S(1)}, f32[4,64]{1,0:T(4,128)S(1)}, u32[]{:S(2)}, u32[]{:S(2)}) collective-permute-start(f32[4,64]{1,0:T(4,128)S(1)} %add_select_fusion.9), channel_id=1, source_target_pairs={{0,4},{4,8},{8,12},{12,16},{16,20},{20,24},{24,28},{1,5},{5,9},{9,... | collective-permute-start | bytes 3080 | tf_op jit(solution)/shard_map/while/body/eval_jaxpr/ppermute | solution.py:20
  75.7 6.4 collective-permute-start.2
  83.4 12.4 %collective-permute-start = (f32[4,64,64]{2,1,0:T(8,128)S(1)}, f32[4,64,64]{2,1,0:T(8,128)S(1)}, u32[]{:S(2)}, u32[]{:S(2)}) collective-permute-start(f32[4,64,64]{2,1,0:T(8,128)S(1)} %add_select_fusion.8), channel_id=1, source_target_pairs={{0,4},{4,8},{8,12},{12,16},{16,20},{20,24},{24,28},{1,5},{5,9},{9,... | collective-permute-start | bytes 196616 | tf_op jit(solution)/shard_map/while/body/eval_jaxpr/ppermute | solution.py:20
  85.4 10.5 %collective-permute-start.1 = (f32[4,64]{1,0:T(4,128)S(1)}, f32[4,64]{1,0:T(4,128)S(1)}, u32[]{:S(2)}, u32[]{:S(2)}) collective-permute-start(f32[4,64]{1,0:T(4,128)S(1)} %add_select_fusion.9), channel_id=1, source_target_pairs={{0,4},{4,8},{8,12},{12,16},{16,20},{20,24},{24,28},{1,5},{5,9},{9,... | collective-permute-start | bytes 3080 | tf_op jit(solution)/shard_map/while/body/eval_jaxpr/ppermute | solution.py:20
  89.4 6.4 collective-permute-start.2
  97.2 11.0 %collective-permute-start = (f32[4,64,64]{2,1,0:T(8,128)S(1)}, f32[4,64,64]{2,1,0:T(8,128)S(1)}, u32[]{:S(2)}, u32[]{:S(2)}) collective-permute-start(f32[4,64,64]{2,1,0:T(8,128)S(1)} %add_select_fusion.8), channel_id=1, source_target_pairs={{0,4},{4,8},{8,12},{12,16},{16,20},{20,24},{24,28},{1,5},{5,9},{9,... | collective-permute-start | bytes 196616 | tf_op jit(solution)/shard_map/while/body/eval_jaxpr/ppermute | solution.py:20
  99.1 9.0 collective-permute-start.1
  101.7 6.4 collective-permute-start.2
  109.5 11.0 %collective-permute-start = (f32[4,64,64]{2,1,0:T(8,128)S(1)}, f32[4,64,64]{2,1,0:T(8,128)S(1)}, u32[]{:S(2)}, u32[]{:S(2)}) collective-permute-start(f32[4,64,64]{2,1,0:T(8,128)S(1)} %add_select_fusion.8), channel_id=1, source_target_pairs={{0,4},{4,8},{8,12},{12,16},{16,20},{20,24},{24,28},{1,5},{5,9},{9,... | collective-permute-start | bytes 196616 | tf_op jit(solution)/shard_map/while/body/eval_jaxpr/ppermute | solution.py:20
  111.4 9.0 collective-permute-start.1
  114.0 6.4 collective-permute-start.2
  121.8 11.0 %collective-permute-start = (f32[4,64,64]{2,1,0:T(8,128)S(1)}, f32[4,64,64]{2,1,0:T(8,128)S(1)}, u32[]{:S(2)}, u32[]{:S(2)}) collective-permute-start(f32[4,64,64]{2,1,0:T(8,128)S(1)} %add_select_fusion.8), channel_id=1, source_target_pairs={{0,4},{4,8},{8,12},{12,16},{16,20},{20,24},{24,28},{1,5},{5,9},{9,... | collective-permute-start | bytes 196616 | tf_op jit(solution)/shard_map/while/body/eval_jaxpr/ppermute | solution.py:20
  123.7 9.1 collective-permute-start.1
  126.3 6.5 collective-permute-start.2
  134.1 11.0 %collective-permute-start = (f32[4,64,64]{2,1,0:T(8,128)S(1)}, f32[4,64,64]{2,1,0:T(8,128)S(1)}, u32[]{:S(2)}, u32[]{:S(2)}) collective-permute-start(f32[4,64,64]{2,1,0:T(8,128)S(1)} %add_select_fusion.8), channel_id=1, source_target_pairs={{0,4},{4,8},{8,12},{12,16},{16,20},{20,24},{24,28},{1,5},{5,9},{9,... | collective-permute-start | bytes 196616 | tf_op jit(solution)/shard_map/while/body/eval_jaxpr/ppermute | solution.py:20
  136.1 9.0 collective-permute-start.1
  138.7 6.4 collective-permute-start.2
  185.7 91.6 %copy-start.25 = (f32[2,512,4]{1,2,0:T(4,128)S(1)}, f32[2,512,4]{1,2,0:T(4,128)}, u32[]{:S(2)}) copy-start(f32[2,512,4]{1,2,0:T(4,128)} %copy-done.24) | copy-start | bytes 49156
  185.7 91.6 %copy-start.26 = (f32[1024,4]{0,1:T(4,128)S(1)}, f32[1024,4]{0,1:T(4,128)}, u32[]{:S(2)}) copy-start(f32[1024,4]{0,1:T(4,128)} %get-tuple-element.917) | copy-start | bytes 49156
  186.8 94.7 %copy-start.19 = (f32[2,4,64,64]{3,2,1,0:T(8,128)S(1)}, f32[2,4,64,64]{3,2,1,0:T(8,128)}, u32[]{:S(2)}) copy-start(f32[2,4,64,64]{3,2,1,0:T(8,128)} %get-tuple-element.1350) | copy-start | bytes 393220
  187.5 12.1 %collective-permute-start.3 = (f32[4,64,64]{2,1,0:T(8,128)S(1)}, f32[4,64,64]{2,1,0:T(8,128)S(1)}, u32[]{:S(2)}, u32[]{:S(2)}) collective-permute-start(f32[4,64,64]{2,1,0:T(8,128)S(1)} %add_select_fusion.10), channel_id=1, source_target_pairs={{4,0},{8,4},{12,8},{16,12},{20,16},{24,20},{28,24},{5,1},{9,5},{13... | collective-permute-start | bytes 196616 | tf_op jit(solution)/shard_map/while/body/eval_jaxpr/ppermute | solution.py:20
  191.5 8.1 collective-permute-start.4
  194.0 5.5 collective-permute-start.5
  200.9 11.0 %collective-permute-start.3 = (f32[4,64,64]{2,1,0:T(8,128)S(1)}, f32[4,64,64]{2,1,0:T(8,128)S(1)}, u32[]{:S(2)}, u32[]{:S(2)}) collective-permute-start(f32[4,64,64]{2,1,0:T(8,128)S(1)} %add_select_fusion.10), channel_id=1, source_target_pairs={{4,0},{8,4},{12,8},{16,12},{20,16},{24,20},{28,24},{5,1},{9,5},{13... | collective-permute-start | bytes 196616 | tf_op jit(solution)/shard_map/while/body/eval_jaxpr/ppermute | solution.py:20
  203.8 8.1 collective-permute-start.4
  206.3 5.5 collective-permute-start.5
  213.2 11.0 %collective-permute-start.3 = (f32[4,64,64]{2,1,0:T(8,128)S(1)}, f32[4,64,64]{2,1,0:T(8,128)S(1)}, u32[]{:S(2)}, u32[]{:S(2)}) collective-permute-start(f32[4,64,64]{2,1,0:T(8,128)S(1)} %add_select_fusion.10), channel_id=1, source_target_pairs={{4,0},{8,4},{12,8},{16,12},{20,16},{24,20},{28,24},{5,1},{9,5},{13... | collective-permute-start | bytes 196616 | tf_op jit(solution)/shard_map/while/body/eval_jaxpr/ppermute | solution.py:20
  216.0 8.1 collective-permute-start.4
  218.6 5.5 collective-permute-start.5
  225.5 11.0 %collective-permute-start.3 = (f32[4,64,64]{2,1,0:T(8,128)S(1)}, f32[4,64,64]{2,1,0:T(8,128)S(1)}, u32[]{:S(2)}, u32[]{:S(2)}) collective-permute-start(f32[4,64,64]{2,1,0:T(8,128)S(1)} %add_select_fusion.10), channel_id=1, source_target_pairs={{4,0},{8,4},{12,8},{16,12},{20,16},{24,20},{28,24},{5,1},{9,5},{13... | collective-permute-start | bytes 196616 | tf_op jit(solution)/shard_map/while/body/eval_jaxpr/ppermute | solution.py:20
  228.3 8.1 collective-permute-start.4
  230.9 5.5 collective-permute-start.5
  237.8 11.0 %collective-permute-start.3 = (f32[4,64,64]{2,1,0:T(8,128)S(1)}, f32[4,64,64]{2,1,0:T(8,128)S(1)}, u32[]{:S(2)}, u32[]{:S(2)}) collective-permute-start(f32[4,64,64]{2,1,0:T(8,128)S(1)} %add_select_fusion.10), channel_id=1, source_target_pairs={{4,0},{8,4},{12,8},{16,12},{20,16},{24,20},{28,24},{5,1},{9,5},{13... | collective-permute-start | bytes 196616 | tf_op jit(solution)/shard_map/while/body/eval_jaxpr/ppermute | solution.py:20
  240.6 8.1 collective-permute-start.4
  243.2 5.5 collective-permute-start.5
  250.1 11.0 %collective-permute-start.3 = (f32[4,64,64]{2,1,0:T(8,128)S(1)}, f32[4,64,64]{2,1,0:T(8,128)S(1)}, u32[]{:S(2)}, u32[]{:S(2)}) collective-permute-start(f32[4,64,64]{2,1,0:T(8,128)S(1)} %add_select_fusion.10), channel_id=1, source_target_pairs={{4,0},{8,4},{12,8},{16,12},{20,16},{24,20},{28,24},{5,1},{9,5},{13... | collective-permute-start | bytes 196616 | tf_op jit(solution)/shard_map/while/body/eval_jaxpr/ppermute | solution.py:20
  252.9 8.1 collective-permute-start.4
  255.5 5.5 collective-permute-start.5
  262.4 11.0 %collective-permute-start.3 = (f32[4,64,64]{2,1,0:T(8,128)S(1)}, f32[4,64,64]{2,1,0:T(8,128)S(1)}, u32[]{:S(2)}, u32[]{:S(2)}) collective-permute-start(f32[4,64,64]{2,1,0:T(8,128)S(1)} %add_select_fusion.10), channel_id=1, source_target_pairs={{4,0},{8,4},{12,8},{16,12},{20,16},{24,20},{28,24},{5,1},{9,5},{13... | collective-permute-start | bytes 196616 | tf_op jit(solution)/shard_map/while/body/eval_jaxpr/ppermute | solution.py:20
  265.2 8.1 collective-permute-start.4
  267.8 5.5 collective-permute-start.5
  396.4 14.0 %copy-start.7 = (bf16[1024,1024]{1,0:T(8,128)(2,1)S(1)}, bf16[1024,1024]{1,0:T(8,128)(2,1)}, u32[]{:S(2)}) copy-start(bf16[1024,1024]{1,0:T(8,128)(2,1)} %all-gather.5.cloned.1.call-done) | copy-start | bytes 6291460
  443.8 145.0 %reduce-scatter.2.cloned.1.call-start = ((), (), s32[]{:S(2)}) async-start(), calls=%async_computation.2 | async-start | bytes 5242880 | tf_op jit(solution)/shard_map/reduce_scatter | solution.py:221
  453.8 530.4 %all-reduce.7.cloned.1.call-start = ((), (), s32[]{:S(2)}) async-start(), calls=%async_computation.5 | async-start | bytes 25165824 | tf_op jit(solution)/shard_map/psum | solution.py:373
  532.4 18.4 %copy-start.14 = (bf16[1024,256]{1,0:T(8,128)(2,1)S(1)}, bf16[1024,256]{1,0:T(8,128)(2,1)}, u32[]{:S(2)}) copy-start(bf16[1024,256]{1,0:T(8,128)(2,1)} %param.41) | copy-start | bytes 1572868
  532.5 21.4 %copy-start.37 = (f32[1024]{0:T(1024)S(1)}, f32[1024]{0:T(1024)}, u32[]{:S(2)}) copy-start(f32[1024]{0:T(1024)} %get-tuple-element.936) | copy-start | bytes 12292
  532.5 56.3 %copy-start.15 = (bf16[1024,256]{1,0:T(8,128)(2,1)S(1)}, bf16[1024,256]{1,0:T(8,128)(2,1)}, u32[]{:S(2)}) copy-start(bf16[1024,256]{1,0:T(8,128)(2,1)} %param.25) | copy-start | bytes 1572868
  588.2 399.6 %copy-start.41 = (f32[256]{0:T(256)}, f32[256]{0:T(256)S(1)}, u32[]{:S(2)}) copy-start(f32[256]{0:T(256)S(1)} %get-tuple-element.1433) | copy-start | bytes 3076
  (37 other events, 216.7 us)
Sparse Core Ops, SparseCore 0:
  9.6 23.9 all-gather.2
  35.2 22.8 all-gather.4
  443.9 88.5 all-reduce.4
  535.6 44.6 reduce-scatter.1
  585.4 398.6 all-reduce.6
where the time goes:
time: 1020 us; the launch traced here: 1000 us
  waiting for transfers between devices  505 us (50%)
  matrix products  128 us (13%)
  starting transfers between devices  116 us (11%)
  local copies, waits for them, and re-layouts  114 us (11%)
  other arithmetic  45 us (4%)
  blocking collectives  44.7 us (4%)
  loops' own time  33.9 us (3%)
  between operations  16.9 us (2%)
    psum x1, waiting for transfers between devices, body(): lax.psum((grad_w_qkv, grad_b_qkv, grad_feat, grad_w_out, grad_w_in, grad_...  393 us
    ppermute x42, starting transfers between devices, from_behind(): return lax.ppermute(block, axis, route)  115 us
    psum x1, waiting for transfers between devices, body(): grad_total, gains_total = lax.psum((mixed_grad, gain_part), 'head')  54.4 us
    dynamic_update_slice x14, local copies, waits for them, and re-layouts, body(): lax.scan(forward_block, carried, (blocks(query_feat), blocks(key_feat), b...  52.1 us
    ppermute x42, waiting for transfers between devices, from_behind(): return lax.ppermute(block, axis, route)  37.1 us
    psum x1, blocking collectives, body(): lax.psum((grad_w_qkv, grad_b_qkv, grad_feat, grad_w_out, grad_w_in, grad_...  34.3 us
  transfers between devices with their start and end apart: 47, of which 17 were waited for; matrix products, arithmetic and copies ran while one was open for 10% of the time, Pallas kernels for 0%

commit v1 on v0

v1 whole, which is shorter than its diff:
```python
import functools
import math
from statistics import NormalDist

import jax
import jax.numpy as jnp
import numpy as np
from jax import lax
from jax.experimental import pallas as pl
from jax.experimental.pallas import tpu as pltpu
from jax.sharding import PartitionSpec as P

ROT = 16
eps_norm = 1e-05
rope_base = 10000.0
feature_scale = 0.5
BT = 256
LANES = 128
bf16 = jnp.bfloat16
f32 = jnp.float32
VMEM_LIMIT = 56 * 1024 * 1024


def nn(a, b):
    return lax.dot_general(a, b, (((1,), (0,)), ((), ())), preferred_element_type=f32)


def nt(a, b):
    return lax.dot_general(a, b, (((1,), (1,)), ((), ())), preferred_element_type=f32)


def tn(a, b):
    return lax.dot_general(a, b, (((0,), (0,)), ((), ())), preferred_element_type=f32)


def split(x):
    hi = x.astype(bf16)
    return hi, (x - hi.astype(f32)).astype(bf16)


def feature_table(feat_count, head_size):
    rows = np.arange(feat_count)
    cols = np.arange(head_size)
    cosines = np.cos(math.pi * (cols[None, :] + 0.5) * rows[:, None] / head_size)
    scaling = np.where(rows == 0, math.sqrt(1.0 / head_size), math.sqrt(2.0 / head_size))
    points = np.array([NormalDist().inv_cdf((r + 0.5) / feat_count) for r in range(feat_count)])
    return feature_scale * (points * scaling)[:, None] * cosines


def lane_head(shape, head_size):
    return lax.broadcasted_iota(jnp.int32, shape, len(shape) - 1) // head_size


def block_ones(size, head_size):
    rows = lax.broadcasted_iota(jnp.int32, (size, size), 0) // head_size
    cols = lax.broadcasted_iota(jnp.int32, (size, size), 1) // head_size
    return rows == cols


def swap_halves(x, head_size):
    width = x.shape[1]
    lane = lax.broadcasted_iota(jnp.int32, x.shape, 1) % head_size
    ahead = pltpu.roll(x, width - ROT // 2, 1)
    behind = pltpu.roll(x, ROT // 2, 1)
    return jnp.where(lane < ROT // 2, ahead, behind)


def widen(table, width):
    return table if table.shape[1] == width else jnp.concatenate([table] * (width // table.shape[1]), 1)


def pack_state(state, norm, head_size):
    size = state.shape[0]
    masked = jnp.where(block_ones(size, head_size), state, 0.0)
    packed = masked[:head_size]
    for h in range(1, size // head_size):
        packed = packed + masked[h * head_size : (h + 1) * head_size]
    return packed, norm


def unpack_state(packed, head_size):
    size = packed.shape[1]
    rows = jnp.concatenate([packed[:head_size]] * (size // head_size), 0)
    return jnp.where(block_ones(size, head_size), rows, 0.0)


def pre_kernel(
    head_size,
    labels_ref,
    x_ref,
    gains_ref,
    w_ref,
    bq_ref,
    fw_ref,
    tab_ref,
    cos_ref,
    sin_ref,
    valid_ref,
    seg_ref,
    ln1t_ref,
    ln2_ref,
    ln2t_ref,
    xhat_ref,
    inv_ref,
    qe_ref,
    ke_ref,
    qf_ref,
    kf_ref,
    v_ref,
    pk_ref,
    state_ref,
    norm_ref,
):
    step = pl.program_id(0)
    width = qe_ref.shape[1]
    x = x_ref[...].astype(f32)
    centered = x - jnp.mean(x, -1, keepdims=True)
    inv = lax.rsqrt(jnp.mean(centered * centered, -1, keepdims=True) + eps_norm)
    xhat = centered * inv
    inv_ref[...] = inv
    xhat_ref[...] = xhat.astype(bf16)
    ln1 = (xhat * gains_ref[0:1] + gains_ref[1:2]).astype(bf16)
    ln2 = (xhat * gains_ref[2:3] + gains_ref[3:4]).astype(bf16)
    ln2_ref[...] = ln2
    ln1t_ref[...] = ln1.T
    ln2t_ref[...] = ln2.T
    cosine = widen(cos_ref[...], width)
    sine = widen(sin_ref[...], width)

    def features(c):
        raw = nn(ln1, w_ref[c]) + bq_ref[c : c + 1]
        turned = raw * cosine + swap_halves(raw, head_size) * sine
        hi, lo = split(turned)
        return jnp.exp(nn(hi, tab_ref[0]) + nn(lo, tab_ref[0]) + nn(hi, tab_ref[1]))

    fw = fw_ref[...]
    qe = features(0)
    ke = features(1) * valid_ref[...]
    qe_ref[...] = qe
    ke_ref[...] = ke
    qf_ref[...] = (fw * qe).astype(bf16)
    kf = (fw * ke).astype(bf16)
    kf_ref[...] = kf
    v = (nn(ln1, w_ref[2]) + bq_ref[2:3]).astype(bf16)
    v_ref[...] = v

    @pl.when(step == 0)
    def _():
        state_ref[...] = jnp.zeros_like(state_ref)
        norm_ref[...] = jnp.zeros_like(norm_ref)

    tail = kf.astype(f32) * (seg_ref[...] == labels_ref[pl.num_programs(0) - 1, 1]).astype(f32)
    state_ref[...] += tn(tail.astype(bf16), v)
    norm_ref[...] += jnp.broadcast_to(jnp.sum(tail, 0, keepdims=True), norm_ref.shape)

    @pl.when(step == pl.num_programs(0) - 1)
    def _():
        packed, norm = pack_state(state_ref[...], norm_ref[...], head_size)
        pk_ref[:head_size] = packed
        pk_ref[head_size:] = norm


def ff_kernel(ln2_ref, ln2t_ref, grad_ref, win_ref, bin_ref, wdown_ref, hid_ref, dpre_ref, gdown_ref, gin_ref, gb_ref):
    rows = ln2_ref.shape[0]
    half = rows // 4
    sums = jnp.zeros((1, win_ref.shape[1]), f32)
    for r in range(4):
        part = slice(r * half, (r + 1) * half)
        pre = nn(ln2_ref[part], win_ref[...]) + bin_ref[...]
        phi_cum = 0.5 + 0.5 * lax.erf(pre * (1.0 / math.sqrt(2.0)))
        hid_ref[part] = (pre * phi_cum).astype(bf16)
        slope = phi_cum + pre * jnp.exp(-0.5 * pre * pre) * (1.0 / math.sqrt(2.0 * math.pi))
        dpre = nt(grad_ref[part], wdown_ref[...]) * slope
        sums = sums + jnp.sum(dpre, 0, keepdims=True)
        dpre_ref[part] = dpre.astype(bf16)
    gb_ref[...] = sums
    gdown_ref[...] = tn(hid_ref[...], grad_ref[...]).astype(bf16)
    gin_ref[...] = nn(ln2t_ref[...], dpre_ref[...]).astype(bf16)


def attn_kernel(
    head_size,
    labels_ref,
    qf_ref,
    kf_ref,
    v_ref,
    grad_ref,
    wout_ref,
    segc_ref,
    segr_ref,
    spk_ref,
    att_ref,
    dq_ref,
    dk_ref,
    dv_ref,
    gb_ref,
    gzb_ref,
    gpk_ref,
    state_ref,
    norm_ref,
    lead_ref,
    leadz_ref,
):
    step = pl.program_id(0)
    last = pl.num_programs(0) - 1
    rows, width = qf_ref.shape
    heads = width // head_size
    same = block_ones(width, head_size)
    ones = same.astype(f32).astype(bf16)

    def head_sum(x):
        hi, lo = split(x)
        return nn(hi, ones) + nn(lo, ones)

    @pl.when(step == 0)
    def _():
        state_ref[...] = unpack_state(spk_ref[...], head_size)
        norm_ref[...] = spk_ref[head_size : head_size + 8]
        lead_ref[...] = jnp.zeros_like(lead_ref)
        leadz_ref[...] = jnp.zeros_like(leadz_ref)

    seg = segc_ref[...]
    enters = (seg == labels_ref[step, 0]).astype(f32)
    tail = (seg == labels_ref[step, 1]).astype(f32)
    lead = (seg == labels_ref[0, 2]).astype(f32)
    linked = (labels_ref[step, 0] == labels_ref[step, 1]).astype(f32)
    qf = qf_ref[...]
    kf = kf_ref[...]
    v = v_ref[...]
    qf32 = qf.astype(f32)
    norm = norm_ref[0:1]
    lane = lane_head((rows, width), head_size)
    zero16 = jnp.zeros((rows, width), bf16)

    def stack(x):
        return jnp.concatenate([jnp.where(lane == h, x, zero16) for h in range(heads)], 0)

    def unstack(x):
        total = jnp.where(lane == 0, x[:rows], 0.0)
        for h in range(1, heads):
            total = jnp.where(lane == h, x[h * rows : (h + 1) * rows], total)
        return total

    causal = lax.broadcasted_iota(jnp.int32, (rows, rows), 0) >= lax.broadcasted_iota(
        jnp.int32, (rows, rows), 1
    )
    joined = causal & (seg == segr_ref[...])
    joined_all = jnp.concatenate([joined.astype(f32)] * heads, 0)
    q_stack = stack(qf)
    scores = (nt(q_stack, kf) * joined_all).astype(bf16)
    ones_v = jnp.ones((rows, LANES), bf16)
    sums = nn(scores, ones_v)
    den_in = jnp.where(lane == 0, widen(sums[:rows], width), 0.0)
    for h in range(1, heads):
        den_in = jnp.where(lane == h, widen(sums[h * rows : (h + 1) * rows], width), den_in)
    s_hi, s_lo = split(state_ref[...])
    num = unstack(nn(scores, v)) + enters * (nn(qf, s_hi) + nn(qf, s_lo))
    den = den_in + enters * head_sum(qf32 * norm)
    inv_den = 1.0 / den
    att = num * inv_den
    att_ref[...] = att.astype(bf16)
    d_att = nt(grad_ref[...], wout_ref[...])
    d_num = d_att * inv_den
    d_den = -head_sum(d_att * att) * inv_den
    dn_hi, dn_lo = split(d_num)
    dn_stack = stack(dn_hi)
    dden_all = jnp.concatenate([d_den[:, h * head_size : h * head_size + 1] for h in range(heads)], 0)
    d_scores = ((nt(dn_stack, v) + dden_all) * joined_all).astype(bf16)
    inter = nt(dn_hi, s_hi) + nt(dn_lo, s_hi) + nt(dn_hi, s_lo) + d_den * norm
    dq_ref[...] = unstack(nn(d_scores, kf)) + enters * inter
    dk_ref[...] = tn(d_scores, q_stack)
    dv_ref[...] = tn(scores, dn_stack)
    q_in = (qf32 * enters).astype(bf16)
    gb_ref[0] = jnp.where(same, tn(q_in, dn_hi) + tn(q_in, dn_lo), 0.0)
    weighted = qf32 * d_den
    gzb_ref[0] = jnp.broadcast_to(jnp.sum(weighted * enters, 0, keepdims=True), (8, width))
    q_lead = (qf32 * lead).astype(bf16)
    lead_ref[...] += tn(q_lead, dn_hi) + tn(q_lead, dn_lo)
    leadz_ref[...] += jnp.broadcast_to(jnp.sum(weighted * lead, 0, keepdims=True), (8, width))
    k_tail = kf.astype(f32) * tail
    state_ref[...] = linked * state_ref[...] + jnp.where(same, tn(k_tail.astype(bf16), v), 0.0)
    norm_ref[...] = linked * norm_ref[...] + jnp.broadcast_to(jnp.sum(k_tail, 0, keepdims=True), (8, width))

    @pl.when(step == last)
    def _():
        packed, z = pack_state(lead_ref[...], leadz_ref[...], head_size)
        gpk_ref[:head_size] = packed
        gpk_ref[head_size:] = z


def value_kernel(
    hid_ref,
    wdown_ref,
    att_ref,
    wout_ref,
    dpre_ref,
    win_ref,
    grad_ref,
    xhat_ref,
    gains_ref,
    val_ref,
    e2_ref,
    sums_ref,
    gwout_ref,
    acc_ref,
):
    step = pl.program_id(0)
    val_ref[...] = (nn(hid_ref[...], wdown_ref[...]) + nn(att_ref[...], wout_ref[...])).astype(bf16)
    d_ln2 = nt(dpre_ref[...], win_ref[...])
    e2_ref[...] = (d_ln2 * gains_ref[2:3]).astype(bf16)

    @pl.when(step == 0)
    def _():
        sums_ref[...] = jnp.zeros_like(sums_ref)
        acc_ref[...] = jnp.zeros_like(acc_ref)

    sums_ref[0:1] += jnp.sum(d_ln2 * xhat_ref[...].astype(f32), 0, keepdims=True)
    sums_ref[1:2] += jnp.sum(d_ln2, 0, keepdims=True)
    acc_ref[...] += tn(att_ref[...], grad_ref[...])

    @pl.when(step == pl.num_programs(0) - 1)
    def _():
        gwout_ref[...] = acc_ref[...].astype(bf16)


def tail_kernel(
    head_size,
    labels_ref,
    dq_ref,
    dk_ref,
    dv_ref,
    qe_ref,
    ke_ref,
    kf_ref,
    v_ref,
    gb_ref,
    gzb_ref,
    gin_ref,
    segc_ref,
    cos_ref,
    sin_ref,
    fw_ref,
    tab_ref,
    w_ref,
    ln1t_ref,
    xhat_ref,
    e2_ref,
    gains_ref,
    e_ref,
    stat_ref,
    sums_ref,
    small_ref,
    gw_ref,
    state_ref,
    norm_ref,
    low_ref,
):
    step = pl.program_id(0)
    last = pl.num_programs(0) - 1
    block = last - step
    rows, width = dq_ref.shape

    @pl.when(step == 0)
    def _():
        state_ref[...] = unpack_state(gin_ref[...], head_size)
        norm_ref[...] = gin_ref[head_size : head_size + 8]
        sums_ref[...] = jnp.zeros_like(sums_ref)
        small_ref[...] = jnp.zeros_like(small_ref)

    tail = (segc_ref[...] == labels_ref[block, 1]).astype(f32)
    linked = (labels_ref[block, 0] == labels_ref[block, 1]).astype(f32)
    g_hi, g_lo = split(state_ref[...])
    v = v_ref[...]
    kf = kf_ref[...]
    dk = dk_ref[...] + tail * (nt(v, g_hi) + nt(v, g_lo) + norm_ref[0:1])
    dv = dv_ref[...] + tail * (nn(kf, g_hi) + nn(kf, g_lo))
    state_ref[...] = linked * state_ref[...] + gb_ref[0]
    norm_ref[...] = linked * norm_ref[...] + gzb_ref[0]
    fw = fw_ref[...]
    gq = dq_ref[...] * qe_ref[...]
    gk = dk * ke_ref[...]
    cosine = widen(cos_ref[...], width)
    sine = widen(sin_ref[...], width)

    def back(g):
        hi, lo = split(g * fw)
        turned = nt(hi, tab_ref[0]) + nt(lo, tab_ref[0]) + nt(hi, tab_ref[1])
        return turned * cosine - swap_halves(turned, head_size) * sine

    dq_raw = back(gq)
    dk_raw = back(gk)
    small_ref[0:1] += jnp.sum(dq_raw, 0, keepdims=True)
    small_ref[1:2] += jnp.sum(dk_raw, 0, keepdims=True)
    small_ref[2:3] += jnp.sum(dv, 0, keepdims=True)
    small_ref[3:4] += jnp.sum(gq + gk, 0, keepdims=True)
    lows = [d.astype(bf16) for d in (dq_raw, dk_raw, dv)]
    d_ln1 = nt(lows[0], w_ref[0]) + nt(lows[1], w_ref[1]) + nt(lows[2], w_ref[2])
    start = pl.multiple_of(block * rows, rows)
    for c in range(3):
        low_ref[c, pl.ds(start, rows)] = lows[c]
    xhat = xhat_ref[...].astype(f32)
    e = d_ln1 * gains_ref[0:1] + e2_ref[...].astype(f32)
    e_ref[...] = e.astype(bf16)
    stat_ref[:, 0:1] = jnp.sum(e, 1, keepdims=True)
    stat_ref[:, 1:2] = jnp.sum(e * xhat, 1, keepdims=True)
    sums_ref[0:1] += jnp.sum(d_ln1 * xhat, 0, keepdims=True)
    sums_ref[1:2] += jnp.sum(d_ln1, 0, keepdims=True)

    @pl.when(step == last)
    def _():
        for c in range(3):
            gw_ref[c] = nn(ln1t_ref[...], low_ref[c]).astype(bf16)


def whole(*shape):
    return pl.BlockSpec(shape, lambda *_: (0,) * len(shape))


def rows_of(*shape):
    return pl.BlockSpec(shape, lambda i: (i,) + (0,) * (len(shape) - 1))


def smem():
    return pl.BlockSpec(memory_space=pltpu.SMEM)


def sds(shape, dtype):
    return jax.ShapeDtypeStruct(shape, dtype)


def call(kernel, grid, in_specs, out_specs, out_shape, scratch, flops, moved):
    return pl.pallas_call(
        kernel,
        grid=(grid,),
        in_specs=in_specs,
        out_specs=out_specs,
        out_shape=out_shape,
        scratch_shapes=scratch,
        compiler_params=pltpu.CompilerParams(vmem_limit_bytes=VMEM_LIMIT),
        cost_estimate=pl.CostEstimate(flops=int(flops), bytes_accessed=int(moved), transcendentals=0),
    )


def neighbour_sum(packet, sign):
    count = lax.axis_size("seq")
    outer = 4 if count % 4 == 0 else 1
    inner = count // outer
    me = lax.axis_index("seq")
    mine = me % inner
    group = packet
    before = jnp.zeros_like(packet)
    for k in range(1, inner):
        route = [(i, i - i % inner + (i % inner + k) % inner) for i in range(count)]
        got = lax.ppermute(packet, "seq", route)
        sender = (mine - k) % inner
        group = group + got
        before = before + jnp.where((sender < mine) if sign > 0 else (sender > mine), got, 0.0)
    for k in range(1, outer):
        shift = sign * k * inner
        route = [(i, i + shift) for i in range(count) if 0 <= i + shift < count]
        before = before + lax.ppermute(group, "seq", route)
    return before


def body(
    tokens,
    lengths,
    pad_mask,
    ln1_gain,
    ln1_bias,
    ln2_gain,
    ln2_bias,
    w_qkv,
    b_qkv,
    feat_weight,
    w_out,
    b_out,
    w_in,
    b_in,
    w_down,
    b_down,
    grad_out,
):
    rows, share = tokens.shape
    heads, feats = feat_weight.shape
    width = w_qkv.shape[2]
    head_size = width // heads
    model, hidden = w_in.shape
    blocks = rows // BT
    n_head = lax.axis_size("head")
    offset = lax.axis_index("head") * share
    full_tokens = lax.all_gather(tokens, "head", axis=1, tiled=True)
    full_grad = lax.all_gather(grad_out, "head", axis=1, tiled=True)

    index_all = lax.axis_index("seq") * rows + jnp.arange(rows, dtype=jnp.int32)
    seq_ends = jnp.cumsum(lengths).astype(jnp.int32)
    starts = seq_ends - lengths

    def seg_of(index):
        return jnp.sum((index[:, None] >= seq_ends[None, :]).astype(jnp.int32), 1)

    segment = seg_of(index_all)
    picked = segment[:, None] == jnp.arange(lengths.shape[0])[None, :]
    position = index_all - jnp.sum(jnp.where(picked, starts[None, :], 0), 1)
    base = lax.axis_index("seq") * rows + jnp.arange(blocks, dtype=jnp.int32) * BT
    label_in = seg_of(jnp.maximum(base - 1, 0))
    label_last = seg_of(base + (BT - 1))
    label_first = jnp.broadcast_to(segment[0], (blocks,))
    labels = jnp.stack([label_in, label_last, label_first], 1)
    seg_col = segment[:, None]
    seg_row = segment[None, :]
    lane = np.arange(LANES) % head_size
    inverse = np.where(lane < ROT, rope_base ** (-2.0 * (lane % (ROT // 2)) / ROT), 0.0)
    angles = position.astype(f32)[:, None] * jnp.asarray(inverse, f32)[None, :]
    sign = np.where(lane < ROT // 2, -1.0, np.where(lane < ROT, 1.0, 0.0))
    cosine = jnp.cos(angles)
    sine = jnp.sin(angles) * jnp.asarray(sign, f32)[None, :]
    valid = pad_mask.astype(f32)[:, None]
    table = np.kron(np.eye(heads), feature_table(feats, head_size).T).astype(np.float32)
    table_hi = table.astype(bf16)
    table_lo = (table - table_hi.astype(np.float32)).astype(bf16)
    tab = jnp.asarray(np.stack([table_hi, table_lo]))
    gains = jnp.stack([ln1_gain, ln1_bias, ln2_gain, ln2_bias])
    fw = feat_weight.reshape(1, width)
    packet_shape = (head_size + 8, width)

    ln1t, ln2, ln2t, xhat, inv_std, q_expo, k_expo, qf, kf, v, s_own = call(
        functools.partial(pre_kernel, head_size),
        blocks,
        [
            smem(),
            rows_of(BT, model),
            whole(4, model),
            whole(3, model, width),
            whole(3, width),
            whole(1, width),
            whole(2, width, width),
            rows_of(BT, LANES),
            rows_of(BT, LANES),
            rows_of(BT, 1),
            rows_of(BT, 1),
        ],
        [
            pl.BlockSpec((model, BT), lambda i: (0, i)),
            rows_of(BT, model),
            pl.BlockSpec((model, BT), lambda i: (0, i)),
            rows_of(BT, model),
            rows_of(BT, 1),
            rows_of(BT, width),
            rows_of(BT, width),
            rows_of(BT, width),
            rows_of(BT, width),
            rows_of(BT, width),
            whole(*packet_shape),
        ],
        [
            sds((model, rows), bf16),
            sds((rows, model), bf16),
            sds((model, rows), bf16),
            sds((rows, model), bf16),
            sds((rows, 1), f32),
            sds((rows, width), f32),
            sds((rows, width), f32),
            sds((rows, width), bf16),
            sds((rows, width), bf16),
            sds((rows, width), bf16),
            sds(packet_shape, f32),
        ],
        [pltpu.VMEM((width, width), f32), pltpu.VMEM((8, width), f32)],
        2 * rows * model * 3 * width + 16 * rows * width * width,
        rows * model * 10 + 6 * model * width,
    )(labels, full_tokens, gains, w_qkv, b_qkv, fw, tab, cosine, sine, valid, seg_col)

    s_in = neighbour_sum(s_own, 1)

    fb = 256
    hid, dpre, g_down, g_in, gb_in = call(
        ff_kernel,
        hidden // fb,
        [
            whole(rows, model),
            whole(model, rows),
            whole(rows, model),
            pl.BlockSpec((model, fb), lambda i: (0, i)),
            pl.BlockSpec((1, fb), lambda i: (0, i)),
            pl.BlockSpec((fb, model), lambda i: (i, 0)),
        ],
        [
            pl.BlockSpec((rows, fb), lambda i: (0, i)),
            pl.BlockSpec((rows, fb), lambda i: (0, i)),
            pl.BlockSpec((fb, model), lambda i: (i, 0)),
            pl.BlockSpec((model, fb), lambda i: (0, i)),
            pl.BlockSpec((1, fb), lambda i: (0, i)),
        ],
        [
            sds((rows, hidden), bf16),
            sds((rows, hidden), bf16),
            sds((hidden, model), bf16),
            sds((model, hidden), bf16),
            sds((1, hidden), f32),
        ],
        [],
        8 * rows * model * hidden,
        6 * rows * model + 8 * model * hidden,
    )(ln2, ln2t, full_grad, w_in, b_in[None, :], w_down)

    g_down = lax.psum(g_down, "seq")
    g_in = lax.psum(g_in, "seq")

    att, dq, dk, dv, gb, gzb, g_own = call(
        functools.partial(attn_kernel, head_size),
        blocks,
        [
            smem(),
            rows_of(BT, width),
            rows_of(BT, width),
            rows_of(BT, width),
            rows_of(BT, model),
            whole(width, model),
            rows_of(BT, 1),
            pl.BlockSpec((1, BT), lambda i: (0, i)),
            whole(*packet_shape),
        ],
        [
            rows_of(BT, width),
            rows_of(BT, width),
            rows_of(BT, width),
            rows_of(BT, width),
            rows_of(1, width, width),
            rows_of(1, 8, width),
            whole(*packet_shape),
        ],
        [
            sds((rows, width), bf16),
            sds((rows, width), f32),
            sds((rows, width), f32),
            sds((rows, width), f32),
            sds((blocks, width, width), f32),
            sds((blocks, 8, width), f32),
            sds(packet_shape, f32),
        ],
        [
            pltpu.VMEM((width, width), f32),
            pltpu.VMEM((8, width), f32),
            pltpu.VMEM((width, width), f32),
            pltpu.VMEM((8, width), f32),
        ],
        24 * rows * heads * BT * width,
        rows * model * 2 + rows * width * 20,
    )(labels, qf, kf, v, full_grad, w_out, seg_col, seg_row, s_in)

    grad_in = neighbour_sum(g_own, -1)

    value, e2, sums2, g_out = call(
        value_kernel,
        blocks,
        [
            rows_of(BT, hidden),
            whole(hidden, model),
            rows_of(BT, width),
            whole(width, model),
            rows_of(BT, hidden),
            whole(model, hidden),
            rows_of(BT, model),
            rows_of(BT, model),
            whole(4, model),
        ],
        [rows_of(BT, model), rows_of(BT, model), whole(8, model), whole(width, model)],
        [
            sds((rows, model), bf16),
            sds((rows, model), bf16),
            sds((8, model), f32),
            sds((width, model), bf16),
        ],
        [pltpu.VMEM((width, model), f32)],
        4 * rows * model * (hidden + width),
        12 * rows * model + 4 * model * hidden,
    )(hid, w_down, att, w_out, dpre, w_in, full_grad, xhat, gains)

    mixed_share = lax.psum_scatter(value, "head", scatter_dimension=1, tiled=True)

    def back_rows(*shape):
        return pl.BlockSpec(shape, lambda i: (blocks - 1 - i,) + (0,) * (len(shape) - 1))

    e_part, stats, sums1, small, g_qkv = call(
        functools.partial(tail_kernel, head_size),
        blocks,
        [
            smem(),
            back_rows(BT, width),
            back_rows(BT, width),
            back_rows(BT, width),
            back_rows(BT, width),
            back_rows(BT, width),
            back_rows(BT, width),
            back_rows(BT, width),
            back_rows(1, width, width),
            back_rows(1, 8, width),
            whole(*packet_shape),
            back_rows(BT, 1),
            back_rows(BT, LANES),
            back_rows(BT, LANES),
            whole(1, width),
            whole(2, width, width),
            whole(3, model, width),
            whole(model, rows),
            back_rows(BT, model),
            back_rows(BT, model),
            whole(4, model),
        ],
        [
            back_rows(BT, model),
            back_rows(BT, 2),
            whole(8, model),
            whole(8, width),
            whole(3, model, width),
        ],
        [
            sds((rows, model), bf16),
            sds((rows, 2), f32),
            sds((8, model), f32),
            sds((8, width), f32),
            sds((3, model, width), bf16),
        ],
        [
            pltpu.VMEM((width, width), f32),
            pltpu.VMEM((8, width), f32),
            pltpu.VMEM((3, rows, width), bf16),
        ],
        4 * rows * model * 3 * width,
        rows * width * 30 + rows * model * 8,
    )(
        labels,
        dq,
        dk,
        dv,
        q_expo,
        k_expo,
        kf,
        v,
        gb,
        gzb,
        grad_in,
        seg_col,
        cosine,
        sine,
        fw,
        tab,
        w_qkv,
        ln1t,
        xhat,
        e2,
        gains,
    )

    g_qkv, g_out = lax.psum((g_qkv, g_out), "seq")
    e_share = lax.psum_scatter(e_part, "head", scatter_dimension=1, tiled=True)
    stats, gain_sums = lax.psum((stats, jnp.concatenate([sums1[:2], sums2[:2]], 0)), "head")
    bias_out = jnp.sum(grad_out.astype(f32), 0)
    gain_share = lax.dynamic_slice_in_dim(gain_sums, offset, share, 1)
    gain_share, small, gb_in, bias_out = lax.psum((gain_share, small[:4], gb_in, bias_out), "seq")

    bias = lax.dynamic_slice_in_dim(b_out, offset, share) + lax.dynamic_slice_in_dim(b_down, offset, share)
    mixed = (tokens.astype(f32) + mixed_share.astype(f32) + bias).astype(bf16)
    xhat_share = lax.dynamic_slice_in_dim(xhat, offset, share, 1).astype(f32)
    stats = stats * (1.0 / model)
    grad_input = grad_out.astype(f32) + inv_std * (
        e_share.astype(f32) - stats[:, 0:1] - xhat_share * stats[:, 1:2]
    )
    return (
        mixed,
        grad_input,
        gain_share[0],
        gain_share[1],
        gain_share[2],
        gain_share[3],
        g_qkv.astype(f32),
        small[:3],
        small[3].reshape(heads, feats),
        g_out.astype(f32),
        bias_out,
        g_in.astype(f32),
        gb_in[0],
        g_down.astype(f32),
        bias_out,
    )


def solution(mesh):
    in_specs = (
        P("seq", "head"),
        P(),
        P("seq"),
        P(),
        P(),
        P(),
        P(),
        P(None, None, "head"),
        P(None, "head"),
        P("head", None),
        P("head", None),
        P(),
        P(None, "head"),
        P("head"),
        P("head", None),
        P(),
        P("seq", "head"),
    )
    out_specs = (
        P("seq", "head"),
        P("seq", "head"),
        P("head"),
        P("head"),
        P("head"),
        P("head"),
        P(None, None, "head"),
        P(None, "head"),
        P("head", None),
        P("head", None),
        P("head"),
        P(None, "head"),
        P("head"),
        P("head", None),
        P("head"),
    )
    return jax.shard_map(body, mesh=mesh, in_specs=in_specs, out_specs=out_specs, check_vma=False)
```

time: 1020 us -> 403 us (0.40); the launches traced: 1000 us -> 399 us
  waiting for transfers between devices: 505 us -> 216 us
  matrix products: 128 us -> 0 us
  local copies, waits for them, and re-layouts: 114 us -> 10.1 us
  starting transfers between devices: 116 us -> 17.4 us
  Pallas kernels: 0 us -> 66.5 us
  loops' own time: 33.9 us -> 0 us
  other arithmetic: 45 us -> 23.4 us
    psum x2 -> x1, waiting for transfers between devices: 448 us -> 178 us  [body(): g_qkv, g_out = lax.psum((g_qkv, g_out), 'seq')]
    dot_general x47 -> x0, matrix products: 128 us -> none  [the longest x1 14 us: body(): pre_act = jnp.dot(ln2_out, w_in, preferred_element_type=jnp.float32) + b_in]
    ppermute x42 -> x8, starting transfers between devices: 115 us -> 17.2 us  [the longest x6 14.2 us: neighbour_sum(): before = before + lax.ppermute(group, 'seq', route)]
    pallas_call x0 -> x5, Pallas kernels: none -> 66.5 us  [the longest x1 14.9 us: body(): call(ff_kernel, hidden // fb, [whole(rows, model), whole(model, rows), wh...]
    dynamic_update_slice x14 -> x0, local copies, waits for them, and re-layouts: 52.1 us -> none  [body(): lax.scan(forward_block, carried, (blocks(query_feat), blocks(key_feat), b...]
    another operation x4 -> x0, loops' own time: 33.9 us -> none  [the longest x1 14.4 us: body(): lax.fori_loop(0, lax.axis_size('seq') - 1, forward_turn, zero_carry)]
    ppermute x42 -> x8, waiting for transfers between devices: 37.1 us -> 10.4 us  [the longest x2 6.1 us: neighbour_sum(): got = lax.ppermute(packet, 'seq', route)]
    reduce_sum x10 -> x4, other arithmetic: 21.8 us -> 3.03 us  [the longest x1 2.65 us: body(): bias_out = jnp.sum(grad_out.astype(f32), 0)]
  transfers between devices with their start and end apart: 47 -> 13, of which waited for: 17 -> 7; matrix products, arithmetic and copies ran while one was open for 10% -> 5% of each run, Pallas kernels for 0% -> 10%
where the time goes in v1:
time: 403 us; the launch traced here: 399 us
  waiting for transfers between devices  216 us (54%)
  Pallas kernels  66.5 us (17%)
  blocking collectives  51.8 us (13%)
  other arithmetic  23.4 us (6%)
  starting transfers between devices  17.4 us (4%)
  between operations  14.1 us (3%)
  local copies, waits for them, and re-layouts  10.1 us (3%)
    psum x1, waiting for transfers between devices, body(): g_qkv, g_out = lax.psum((g_qkv, g_out), 'seq')  178 us
    psum x1, blocking collectives, body(): lax.psum((gain_share, small[:4], gb_in, bias_out), 'seq')  35.6 us
    psum x1, blocking collectives, body(): lax.psum((stats, jnp.concatenate([sums1[:2], sums2[:2]], 0)), 'head')  16.2 us
    pallas_call x1, Pallas kernels, body(): call(ff_kernel, hidden // fb, [whole(rows, model), whole(model, rows), wh...  14.9 us
    ppermute x6, starting transfers between devices, neighbour_sum(): before = before + lax.ppermute(group, 'seq', route)  14.2 us
    all_gather x1, waiting for transfers between devices, body(): full_tokens = lax.all_gather(tokens, 'head', axis=1, tiled=True)  13.7 us
    pallas_call x1, Pallas kernels, body(): call(functools.partial(tail_kernel, head_size), blocks, [smem(), back_row...  13.6 us
    pallas_call x1, Pallas kernels, body(): call(functools.partial(pre_kernel, head_size), blocks, [smem(), rows_of(B...  13.2 us
  transfers between devices with their start and end apart: 13, of which 7 were waited for; matrix products, arithmetic and copies ran while one was open for 5% of the time, Pallas kernels for 10%

profile of v1, /device:TPU:8, one launch (start us, length us, event | category | flops | bytes accessed | tf_op | source)
XLA Modules:
  0.0 399.4 jit_solution(12903215807562373697)
XLA Ops:
  7.3 0.0 all-gather.3.cloned.1.call-start
  7.3 0.7 all-gather.3.cloned.1.call-update
  8.0 0.0 all-gather.5.cloned.1.call-start
  8.0 0.7 all-gather.5.cloned.1.call-update
  8.7 0.0 reduce-scatter.3.cloned.1.call-start
  8.8 1.3 reshape.83.fw_ref
  10.1 0.8 reduce-window.8
  11.0 0.2 convert_reduce_fusion.3
  11.2 0.1 copy.44
  11.3 0.1 copy.43
  11.4 0.7 convert_element_type.55
  12.1 0.1 convert_reduce_fusion.1
  12.2 0.5 slice.36
  12.7 0.7 pad.8.clone
  13.4 1.0 copy.45.valid_ref
  14.4 1.1 copy.46.seg_ref.segc_ref
  15.5 0.6 pad_maximum_fusion.gains_ref
  16.1 0.1 select_reduce_fusion
  16.2 0.7 add_add_fusion.2.labels_ref
  16.9 3.1 fusion
  19.9 13.7 %all-gather.3.cloned.1.call-done.x_ref = bf16[1024,1024]{1,0:T(8,128)(2,1)} async-done(((bf16[1024,256]{1,0:T(8,128)(2,1)}), bf16[1024,1024]{1,0:T(8,128)(2,1)}) %all-gather.3.cloned.1.call-update) | async-done | bytes 2097168 | tf_op jit(solution)/shard_map/all_gather | solution.py:492
  33.7 13.2 %shard_map.307 = (bf16[1024,1024]{1,0:T(8,128)(2,1)}, bf16[1024,1024]{1,0:T(8,128)(2,1)}, bf16[1024,1024]{1,0:T(8,128)(2,1)}, bf16[1024,1024]{1,0:T(8,128)(2,1)}...) custom-call(s32[4,3]{1,0:T(4,128)} %add_add_fusion.2.labels_ref, ...), custom_call_target="tpu_custom_call" | custom-call | flops 2684354560 | bytes 12058624 | tf_op jit(solution)/shard_map/pallas_call | solution.py:527
  46.9 1.5 collective-permute-start
  48.4 3.2 collective-permute-done
  51.6 0.9 add.126
  52.5 0.7 collective-permute-start.3
  53.2 5.0 %collective-permute-start.2 = (f32[72,256]{1,0:T(8,128)S(1)}, f32[72,256]{1,0:T(8,128)S(1)}, u32[]{:S(2)}, u32[]{:S(2)}) collective-permute-start(f32[72,256]{1,0:T(8,128)S(1)} %add.126), channel_id=1, source_target_pairs={{0,16},{4,20},{8,24},{12,28},{1,17},{5,21},{9,25},{13,29},{2,18},{... | collective-permute-start | bytes 221192 | tf_op jit(solution)/shard_map/ppermute | solution.py:461
  58.2 1.9 collective-permute-start.1
  60.1 14.9 %shard_map.308 = (bf16[1024,1024]{1,0:T(8,128)(2,1)}, bf16[1024,1024]{1,0:T(8,128)(2,1)}, bf16[1024,1024]{1,0:T(8,128)(2,1)}, bf16[1024,1024]{1,0:T(8,128)(2,1)}, f32[1,1024]{1,0:T(1,128)}) custom-call(bf16[1024,1024]{1,0:T(8,128)(2,1)} %get-tuple-element.47.ln2_ref, bf16[1024,1024]{1,0:T(8,128)(2,1)} %get-tuple-element.48.ln2t_ref, ...), custom_call_target="tpu_custom_call" | custom-call | flops 8589934592 | bytes 14680064 | tf_op jit(solution)/shard_map/pallas_call | solution.py:577
  75.0 0.7 add_add_fusion.1.spk_ref
  75.7 12.4 %shard_map.309 = (bf16[1024,256]{1,0:T(8,128)(2,1)}, f32[1024,256]{1,0:T(8,128)}, f32[1024,256]{1,0:T(8,128)}, f32[1024,256]{1,0:T(8,128)}, f32[4,256,256]{2,1,0...) custom-call(s32[4,3]{1,0:T(4,128)} %add_add_fusion.2.labels_ref, bf16[1024,256]{1,0:T(8,128)(2,1)} %get-tuple-element.50.qf_ref, ...), custom_call_target="tpu_custom_call" | custom-call | flops 6442450944 | bytes 7340032 | tf_op jit(solution)/shard_map/pallas_call | solution.py:610
  88.1 12.4 %shard_map.310 = (bf16[1024,1024]{1,0:T(8,128)(2,1)}, bf16[1024,1024]{1,0:T(8,128)(2,1)}, f32[8,1024]{1,0:T(8,128)}, bf16[256,1024]{1,0:T(8,128)(2,1)}) custom-call(bf16[1024,1024]{1,0:T(8,128)(2,1)} %get-tuple-element.49.hid_ref, bf16[1024,1024]{1,0:T(8,128)(2,1)} %wdown_ref.3, bf16[1024,256]{1,0:T(8,128)(2,1)} %get-tuple-element.54.att_ref, ...), custom_call_target="tpu_custom_call" | custom-call | flops 5368709120 | bytes 16777216 | tf_op jit(solution)/shard_map/pallas_call | solution.py:654
  100.6 0.0 reduce-scatter.5.cloned.1.call-start
  100.6 0.8 copy-done.7
  101.4 1.4 collective-permute-start.4
  102.8 2.9 collective-permute-done.4
  105.8 0.7 collective-permute-start.7
  106.5 1.3 collective-permute-start.6
  107.8 4.7 %collective-permute-start.5 = (f32[72,256]{1,0:T(8,128)S(1)}, f32[72,256]{1,0:T(8,128)S(1)}, u32[]{:S(2)}, u32[]{:S(2)}) collective-permute-start(f32[72,256]{1,0:T(8,128)S(1)} %add.135), channel_id=1, source_target_pairs={{8,0},{12,4},{16,8},{20,12},{24,16},{28,20},{9,1},{13,5},{17,9},{2... | collective-permute-start | bytes 221192 | tf_op jit(solution)/shard_map/ppermute | solution.py:461
  112.5 3.5 collective-permute-done.6
  116.0 0.8 collective-permute-done.5
  116.8 0.6 add_add_fusion.gin_ref
  117.4 13.6 %shard_map.311 = (bf16[1024,1024]{1,0:T(8,128)(2,1)}, f32[1024,2]{1,0:T(8,128)}, f32[8,1024]{1,0:T(8,128)}, f32[8,256]{1,0:T(8,128)}, bf16[3,1024,256]{2,1,0:T(8,128)(2,1)}) custom-call(s32[4,3]{1,0:T(4,128)} %add_add_fusion.2.labels_ref, f32[1024,256]{1,0:T(8,128)} %get-tuple-element.59.dq_ref, f32[1024,256]{1,0:T(8,128)} %get-tuple-element.60.dk_ref, ...), custom_call_target="tpu_custom_call" | custom-call | flops 3221225472 | bytes 16252928 | tf_op jit(solution)/shard_map/pallas_call | solution.py:685
  131.1 0.0 all-reduce.5.cloned.1.call-start
  131.2 0.5 all-reduce.5.cloned.1.call-update
  131.7 0.8 dynamic-slice_add_fusion
  132.5 0.2 reduce
  132.7 0.8 slice.40
  133.5 0.8 slice.39
  134.3 16.2 %all-reduce.1 = (f32[1024,2]{1,0:T(8,128)S(1)}, f32[4,1024]{1,0:T(4,128)S(1)}) all-reduce(f32[1024,2]{1,0:T(8,128)S(1)} %copy-done.6, f32[4,1024]{1,0:T(4,128)S(1)} %pad_maximum_fusion.1), channel_id=1, replica_groups=mesh['seq'=8,'head'=4] {'head'}, use_global_device_ids=true, to_apply=%region_7.8 | all-reduce | flops 6144 | bytes 49152 | tf_op jit(solution)/shard_map/psum | solution.py:758
  150.6 0.5 slice_reduce_fusion.1
  151.1 2.0 add_convert_fusion
  153.1 11.9 %reduce-scatter.5.cloned.1.call-done = bf16[1024,256]{1,0:T(8,128)(2,1)} async-done(((bf16[1024,1024]{1,0:T(8,128)(2,1)}), bf16[1024,256]{1,0:T(8,128)(2,1)}) %reduce-scatter.5.cloned.1.call-update) | async-done | bytes 524304 | tf_op jit(solution)/shard_map/reduce_scatter | solution.py:757
  165.0 2.7 convert_reduce_fusion
  167.6 35.6 %all-reduce = (f32[4,256]{1,0:T(4,128)S(1)}, f32[4,256]{1,0:T(4,128)S(1)}, f32[256]{0:T(256)S(1)}, f32[1024]{0:T(1024)}) all-reduce(f32[4,256]{1,0:T(4,128)S(1)} %constant_dynamic-slice_fusion, f32[4,256]{1,0:T(4,128)S(1)} %slice.45, f32[256]{0:T(256)S(1)} %get-tuple-element.93, ...), channel_id=1, replica_groups=mesh['seq'=8,'head'=4] {'seq'}, use_global_device_ids=true, to_apply=%region_9.10 | all-reduce | flops 3328 | bytes 26624 | tf_op jit(solution)/shard_map/psum | solution.py:761
  203.3 0.7 reshape_squeeze.3
  203.9 0.6 fusion.2
  204.5 178.1 %all-reduce.5.cloned.1.call-done = (bf16[3,1024,256]{2,1,0:T(8,128)(2,1)}, bf16[256,1024]{1,0:T(8,128)(2,1)}, bf16[1024,1024]{1,0:T(8,128)(2,1)}, bf16[1024,1024]{1,0:T(8,128)(2,1)}) async-done(((bf16[3,1024,256]{2,1,0:T(8,128)(2,1)}, bf16[256,1024]{1,0:T(8,128)(2,1)}, bf16[1024,1024]{1,0:T(8,128)(2,1)}, bf16[1024,1024]{1,0:T(8,128)(2,1)}), (bf16[3,1024,256]{2,1,0:T(8,128)(2,1)}, ...) | async-done | bytes 6291472 | tf_op jit(solution)/shard_map/psum | solution.py:756
  382.6 2.2 convert_element_type.62
  384.9 1.9 convert_element_type.61
  386.8 0.5 copy-done.1
  387.3 2.5 convert_element_type.63
  389.8 2.5 convert_element_type.64
  392.3 0.6 copy.54
  (56 shorter events, 0.3 us)
Async XLA Ops:
  7.2 9.7 %copy-start.16 = (f32[128]{0:T(128)S(1)}, f32[128]{0:T(128)}, u32[]{:S(2)}) copy-start(f32[128]{0:T(128)} %constant.58.clone) | copy-start | bytes 1540
  7.2 9.7 %copy-start.17 = (f32[128]{0:T(128)S(1)}, f32[128]{0:T(128)}, u32[]{:S(2)}) copy-start(f32[128]{0:T(128)} %constant.57.clone) | copy-start | bytes 1540
  7.2 8.9 %copy-start.19 = (s32[4]{0:T(128)S(1)}, s32[4]{0:T(128)}, u32[]{:S(2)}) copy-start(s32[4]{0:T(128)} %param.21) | copy-start | bytes 52
  7.2 8.3 %copy-start.10 = (f32[1024]{0:T(1024)S(1)}, f32[1024]{0:T(1024)}, u32[]{:S(2)}) copy-start(f32[1024]{0:T(1024)} %param.26) | copy-start | bytes 12292
  7.2 8.2 %copy-start.11 = (f32[1024]{0:T(1024)S(1)}, f32[1024]{0:T(1024)}, u32[]{:S(2)}) copy-start(f32[1024]{0:T(1024)} %param.25) | copy-start | bytes 12292
  7.2 8.2 %copy-start.12 = (f32[1024]{0:T(1024)S(1)}, f32[1024]{0:T(1024)}, u32[]{:S(2)}) copy-start(f32[1024]{0:T(1024)} %param.24) | copy-start | bytes 12292
  7.2 8.2 %copy-start.13 = (f32[1024]{0:T(1024)S(1)}, f32[1024]{0:T(1024)}, u32[]{:S(2)}) copy-start(f32[1024]{0:T(1024)} %param.23) | copy-start | bytes 12292
  7.3 26.4 %all-gather.3.cloned.1.call-start = ((), (), s32[]{:S(2)}) async-start(), calls=%async_computation.2 | async-start | bytes 2621440 | tf_op jit(solution)/shard_map/all_gather | solution.py:492
  8.0 52.1 %all-gather.5.cloned.1.call-start = ((), (), s32[]{:S(2)}) async-start(), calls=%async_computation.3 | async-start | bytes 2621440 | tf_op jit(solution)/shard_map/all_gather | solution.py:493
  8.7 142.3 %reduce-scatter.3.cloned.1.call-start = ((), (), s32[]{:S(2)}) async-start(), calls=%async_computation.4 | async-start | bytes 2621440 | tf_op jit(solution)/shard_map/reduce_scatter | solution.py:680
  12.1 34.7 %copy-start.8 = (s32[1024]{0:T(1024)}, s32[1024]{0:T(1024)S(1)}, u32[]{:S(2)}) copy-start(s32[1024]{0:T(1024)S(1)} %convert_reduce_fusion.1) | copy-start | bytes 12292
  46.9 4.7 %collective-permute-start = (f32[72,256]{1,0:T(8,128)}, f32[72,256]{1,0:T(8,128)S(1)}, u32[]{:S(2)}, u32[]{:S(2)}) collective-permute-start(f32[72,256]{1,0:T(8,128)} %get-tuple-element.53), channel_id=1, source_target_pairs={{0,4},{4,0},{8,12},{12,8},{16,20},{20,16},{24,28},{28,24},{1,5},{5... | collective-permute-start | bytes 221192 | tf_op jit(solution)/shard_map/ppermute | solution.py:454
  52.5 22.5 %collective-permute-start.3 = (f32[72,256]{1,0:T(8,128)S(1)}, f32[72,256]{1,0:T(8,128)S(1)}, u32[]{:S(2)}, u32[]{:S(2)}) collective-permute-start(f32[72,256]{1,0:T(8,128)S(1)} %add.126), channel_id=1, source_target_pairs={{0,24},{4,28},{1,25},{5,29},{2,26},{6,30},{3,27},{7,31}} | collective-permute-start | bytes 221192 | tf_op jit(solution)/shard_map/ppermute | solution.py:461
  53.2 21.9 %collective-permute-start.2 = (f32[72,256]{1,0:T(8,128)S(1)}, f32[72,256]{1,0:T(8,128)S(1)}, u32[]{:S(2)}, u32[]{:S(2)}) collective-permute-start(f32[72,256]{1,0:T(8,128)S(1)} %add.126), channel_id=1, source_target_pairs={{0,16},{4,20},{8,24},{12,28},{1,17},{5,21},{9,25},{13,29},{2,18},{... | collective-permute-start | bytes 221192 | tf_op jit(solution)/shard_map/ppermute | solution.py:461
  58.2 16.9 %collective-permute-start.1 = (f32[72,256]{1,0:T(8,128)S(1)}, f32[72,256]{1,0:T(8,128)S(1)}, u32[]{:S(2)}, u32[]{:S(2)}) collective-permute-start(f32[72,256]{1,0:T(8,128)S(1)} %add.126), channel_id=1, source_target_pairs={{0,8},{4,12},{8,16},{12,20},{16,24},{20,28},{1,9},{5,13},{9,17},{1... | collective-permute-start | bytes 221192 | tf_op jit(solution)/shard_map/ppermute | solution.py:461
  100.5 0.9 copy-start.7
  100.6 64.4 %reduce-scatter.5.cloned.1.call-start = ((), (), s32[]{:S(2)}) async-start(), calls=%async_computation.5 | async-start | bytes 2621440 | tf_op jit(solution)/shard_map/reduce_scatter | solution.py:757
  101.4 4.4 %collective-permute-start.4 = (f32[72,256]{1,0:T(8,128)S(1)}, f32[72,256]{1,0:T(8,128)S(1)}, u32[]{:S(2)}, u32[]{:S(2)}) collective-permute-start(f32[72,256]{1,0:T(8,128)S(1)} %copy-done.7), channel_id=1, source_target_pairs={{0,4},{4,0},{8,12},{12,8},{16,20},{20,16},{24,28},{28,24},{1,5},{5... | collective-permute-start | bytes 221192 | tf_op jit(solution)/shard_map/ppermute | solution.py:454
  105.8 6.7 %collective-permute-start.7 = (f32[72,256]{1,0:T(8,128)S(1)}, f32[72,256]{1,0:T(8,128)S(1)}, u32[]{:S(2)}, u32[]{:S(2)}) collective-permute-start(f32[72,256]{1,0:T(8,128)S(1)} %add.135), channel_id=1, source_target_pairs={{24,0},{28,4},{25,1},{29,5},{26,2},{30,6},{27,3},{31,7}} | collective-permute-start | bytes 221192 | tf_op jit(solution)/shard_map/ppermute | solution.py:461
  106.5 9.5 %collective-permute-start.6 = (f32[72,256]{1,0:T(8,128)S(1)}, f32[72,256]{1,0:T(8,128)S(1)}, u32[]{:S(2)}, u32[]{:S(2)}) collective-permute-start(f32[72,256]{1,0:T(8,128)S(1)} %add.135), channel_id=1, source_target_pairs={{16,0},{20,4},{24,8},{28,12},{17,1},{21,5},{25,9},{29,13},{18,2},{... | collective-permute-start | bytes 221192 | tf_op jit(solution)/shard_map/ppermute | solution.py:461
  107.8 9.0 %collective-permute-start.5 = (f32[72,256]{1,0:T(8,128)S(1)}, f32[72,256]{1,0:T(8,128)S(1)}, u32[]{:S(2)}, u32[]{:S(2)}) collective-permute-start(f32[72,256]{1,0:T(8,128)S(1)} %add.135), channel_id=1, source_target_pairs={{8,0},{12,4},{16,8},{20,12},{24,16},{28,20},{9,1},{13,5},{17,9},{2... | collective-permute-start | bytes 221192 | tf_op jit(solution)/shard_map/ppermute | solution.py:461
  131.1 251.5 %all-reduce.5.cloned.1.call-start = ((), (), s32[]{:S(2)}) async-start(), calls=%async_computation.6 | async-start | bytes 12582912 | tf_op jit(solution)/shard_map/psum | solution.py:756
  131.1 1.4 copy-start.5
  131.1 2.4 copy-start.14
  131.1 3.1 copy-start.6
  131.7 19.4 %copy-start.2 = (bf16[1024,256]{1,0:T(8,128)(2,1)S(1)}, bf16[1024,256]{1,0:T(8,128)(2,1)}, u32[]{:S(2)}) copy-start(bf16[1024,256]{1,0:T(8,128)(2,1)} %param.20) | copy-start | bytes 1572868
  134.3 30.7 %copy-start.3 = (bf16[1024,256]{1,0:T(8,128)(2,1)S(1)}, bf16[1024,256]{1,0:T(8,128)(2,1)}, u32[]{:S(2)}) copy-start(bf16[1024,256]{1,0:T(8,128)(2,1)} %param.36) | copy-start | bytes 1572868
  151.1 16.6 %copy-start.9 = (f32[1,1024]{1,0:T(1,128)S(1)}, f32[1,1024]{1,0:T(1,128)}, u32[]{:S(2)}) copy-start(f32[1,1024]{1,0:T(1,128)} %get-tuple-element.77) | copy-start | bytes 12292
  203.3 183.5 %copy-start.18 = (f32[4,256]{1,0:T(4,128)}, f32[4,256]{1,0:T(4,128)S(1)}, u32[]{:S(2)}) copy-start(f32[4,256]{1,0:T(4,128)S(1)} %get-tuple-element.84) | copy-start | bytes 12292
  203.3 189.0 %copy-start.15 = (f32[256]{0:T(256)}, f32[256]{0:T(256)S(1)}, u32[]{:S(2)}) copy-start(f32[256]{0:T(256)S(1)} %get-tuple-element.132) | copy-start | bytes 3076
  382.6 2.2 copy-start.4
  384.9 2.4 copy-start.1
  387.3 2.5 copy-start
Sparse Core Ops, SparseCore 0:
  9.6 23.9 all-gather.2
  35.2 22.8 all-gather.4
  100.7 30.0 reduce-scatter.2
  133.3 31.5 reduce-scatter.4
  169.2 213.3 all-reduce.4

commit v2 on v1

--- a/solution.py
+++ b/solution.py
@@ -18,6 +18,8 @@
 LANES = 128
 bf16 = jnp.bfloat16
 f32 = jnp.float32
+COST_SCALE = 0.02
+END_COST = 12
 VMEM_LIMIT = 56 * 1024 * 1024
 
 
@@ -84,36 +86,50 @@
     return jnp.where(block_ones(size, head_size), rows, 0.0)
 
 
+def place(full_ref, piece_refs, me_ref):
+    for k, ref in enumerate(piece_refs):
+        size = ref.shape[1]
+        start = pl.multiple_of((me_ref[0] ^ k) * size, LANES)
+        full_ref[:, pl.ds(start, size)] = ref[...]
+
+
 def pre_kernel(
     head_size,
+    pieces,
     labels_ref,
-    x_ref,
-    gains_ref,
-    w_ref,
-    bq_ref,
-    fw_ref,
-    tab_ref,
-    cos_ref,
-    sin_ref,
-    valid_ref,
-    seg_ref,
-    ln1t_ref,
-    ln2_ref,
-    ln2t_ref,
-    xhat_ref,
-    inv_ref,
-    qe_ref,
-    ke_ref,
-    qf_ref,
-    kf_ref,
-    v_ref,
-    pk_ref,
-    state_ref,
-    norm_ref,
+    me_ref,
+    *refs,
 ):
+    x_refs = refs[:pieces]
+    (
+        gains_ref,
+        w_ref,
+        bq_ref,
+        fw_ref,
+        tab_ref,
+        cos_ref,
+        sin_ref,
+        valid_ref,
+        seg_ref,
+        ln1t_ref,
+        ln2_ref,
+        ln2t_ref,
+        xhat_ref,
+        inv_ref,
+        qe_ref,
+        ke_ref,
+        qf_ref,
+        kf_ref,
+        v_ref,
+        pk_ref,
+        full_ref,
+        state_ref,
+        norm_ref,
+    ) = refs[pieces:]
     step = pl.program_id(0)
     width = qe_ref.shape[1]
-    x = x_ref[...].astype(f32)
+    place(full_ref, x_refs, me_ref)
+    x = full_ref[...].astype(f32)
     centered = x - jnp.mean(x, -1, keepdims=True)
     inv = lax.rsqrt(jnp.mean(centered * centered, -1, keepdims=True) + eps_norm)
     xhat = centered * inv
@@ -160,12 +176,40 @@
         pk_ref[head_size:] = norm
 
 
-def ff_kernel(ln2_ref, ln2t_ref, grad_ref, win_ref, bin_ref, wdown_ref, hid_ref, dpre_ref, gdown_ref, gin_ref, gb_ref):
-    rows = ln2_ref.shape[0]
-    half = rows // 4
+def store_blocks(block, base, me, keep_at, send_at, part):
+    for parity in range(2):
+
+        @pl.when(me % 2 == parity)
+        def _():
+            for j in range(block.shape[0] // part):
+                put = keep_at if j % 2 == parity else send_at
+                put((me ^ (base + j)) // 2, block[j * part : (j + 1) * part])
+
+
+def ff_kernel(pieces, me_ref, *refs):
+    grad_refs = refs[:pieces]
+    (
+        ln2_ref,
+        ln2t_ref,
+        win_ref,
+        bin_ref,
+        wdown_ref,
+        grad_ref,
+        hid_ref,
+        dpre_ref,
+        gdown_ref,
+        gin_ref,
+        gb_ref,
+    ) = refs[pieces:]
+
+    @pl.when(pl.program_id(0) == 0)
+    def _():
+        place(grad_ref, grad_refs, me_ref)
+
+    chunk = ln2_ref.shape[0] // 4
     sums = jnp.zeros((1, win_ref.shape[1]), f32)
     for r in range(4):
-        part = slice(r * half, (r + 1) * half)
+        part = slice(r * chunk, (r + 1) * chunk)
         pre = nn(ln2_ref[part], win_ref[...]) + bin_ref[...]
         phi_cum = 0.5 + 0.5 * lax.erf(pre * (1.0 / math.sqrt(2.0)))
         hid_ref[part] = (pre * phi_cum).astype(bf16)
@@ -288,39 +332,12 @@
         gpk_ref[head_size:] = z
 
 
-def value_kernel(
-    hid_ref,
-    wdown_ref,
-    att_ref,
-    wout_ref,
-    dpre_ref,
-    win_ref,
-    grad_ref,
-    xhat_ref,
-    gains_ref,
-    val_ref,
-    e2_ref,
-    sums_ref,
-    gwout_ref,
-    acc_ref,
-):
-    step = pl.program_id(0)
-    val_ref[...] = (nn(hid_ref[...], wdown_ref[...]) + nn(att_ref[...], wout_ref[...])).astype(bf16)
-    d_ln2 = nt(dpre_ref[...], win_ref[...])
-    e2_ref[...] = (d_ln2 * gains_ref[2:3]).astype(bf16)
-
-    @pl.when(step == 0)
-    def _():
-        sums_ref[...] = jnp.zeros_like(sums_ref)
-        acc_ref[...] = jnp.zeros_like(acc_ref)
-
-    sums_ref[0:1] += jnp.sum(d_ln2 * xhat_ref[...].astype(f32), 0, keepdims=True)
-    sums_ref[1:2] += jnp.sum(d_ln2, 0, keepdims=True)
-    acc_ref[...] += tn(att_ref[...], grad_ref[...])
-
-    @pl.when(step == pl.num_programs(0) - 1)
-    def _():
-        gwout_ref[...] = acc_ref[...].astype(bf16)
+def spread(full, keep_ref, send_ref, scratch_ref, me_ref):
+    scratch_ref[...] = full.astype(bf16)
+    size = keep_ref.shape[2]
+    for k in range(2 * keep_ref.shape[0]):
+        start = pl.multiple_of((me_ref[0] ^ k) * size, LANES)
+        (send_ref if k % 2 else keep_ref)[k // 2] = scratch_ref[:, pl.ds(start, size)]
 
 
 def tail_kernel(
@@ -341,19 +358,18 @@
     sin_ref,
     fw_ref,
     tab_ref,
-    w_ref,
     ln1t_ref,
-    xhat_ref,
-    e2_ref,
-    gains_ref,
-    e_ref,
-    stat_ref,
-    sums_ref,
+    gout_ref,
+    rank_ref,
+    low_ref,
     small_ref,
-    gw_ref,
+    keep0_ref,
+    send0_ref,
+    keep1_ref,
+    send1_ref,
     state_ref,
     norm_ref,
-    low_ref,
+    all_ref,
 ):
     step = pl.program_id(0)
     last = pl.num_programs(0) - 1
@@ -364,7 +380,6 @@
     def _():
         state_ref[...] = unpack_state(gin_ref[...], head_size)
         norm_ref[...] = gin_ref[head_size : head_size + 8]
-        sums_ref[...] = jnp.zeros_like(sums_ref)
         small_ref[...] = jnp.zeros_like(small_ref)
 
     tail = (segc_ref[...] == labels_ref[block, 1]).astype(f32)
@@ -393,23 +408,102 @@
     small_ref[1:2] += jnp.sum(dk_raw, 0, keepdims=True)
     small_ref[2:3] += jnp.sum(dv, 0, keepdims=True)
     small_ref[3:4] += jnp.sum(gq + gk, 0, keepdims=True)
-    lows = [d.astype(bf16) for d in (dq_raw, dk_raw, dv)]
-    d_ln1 = nt(lows[0], w_ref[0]) + nt(lows[1], w_ref[1]) + nt(lows[2], w_ref[2])
     start = pl.multiple_of(block * rows, rows)
-    for c in range(3):
-        low_ref[c, pl.ds(start, rows)] = lows[c]
-    xhat = xhat_ref[...].astype(f32)
-    e = d_ln1 * gains_ref[0:1] + e2_ref[...].astype(f32)
-    e_ref[...] = e.astype(bf16)
-    stat_ref[:, 0:1] = jnp.sum(e, 1, keepdims=True)
-    stat_ref[:, 1:2] = jnp.sum(e * xhat, 1, keepdims=True)
-    sums_ref[0:1] += jnp.sum(d_ln1 * xhat, 0, keepdims=True)
-    sums_ref[1:2] += jnp.sum(d_ln1, 0, keepdims=True)
+    for c, d in enumerate((dq_raw, dk_raw, dv)):
+        low = d.astype(bf16)
+        low_ref[c] = low
+        all_ref[c, pl.ds(start, rows)] = low
 
     @pl.when(step == last)
     def _():
-        for c in range(3):
-            gw_ref[c] = nn(ln1t_ref[...], low_ref[c]).astype(bf16)
+        me = rank_ref[0]
+        part = keep0_ref.shape[2]
+        for c in range(4):
+            g = gout_ref[...] if c == 3 else nn(ln1t_ref[...], all_ref[c]).astype(bf16)
+
+            def put(ref, slot, value):
+                ref[slot, c % 2] = value
+
+            pair = (keep1_ref, send1_ref) if c >= 2 else (keep0_ref, send0_ref)
+            store_blocks(g, 0, me, functools.partial(put, pair[0]), functools.partial(put, pair[1]), part)
+
+
+def e_kernel(
+    me_ref,
+    dpre_ref,
+    low_ref,
+    w_ref,
+    win_ref,
+    xhat_ref,
+    gains_ref,
+    keep_ref,
+    send_ref,
+    stat_ref,
+    scratch_ref,
+):
+    step = pl.program_id(0)
+    rows, model = xhat_ref.shape
+
+    @pl.when(step == 0)
+    def _():
+        stat_ref[8:16] = jnp.zeros((8, stat_ref.shape[1]), f32)
+
+    d_ln1 = nt(low_ref[0], w_ref[0]) + nt(low_ref[1], w_ref[1]) + nt(low_ref[2], w_ref[2])
+    d_ln2 = nt(dpre_ref[...], win_ref[...])
+    xhat = xhat_ref[...].astype(f32)
+    e = d_ln1 * gains_ref[0:1] + d_ln2 * gains_ref[2:3]
+    spread(e, keep_ref, send_ref, scratch_ref, me_ref)
+    ones = jnp.ones((8, model), bf16)
+    hi, lo = split(e)
+    sum_e = nt(ones, hi) + nt(ones, lo)
+    hi, lo = split(e * xhat)
+    sum_ex = nt(ones, hi) + nt(ones, lo)
+    row = lax.broadcasted_iota(jnp.int32, sum_e.shape, 0)
+    start = pl.multiple_of(step * rows, rows)
+    stat_ref[0:8, pl.ds(start, rows)] = jnp.where(row == 0, sum_e, sum_ex)
+    stat_ref[8:9, :model] += jnp.sum(d_ln1 * xhat, 0, keepdims=True)
+    stat_ref[9:10, :model] += jnp.sum(d_ln1, 0, keepdims=True)
+    stat_ref[10:11, :model] += jnp.sum(d_ln2 * xhat, 0, keepdims=True)
+    stat_ref[11:12, :model] += jnp.sum(d_ln2, 0, keepdims=True)
+
+
+def spread_rows(rank_ref, own_ref, other_ref, slab, write):
+    half, _, part, _ = own_ref.shape
+    for parity in range(2):
+
+        @pl.when(rank_ref[0] % 2 == parity)
+        def _():
+            for i in range(half):
+                for odd in range(2):
+                    ref = own_ref if odd == parity else other_ref
+                    slot = (rank_ref[0] // 2) ^ i
+                    write((2 * i + odd) * part, part, ref[slot, slab].astype(f32))
+
+
+def widen0_kernel(rank_ref, own_ref, other_ref, qkv_ref):
+    def write(start, size, value):
+        qkv_ref[0, start : start + size] = value
+
+    spread_rows(rank_ref, own_ref, other_ref, 0, write)
+
+
+def widen1_kernel(rank_ref, own_ref, other_ref, qkv_in_ref, qkv_ref, out_ref, scratch_ref):
+    c = pl.program_id(0)
+
+    def write_qkv(start, size, value):
+        qkv_ref[0, start : start + size] = value
+
+    def write_out(start, size, value):
+        scratch_ref[start : start + size] = value
+
+    @pl.when(c == 0)
+    def _():
+        spread_rows(rank_ref, own_ref, other_ref, 0, write_qkv)
+
+    @pl.when(c == 1)
+    def _():
+        spread_rows(rank_ref, own_ref, other_ref, 0, write_out)
+        out_ref[...] = scratch_ref[...].T
 
 
 def whole(*shape):
@@ -428,7 +522,7 @@
     return jax.ShapeDtypeStruct(shape, dtype)
 
 
-def call(kernel, grid, in_specs, out_specs, out_shape, scratch, flops, moved):
+def call(kernel, grid, in_specs, out_specs, out_shape, scratch, flops, moved, aliases={}):
     return pl.pallas_call(
         kernel,
         grid=(grid,),
@@ -436,12 +530,84 @@
         out_specs=out_specs,
         out_shape=out_shape,
         scratch_shapes=scratch,
+        input_output_aliases=aliases,
         compiler_params=pltpu.CompilerParams(vmem_limit_bytes=VMEM_LIMIT),
-        cost_estimate=pl.CostEstimate(flops=int(flops), bytes_accessed=int(moved), transcendentals=0),
+        cost_estimate=pl.CostEstimate(
+            flops=int(flops * COST_SCALE), bytes_accessed=int(moved * COST_SCALE), transcendentals=0
+        ),
+        name=getattr(kernel, "func", kernel).__name__,
     )
 
 
-def neighbour_sum(packet, sign):
+def exchange(x, axis, mask):
+    count = lax.axis_size(axis)
+    return lax.ppermute(x, axis, [(i, i ^ mask) for i in range(count)])
+
+
+def gather_far(x, axis):
+    pieces = {0: x}
+    mask = lax.axis_size(axis) // 2
+    while mask > 1:
+        pieces.update({k ^ mask: exchange(p, axis, mask) for k, p in sorted(pieces.items())})
+        mask //= 2
+    return pieces
+
+
+def gather_near(pieces, axis):
+    pieces = pieces | {k ^ 1: exchange(p, axis, 1) for k, p in sorted(pieces.items())}
+    return [pieces[k] for k in sorted(pieces)]
+
+
+def scatter_sum(keep, send, axis):
+    mask = 1
+    while True:
+        got = exchange(send, axis, mask)
+        if keep.shape[0] == 1:
+            return keep[0].astype(f32) + got[0].astype(f32)
+        total_keep = keep[0::2].astype(f32) + got[0::2].astype(f32)
+        total_send = keep[1::2].astype(f32) + got[1::2].astype(f32)
+        keep, send = total_keep.astype(bf16), total_send.astype(bf16)
+        mask *= 2
+
+
+def sum_all(x, axis):
+    mask = 1
+    while mask < lax.axis_size(axis):
+        x = x + exchange(x, axis, mask)
+        mask *= 2
+    return x
+
+
+def reduce_pairs(keep, send, pin):
+    got = after(exchange(send, "seq", 1), pin)
+    return (keep.astype(f32) + got.astype(f32)).astype(bf16)
+
+
+def reduce_groups(half, pin):
+    terms = [half[0]] + [exchange(half[k], "seq", 2 * k) for k in range(1, half.shape[0])]
+    terms = after(tuple(terms), pin)
+    return sum(t.astype(f32) for t in terms).astype(bf16)
+
+
+def gather_blocks(block):
+    count = lax.axis_size("seq")
+    own = jnp.stack([block] + [exchange(block, "seq", 2 * k) for k in range(1, count // 2)])
+    return own, exchange(own, "seq", 1)
+
+
+def sum_before(packet):
+    count = lax.axis_size("seq")
+    copies = jnp.broadcast_to(packet[None], (count,) + packet.shape)
+    packets = lax.all_to_all(copies, "seq", 0, 0, tiled=True)
+    wanted = (jnp.arange(count) < lax.axis_index("seq")).astype(f32)
+    return jnp.sum(packets * wanted[:, None, None], 0)
+
+
+def after(x, *others):
+    return lax.optimization_barrier((x,) + others)[0]
+
+
+def neighbour_sum(packet, sign, pin):
     count = lax.axis_size("seq")
     outer = 4 if count % 4 == 0 else 1
     inner = count // outer
@@ -451,7 +617,7 @@
     before = jnp.zeros_like(packet)
     for k in range(1, inner):
         route = [(i, i - i % inner + (i % inner + k) % inner) for i in range(count)]
-        got = lax.ppermute(packet, "seq", route)
+        got = after(lax.ppermute(packet, "seq", route), pin)
         sender = (mine - k) % inner
         group = group + got
         before = before + jnp.where((sender < mine) if sign > 0 else (sender > mine), got, 0.0)
@@ -489,8 +655,11 @@
     blocks = rows // BT
     n_head = lax.axis_size("head")
     offset = lax.axis_index("head") * share
-    full_tokens = lax.all_gather(tokens, "head", axis=1, tiled=True)
-    full_grad = lax.all_gather(grad_out, "head", axis=1, tiled=True)
+    with jax.named_scope("gather_tokens"):
+        token_far = gather_far(tokens, "head")
+    me_head = jnp.reshape(lax.axis_index("head"), (1,)).astype(jnp.int32)
+    me_seq = jnp.reshape(lax.axis_index("seq"), (1,)).astype(jnp.int32)
+    n_seq = lax.axis_size("seq")
 
     index_all = lax.axis_index("seq") * rows + jnp.arange(rows, dtype=jnp.int32)
     seq_ends = jnp.cumsum(lengths).astype(jnp.int32)
@@ -522,14 +691,21 @@
     tab = jnp.asarray(np.stack([table_hi, table_lo]))
     gains = jnp.stack([ln1_gain, ln1_bias, ln2_gain, ln2_bias])
     fw = feat_weight.reshape(1, width)
+    bias_out = jnp.sum(grad_out.astype(f32), 0, keepdims=True)
+    with jax.named_scope("gather_grads"):
+        early = (cosine, sine, gains, bias_out, labels, valid, seg_col, seg_row, fw)
+        grad_far = gather_far(after(grad_out, *early), "head")
+    with jax.named_scope("gather_tokens"):
+        token_pieces = gather_near({k: after(p, *early) if k else p for k, p in token_far.items()}, "head")
     packet_shape = (head_size + 8, width)
 
     ln1t, ln2, ln2t, xhat, inv_std, q_expo, k_expo, qf, kf, v, s_own = call(
-        functools.partial(pre_kernel, head_size),
+        functools.partial(pre_kernel, head_size, n_head),
         blocks,
         [
             smem(),
-            rows_of(BT, model),
+            smem(),
+            *[rows_of(BT, share)] * n_head,
             whole(4, model),
             whole(3, model, width),
             whole(3, width),
@@ -566,26 +742,31 @@
             sds((rows, width), bf16),
             sds(packet_shape, f32),
         ],
-        [pltpu.VMEM((width, width), f32), pltpu.VMEM((8, width), f32)],
+        [pltpu.VMEM((BT, model), bf16), pltpu.VMEM((width, width), f32), pltpu.VMEM((8, width), f32)],
         2 * rows * model * 3 * width + 16 * rows * width * width,
         rows * model * 10 + 6 * model * width,
-    )(labels, full_tokens, gains, w_qkv, b_qkv, fw, tab, cosine, sine, valid, seg_col)
-
-    s_in = neighbour_sum(s_own, 1)
+    )(labels, me_head, *token_pieces, gains, w_qkv, b_qkv, fw, tab, cosine, sine, valid, seg_col)
+
+    with jax.named_scope("gather_grads"):
+        grad_pieces = gather_near({k: after(p, s_own) for k, p in grad_far.items()}, "head")
+    with jax.named_scope("state"):
+        s_in = sum_before(s_own)
 
     fb = 256
-    hid, dpre, g_down, g_in, gb_in = call(
-        ff_kernel,
+    full_grad, hid, dpre, g_down, g_in, gb_in = call(
+        functools.partial(ff_kernel, n_head),
         hidden // fb,
         [
+            smem(),
+            *[whole(rows, share)] * n_head,
             whole(rows, model),
             whole(model, rows),
-            whole(rows, model),
             pl.BlockSpec((model, fb), lambda i: (0, i)),
             pl.BlockSpec((1, fb), lambda i: (0, i)),
             pl.BlockSpec((fb, model), lambda i: (i, 0)),
         ],
         [
+            whole(rows, model),
             pl.BlockSpec((rows, fb), lambda i: (0, i)),
             pl.BlockSpec((rows, fb), lambda i: (0, i)),
             pl.BlockSpec((fb, model), lambda i: (i, 0)),
@@ -593,6 +774,7 @@
             pl.BlockSpec((1, fb), lambda i: (0, i)),
         ],
         [
+            sds((rows, model), bf16),
             sds((rows, hidden), bf16),
             sds((rows, hidden), bf16),
             sds((hidden, model), bf16),
@@ -602,10 +784,11 @@
         [],
         8 * rows * model * hidden,
         6 * rows * model + 8 * model * hidden,
-    )(ln2, ln2t, full_grad, w_in, b_in[None, :], w_down)
-
-    g_down = lax.psum(g_down, "seq")
-    g_in = lax.psum(g_in, "seq")
+    )(me_head, *grad_pieces, ln2, ln2t, w_in, b_in[None, :], w_down)
+
+    with jax.named_scope("ff_sum"):
+        g_down, g_in = lax.psum((g_down, g_in), "seq")
+    s_in = after(s_in, hid)
 
     att, dq, dk, dv, gb, gzb, g_own = call(
         functools.partial(attn_kernel, head_size),
@@ -649,51 +832,28 @@
         rows * model * 2 + rows * width * 20,
     )(labels, qf, kf, v, full_grad, w_out, seg_col, seg_row, s_in)
 
-    grad_in = neighbour_sum(g_own, -1)
-
-    value, e2, sums2, g_out = call(
-        value_kernel,
-        blocks,
-        [
-            rows_of(BT, hidden),
-            whole(hidden, model),
-            rows_of(BT, width),
-            whole(width, model),
-            rows_of(BT, hidden),
-            whole(model, hidden),
-            rows_of(BT, model),
-            rows_of(BT, model),
-            whole(4, model),
-        ],
-        [rows_of(BT, model), rows_of(BT, model), whole(8, model), whole(width, model)],
-        [
-            sds((rows, model), bf16),
-            sds((rows, model), bf16),
-            sds((8, model), f32),
-            sds((width, model), bf16),
-        ],
-        [pltpu.VMEM((width, model), f32)],
-        4 * rows * model * (hidden + width),
-        12 * rows * model + 4 * model * hidden,
-    )(hid, w_down, att, w_out, dpre, w_in, full_grad, xhat, gains)
-
-    mixed_share = lax.psum_scatter(value, "head", scatter_dimension=1, tiled=True)
+    with jax.named_scope("grad_state"):
+        grad_in = neighbour_sum(g_own, -1, hid)
+
+    value = jnp.dot(hid, w_down, preferred_element_type=f32) + jnp.dot(att, w_out, preferred_element_type=f32)
+    value = value.astype(bf16)
+    me = lax.axis_index("head")
+    order = [lax.dynamic_slice_in_dim(value, (me ^ k) * share, share, 1) for k in range(n_head)]
+    val_keep, val_send = jnp.stack(order[0::2]), jnp.stack(order[1::2])
+    g_out = lax.dot_general(full_grad, att, (((0,), (0,)), ((), ())), preferred_element_type=f32).astype(bf16)
+    grad_in = after(grad_in, g_out, value)
+
 
     def back_rows(*shape):
         return pl.BlockSpec(shape, lambda i: (blocks - 1 - i,) + (0,) * (len(shape) - 1))
 
-    e_part, stats, sums1, small, g_qkv = call(
+    part = model // n_seq
+    low, small, *w_parts = call(
         functools.partial(tail_kernel, head_size),
         blocks,
         [
             smem(),
-            back_rows(BT, width),
-            back_rows(BT, width),
-            back_rows(BT, width),
-            back_rows(BT, width),
-            back_rows(BT, width),
-            back_rows(BT, width),
-            back_rows(BT, width),
+            *[back_rows(BT, width)] * 7,
             back_rows(1, width, width),
             back_rows(1, 8, width),
             whole(*packet_shape),
@@ -702,70 +862,115 @@
             back_rows(BT, LANES),
             whole(1, width),
             whole(2, width, width),
-            whole(3, model, width),
             whole(model, rows),
-            back_rows(BT, model),
-            back_rows(BT, model),
-            whole(4, model),
-        ],
-        [
-            back_rows(BT, model),
-            back_rows(BT, 2),
-            whole(8, model),
+            whole(model, width),
+            smem(),
+        ],
+        [
+            pl.BlockSpec((3, BT, width), lambda i: (0, blocks - 1 - i, 0)),
             whole(8, width),
-            whole(3, model, width),
-        ],
-        [
-            sds((rows, model), bf16),
-            sds((rows, 2), f32),
-            sds((8, model), f32),
+            *[whole(n_seq // 2, 2, part, width)] * 4,
+        ],
+        [
+            sds((3, rows, width), bf16),
             sds((8, width), f32),
-            sds((3, model, width), bf16),
+            *[sds((n_seq // 2, 2, part, width), bf16)] * 4,
         ],
         [
             pltpu.VMEM((width, width), f32),
             pltpu.VMEM((8, width), f32),
             pltpu.VMEM((3, rows, width), bf16),
         ],
-        4 * rows * model * 3 * width,
-        rows * width * 30 + rows * model * 8,
-    )(
-        labels,
-        dq,
-        dk,
-        dv,
-        q_expo,
-        k_expo,
-        kf,
-        v,
-        gb,
-        gzb,
-        grad_in,
-        seg_col,
-        cosine,
-        sine,
-        fw,
-        tab,
-        w_qkv,
-        ln1t,
-        xhat,
-        e2,
-        gains,
-    )
-
-    g_qkv, g_out = lax.psum((g_qkv, g_out), "seq")
-    e_share = lax.psum_scatter(e_part, "head", scatter_dimension=1, tiled=True)
-    stats, gain_sums = lax.psum((stats, jnp.concatenate([sums1[:2], sums2[:2]], 0)), "head")
-    bias_out = jnp.sum(grad_out.astype(f32), 0)
-    gain_share = lax.dynamic_slice_in_dim(gain_sums, offset, share, 1)
-    gain_share, small, gb_in, bias_out = lax.psum((gain_share, small[:4], gb_in, bias_out), "seq")
+        2 * rows * model * 3 * width,
+        rows * width * 30 + rows * model * 2 + 6 * model * width,
+    )(labels, dq, dk, dv, q_expo, k_expo, kf, v, gb, gzb, grad_in, seg_col, cosine, sine, fw, tab, ln1t, g_out, me_seq)
+
+    stat_width = max(rows, model)
+    e_keep, e_send, stats = call(
+        e_kernel,
+        blocks,
+        [
+            smem(),
+            rows_of(BT, hidden),
+            pl.BlockSpec((3, BT, width), lambda i: (0, i, 0)),
+            whole(3, model, width),
+            whole(model, hidden),
+            rows_of(BT, model),
+            whole(4, model),
+        ],
+        [
+            pl.BlockSpec((n_head // 2, BT, share), lambda i: (0, i, 0)),
+            pl.BlockSpec((n_head // 2, BT, share), lambda i: (0, i, 0)),
+            whole(16, stat_width),
+        ],
+        [
+            sds((n_head // 2, rows, share), bf16),
+            sds((n_head // 2, rows, share), bf16),
+            sds((16, stat_width), f32),
+        ],
+        [pltpu.VMEM((BT, model), bf16)],
+        2 * rows * model * (3 * width + hidden),
+        rows * width * 6 + rows * model * 6 + 8 * model * width + 2 * hidden * model,
+    )(me_head, dpre, low, w_qkv, w_in, xhat, gains)
+
+    with jax.named_scope("reduce_qk"):
+        first = reduce_pairs(*w_parts[:2], low)
+    with jax.named_scope("reduce_vo"):
+        second = reduce_pairs(*w_parts[2:], low)
+    with jax.named_scope("reduce_qk"):
+        first = gather_blocks(reduce_groups(first, low))
+    with jax.named_scope("reduce_vo"):
+        second = gather_blocks(reduce_groups(second, low))
+    g_down = g_down.astype(f32)
+    g_in = g_in.astype(f32)
+
+    def slab():
+        return pl.BlockSpec((n_seq // 2, 1, part, width), lambda c: (0, c, 0, 0))
+
+    g_qkv = call(
+        widen0_kernel,
+        2,
+        [smem(), slab(), slab()],
+        pl.BlockSpec((1, model, width), lambda c: (c, 0, 0)),
+        sds((3, model, width), f32),
+        [],
+        0,
+        END_COST * model * width,
+    )(me_seq, *first)
+    g_qkv, g_out = call(
+        widen1_kernel,
+        2,
+        [smem(), slab(), slab(), pl.BlockSpec(memory_space=pl.ANY)],
+        [pl.BlockSpec((1, model, width), lambda c: (2, 0, 0)), whole(width, model)],
+        [sds((3, model, width), f32), sds((width, model), f32)],
+        [pltpu.VMEM((model, width), f32)],
+        0,
+        END_COST * model * width,
+        {3: 0},
+    )(me_seq, *second, g_qkv)
+
+    with jax.named_scope("mixed_sum"):
+        mixed_share = scatter_sum(val_keep, after(val_send, low), "head")
+    with jax.named_scope("e_sum"):
+        e_share = scatter_sum(e_keep, e_send, "head")
+    with jax.named_scope("stats_sum"):
+        gains_own = stats[8:12, :model]
+        stats = sum_all(stats[:8], "head")
+    with jax.named_scope("small_sum"):
+        local = jnp.concatenate([small[:4], gb_in.reshape(-1, share), bias_out], 0)
+        mine = (jnp.arange(n_head) == lax.axis_index("head")).astype(f32)
+        spread_gains = gains_own.reshape(4, n_head, share).transpose(1, 0, 2)
+        packet = jnp.concatenate([spread_gains, mine[:, None, None] * local[None]], 1)
+        packet = jnp.broadcast_to(packet[None], (n_seq,) + packet.shape).reshape((-1,) + packet.shape[1:])
+        packet = jnp.sum(lax.all_to_all(packet, ("seq", "head"), 0, 0, tiled=True), 0)
+    gain_share, small, gb_in, bias_out = packet[:4], packet[4:8], packet[8:-1].reshape(-1), packet[-1]
+    stats = stats[:2, :rows].T * (1.0 / model)
 
     bias = lax.dynamic_slice_in_dim(b_out, offset, share) + lax.dynamic_slice_in_dim(b_down, offset, share)
-    mixed = (tokens.astype(f32) + mixed_share.astype(f32) + bias).astype(bf16)
+    mixed = (tokens.astype(f32) + mixed_share + bias).astype(bf16)
     xhat_share = lax.dynamic_slice_in_dim(xhat, offset, share, 1).astype(f32)
-    stats = stats * (1.0 / model)
     grad_input = grad_out.astype(f32) + inv_std * (
-        e_share.astype(f32) - stats[:, 0:1] - xhat_share * stats[:, 1:2]
+        e_share - stats[:, 0:1] - xhat_share * stats[:, 1:2]
     )
     return (
         mixed,
@@ -774,14 +979,14 @@
         gain_share[1],
         gain_share[2],
         gain_share[3],
-        g_qkv.astype(f32),
+        g_qkv,
         small[:3],
         small[3].reshape(heads, feats),
-        g_out.astype(f32),
+        g_out,
         bias_out,
-        g_in.astype(f32),
-        gb_in[0],
-        g_down.astype(f32),
+        g_in,
+        gb_in,
+        g_down,
         bias_out,
     )
 

time: 403 us -> 300 us (0.74)
  waiting for transfers between devices: 216 us -> 105 us
  blocking collectives: 51.8 us -> 0 us
  starting transfers between devices: 17.4 us -> 55 us
  other arithmetic: 23.4 us -> 31.6 us
  local copies, waits for them, and re-layouts: 10.1 us -> 16.3 us
  matrix products: 0 us -> 5.78 us
    psum x1, waiting for transfers between devices: 178 us -> 0.01 us  [body(): g_down, g_in = lax.psum((g_down, g_in), 'seq')]
    ppermute x2 -> x29, waiting for transfers between devices: 6.1 us -> 97.6 us  [the longest x28 95.2 us: exchange(): return lax.ppermute(x, axis, [(i, i ^ mask) for i in range(count)])]
    psum x2 -> x0, blocking collectives: 51.8 us -> none  [the longest x1 35.6 us: body(): lax.psum((gain_share, small[:4], gb_in, bias_out), 'seq')]
    ppermute x2 -> x29, starting transfers between devices: 2.96 us -> 35.8 us  [the longest x28 34.3 us: exchange(): return lax.ppermute(x, axis, [(i, i ^ mask) for i in range(count)])]
    all_to_all x0 -> x2, starting transfers between devices: none -> 14.8 us  [the longest x1 8.56 us: body(): lax.all_to_all(packet, ('seq', 'head'), 0, 0, tiled=True)]
    all_gather x2 -> x0, waiting for transfers between devices: 13.8 us -> none  [the longest x1 13.7 us: body(): full_tokens = lax.all_gather(tokens, 'head', axis=1, tiled=True)]
    reduce_scatter x2 -> x0, waiting for transfers between devices: 11.9 us -> none  [the longest x1 11.9 us: body(): e_share = lax.psum_scatter(e_part, 'head', scatter_dimension=1, tiled=True)]
    ppermute x6 -> x3, starting transfers between devices: 14.2 us -> 4.33 us  [neighbour_sum(): before = before + lax.ppermute(group, 'seq', route)]
  transfers between devices with their start and end apart: 13 -> 35, of which waited for: 7 -> 19; matrix products, arithmetic and copies ran while one was open for 5% -> 15% of each run, Pallas kernels for 10% -> 24%
where the time goes in v2:
time: 300 us; the launch traced here: 298 us
  waiting for transfers between devices  105 us (35%)
  Pallas kernels  70.2 us (23%)
  starting transfers between devices  55 us (18%)
  other arithmetic  31.6 us (11%)
  local copies, waits for them, and re-layouts  16.3 us (5%)
  between operations  14.5 us (5%)
  matrix products  5.78 us (2%)
    ppermute x28, waiting for transfers between devices, exchange(): return lax.ppermute(x, axis, [(i, i ^ mask) for i in range(count)])  95.2 us
    ppermute x28, starting transfers between devices, exchange(): return lax.ppermute(x, axis, [(i, i ^ mask) for i in range(count)])  34.3 us
    pallas_call x1, Pallas kernels, body(): call(functools.partial(ff_kernel, n_head), hidden // fb, [smem(), *[whole...  15.7 us
    pallas_call x1, Pallas kernels, body(): call(functools.partial(pre_kernel, head_size, n_head), blocks, [smem(), s...  13.5 us
    pallas_call x1, Pallas kernels, body(): call(functools.partial(attn_kernel, head_size), blocks, [smem(), rows_of(...  12.5 us
    pallas_call x1, Pallas kernels, body(): call(functools.partial(tail_kernel, head_size), blocks, [smem(), *[back_r...  12.1 us
    pallas_call x1, Pallas kernels, body(): call(e_kernel, blocks, [smem(), rows_of(BT, hidden), pl.BlockSpec((3, BT,...  11.1 us
    all_to_all x1, starting transfers between devices, body(): lax.all_to_all(packet, ('seq', 'head'), 0, 0, tiled=True)  8.56 us
  transfers between devices with their start and end apart: 35, of which 19 were waited for; matrix products, arithmetic and copies ran while one was open for 15% of the time, Pallas kernels for 24%

profile of v2, /device:TPU:8, one launch (start us, length us, event | category | flops | bytes accessed | tf_op | source)
XLA Modules:
  0.0 298.5 jit_solution(10864026986909051394)
XLA Ops:
  7.2 1.6 collective-permute-start.1
  8.8 0.8 reduce-window.8
  12.1 1.2 convert_reduce_fusion
  13.9 1.4 pad_maximum_fusion.4.refs_4_.gains_ref
  15.3 1.3 reshape.125.refs_7_.fw_ref
  17.3 3.7 %fusion.6 = (f32[1024,128]{1,0:T(8,128)}, f32[1024,128]{1,0:T(8,128)}) fusion(f32[128]{0:T(128)} %constant.56.clone, f32[128]{0:T(128)} %constant.55.clone, f32[1024]{0:T(1024)S(1)} %subtract_convert_fusion), kind=kLoop, calls=%fused_computation.22 | loop fusion | flops 262144 | bytes 1053696 | tf_op jit(solution)/shard_map/mul | solution.py:686
  21.6 1.0 collective-permute-start.4
  22.6 1.0 copy.55.refs_12_.segc_ref
  23.6 1.0 copy.54.refs_11_
  24.7 0.8 copy-done.20
  25.7 13.5 %pre_kernel.1 = (bf16[1024,1024]{1,0:T(8,128)(2,1)}, bf16[1024,1024]{1,0:T(8,128)(2,1)}, bf16[1024,1024]{1,0:T(8,128)(2,1)}, bf16[1024,1024]{1,0:T(8,128)(2,1)},...) custom-call(s32[4,3]{1,0:T(4,128)} %add_add_fusion.1.labels_ref, ...), custom_call_target="tpu_custom_call" | custom-call | flops 53687092 | bytes 241172 | tf_op jit(solution)/shard_map/pre_kernel/pallas_call | solution.py:702
  39.2 1.8 broadcast_in_dim.37
  41.0 6.3 %all-to-all-start = ((f32[8,72,256]{2,1,0:T(8,128)}), f32[8,72,256]{2,1,0:T(8,128)S(1)}, u32[]{:S(2)}, u32[]{:S(2)}) async-start(f32[8,72,256]{2,1,0:T(8,128)} %broadcast_in_dim.37), calls=%async_computation | async-start | bytes 1179648 | tf_op jit(solution)/shard_map/state/all_to_all | solution.py:601
  47.9 0.8 dynamic-slice_add_fusion
  50.8 15.7 %ff_kernel.1 = (bf16[1024,1024]{1,0:T(8,128)(2,1)}, bf16[1024,1024]{1,0:T(8,128)(2,1)}, bf16[1024,1024]{1,0:T(8,128)(2,1)}, bf16[1024,1024]{1,0:T(8,128)(2,1)}, ...) custom-call(s32[1]{0:T(128)} %bitcast.me_ref, bf16[1024,256]{1,0:T(8,128)(2,1)} %refs_0_.2, bf16[1024,256]{1,0:T(8,128)(2,1)} %copy-done.15, ...), custom_call_target="tpu_custom_call" | custom-call | flops 171798688 | bytes 293601 | tf_op jit(solution)/shard_map/ff_kernel/pallas_call | solution.py:756
  67.0 1.3 reduce.8
  69.1 12.5 %attn_kernel.1 = (bf16[1024,256]{1,0:T(8,128)(2,1)}, f32[1024,256]{1,0:T(8,128)}, f32[1024,256]{1,0:T(8,128)}, f32[1024,256]{1,0:T(8,128)}, f32[4,256,256]{2,1,0...) custom-call(s32[4,3]{1,0:T(4,128)} %add_add_fusion.1.labels_ref, bf16[1024,256]{1,0:T(8,128)(2,1)} %get-tuple-element.76.qf_ref, ...), custom_call_target="tpu_custom_call" | custom-call | flops 128849016 | bytes 146800 | tf_op jit(solution)/shard_map/attn_kernel/pallas_call | solution.py:793
  81.7 2.7 convolution_convert_fusion.gout_ref
  85.3 1.5 collective-permute-start.6
  86.7 2.3 add_convert_fusion
  89.3 2.4 collective-permute-done.6
  91.7 2.2 collective-permute-start.7
  93.9 1.3 collective-permute-start.8
  95.2 0.9 collective-permute-start.9
  96.0 1.1 pad_maximum_fusion
  97.1 5.6 %collective-permute-done.7 = f32[72,256]{1,0:T(8,128)S(1)} collective-permute-done((f32[72,256]{1,0:T(8,128)S(1)}, f32[72,256]{1,0:T(8,128)S(1)}, u32[]{:S(2)}, u32[]{:S(2)}) %collective-permute-start.7) | collective-permute-done | bytes 73760 | tf_op jit(solution)/shard_map/grad_state/ppermute | solution.py:627
  102.7 1.9 collective-permute-done.8
  105.2 12.1 %tail_kernel.1 = (bf16[3,1024,256]{2,1,0:T(8,128)(2,1)}, f32[8,256]{1,0:T(8,128)}, bf16[4,2,128,256]{3,2,1,0:T(8,128)(2,1)}, bf16[4,2,128,256]{3,2,1,0:T(8,128)(...) custom-call(s32[4,3]{1,0:T(4,128)} %add_add_fusion.1.labels_ref, ...), custom_call_target="tpu_custom_call" | custom-call | flops 32212254 | bytes 230686 | tf_op jit(solution)/shard_map/tail_kernel/pallas_call | solution.py:851
  117.3 1.5 collective-permute-start.24
  120.1 11.1 %e_kernel.1 = (bf16[2,1024,256]{2,1,0:T(8,128)(2,1)}, bf16[2,1024,256]{2,1,0:T(8,128)(2,1)}, f32[16,1024]{1,0:T(8,128)}) custom-call(s32[1]{0:T(128)} %bitcast.me_ref, bf16[1024,1024]{1,0:T(8,128)(2,1)} %get-tuple-element.96.dpre_ref, bf16[3,1024,256]{2,1,0:T(8,128)(2,1)} %get-tuple-element.93.low_ref, bf16[3,1024,256]{2,1,0:T(8,128)(2,1)} %w_ref.1, ...), custom_call_target="tpu_custom_call" | custom-call | flops 75161928 | bytes 241172 | tf_op jit(solution)/shard_map/e_kernel/pallas_call | solution.py:889
  131.2 0.8 slice.110
  133.3 0.8 slice_add_fusion.1
  134.0 3.7 %collective-permute-start.15 = (f32[8,1024]{1,0:T(8,128)S(1)}, f32[8,1024]{1,0:T(8,128)S(1)}, u32[]{:S(2)}, u32[]{:S(2)}) collective-permute-start(f32[8,1024]{1,0:T(8,128)S(1)} %slice_add_fusion.1), channel_id=1, source_target_pairs={{0,2},{1,3},{2,0},{3,1},{4,6},{5,7},{6,4},{7,5},{8,10},{9,11},{10,... | collective-permute-start | bytes 98312 | tf_op jit(solution)/shard_map/stats_sum/ppermute | solution.py:544
  137.8 0.9 broadcast_in_dim.68
  138.6 8.6 %all-to-all-start.1 = ((f32[32,13,256]{2,1,0:T(8,128)}), f32[32,13,256]{2,1,0:T(8,128)S(1)}, u32[]{:S(2)}, u32[]{:S(2)}) async-start(f32[32,13,256]{2,1,0:T(8,128)} %bitcast.26), calls=%async_computation.1 | async-start | bytes 1048576 | tf_op jit(solution)/shard_map/small_sum/all_to_all | solution.py:965
  148.4 2.7 collective-permute-start.26
  151.0 5.2 %collective-permute-start.27 = (bf16[2,128,256]{2,1,0:T(8,128)(2,1)S(1)}, bf16[2,128,256]{2,1,0:T(8,128)(2,1)S(1)}, u32[]{:S(2)}, u32[]{:S(2)}) collective-permute-start(bf16[2,128,256]{2,1,0:T(8,128)(2,1)S(1)} %get-tuple-element.127), channel_id=1, source_target_pairs={{0,24},{4,28},{8,16},{12,20},{16,8},{20,12},{24,0},{28,4},{1,25},{... | collective-permute-start | bytes 393224 | tf_op jit(solution)/shard_map/reduce_qk/ppermute | solution.py:544
  156.4 9.5 %collective-permute-done.25 = bf16[2,128,256]{2,1,0:T(8,128)(2,1)S(1)} collective-permute-done((bf16[2,128,256]{2,1,0:T(8,128)(2,1)S(1)}, bf16[2,128,256]{2,1,0:T(8,128)(2,1)S(1)}, u32[]{:S(2)}, u32[]{:S(2)}) %collective-permute-start.25) | collective-permute-done | bytes 131104 | tf_op jit(solution)/shard_map/reduce_qk/ppermute | solution.py:544
  166.0 7.8 %collective-permute-done.26 = bf16[2,128,256]{2,1,0:T(8,128)(2,1)S(1)} collective-permute-done((bf16[2,128,256]{2,1,0:T(8,128)(2,1)S(1)}, bf16[2,128,256]{2,1,0:T(8,128)(2,1)S(1)}, u32[]{:S(2)}, u32[]{:S(2)}) %collective-permute-start.26) | collective-permute-done | bytes 131104 | tf_op jit(solution)/shard_map/reduce_qk/ppermute | solution.py:544
  173.8 4.4 %collective-permute-start.18 = (bf16[2,128,256]{2,1,0:T(8,128)(2,1)S(1)}, bf16[2,128,256]{2,1,0:T(8,128)(2,1)S(1)}, u32[]{:S(2)}, u32[]{:S(2)}) collective-permute-start(bf16[2,128,256]{2,1,0:T(8,128)(2,1)S(1)} %get-tuple-element.132), channel_id=1, source_target_pairs={{0,16},{4,20},{8,24},{12,28},{16,0},{20,4},{24,8},{28,12},{1,17},{... | collective-permute-start | bytes 393224 | tf_op jit(solution)/shard_map/reduce_vo/ppermute | solution.py:544
  178.1 15.5 %collective-permute-done.27 = bf16[2,128,256]{2,1,0:T(8,128)(2,1)S(1)} collective-permute-done((bf16[2,128,256]{2,1,0:T(8,128)(2,1)S(1)}, bf16[2,128,256]{2,1,0:T(8,128)(2,1)S(1)}, u32[]{:S(2)}, u32[]{:S(2)}) %collective-permute-start.27) | collective-permute-done | bytes 131104 | tf_op jit(solution)/shard_map/reduce_qk/ppermute | solution.py:544
  193.8 1.4 collective-permute-done.18
  195.2 3.5 %collective-permute-start.29 = (bf16[2,128,256]{2,1,0:T(8,128)(2,1)S(1)}, bf16[2,128,256]{2,1,0:T(8,128)(2,1)S(1)}, u32[]{:S(2)}, u32[]{:S(2)}) collective-permute-start(bf16[2,128,256]{2,1,0:T(8,128)(2,1)S(1)} %add_convert_fusion.5), channel_id=1, source_target_pairs={{0,16},{4,20},{8,24},{12,28},{16,0},{20,4},{24,8},{28,12},{1,17},{... | collective-permute-start | bytes 393224 | tf_op jit(solution)/shard_map/reduce_qk/ppermute | solution.py:544
  198.7 8.1 %collective-permute-done.19 = bf16[2,128,256]{2,1,0:T(8,128)(2,1)S(1)} collective-permute-done((bf16[2,128,256]{2,1,0:T(8,128)(2,1)S(1)}, bf16[2,128,256]{2,1,0:T(8,128)(2,1)S(1)}, u32[]{:S(2)}, u32[]{:S(2)}) %collective-permute-start.19) | collective-permute-done | bytes 131104 | tf_op jit(solution)/shard_map/reduce_vo/ppermute | solution.py:544
  206.9 7.1 %collective-permute-done.29 = bf16[2,128,256]{2,1,0:T(8,128)(2,1)S(1)} collective-permute-done((bf16[2,128,256]{2,1,0:T(8,128)(2,1)S(1)}, bf16[2,128,256]{2,1,0:T(8,128)(2,1)S(1)}, u32[]{:S(2)}, u32[]{:S(2)}) %collective-permute-start.29) | collective-permute-done | bytes 131104 | tf_op jit(solution)/shard_map/reduce_qk/ppermute | solution.py:544
  214.1 3.4 %collective-permute-start.21 = (bf16[2,128,256]{2,1,0:T(8,128)(2,1)S(1)}, bf16[2,128,256]{2,1,0:T(8,128)(2,1)S(1)}, u32[]{:S(2)}, u32[]{:S(2)}) collective-permute-start(bf16[2,128,256]{2,1,0:T(8,128)(2,1)S(1)} %add_convert_fusion.6), channel_id=1, source_target_pairs={{0,16},{4,20},{8,24},{12,28},{16,0},{20,4},{24,8},{28,12},{1,17},{... | collective-permute-start | bytes 393224 | tf_op jit(solution)/shard_map/reduce_vo/ppermute | solution.py:544
  217.5 15.7 %collective-permute-done.30 = bf16[2,128,256]{2,1,0:T(8,128)(2,1)S(1)} collective-permute-done((bf16[2,128,256]{2,1,0:T(8,128)(2,1)S(1)}, bf16[2,128,256]{2,1,0:T(8,128)(2,1)S(1)}, u32[]{:S(2)}, u32[]{:S(2)}) %collective-permute-start.30) | collective-permute-done | bytes 131104 | tf_op jit(solution)/shard_map/reduce_qk/ppermute | solution.py:544
  233.6 1.4 collective-permute-start.31
  235.0 5.0 %collective-permute-done.21 = bf16[2,128,256]{2,1,0:T(8,128)(2,1)S(1)} collective-permute-done((bf16[2,128,256]{2,1,0:T(8,128)(2,1)S(1)}, bf16[2,128,256]{2,1,0:T(8,128)(2,1)S(1)}, u32[]{:S(2)}, u32[]{:S(2)}) %collective-permute-start.21) | collective-permute-done | bytes 131104 | tf_op jit(solution)/shard_map/reduce_vo/ppermute | solution.py:544
  240.0 13.7 %collective-permute-done.22 = bf16[2,128,256]{2,1,0:T(8,128)(2,1)S(1)} collective-permute-done((bf16[2,128,256]{2,1,0:T(8,128)(2,1)S(1)}, bf16[2,128,256]{2,1,0:T(8,128)(2,1)S(1)}, u32[]{:S(2)}, u32[]{:S(2)}) %collective-permute-start.22) | collective-permute-done | bytes 131104 | tf_op jit(solution)/shard_map/reduce_vo/ppermute | solution.py:544
  253.8 0.9 collective-permute-start.23
  254.7 2.1 fusion
  256.9 1.1 collective-permute-start.11
  258.0 2.0 add_convert_fusion.3
  259.9 0.9 collective-permute-start.13
  263.3 0.8 copy-done.17
  264.1 2.4 widen0_kernel.1.qkv_in_ref
  267.2 2.9 widen1_kernel.1
  270.1 1.9 collective-permute-done.11
  272.0 2.4 fusion.5
  274.5 7.2 %collective-permute-done.13 = bf16[1,1024,256]{2,1,0:T(8,128)(2,1)S(1)} collective-permute-done((bf16[1,1024,256]{2,1,0:T(8,128)(2,1)}, bf16[1,1024,256]{2,1,0:T(8,128)(2,1)S(1)}, u32[]{:S(2)}, u32[]{:S(2)}) %collective-permute-start.13) | collective-permute-done | bytes 524320 | tf_op jit(solution)/shard_map/e_sum/ppermute | solution.py:544
  281.7 2.6 convert_add_fusion
  284.4 4.2 %convert_element_type.211 = f32[1024,1024]{1,0:T(8,128)} convert(bf16[1024,1024]{1,0:T(8,128)(2,1)} %get-tuple-element.123) | non-fusion elementwise | flops 1048576 | bytes 6291456 | tf_op jit(solution)/shard_map/convert_element_type | solution.py:925
  288.6 2.5 convert_element_type.212
  (135 shorter events, 18.6 us)
Async XLA Ops:
  7.2 13.9 %collective-permute-start.1 = (bf16[1024,256]{1,0:T(8,128)(2,1)}, bf16[1024,256]{1,0:T(8,128)(2,1)S(1)}, u32[]{:S(2)}, u32[]{:S(2)}) collective-permute-start(bf16[1024,256]{1,0:T(8,128)(2,1)} %refs_0_.1), channel_id=1, source_target_pairs={{0,2},{1,3},{2,0},{3,1},{4,6},{5,7},{6,4},{7,5},{8,10},{9,11},{10,... | collective-permute-start | bytes 1572872 | tf_op jit(solution)/shard_map/gather_tokens/ppermute | solution.py:544
  8.7 15.9 %collective-permute-start = (bf16[1024,256]{1,0:T(8,128)(2,1)}, bf16[1024,256]{1,0:T(8,128)(2,1)S(1)}, u32[]{:S(2)}, u32[]{:S(2)}) collective-permute-start(bf16[1024,256]{1,0:T(8,128)(2,1)} %refs_0_.1), channel_id=1, source_target_pairs={{0,1},{1,0},{2,3},{3,2},{4,5},{5,4},{6,7},{7,6},{8,9},{9,8},{10,11... | collective-permute-start | bytes 1572872 | tf_op jit(solution)/shard_map/gather_tokens/ppermute | solution.py:544
  10.7 28.4 %copy-start.23 = (s32[1024]{0:T(1024)}, s32[1024]{0:T(1024)S(1)}, u32[]{:S(2)}) copy-start(s32[1024]{0:T(1024)S(1)} %convert_reduce_fusion.1) | copy-start | bytes 12292
  21.1 3.6 %copy-start.19 = (bf16[1024,256]{1,0:T(8,128)(2,1)}, bf16[1024,256]{1,0:T(8,128)(2,1)S(1)}, u32[]{:S(2)}) copy-start(bf16[1024,256]{1,0:T(8,128)(2,1)S(1)} %collective-permute-done.1.refs_2_) | copy-start | bytes 1572868
  21.1 3.6 %collective-permute-start.2 = (bf16[1024,256]{1,0:T(8,128)(2,1)S(1)}, bf16[1024,256]{1,0:T(8,128)(2,1)S(1)}, u32[]{:S(2)}, u32[]{:S(2)}) collective-permute-start(bf16[1024,256]{1,0:T(8,128)(2,1)S(1)} %collective-permute-done.1.refs_2_), channel_id=1, source_target_pairs={{0,1},{1,0},{2,3},{3,2},{4,5},{5,4},{6,7},{7,6},{8,9},{9,8},{10,11... | collective-permute-start | bytes 1572872 | tf_op jit(solution)/shard_map/gather_tokens/ppermute | solution.py:544
  21.6 25.7 %collective-permute-start.4 = (bf16[1024,256]{1,0:T(8,128)(2,1)}, bf16[1024,256]{1,0:T(8,128)(2,1)S(1)}, u32[]{:S(2)}, u32[]{:S(2)}) collective-permute-start(bf16[1024,256]{1,0:T(8,128)(2,1)} %refs_0_.2), channel_id=1, source_target_pairs={{0,2},{1,3},{2,0},{3,1},{4,6},{5,7},{6,4},{7,5},{8,10},{9,11},{10,... | collective-permute-start | bytes 1572872 | tf_op jit(solution)/shard_map/gather_grads/ppermute | solution.py:544
  24.7 0.8 copy-start.20
  24.7 1.0 copy-start.21
  25.7 21.7 %copy-start = (bf16[1024,256]{1,0:T(8,128)(2,1)S(1)}, bf16[1024,256]{1,0:T(8,128)(2,1)}, u32[]{:S(2)}) copy-start(bf16[1024,256]{1,0:T(8,128)(2,1)} %refs_0_.2) | copy-start | bytes 1572868
  39.2 9.5 %copy-start.18 = (f32[1024,1]{1,0:T(8,128)S(1)}, f32[1024,1]{1,0:T(8,128)}, u32[]{:S(2)}) copy-start(f32[1024,1]{1,0:T(8,128)} %get-tuple-element.95) | copy-start | bytes 12292
  41.0 27.4 %all-to-all-start = ((f32[8,72,256]{2,1,0:T(8,128)}), f32[8,72,256]{2,1,0:T(8,128)S(1)}, u32[]{:S(2)}, u32[]{:S(2)}) async-start(f32[8,72,256]{2,1,0:T(8,128)} %broadcast_in_dim.37), calls=%async_computation | async-start | bytes 1179648 | tf_op jit(solution)/shard_map/state/all_to_all | solution.py:601
  47.3 237.1 %all-reduce.3.cloned.1.call-start = ((), (), s32[]{:S(2)}) async-start(), calls=%async_computation.2 | async-start | bytes 8388608 | tf_op jit(solution)/shard_map/ff_sum/psum | solution.py:790
  47.3 2.7 copy-start.12
  47.3 2.0 collective-permute-start.5
  47.4 2.6 collective-permute-start.3
  49.3 0.8 copy-start.14
  50.0 0.8 copy-start.15
  69.1 12.5 %copy-start.5 = (bf16[1024,1024]{1,0:T(8,128)(2,1)S(1)}, bf16[1024,1024]{1,0:T(8,128)(2,1)}, u32[]{:S(2)}) copy-start(bf16[1024,1024]{1,0:T(8,128)(2,1)} %get-tuple-element.79.grad_ref) | copy-start | bytes 6291460
  81.6 2.8 copy-start.4
  81.6 2.8 copy-start.10
  84.4 0.9 copy-start.22
  84.4 2.3 copy-start.2
  84.4 2.3 copy-start.25
  85.3 6.4 %collective-permute-start.6 = (f32[72,256]{1,0:T(8,128)S(1)}, f32[72,256]{1,0:T(8,128)S(1)}, u32[]{:S(2)}, u32[]{:S(2)}) collective-permute-start(f32[72,256]{1,0:T(8,128)S(1)} %copy-done.22), channel_id=1, source_target_pairs={{0,4},{4,0},{8,12},{12,8},{16,20},{20,16},{24,28},{28,24},{1,5},{5... | collective-permute-start | bytes 221192 | tf_op jit(solution)/shard_map/grad_state/ppermute | solution.py:620
  89.1 8.0 %copy-start.8 = (bf16[1024,1024]{1,0:T(8,128)(2,1)}, bf16[1024,1024]{1,0:T(8,128)(2,1)S(1)}, u32[]{:S(2)}) copy-start(bf16[1024,1024]{1,0:T(8,128)(2,1)S(1)} %add_convert_fusion) | copy-start | bytes 6291460
  91.7 11.0 %collective-permute-start.7 = (f32[72,256]{1,0:T(8,128)S(1)}, f32[72,256]{1,0:T(8,128)S(1)}, u32[]{:S(2)}, u32[]{:S(2)}) collective-permute-start(f32[72,256]{1,0:T(8,128)S(1)} %add.162), channel_id=1, source_target_pairs={{8,0},{12,4},{16,8},{20,12},{24,16},{28,20},{9,1},{13,5},{17,9},{2... | collective-permute-start | bytes 221192 | tf_op jit(solution)/shard_map/grad_state/ppermute | solution.py:627
  93.9 10.7 %collective-permute-start.8 = (f32[72,256]{1,0:T(8,128)S(1)}, f32[72,256]{1,0:T(8,128)S(1)}, u32[]{:S(2)}, u32[]{:S(2)}) collective-permute-start(f32[72,256]{1,0:T(8,128)S(1)} %add.162), channel_id=1, source_target_pairs={{16,0},{20,4},{24,8},{28,12},{17,1},{21,5},{25,9},{29,13},{18,2},{... | collective-permute-start | bytes 221192 | tf_op jit(solution)/shard_map/grad_state/ppermute | solution.py:627
  95.2 9.4 %collective-permute-start.9 = (f32[72,256]{1,0:T(8,128)S(1)}, f32[72,256]{1,0:T(8,128)S(1)}, u32[]{:S(2)}, u32[]{:S(2)}) collective-permute-start(f32[72,256]{1,0:T(8,128)S(1)} %add.162), channel_id=1, source_target_pairs={{24,0},{28,4},{25,1},{29,5},{26,2},{30,6},{27,3},{31,7}} | collective-permute-start | bytes 221192 | tf_op jit(solution)/shard_map/grad_state/ppermute | solution.py:627
  117.3 30.5 %collective-permute-start.24 = (bf16[4,2,128,256]{3,2,1,0:T(8,128)(2,1)}, bf16[4,2,128,256]{3,2,1,0:T(8,128)(2,1)S(1)}, u32[]{:S(2)}, u32[]{:S(2)}) collective-permute-start(bf16[4,2,128,256]{3,2,1,0:T(8,128)(2,1)} %get-tuple-element.111), channel_id=1, source_target_pairs={{0,4},{4,0},{8,12},{12,8},{16,20},{20,16},{24,28},{28,24},{1,5},{5... | collective-permute-start | bytes 1572872 | tf_op jit(solution)/shard_map/reduce_qk/ppermute | solution.py:544
  118.8 32.2 %collective-permute-start.16 = (bf16[4,2,128,256]{3,2,1,0:T(8,128)(2,1)}, bf16[4,2,128,256]{3,2,1,0:T(8,128)(2,1)S(1)}, u32[]{:S(2)}, u32[]{:S(2)}) collective-permute-start(bf16[4,2,128,256]{3,2,1,0:T(8,128)(2,1)} %get-tuple-element.104), channel_id=1, source_target_pairs={{0,4},{4,0},{8,12},{12,8},{16,20},{20,16},{24,28},{28,24},{1,5},{5... | collective-permute-start | bytes 1572872 | tf_op jit(solution)/shard_map/reduce_vo/ppermute | solution.py:544
  131.2 16.6 %copy-start.16 = (bf16[4,2,128,256]{3,2,1,0:T(8,128)(2,1)S(1)}, bf16[4,2,128,256]{3,2,1,0:T(8,128)(2,1)}, u32[]{:S(2)}) copy-start(bf16[4,2,128,256]{3,2,1,0:T(8,128)(2,1)} %get-tuple-element.110) | copy-start | bytes 1572868
  132.1 1.2 collective-permute-start.14
  134.0 13.7 %collective-permute-start.15 = (f32[8,1024]{1,0:T(8,128)S(1)}, f32[8,1024]{1,0:T(8,128)S(1)}, u32[]{:S(2)}, u32[]{:S(2)}) collective-permute-start(f32[8,1024]{1,0:T(8,128)S(1)} %slice_add_fusion.1), channel_id=1, source_target_pairs={{0,2},{1,3},{2,0},{3,1},{4,6},{5,7},{6,4},{7,5},{8,10},{9,11},{10,... | collective-permute-start | bytes 98312 | tf_op jit(solution)/shard_map/stats_sum/ppermute | solution.py:544
  137.8 18.5 %copy-start.13 = (bf16[4,2,128,256]{3,2,1,0:T(8,128)(2,1)S(1)}, bf16[4,2,128,256]{3,2,1,0:T(8,128)(2,1)}, u32[]{:S(2)}) copy-start(bf16[4,2,128,256]{3,2,1,0:T(8,128)(2,1)} %get-tuple-element.103) | copy-start | bytes 1572868
  138.6 116.1 %all-to-all-start.1 = ((f32[32,13,256]{2,1,0:T(8,128)}), f32[32,13,256]{2,1,0:T(8,128)S(1)}, u32[]{:S(2)}, u32[]{:S(2)}) async-start(f32[32,13,256]{2,1,0:T(8,128)} %bitcast.26), calls=%async_computation.1 | async-start | bytes 1048576 | tf_op jit(solution)/shard_map/small_sum/all_to_all | solution.py:965
  147.2 110.8 %collective-permute-start.12 = (bf16[2,1024,256]{2,1,0:T(8,128)(2,1)}, bf16[2,1024,256]{2,1,0:T(8,128)(2,1)}, u32[]{:S(2)}, u32[]{:S(2)}) collective-permute-start(bf16[2,1024,256]{2,1,0:T(8,128)(2,1)} %get-tuple-element.99), channel_id=1, source_target_pairs={{0,1},{1,0},{2,3},{3,2},{4,5},{5,4},{6,7},{7,6},{8,9},{9,8},{10,11... | collective-permute-start | bytes 3145736 | tf_op jit(solution)/shard_map/e_sum/ppermute | solution.py:544
  147.4 107.3 %collective-permute-start.10 = (bf16[2,1024,256]{2,1,0:T(8,128)(2,1)}, bf16[2,1024,256]{2,1,0:T(8,128)(2,1)}, u32[]{:S(2)}, u32[]{:S(2)}) collective-permute-start(bf16[2,1024,256]{2,1,0:T(8,128)(2,1)} %pad_maximum_fusion), channel_id=1, source_target_pairs={{0,1},{1,0},{2,3},{3,2},{4,5},{5,4},{6,7},{7,6},{8,9},{9,8},{10,11... | collective-permute-start | bytes 3145736 | tf_op jit(solution)/shard_map/mixed_sum/ppermute | solution.py:544
  148.0 18.0 %collective-permute-start.25 = (bf16[2,128,256]{2,1,0:T(8,128)(2,1)S(1)}, bf16[2,128,256]{2,1,0:T(8,128)(2,1)S(1)}, u32[]{:S(2)}, u32[]{:S(2)}) collective-permute-start(bf16[2,128,256]{2,1,0:T(8,128)(2,1)S(1)} %get-tuple-element.129), channel_id=1, source_target_pairs={{0,8},{4,12},{8,0},{12,4},{16,24},{20,28},{24,16},{28,20},{1,9},{5... | collective-permute-start | bytes 393224 | tf_op jit(solution)/shard_map/reduce_qk/ppermute | solution.py:544
  148.4 25.4 %collective-permute-start.26 = (bf16[2,128,256]{2,1,0:T(8,128)(2,1)S(1)}, bf16[2,128,256]{2,1,0:T(8,128)(2,1)S(1)}, u32[]{:S(2)}, u32[]{:S(2)}) collective-permute-start(bf16[2,128,256]{2,1,0:T(8,128)(2,1)S(1)} %get-tuple-element.128), channel_id=1, source_target_pairs={{0,16},{4,20},{8,24},{12,28},{16,0},{20,4},{24,8},{28,12},{1,17},{... | collective-permute-start | bytes 393224 | tf_op jit(solution)/shard_map/reduce_qk/ppermute | solution.py:544
  151.0 42.6 %collective-permute-start.27 = (bf16[2,128,256]{2,1,0:T(8,128)(2,1)S(1)}, bf16[2,128,256]{2,1,0:T(8,128)(2,1)S(1)}, u32[]{:S(2)}, u32[]{:S(2)}) collective-permute-start(bf16[2,128,256]{2,1,0:T(8,128)(2,1)S(1)} %get-tuple-element.127), channel_id=1, source_target_pairs={{0,24},{4,28},{8,16},{12,20},{16,8},{20,12},{24,0},{28,4},{1,25},{... | collective-permute-start | bytes 393224 | tf_op jit(solution)/shard_map/reduce_qk/ppermute | solution.py:544
  166.0 27.7 %collective-permute-start.17 = (bf16[2,128,256]{2,1,0:T(8,128)(2,1)S(1)}, bf16[2,128,256]{2,1,0:T(8,128)(2,1)S(1)}, u32[]{:S(2)}, u32[]{:S(2)}) collective-permute-start(bf16[2,128,256]{2,1,0:T(8,128)(2,1)S(1)} %get-tuple-element.133), channel_id=1, source_target_pairs={{0,8},{4,12},{8,0},{12,4},{16,24},{20,28},{24,16},{28,20},{1,9},{5... | collective-permute-start | bytes 393224 | tf_op jit(solution)/shard_map/reduce_vo/ppermute | solution.py:544
  173.8 21.4 %collective-permute-start.18 = (bf16[2,128,256]{2,1,0:T(8,128)(2,1)S(1)}, bf16[2,128,256]{2,1,0:T(8,128)(2,1)S(1)}, u32[]{:S(2)}, u32[]{:S(2)}) collective-permute-start(bf16[2,128,256]{2,1,0:T(8,128)(2,1)S(1)} %get-tuple-element.132), channel_id=1, source_target_pairs={{0,16},{4,20},{8,24},{12,28},{16,0},{20,4},{24,8},{28,12},{1,17},{... | collective-permute-start | bytes 393224 | tf_op jit(solution)/shard_map/reduce_vo/ppermute | solution.py:544
  193.6 13.2 %collective-permute-start.19 = (bf16[2,128,256]{2,1,0:T(8,128)(2,1)S(1)}, bf16[2,128,256]{2,1,0:T(8,128)(2,1)S(1)}, u32[]{:S(2)}, u32[]{:S(2)}) collective-permute-start(bf16[2,128,256]{2,1,0:T(8,128)(2,1)S(1)} %get-tuple-element.131), channel_id=1, source_target_pairs={{0,24},{4,28},{8,16},{12,20},{16,8},{20,12},{24,0},{28,4},{1,25},{... | collective-permute-start | bytes 393224 | tf_op jit(solution)/shard_map/reduce_vo/ppermute | solution.py:544
  193.7 13.2 %collective-permute-start.28 = (bf16[2,128,256]{2,1,0:T(8,128)(2,1)S(1)}, bf16[2,128,256]{2,1,0:T(8,128)(2,1)S(1)}, u32[]{:S(2)}, u32[]{:S(2)}) collective-permute-start(bf16[2,128,256]{2,1,0:T(8,128)(2,1)S(1)} %add_convert_fusion.5), channel_id=1, source_target_pairs={{0,8},{4,12},{8,0},{12,4},{16,24},{20,28},{24,16},{28,20},{1,9},{5... | collective-permute-start | bytes 393224 | tf_op jit(solution)/shard_map/reduce_qk/ppermute | solution.py:544
  195.2 18.9 %collective-permute-start.29 = (bf16[2,128,256]{2,1,0:T(8,128)(2,1)S(1)}, bf16[2,128,256]{2,1,0:T(8,128)(2,1)S(1)}, u32[]{:S(2)}, u32[]{:S(2)}) collective-permute-start(bf16[2,128,256]{2,1,0:T(8,128)(2,1)S(1)} %add_convert_fusion.5), channel_id=1, source_target_pairs={{0,16},{4,20},{8,24},{12,28},{16,0},{20,4},{24,8},{28,12},{1,17},{... | collective-permute-start | bytes 393224 | tf_op jit(solution)/shard_map/reduce_qk/ppermute | solution.py:544
  206.8 26.4 %collective-permute-start.30 = (bf16[2,128,256]{2,1,0:T(8,128)(2,1)S(1)}, bf16[2,128,256]{2,1,0:T(8,128)(2,1)S(1)}, u32[]{:S(2)}, u32[]{:S(2)}) collective-permute-start(bf16[2,128,256]{2,1,0:T(8,128)(2,1)S(1)} %add_convert_fusion.5), channel_id=1, source_target_pairs={{0,24},{4,28},{8,16},{12,20},{16,8},{20,12},{24,0},{28,4},{1,25},{... | collective-permute-start | bytes 393224 | tf_op jit(solution)/shard_map/reduce_qk/ppermute | solution.py:544
  206.9 26.7 %collective-permute-start.20 = (bf16[2,128,256]{2,1,0:T(8,128)(2,1)S(1)}, bf16[2,128,256]{2,1,0:T(8,128)(2,1)S(1)}, u32[]{:S(2)}, u32[]{:S(2)}) collective-permute-start(bf16[2,128,256]{2,1,0:T(8,128)(2,1)S(1)} %add_convert_fusion.6), channel_id=1, source_target_pairs={{0,8},{4,12},{8,0},{12,4},{16,24},{20,28},{24,16},{28,20},{1,9},{5... | collective-permute-start | bytes 393224 | tf_op jit(solution)/shard_map/reduce_vo/ppermute | solution.py:544
  214.1 25.9 %collective-permute-start.21 = (bf16[2,128,256]{2,1,0:T(8,128)(2,1)S(1)}, bf16[2,128,256]{2,1,0:T(8,128)(2,1)S(1)}, u32[]{:S(2)}, u32[]{:S(2)}) collective-permute-start(bf16[2,128,256]{2,1,0:T(8,128)(2,1)S(1)} %add_convert_fusion.6), channel_id=1, source_target_pairs={{0,16},{4,20},{8,24},{12,28},{16,0},{20,4},{24,8},{28,12},{1,17},{... | collective-permute-start | bytes 393224 | tf_op jit(solution)/shard_map/reduce_vo/ppermute | solution.py:544
  233.2 20.5 %collective-permute-start.22 = (bf16[2,128,256]{2,1,0:T(8,128)(2,1)S(1)}, bf16[2,128,256]{2,1,0:T(8,128)(2,1)S(1)}, u32[]{:S(2)}, u32[]{:S(2)}) collective-permute-start(bf16[2,128,256]{2,1,0:T(8,128)(2,1)S(1)} %add_convert_fusion.6), channel_id=1, source_target_pairs={{0,24},{4,28},{8,16},{12,20},{16,8},{20,12},{24,0},{28,4},{1,25},{... | collective-permute-start | bytes 393224 | tf_op jit(solution)/shard_map/reduce_vo/ppermute | solution.py:544
  233.5 24.5 %copy-start.11 = (bf16[2,1024,256]{2,1,0:T(8,128)(2,1)S(1)}, bf16[2,1024,256]{2,1,0:T(8,128)(2,1)}, u32[]{:S(2)}) copy-start(bf16[2,1024,256]{2,1,0:T(8,128)(2,1)} %get-tuple-element.98) | copy-start | bytes 3145732
  233.6 26.3 %copy-start.6 = (bf16[4,2,128,256]{3,2,1,0:T(8,128)(2,1)}, bf16[4,2,128,256]{3,2,1,0:T(8,128)(2,1)S(1)}, u32[]{:S(2)}) copy-start(bf16[4,2,128,256]{3,2,1,0:T(8,128)(2,1)S(1)} %pad_maximum_fusion.2.own_ref) | copy-start | bytes 1572868
  233.6 29.7 %collective-permute-start.31 = (bf16[4,2,128,256]{3,2,1,0:T(8,128)(2,1)S(1)}, bf16[4,2,128,256]{3,2,1,0:T(8,128)(2,1)S(1)}, u32[]{:S(2)}, u32[]{:S(2)}) collective-permute-start(bf16[4,2,128,256]{3,2,1,0:T(8,128)(2,1)S(1)} %pad_maximum_fusion.2.own_ref), channel_id=1, source_target_pairs={{0,4},{4,0},{8,12},{12,8},{16,20},{20,16},{24,28},{28,24},{1,5},{5... | collective-permute-start | bytes 1572872 | tf_op jit(solution)/shard_map/reduce_qk/ppermute | solution.py:544
  253.8 12.7 %copy-start.7 = (bf16[4,2,128,256]{3,2,1,0:T(8,128)(2,1)}, bf16[4,2,128,256]{3,2,1,0:T(8,128)(2,1)S(1)}, u32[]{:S(2)}) copy-start(bf16[4,2,128,256]{3,2,1,0:T(8,128)(2,1)S(1)} %pad_maximum_fusion.1.own_ref) | copy-start | bytes 1572868
  253.8 13.4 %collective-permute-start.23 = (bf16[4,2,128,256]{3,2,1,0:T(8,128)(2,1)S(1)}, bf16[4,2,128,256]{3,2,1,0:T(8,128)(2,1)}, u32[]{:S(2)}, u32[]{:S(2)}) collective-permute-start(bf16[4,2,128,256]{3,2,1,0:T(8,128)(2,1)S(1)} %pad_maximum_fusion.1.own_ref), channel_id=1, source_target_pairs={{0,4},{4,0},{8,12},{12,8},{16,20},{20,16},{24,28},{28,24},{1,5},{5... | collective-permute-start | bytes 1572872 | tf_op jit(solution)/shard_map/reduce_vo/ppermute | solution.py:544
  256.9 15.2 %collective-permute-start.11 = (bf16[1,1024,256]{2,1,0:T(8,128)(2,1)}, bf16[1,1024,256]{2,1,0:T(8,128)(2,1)}, u32[]{:S(2)}, u32[]{:S(2)}) collective-permute-start(bf16[1,1024,256]{2,1,0:T(8,128)(2,1)} %fusion), channel_id=1, source_target_pairs={{0,2},{1,3},{2,0},{3,1},{4,6},{5,7},{6,4},{7,5},{8,10},{9,11},{10,... | collective-permute-start | bytes 1572872 | tf_op jit(solution)/shard_map/mixed_sum/ppermute | solution.py:544
  259.9 21.8 %collective-permute-start.13 = (bf16[1,1024,256]{2,1,0:T(8,128)(2,1)}, bf16[1,1024,256]{2,1,0:T(8,128)(2,1)S(1)}, u32[]{:S(2)}, u32[]{:S(2)}) collective-permute-start(bf16[1,1024,256]{2,1,0:T(8,128)(2,1)} %add_convert_fusion.3), channel_id=1, source_target_pairs={{0,2},{1,3},{2,0},{3,1},{4,6},{5,7},{6,4},{7,5},{8,10},{9,11},{10,... | collective-permute-start | bytes 1572872 | tf_op jit(solution)/shard_map/e_sum/ppermute | solution.py:544
  261.4 29.6 %copy-start.24 = (f32[1,256]{1,0:T(1,128)}, f32[1,256]{1,0:T(1,128)S(1)}, u32[]{:S(2)}) copy-start(f32[1,256]{1,0:T(1,128)S(1)} %get-tuple-element.135) | copy-start | bytes 3076
  263.3 0.8 copy-start.17
  266.5 5.5 %copy-start.9 = (bf16[1024,256]{1,0:T(8,128)(2,1)S(1)}, bf16[1024,256]{1,0:T(8,128)(2,1)}, u32[]{:S(2)}) copy-start(bf16[1024,256]{1,0:T(8,128)(2,1)} %refs_0_.1) | copy-start | bytes 1572868
  270.1 11.6 %copy-start.1 = (bf16[1024,256]{1,0:T(8,128)(2,1)S(1)}, bf16[1024,256]{1,0:T(8,128)(2,1)}, u32[]{:S(2)}) copy-start(bf16[1024,256]{1,0:T(8,128)(2,1)} %refs_0_.2) | copy-start | bytes 1572868
  284.4 4.2 %copy-start.3 = (bf16[1024,1024]{1,0:T(8,128)(2,1)S(1)}, bf16[1024,1024]{1,0:T(8,128)(2,1)}, u32[]{:S(2)}) copy-start(bf16[1024,1024]{1,0:T(8,128)(2,1)} %get-tuple-element.124) | copy-start | bytes 6291460
Sparse Core Ops, SparseCore 0:
  68.5 197.7 all-reduce.2

commit v3 on v2

--- a/solution.py
+++ b/solution.py
@@ -20,6 +20,10 @@
 f32 = jnp.float32
 COST_SCALE = 0.02
 END_COST = 12
+BEFORE = "DI"
+AFTER = "DCIICDCIC"
+PINNED = "C"
+LATE = 3
 VMEM_LIMIT = 56 * 1024 * 1024
 
 
@@ -176,17 +180,27 @@
         pk_ref[head_size:] = norm
 
 
-def store_blocks(block, base, me, keep_at, send_at, part):
-    for parity in range(2):
-
-        @pl.when(me % 2 == parity)
+def slot_of(relative, count):
+    place = 0
+    mask = 4
+    while mask < count:
+        place = 2 * place + (relative // mask) % 2
+        mask *= 2
+    return place
+
+
+def store_blocks(block, base, me, refs, part, rest=()):
+    count = 4 * refs[0].shape[0]
+    for low in range(4):
+
+        @pl.when(me % 4 == low)
         def _():
             for j in range(block.shape[0] // part):
-                put = keep_at if j % 2 == parity else send_at
-                put((me ^ (base + j)) // 2, block[j * part : (j + 1) * part])
-
-
-def ff_kernel(pieces, me_ref, *refs):
+                ref = refs[(low ^ (base + j)) % 4]
+                ref[(slot_of(me ^ (base + j), count),) + rest] = block[j * part : (j + 1) * part]
+
+
+def ff_kernel(pieces, me_ref, rank_ref, *refs):
     grad_refs = refs[:pieces]
     (
         ln2_ref,
@@ -197,8 +211,7 @@
         grad_ref,
         hid_ref,
         dpre_ref,
-        gdown_ref,
-        gin_ref,
+        *sum_refs,
         gb_ref,
     ) = refs[pieces:]
 
@@ -218,8 +231,29 @@
         sums = sums + jnp.sum(dpre, 0, keepdims=True)
         dpre_ref[part] = dpre.astype(bf16)
     gb_ref[...] = sums
-    gdown_ref[...] = tn(hid_ref[...], grad_ref[...]).astype(bf16)
-    gin_ref[...] = nn(ln2t_ref[...], dpre_ref[...]).astype(bf16)
+    me = rank_ref[0]
+    g_down = tn(hid_ref[...], grad_ref[...]).astype(bf16)
+    part = sum_refs[0].shape[1]
+    steps = 4 * sum_refs[0].shape[0] * part // g_down.shape[0]
+    for step in range(steps):
+
+        @pl.when(pl.program_id(0) == step)
+        def _():
+            store_blocks(g_down, step * (g_down.shape[0] // part), me, sum_refs[:4], part)
+
+    g_in = nn(ln2t_ref[...], dpre_ref[...]).astype(bf16)
+    store_blocks(g_in, 0, me, sum_refs[4:], sum_refs[4].shape[1])
+
+
+def block_out_kernel(rank_ref, *refs):
+    out_ref = refs[4]
+    part = refs[0].shape[1]
+    for low in range(4):
+
+        @pl.when(rank_ref[0] % 4 == low)
+        def _():
+            for j in range(4):
+                out_ref[j * part : (j + 1) * part] = refs[low ^ j][0].astype(f32)
 
 
 def attn_kernel(
@@ -240,10 +274,12 @@
     gb_ref,
     gzb_ref,
     gpk_ref,
+    gout_ref,
     state_ref,
     norm_ref,
     lead_ref,
     leadz_ref,
+    acc_ref,
 ):
     step = pl.program_id(0)
     last = pl.num_programs(0) - 1
@@ -262,6 +298,7 @@
         norm_ref[...] = spk_ref[head_size : head_size + 8]
         lead_ref[...] = jnp.zeros_like(lead_ref)
         leadz_ref[...] = jnp.zeros_like(leadz_ref)
+        acc_ref[...] = jnp.zeros_like(acc_ref)
 
     seg = segc_ref[...]
     enters = (seg == labels_ref[step, 0]).astype(f32)
@@ -302,7 +339,9 @@
     den = den_in + enters * head_sum(qf32 * norm)
     inv_den = 1.0 / den
     att = num * inv_den
-    att_ref[...] = att.astype(bf16)
+    att_low = att.astype(bf16)
+    att_ref[...] = att_low
+    acc_ref[...] += tn(att_low, grad_ref[...])
     d_att = nt(grad_ref[...], wout_ref[...])
     d_num = d_att * inv_den
     d_den = -head_sum(d_att * att) * inv_den
@@ -330,6 +369,7 @@
         packed, z = pack_state(lead_ref[...], leadz_ref[...], head_size)
         gpk_ref[:head_size] = packed
         gpk_ref[head_size:] = z
+        gout_ref[...] = acc_ref[...].T.astype(bf16)
 
 
 def spread(full, keep_ref, send_ref, scratch_ref, me_ref):
@@ -363,10 +403,10 @@
     rank_ref,
     low_ref,
     small_ref,
-    keep0_ref,
-    send0_ref,
-    keep1_ref,
-    send1_ref,
+    sum0_ref,
+    sum1_ref,
+    sum2_ref,
+    sum3_ref,
     state_ref,
     norm_ref,
     all_ref,
@@ -417,30 +457,34 @@
     @pl.when(step == last)
     def _():
         me = rank_ref[0]
-        part = keep0_ref.shape[2]
+        part = sum0_ref.shape[2]
         for c in range(4):
             g = gout_ref[...] if c == 3 else nn(ln1t_ref[...], all_ref[c]).astype(bf16)
 
-            def put(ref, slot, value):
-                ref[slot, c % 2] = value
-
-            pair = (keep1_ref, send1_ref) if c >= 2 else (keep0_ref, send0_ref)
-            store_blocks(g, 0, me, functools.partial(put, pair[0]), functools.partial(put, pair[1]), part)
-
-
-def e_kernel(
+            store_blocks(g, 0, me, (sum0_ref, sum1_ref, sum2_ref, sum3_ref), part, (c,))
+
+
+def finish_kernel(
     me_ref,
+    hid_ref,
+    wdown_ref,
+    att_ref,
+    wout_ref,
     dpre_ref,
     low_ref,
     w_ref,
     win_ref,
     xhat_ref,
     gains_ref,
+    val_keep_ref,
+    val_send_ref,
     keep_ref,
     send_ref,
     stat_ref,
     scratch_ref,
 ):
+    value = nn(hid_ref[...], wdown_ref[...]) + nn(att_ref[...], wout_ref[...])
+    spread(value, val_keep_ref, val_send_ref, scratch_ref, me_ref)
     step = pl.program_id(0)
     rows, model = xhat_ref.shape
 
@@ -467,42 +511,25 @@
     stat_ref[11:12, :model] += jnp.sum(d_ln2, 0, keepdims=True)
 
 
-def spread_rows(rank_ref, own_ref, other_ref, slab, write):
-    half, _, part, _ = own_ref.shape
-    for parity in range(2):
-
-        @pl.when(rank_ref[0] % 2 == parity)
+def widen_kernel(rank_ref, *refs):
+    qkv_ref, out_ref, scratch_ref = refs[4:]
+    c = pl.program_id(0)
+    quarter, _, part, _ = refs[0].shape
+    me = rank_ref[0]
+    for low in range(4):
+
+        @pl.when(me % 4 == low)
         def _():
-            for i in range(half):
-                for odd in range(2):
-                    ref = own_ref if odd == parity else other_ref
-                    slot = (rank_ref[0] // 2) ^ i
-                    write((2 * i + odd) * part, part, ref[slot, slab].astype(f32))
-
-
-def widen0_kernel(rank_ref, own_ref, other_ref, qkv_ref):
-    def write(start, size, value):
-        qkv_ref[0, start : start + size] = value
-
-    spread_rows(rank_ref, own_ref, other_ref, 0, write)
-
-
-def widen1_kernel(rank_ref, own_ref, other_ref, qkv_in_ref, qkv_ref, out_ref, scratch_ref):
-    c = pl.program_id(0)
-
-    def write_qkv(start, size, value):
-        qkv_ref[0, start : start + size] = value
-
-    def write_out(start, size, value):
-        scratch_ref[start : start + size] = value
-
-    @pl.when(c == 0)
+            for j in range(4 * quarter):
+                slot = slot_of(me ^ j, 4 * quarter)
+                scratch_ref[j * part : (j + 1) * part] = refs[(low ^ j) % 4][slot, 0].astype(f32)
+
+    @pl.when(c < 3)
     def _():
-        spread_rows(rank_ref, own_ref, other_ref, 0, write_qkv)
-
-    @pl.when(c == 1)
+        qkv_ref[0] = scratch_ref[...]
+
+    @pl.when(c == 3)
     def _():
-        spread_rows(rank_ref, own_ref, other_ref, 0, write_out)
         out_ref[...] = scratch_ref[...].T
 
 
@@ -578,21 +605,58 @@
     return x
 
 
-def reduce_pairs(keep, send, pin):
-    got = after(exchange(send, "seq", 1), pin)
-    return (keep.astype(f32) + got.astype(f32)).astype(bf16)
-
-
-def reduce_groups(half, pin):
-    terms = [half[0]] + [exchange(half[k], "seq", 2 * k) for k in range(1, half.shape[0])]
-    terms = after(tuple(terms), pin)
-    return sum(t.astype(f32) for t in terms).astype(bf16)
-
-
-def gather_blocks(block):
-    count = lax.axis_size("seq")
-    own = jnp.stack([block] + [exchange(block, "seq", 2 * k) for k in range(1, count // 2)])
-    return own, exchange(own, "seq", 1)
+class Sum:
+    def __init__(self, name, arrays):
+        self.name, self.arrays = name, list(arrays)
+        masks = []
+        while 4 * 2 ** len(masks) < lax.axis_size("seq"):
+            masks.append(4 * 2 ** len(masks))
+        self.plan = [("group", 0)] + [("reduce", m) for m in masks]
+        self.plan += [("gather", m) for m in masks[::-1]] + [("spread", 0)]
+
+    def halves(self, terms):
+        half = terms[0].shape[0] // 2
+
+        def total(part):
+            return sum(t[part].astype(f32) for t in terms).astype(bf16)
+
+        if half:
+            self.keep, self.send = total(slice(0, half)), total(slice(half, None))
+        else:
+            self.keep = self.send = total(slice(None))
+        return self.send
+
+    def step(self, *pins):
+        kind, mask = self.plan.pop(0)
+        with jax.named_scope(self.name):
+            if kind == "group":
+                got = after(tuple(exchange(self.arrays[g], "seq", g) for g in (1, 2, 3)), *pins)
+                return self.halves([self.arrays[0], *got])
+            if kind == "reduce":
+                return self.halves([self.keep, after(exchange(self.send, "seq", mask), *pins)])
+            if kind == "gather":
+                self.keep = jnp.concatenate([self.keep, after(exchange(self.keep, "seq", mask), *pins)])
+                return self.keep
+            self.arrays = [self.keep, *after(tuple(exchange(self.keep, "seq", g) for g in (1, 2, 3)), *pins)]
+            return self.arrays[1]
+
+
+def block_out(chunk, me_seq):
+    quarter, part, width = chunk.keep.shape
+    block = pl.BlockSpec((1, part, width), lambda i, me: (slot_of(((me[0] // 4) ^ i) * 4, 4 * quarter), 0, 0))
+    return pl.pallas_call(
+        block_out_kernel,
+        grid_spec=pltpu.PrefetchScalarGridSpec(
+            num_scalar_prefetch=1,
+            grid=(quarter,),
+            in_specs=[block] * 4,
+            out_specs=pl.BlockSpec((4 * part, width), lambda i, me: (i, 0)),
+        ),
+        out_shape=sds((4 * quarter * part, width), f32),
+        compiler_params=pltpu.CompilerParams(vmem_limit_bytes=VMEM_LIMIT),
+        cost_estimate=pl.CostEstimate(flops=0, bytes_accessed=24 * quarter * part * width, transcendentals=0),
+        name="block_out_kernel",
+    )(me_seq, *chunk.arrays)
 
 
 def sum_before(packet):
@@ -607,7 +671,7 @@
     return lax.optimization_barrier((x,) + others)[0]
 
 
-def neighbour_sum(packet, sign, pin):
+def neighbour_sum(packet, sign, pin, event):
     count = lax.axis_size("seq")
     outer = 4 if count % 4 == 0 else 1
     inner = count // outer
@@ -618,6 +682,7 @@
     for k in range(1, inner):
         route = [(i, i - i % inner + (i % inner + k) % inner) for i in range(count)]
         got = after(lax.ppermute(packet, "seq", route), pin)
+        event(got)
         sender = (mine - k) % inner
         group = group + got
         before = before + jnp.where((sender < mine) if sign > 0 else (sender > mine), got, 0.0)
@@ -753,10 +818,12 @@
         s_in = sum_before(s_own)
 
     fb = 256
-    full_grad, hid, dpre, g_down, g_in, gb_in = call(
+    quarter = n_seq // 4
+    full_grad, hid, dpre, *ff_sums, gb_in = call(
         functools.partial(ff_kernel, n_head),
         hidden // fb,
         [
+            smem(),
             smem(),
             *[whole(rows, share)] * n_head,
             whole(rows, model),
@@ -769,28 +836,26 @@
             whole(rows, model),
             pl.BlockSpec((rows, fb), lambda i: (0, i)),
             pl.BlockSpec((rows, fb), lambda i: (0, i)),
-            pl.BlockSpec((fb, model), lambda i: (i, 0)),
-            pl.BlockSpec((model, fb), lambda i: (0, i)),
+            *[whole(quarter, hidden // n_seq, model)] * 4,
+            *[pl.BlockSpec((quarter, model // n_seq, fb), lambda i: (0, 0, i))] * 4,
             pl.BlockSpec((1, fb), lambda i: (0, i)),
         ],
         [
             sds((rows, model), bf16),
             sds((rows, hidden), bf16),
             sds((rows, hidden), bf16),
-            sds((hidden, model), bf16),
-            sds((model, hidden), bf16),
+            *[sds((quarter, hidden // n_seq, model), bf16)] * 4,
+            *[sds((quarter, model // n_seq, hidden), bf16)] * 4,
             sds((1, hidden), f32),
         ],
         [],
         8 * rows * model * hidden,
         6 * rows * model + 8 * model * hidden,
-    )(me_head, *grad_pieces, ln2, ln2t, w_in, b_in[None, :], w_down)
-
-    with jax.named_scope("ff_sum"):
-        g_down, g_in = lax.psum((g_down, g_in), "seq")
+    )(me_head, me_seq, *grad_pieces, ln2, ln2t, w_in, b_in[None, :], w_down)
+
     s_in = after(s_in, hid)
 
-    att, dq, dk, dv, gb, gzb, g_own = call(
+    att, dq, dk, dv, gb, gzb, g_own, g_out = call(
         functools.partial(attn_kernel, head_size),
         blocks,
         [
@@ -812,6 +877,7 @@
             rows_of(1, width, width),
             rows_of(1, 8, width),
             whole(*packet_shape),
+            whole(model, width),
         ],
         [
             sds((rows, width), bf16),
@@ -821,28 +887,26 @@
             sds((blocks, width, width), f32),
             sds((blocks, 8, width), f32),
             sds(packet_shape, f32),
+            sds((model, width), bf16),
         ],
         [
             pltpu.VMEM((width, width), f32),
             pltpu.VMEM((8, width), f32),
             pltpu.VMEM((width, width), f32),
             pltpu.VMEM((8, width), f32),
+            pltpu.VMEM((width, model), f32),
         ],
         24 * rows * heads * BT * width,
         rows * model * 2 + rows * width * 20,
     )(labels, qf, kf, v, full_grad, w_out, seg_col, seg_row, s_in)
 
+    down = Sum("reduce_down", ff_sums[:4])
+    seen = []
     with jax.named_scope("grad_state"):
-        grad_in = neighbour_sum(g_own, -1, hid)
-
-    value = jnp.dot(hid, w_down, preferred_element_type=f32) + jnp.dot(att, w_out, preferred_element_type=f32)
-    value = value.astype(bf16)
-    me = lax.axis_index("head")
-    order = [lax.dynamic_slice_in_dim(value, (me ^ k) * share, share, 1) for k in range(n_head)]
-    val_keep, val_send = jnp.stack(order[0::2]), jnp.stack(order[1::2])
-    g_out = lax.dot_general(full_grad, att, (((0,), (0,)), ((), ())), preferred_element_type=f32).astype(bf16)
-    grad_in = after(grad_in, g_out, value)
-
+        grad_in = neighbour_sum(g_own, -1, hid, seen.append)
+    inn = Sum("reduce_in", [ff_sums[4], *after(tuple(ff_sums[5:]), *seen)])
+    event = down.step(*seen)
+    grad_in = after(grad_in, event)
 
     def back_rows(*shape):
         return pl.BlockSpec(shape, lambda i: (blocks - 1 - i,) + (0,) * (len(shape) - 1))
@@ -869,12 +933,12 @@
         [
             pl.BlockSpec((3, BT, width), lambda i: (0, blocks - 1 - i, 0)),
             whole(8, width),
-            *[whole(n_seq // 2, 2, part, width)] * 4,
+            *[whole(quarter, 4, part, width)] * 4,
         ],
         [
             sds((3, rows, width), bf16),
             sds((8, width), f32),
-            *[sds((n_seq // 2, 2, part, width), bf16)] * 4,
+            *[sds((quarter, 4, part, width), bf16)] * 4,
         ],
         [
             pltpu.VMEM((width, width), f32),
@@ -885,12 +949,22 @@
         rows * width * 30 + rows * model * 2 + 6 * model * width,
     )(labels, dq, dk, dv, q_expo, k_expo, kf, v, gb, gzb, grad_in, seg_col, cosine, sine, fw, tab, ln1t, g_out, me_seq)
 
+    qkvo = Sum("reduce_attn", w_parts)
+    event = low
+    chunks = {"D": down, "I": inn, "C": qkvo}
+    for name in BEFORE:
+        event = chunks[name].step(event)
+
     stat_width = max(rows, model)
-    e_keep, e_send, stats = call(
-        e_kernel,
+    val_keep, val_send, e_keep, e_send, stats = call(
+        finish_kernel,
         blocks,
         [
             smem(),
+            rows_of(BT, hidden),
+            whole(hidden, model),
+            rows_of(BT, width),
+            whole(width, model),
             rows_of(BT, hidden),
             pl.BlockSpec((3, BT, width), lambda i: (0, i, 0)),
             whole(3, model, width),
@@ -899,56 +973,17 @@
             whole(4, model),
         ],
         [
-            pl.BlockSpec((n_head // 2, BT, share), lambda i: (0, i, 0)),
-            pl.BlockSpec((n_head // 2, BT, share), lambda i: (0, i, 0)),
+            *[pl.BlockSpec((n_head // 2, BT, share), lambda i: (0, i, 0))] * 4,
             whole(16, stat_width),
         ],
         [
-            sds((n_head // 2, rows, share), bf16),
-            sds((n_head // 2, rows, share), bf16),
+            *[sds((n_head // 2, rows, share), bf16)] * 4,
             sds((16, stat_width), f32),
         ],
         [pltpu.VMEM((BT, model), bf16)],
         2 * rows * model * (3 * width + hidden),
         rows * width * 6 + rows * model * 6 + 8 * model * width + 2 * hidden * model,
-    )(me_head, dpre, low, w_qkv, w_in, xhat, gains)
-
-    with jax.named_scope("reduce_qk"):
-        first = reduce_pairs(*w_parts[:2], low)
-    with jax.named_scope("reduce_vo"):
-        second = reduce_pairs(*w_parts[2:], low)
-    with jax.named_scope("reduce_qk"):
-        first = gather_blocks(reduce_groups(first, low))
-    with jax.named_scope("reduce_vo"):
-        second = gather_blocks(reduce_groups(second, low))
-    g_down = g_down.astype(f32)
-    g_in = g_in.astype(f32)
-
-    def slab():
-        return pl.BlockSpec((n_seq // 2, 1, part, width), lambda c: (0, c, 0, 0))
-
-    g_qkv = call(
-        widen0_kernel,
-        2,
-        [smem(), slab(), slab()],
-        pl.BlockSpec((1, model, width), lambda c: (c, 0, 0)),
-        sds((3, model, width), f32),
-        [],
-        0,
-        END_COST * model * width,
-    )(me_seq, *first)
-    g_qkv, g_out = call(
-        widen1_kernel,
-        2,
-        [smem(), slab(), slab(), pl.BlockSpec(memory_space=pl.ANY)],
-        [pl.BlockSpec((1, model, width), lambda c: (2, 0, 0)), whole(width, model)],
-        [sds((3, model, width), f32), sds((width, model), f32)],
-        [pltpu.VMEM((model, width), f32)],
-        0,
-        END_COST * model * width,
-        {3: 0},
-    )(me_seq, *second, g_qkv)
-
+    )(me_head, hid, w_down, att, w_out, dpre, after(low, event), w_qkv, w_in, xhat, gains)
     with jax.named_scope("mixed_sum"):
         mixed_share = scatter_sum(val_keep, after(val_send, low), "head")
     with jax.named_scope("e_sum"):
@@ -956,22 +991,48 @@
     with jax.named_scope("stats_sum"):
         gains_own = stats[8:12, :model]
         stats = sum_all(stats[:8], "head")
+    stats = stats[:2, :rows].T * (1.0 / model)
+
+    bias = lax.dynamic_slice_in_dim(b_out, offset, share) + lax.dynamic_slice_in_dim(b_down, offset, share)
+    mixed = (tokens.astype(f32) + mixed_share + bias).astype(bf16)
+    xhat_share = lax.dynamic_slice_in_dim(xhat, offset, share, 1).astype(f32)
+    grad_input = grad_out.astype(f32) + inv_std * (
+        e_share - stats[:, 0:1] - xhat_share * stats[:, 1:2]
+    )
+    event = late = e_send
+    for name in AFTER:
+        chunk = chunks[name]
+        if chunk.plan:
+            pins = (mixed, grad_input) if len(chunk.plan) == 1 and name in PINNED else ()
+            event = chunk.step(event, *pins)
+        late = event if len(qkvo.plan) == LATE else late
+    for chunk in chunks.values():
+        while chunk.plan:
+            event = chunk.step(event)
+    g_down = block_out(down, me_seq)
+    g_in = block_out(inn, me_seq)
+    g_qkv, g_out = call(
+        widen_kernel,
+        4,
+        [smem(), *[pl.BlockSpec((quarter, 1, part, width), lambda c: (0, c, 0, 0))] * 4],
+        [
+            pl.BlockSpec((1, model, width), lambda c: (jnp.minimum(c, 2), 0, 0)),
+            whole(width, model),
+        ],
+        [sds((3, model, width), f32), sds((width, model), f32)],
+        [pltpu.VMEM((model, width), f32)],
+        0,
+        END_COST * model * width,
+    )(me_seq, *qkvo.arrays)
+
     with jax.named_scope("small_sum"):
         local = jnp.concatenate([small[:4], gb_in.reshape(-1, share), bias_out], 0)
         mine = (jnp.arange(n_head) == lax.axis_index("head")).astype(f32)
         spread_gains = gains_own.reshape(4, n_head, share).transpose(1, 0, 2)
         packet = jnp.concatenate([spread_gains, mine[:, None, None] * local[None]], 1)
         packet = jnp.broadcast_to(packet[None], (n_seq,) + packet.shape).reshape((-1,) + packet.shape[1:])
-        packet = jnp.sum(lax.all_to_all(packet, ("seq", "head"), 0, 0, tiled=True), 0)
+        packet = jnp.sum(lax.all_to_all(after(packet, late), ("seq", "head"), 0, 0, tiled=True), 0)
     gain_share, small, gb_in, bias_out = packet[:4], packet[4:8], packet[8:-1].reshape(-1), packet[-1]
-    stats = stats[:2, :rows].T * (1.0 / model)
-
-    bias = lax.dynamic_slice_in_dim(b_out, offset, share) + lax.dynamic_slice_in_dim(b_down, offset, share)
-    mixed = (tokens.astype(f32) + mixed_share + bias).astype(bf16)
-    xhat_share = lax.dynamic_slice_in_dim(xhat, offset, share, 1).astype(f32)
-    grad_input = grad_out.astype(f32) + inv_std * (
-        e_share - stats[:, 0:1] - xhat_share * stats[:, 1:2]
-    )
     return (
         mixed,
         grad_input,

time: 300 us -> 276 us (0.920); the launches traced: 298 us -> 271 us
  waiting for transfers between devices: 105 us -> 81.6 us
  Pallas kernels: 70.2 us -> 86.2 us
  between operations: 14.5 us -> 1.18 us
  matrix products: 5.78 us -> 0 us
  other arithmetic: 31.6 us -> 27.3 us
  starting transfers between devices: 55 us -> 58.6 us
    ppermute x28 -> x36, waiting for transfers between devices: 95.2 us -> 71.9 us  [exchange(): return lax.ppermute(x, axis, [(i, i ^ mask) for i in range(count)])]
    pallas_call x4 -> x5, Pallas kernels: 32.1 us -> 46.4 us  [the longest x1 18.4 us: body(): call(functools.partial(ff_kernel, n_head), hidden // fb, [smem(), smem(),...]
    ppermute x28 -> x36, starting transfers between devices: 34.3 us -> 41.4 us  [exchange(): return lax.ppermute(x, axis, [(i, i ^ mask) for i in range(count)])]
    dot_general x3 -> x0, matrix products: 5.78 us -> none  [the longest x1 2.73 us: body(): lax.dot_general(full_grad, att, (((0,), (0,)), ((), ())), preferred_eleme...]
    all_to_all x1, starting transfers between devices: 8.56 us -> 4.45 us  [body(): lax.all_to_all(after(packet, late), ('seq', 'head'), 0, 0, tiled=True)]
    ppermute x3, waiting for transfers between devices: 7.43 us -> 3.56 us  [neighbour_sum(): before = before + lax.ppermute(group, 'seq', route)]
    ppermute x1, waiting for transfers between devices: 2.42 us -> 6.15 us  [neighbour_sum(): got = after(lax.ppermute(packet, 'seq', route), pin)]
  transfers between devices with their start and end apart: 35 -> 42, of which waited for: 19 -> 17; matrix products, arithmetic and copies ran while one was open for 15% -> 15% of each run, Pallas kernels for 24% -> 30%
where the time goes in v3:
time: 276 us; the launch traced here: 271 us
  Pallas kernels  86.2 us (31%)
  waiting for transfers between devices  81.6 us (30%)
  starting transfers between devices  58.6 us (21%)
  other arithmetic  27.3 us (10%)
  local copies, waits for them, and re-layouts  15.8 us (6%)
    ppermute x36, waiting for transfers between devices, exchange(): return lax.ppermute(x, axis, [(i, i ^ mask) for i in range(count)])  71.9 us
    ppermute x36, starting transfers between devices, exchange(): return lax.ppermute(x, axis, [(i, i ^ mask) for i in range(count)])  41.4 us
    pallas_call x1, Pallas kernels, body(): call(functools.partial(ff_kernel, n_head), hidden // fb, [smem(), smem(),...  18.4 us
    pallas_call x1, Pallas kernels, body(): call(finish_kernel, blocks, [smem(), rows_of(BT, hidden), whole(hidden, m...  16.1 us
    pallas_call x1, Pallas kernels, body(): call(functools.partial(attn_kernel, head_size), blocks, [smem(), rows_of(...  14.1 us
    pallas_call x1, Pallas kernels, body(): call(functools.partial(pre_kernel, head_size, n_head), blocks, [smem(), s...  13.5 us
    pallas_call x1, Pallas kernels, body(): call(functools.partial(tail_kernel, head_size), blocks, [smem(), *[back_r...  12.3 us
    pallas_call x2, Pallas kernels, block_out(): pl.pallas_call(block_out_kernel, grid_spec=pltpu.PrefetchScalarGridSpec(n...  6.83 us
  transfers between devices with their start and end apart: 42, of which 17 were waited for; matrix products, arithmetic and copies ran while one was open for 15% of the time, Pallas kernels for 30%

profile of v3, /device:TPU:8, one launch (start us, length us, event | category | flops | bytes accessed | tf_op | source)
XLA Modules:
  0.0 270.8 jit_solution(3139860312684796385)
XLA Ops:
  0.7 1.6 collective-permute-start.1
  2.3 0.8 reduce-window.8
  3.8 1.2 convert_reduce_fusion
  7.4 1.4 pad_maximum_fusion.4.refs_4_.gains_ref
  8.8 1.3 reshape.122.refs_7_.fw_ref
  10.8 3.8 %fusion.4 = (f32[1024,128]{1,0:T(8,128)}, f32[1024,128]{1,0:T(8,128)}) fusion(f32[128]{0:T(128)} %constant.54.clone, f32[128]{0:T(128)} %constant.53.clone, f32[1024]{0:T(1024)S(1)} %subtract_convert_fusion), kind=kLoop, calls=%fused_computation.15 | loop fusion | flops 262144 | bytes 1053696 | tf_op jit(solution)/shard_map/mul | solution.py:751
  15.3 1.5 collective-permute-start.4
  16.8 1.0 copy.54.refs_12_.segc_ref
  17.8 1.0 copy.53.refs_11_
  19.8 13.5 %pre_kernel.1 = (bf16[1024,1024]{1,0:T(8,128)(2,1)}, bf16[1024,1024]{1,0:T(8,128)(2,1)}, bf16[1024,1024]{1,0:T(8,128)(2,1)}, bf16[1024,1024]{1,0:T(8,128)(2,1)},...) custom-call(s32[4,3]{1,0:T(4,128)} %add_add_fusion.1.labels_ref, ...), custom_call_target="tpu_custom_call" | custom-call | flops 53687092 | bytes 241172 | tf_op jit(solution)/shard_map/pre_kernel/pallas_call | solution.py:767
  33.3 1.8 broadcast_in_dim.37
  35.1 6.3 %all-to-all-start = ((f32[8,72,256]{2,1,0:T(8,128)}), f32[8,72,256]{2,1,0:T(8,128)S(1)}, u32[]{:S(2)}, u32[]{:S(2)}) async-start(f32[8,72,256]{2,1,0:T(8,128)} %broadcast_in_dim.37), calls=%async_computation | async-start | bytes 1179648 | tf_op jit(solution)/shard_map/state/all_to_all | solution.py:665
  41.9 1.4 collective-permute-done.3.refs_1_
  44.9 18.4 %ff_kernel.1 = (bf16[1024,1024]{1,0:T(8,128)(2,1)}, bf16[1024,1024]{1,0:T(8,128)(2,1)}, bf16[1024,1024]{1,0:T(8,128)(2,1)}, bf16[2,128,1024]{2,1,0:T(8,128)(2,1)...) custom-call(s32[1]{0:T(128)} %bitcast.me_ref, ...), custom_call_target="tpu_custom_call" | custom-call | flops 171798688 | bytes 293601 | tf_op jit(solution)/shard_map/ff_kernel/pallas_call | solution.py:822
  63.3 1.5 collective-permute-start.10
  65.4 1.5 collective-permute-start.12
  68.4 14.1 %attn_kernel.1 = (bf16[1024,256]{1,0:T(8,128)(2,1)}, f32[1024,256]{1,0:T(8,128)}, f32[1024,256]{1,0:T(8,128)}, f32[1024,256]{1,0:T(8,128)}, f32[4,256,256]{2,1,0...) custom-call(s32[4,3]{1,0:T(4,128)} %add_add_fusion.1.labels_ref, ...), custom_call_target="tpu_custom_call" | custom-call | flops 128849016 | bytes 146800 | tf_op jit(solution)/shard_map/attn_kernel/pallas_call | solution.py:858
  82.5 1.5 collective-permute-start.6
  85.4 6.2 %collective-permute-done.6 = f32[72,256]{1,0:T(8,128)S(1)} collective-permute-done((f32[72,256]{1,0:T(8,128)}, f32[72,256]{1,0:T(8,128)S(1)}, u32[]{:S(2)}, u32[]{:S(2)}) %collective-permute-start.6) | collective-permute-done | bytes 73760 | tf_op jit(solution)/shard_map/grad_state/ppermute | solution.py:684
  91.6 0.9 add.180
  93.1 1.3 collective-permute-start.8
  94.4 3.1 %collective-permute-start.7 = (f32[72,256]{1,0:T(8,128)S(1)}, f32[72,256]{1,0:T(8,128)S(1)}, u32[]{:S(2)}, u32[]{:S(2)}) collective-permute-start(f32[72,256]{1,0:T(8,128)S(1)} %add.180), channel_id=1, source_target_pairs={{8,0},{12,4},{16,8},{20,12},{24,16},{28,20},{9,1},{13,5},{17,9},{2... | collective-permute-start | bytes 221192 | tf_op jit(solution)/shard_map/grad_state/ppermute | solution.py:692
  97.7 3.6 %collective-permute-start.16 = (bf16[1,128,1024]{2,1,0:T(8,128)(2,1)S(1)}, bf16[1,128,1024]{2,1,0:T(8,128)(2,1)S(1)}, u32[]{:S(2)}, u32[]{:S(2)}) collective-permute-start(bf16[1,128,1024]{2,1,0:T(8,128)(2,1)S(1)} %add_convert_fusion.12), channel_id=1, source_target_pairs={{0,16},{4,20},{8,24},{12,28},{16,0},{20,4},{24,8},{28,12},{1,17},{... | collective-permute-start | bytes 786440 | tf_op jit(solution)/shard_map/reduce_down/ppermute | solution.py:571
  101.3 1.7 collective-permute-start.13
  103.0 3.2 %collective-permute-start.15 = (bf16[2,128,1024]{2,1,0:T(8,128)(2,1)}, bf16[2,128,1024]{2,1,0:T(8,128)(2,1)S(1)}, u32[]{:S(2)}, u32[]{:S(2)}) collective-permute-start(bf16[2,128,1024]{2,1,0:T(8,128)(2,1)} %get-tuple-element.137), channel_id=1, source_target_pairs={{0,12},{4,8},{8,4},{12,0},{16,28},{20,24},{24,20},{28,16},{1,13},{... | collective-permute-start | bytes 1572872 | tf_op jit(solution)/shard_map/reduce_in/ppermute | solution.py:571
  106.2 3.6 %collective-permute-done.7 = f32[72,256]{1,0:T(8,128)S(1)} collective-permute-done((f32[72,256]{1,0:T(8,128)S(1)}, f32[72,256]{1,0:T(8,128)S(1)}, u32[]{:S(2)}, u32[]{:S(2)}) %collective-permute-start.7) | collective-permute-done | bytes 73760 | tf_op jit(solution)/shard_map/grad_state/ppermute | solution.py:692
  110.4 12.3 %tail_kernel.1 = (bf16[3,1024,256]{2,1,0:T(8,128)(2,1)}, f32[8,256]{1,0:T(8,128)}, bf16[2,4,128,256]{3,2,1,0:T(8,128)(2,1)}, bf16[2,4,128,256]{3,2,1,0:T(8,128)(...) custom-call(s32[4,3]{1,0:T(4,128)} %add_add_fusion.1.labels_ref, ...), custom_call_target="tpu_custom_call" | custom-call | flops 32212254 | bytes 230686 | tf_op jit(solution)/shard_map/tail_kernel/pallas_call | solution.py:915
  123.4 1.7 collective-permute-start.24
  125.2 1.8 collective-permute-start.26
  127.3 11.0 %collective-permute-done.15 = bf16[2,128,1024]{2,1,0:T(8,128)(2,1)S(1)} collective-permute-done((bf16[2,128,1024]{2,1,0:T(8,128)(2,1)}, bf16[2,128,1024]{2,1,0:T(8,128)(2,1)S(1)}, u32[]{:S(2)}, u32[]{:S(2)}) %collective-permute-start.15) | collective-permute-done | bytes 524320 | tf_op jit(solution)/shard_map/reduce_in/ppermute | solution.py:571
  138.5 2.2 collective-permute-start.23
  140.6 16.1 %finish_kernel.1 = (bf16[2,1024,256]{2,1,0:T(8,128)(2,1)}, bf16[2,1024,256]{2,1,0:T(8,128)(2,1)}, bf16[2,1024,256]{2,1,0:T(8,128)(2,1)}, bf16[2,1024,256]{2,1,0:T(8,128)(2,1)}, f32[16,1024]{1,0:T(8,128)}) custom-call(s32[1]{0:T(128)} %bitcast.me_ref, bf16[1024,1024]{1,0:T(8,128)(2,1)} %get-tuple-element.103.hid_ref, bf16[1024,1024]{1,0:T(8,128)(2,1)} %wdown_ref.1, ...), custom_call_target="tpu_custom_call" | custom-call | flops 75161928 | bytes 241172 | tf_op jit(solution)/shard_map/finish_kernel/pallas_call | solution.py:959
  156.7 3.5 %collective-permute-done.27 = bf16[1,128,1024]{2,1,0:T(8,128)(2,1)S(1)} collective-permute-done((bf16[1,128,1024]{2,1,0:T(8,128)(2,1)S(1)}, bf16[1,128,1024]{2,1,0:T(8,128)(2,1)S(1)}, u32[]{:S(2)}, u32[]{:S(2)}) %collective-permute-start.27) | collective-permute-done | bytes 262176 | tf_op jit(solution)/shard_map/reduce_down/ppermute | solution.py:571
  160.3 0.9 slice.182
  161.2 1.4 slice.178
  162.7 3.1 %collective-permute-start.32 = (bf16[2,128,1024]{2,1,0:T(8,128)(2,1)S(1)}, bf16[2,128,1024]{2,1,0:T(8,128)(2,1)S(1)}, u32[]{:S(2)}, u32[]{:S(2)}) collective-permute-start(bf16[2,128,1024]{2,1,0:T(8,128)(2,1)S(1)} %pad_maximum_fusion.refs_0_), channel_id=1, source_target_pairs={{0,8},{4,12},{8,0},{12,4},{16,24},{20,28},{24,16},{28,20},{1,9},{5... | collective-permute-start | bytes 1572872 | tf_op jit(solution)/shard_map/reduce_down/ppermute | solution.py:571
  166.4 1.2 add_convert_fusion.7
  167.6 1.3 add_convert_fusion.6
  169.0 2.3 collective-permute-start.28
  171.3 0.8 collective-permute-start.29
  172.1 23.3 %collective-permute-done.28 = bf16[1,128,1024]{2,1,0:T(8,128)(2,1)S(1)} collective-permute-done((bf16[1,128,1024]{2,1,0:T(8,128)(2,1)S(1)}, bf16[1,128,1024]{2,1,0:T(8,128)(2,1)S(1)}, u32[]{:S(2)}, u32[]{:S(2)}) %collective-permute-start.28) | collective-permute-done | bytes 262176 | tf_op jit(solution)/shard_map/reduce_in/ppermute | solution.py:571
  196.0 2.3 collective-permute-done.29
  198.3 1.7 collective-permute-start.31
  200.0 1.3 add_convert_fusion.4
  201.4 0.9 broadcast_in_dim.68
  202.2 4.5 %all-to-all-start.1 = ((f32[32,13,256]{2,1,0:T(8,128)}), f32[32,13,256]{2,1,0:T(8,128)S(1)}, u32[]{:S(2)}, u32[]{:S(2)}) async-start(f32[32,13,256]{2,1,0:T(8,128)} %bitcast.22), calls=%async_computation.1 | async-start | bytes 1048576 | tf_op jit(solution)/shard_map/small_sum/all_to_all | solution.py:1034
  206.8 1.5 collective-permute-start.39
  208.3 4.0 %collective-permute-done.31.refs_1_ = bf16[2,128,1024]{2,1,0:T(8,128)(2,1)} collective-permute-done((bf16[2,128,1024]{2,1,0:T(8,128)(2,1)S(1)}, bf16[2,128,1024]{2,1,0:T(8,128)(2,1)}, u32[]{:S(2)}, u32[]{:S(2)}) %collective-permute-start.31) | collective-permute-done | bytes 524320 | tf_op jit(solution)/shard_map/reduce_down/ppermute | solution.py:571
  212.3 3.4 %block_out_kernel.3 = f32[1024,1024]{1,0:T(8,128)} custom-call(s32[1]{0:T(128)} %bitcast.1.rank_ref, bf16[2,128,1024]{2,1,0:T(8,128)(2,1)} %copy-done.2, bf16[2,128,1024]{2,1,0:T(8,128)(2,1)} %collective-permute-done.31.refs_1_, bf16[2,128,1024]{2,1,0:T(8,128)(2,1)} %copy-done.9, bf16[2,128,1024]{2,1,0:T(8,128)(2,1)} %copy-done.8), custom_call_target="tpu_custom_call" | custom-call | bytes 6291456 | tf_op jit(solution)/shard_map/block_out_kernel/pallas_call | solution.py:647
  215.7 3.5 %collective-permute-done.30 = bf16[1,4,128,256]{3,2,1,0:T(8,128)(2,1)S(1)} collective-permute-done((bf16[1,4,128,256]{3,2,1,0:T(8,128)(2,1)S(1)}, bf16[1,4,128,256]{3,2,1,0:T(8,128)(2,1)S(1)}, u32[]{:S(2)}, u32[]{:S(2)}) %collective-permute-start.30) | collective-permute-done | bytes 262176 | tf_op jit(solution)/shard_map/reduce_attn/ppermute | solution.py:571
  219.7 3.5 %collective-permute-start.36 = (bf16[2,4,128,256]{3,2,1,0:T(8,128)(2,1)S(1)}, bf16[2,4,128,256]{3,2,1,0:T(8,128)(2,1)}, u32[]{:S(2)}, u32[]{:S(2)}) collective-permute-start(bf16[2,4,128,256]{3,2,1,0:T(8,128)(2,1)S(1)} %pad_maximum_fusion.2.refs_0_), channel_id=1, source_target_pairs={{0,12},{4,8},{8,4},{12,0},{16,28},{20,24},{24,20},{28,16},{1,13},{... | collective-permute-start | bytes 1572872 | tf_op jit(solution)/shard_map/reduce_attn/ppermute | solution.py:571
  223.2 2.0 add_convert_fusion.2
  225.7 2.0 add_convert_fusion
  227.7 4.0 %collective-permute-done.39.refs_3_ = bf16[2,128,1024]{2,1,0:T(8,128)(2,1)S(1)} collective-permute-done((bf16[2,128,1024]{2,1,0:T(8,128)(2,1)S(1)}, bf16[2,128,1024]{2,1,0:T(8,128)(2,1)S(1)}, u32[]{:S(2)}, u32[]{:S(2)}) %collective-permute-start.39) | collective-permute-done | bytes 524320 | tf_op jit(solution)/shard_map/reduce_in/ppermute | solution.py:571
  231.7 2.9 %collective-permute-start.35 = (bf16[2,4,128,256]{3,2,1,0:T(8,128)(2,1)S(1)}, bf16[2,4,128,256]{3,2,1,0:T(8,128)(2,1)}, u32[]{:S(2)}, u32[]{:S(2)}) collective-permute-start(bf16[2,4,128,256]{3,2,1,0:T(8,128)(2,1)S(1)} %pad_maximum_fusion.2.refs_0_), channel_id=1, source_target_pairs={{0,8},{4,12},{8,0},{12,4},{16,24},{20,28},{24,16},{28,20},{1,9},{5... | collective-permute-start | bytes 1572872 | tf_op jit(solution)/shard_map/reduce_attn/ppermute | solution.py:571
  234.6 8.2 %collective-permute-done.38.refs_2_ = bf16[2,128,1024]{2,1,0:T(8,128)(2,1)S(1)} collective-permute-done((bf16[2,128,1024]{2,1,0:T(8,128)(2,1)S(1)}, bf16[2,128,1024]{2,1,0:T(8,128)(2,1)S(1)}, u32[]{:S(2)}, u32[]{:S(2)}) %collective-permute-start.38) | collective-permute-done | bytes 524320 | tf_op jit(solution)/shard_map/reduce_in/ppermute | solution.py:571
  242.9 1.1 collective-permute-start.34
  244.0 1.5 collective-permute-start.20
  245.4 3.4 %block_out_kernel.2 = f32[1024,1024]{1,0:T(8,128)} custom-call(s32[1]{0:T(128)} %bitcast.1.rank_ref, bf16[2,128,1024]{2,1,0:T(8,128)(2,1)} %copy-done.3, bf16[2,128,1024]{2,1,0:T(8,128)(2,1)} %copy-done.13, bf16[2,128,1024]{2,1,0:T(8,128)(2,1)} %copy-done.12, bf16[2,128,1024]{2,1,0:T(8,128)(2,1)} %copy-done.11), custom_call_target="tpu_custom_call" | custom-call | bytes 6291456 | tf_op jit(solution)/shard_map/block_out_kernel/pallas_call | solution.py:647
  251.4 2.4 fusion.3
  253.8 3.2 %collective-permute-done.20 = bf16[1,1024,256]{2,1,0:T(8,128)(2,1)} collective-permute-done((bf16[1,1024,256]{2,1,0:T(8,128)(2,1)}, bf16[1,1024,256]{2,1,0:T(8,128)(2,1)}, u32[]{:S(2)}, u32[]{:S(2)}) %collective-permute-start.20) | collective-permute-done | bytes 524320 | tf_op jit(solution)/shard_map/e_sum/ppermute | solution.py:571
  257.0 2.8 %convert_add_fusion = f32[1024,256]{1,0:T(8,128)} fusion(bf16[1024,256]{1,0:T(8,128)(2,1)S(1)} %copy-done.1, bf16[1,1024,256]{2,1,0:T(8,128)(2,1)} %collective-permute-done.20, bf16[2,1024,256]{2,1,0:T(8,128)(2,1)} %collective-permute-done.19, f32[1024]{0:T(1024)S(1)} %bitcast.50, bf16[1024,1024]{1,0:T(8,128)(2,1)} %get-tuple-element.143.xhat_ref, ...), kind=kLoop, calls=%fused_computation | loop fusion | flops 3670016 | bytes 3682308 | tf_op jit(solution)/shard_map/add | solution.py:999
  259.8 5.3 %collective-permute-done.35.refs_2_ = bf16[2,4,128,256]{3,2,1,0:T(8,128)(2,1)} collective-permute-done((bf16[2,4,128,256]{3,2,1,0:T(8,128)(2,1)S(1)}, bf16[2,4,128,256]{3,2,1,0:T(8,128)(2,1)}, u32[]{:S(2)}, u32[]{:S(2)}) %collective-permute-start.35) | collective-permute-done | bytes 524320 | tf_op jit(solution)/shard_map/reduce_attn/ppermute | solution.py:571
  265.2 5.1 %widen_kernel.1 = (f32[3,1024,256]{2,1,0:T(8,128)}, f32[256,1024]{1,0:T(8,128)}) custom-call(s32[1]{0:T(128)} %bitcast.1.rank_ref, bf16[2,4,128,256]{3,2,1,0:T(8,128)(2,1)} %copy-done.4, bf16[2,4,128,256]{3,2,1,0:T(8,128)(2,1)} %collective-permute-done.34.refs_1_, bf16[2,4,128,256]{3,2,1,0:T(8,128)(2,1)} %collective-permute-done.35.refs_2_, ...), custom_call_target="tpu_custom_call" | custom-call | bytes 62914 | tf_op jit(solution)/shard_map/widen_kernel/pallas_call | solution.py:1014
  (153 shorter events, 19.6 us)
Async XLA Ops:
  0.6 18.2 %collective-permute-start = (bf16[1024,256]{1,0:T(8,128)(2,1)}, bf16[1024,256]{1,0:T(8,128)(2,1)S(1)}, u32[]{:S(2)}, u32[]{:S(2)}) collective-permute-start(bf16[1024,256]{1,0:T(8,128)(2,1)} %refs_0_.1), channel_id=1, source_target_pairs={{0,1},{1,0},{2,3},{3,2},{4,5},{5,4},{6,7},{7,6},{8,9},{9,8},{10,11... | collective-permute-start | bytes 1572872 | tf_op jit(solution)/shard_map/gather_tokens/ppermute | solution.py:571
  0.7 14.5 %collective-permute-start.1 = (bf16[1024,256]{1,0:T(8,128)(2,1)}, bf16[1024,256]{1,0:T(8,128)(2,1)S(1)}, u32[]{:S(2)}, u32[]{:S(2)}) collective-permute-start(bf16[1024,256]{1,0:T(8,128)(2,1)} %refs_0_.1), channel_id=1, source_target_pairs={{0,2},{1,3},{2,0},{3,1},{4,6},{5,7},{6,4},{7,5},{8,10},{9,11},{10,... | collective-permute-start | bytes 1572872 | tf_op jit(solution)/shard_map/gather_tokens/ppermute | solution.py:571
  5.5 27.8 %copy-start.28 = (s32[1024]{0:T(1024)}, s32[1024]{0:T(1024)S(1)}, u32[]{:S(2)}) copy-start(s32[1024]{0:T(1024)S(1)} %convert_reduce_fusion.1) | copy-start | bytes 12292
  15.3 3.6 %collective-permute-start.2 = (bf16[1024,256]{1,0:T(8,128)(2,1)S(1)}, bf16[1024,256]{1,0:T(8,128)(2,1)S(1)}, u32[]{:S(2)}, u32[]{:S(2)}) collective-permute-start(bf16[1024,256]{1,0:T(8,128)(2,1)S(1)} %collective-permute-done.1.refs_2_), channel_id=1, source_target_pairs={{0,1},{1,0},{2,3},{3,2},{4,5},{5,4},{6,7},{7,6},{8,9},{9,8},{10,11... | collective-permute-start | bytes 1572872 | tf_op jit(solution)/shard_map/gather_tokens/ppermute | solution.py:571
  15.3 26.1 %collective-permute-start.4 = (bf16[1024,256]{1,0:T(8,128)(2,1)}, bf16[1024,256]{1,0:T(8,128)(2,1)S(1)}, u32[]{:S(2)}, u32[]{:S(2)}) collective-permute-start(bf16[1024,256]{1,0:T(8,128)(2,1)} %refs_0_.2), channel_id=1, source_target_pairs={{0,2},{1,3},{2,0},{3,1},{4,6},{5,7},{6,4},{7,5},{8,10},{9,11},{10,... | collective-permute-start | bytes 1572872 | tf_op jit(solution)/shard_map/gather_grads/ppermute | solution.py:571
  19.8 21.5 %copy-start = (bf16[1024,256]{1,0:T(8,128)(2,1)S(1)}, bf16[1024,256]{1,0:T(8,128)(2,1)}, u32[]{:S(2)}) copy-start(bf16[1024,256]{1,0:T(8,128)(2,1)} %refs_0_.2) | copy-start | bytes 1572868
  35.1 32.6 %all-to-all-start = ((f32[8,72,256]{2,1,0:T(8,128)}), f32[8,72,256]{2,1,0:T(8,128)S(1)}, u32[]{:S(2)}, u32[]{:S(2)}) async-start(f32[8,72,256]{2,1,0:T(8,128)} %broadcast_in_dim.37), calls=%async_computation | async-start | bytes 1179648 | tf_op jit(solution)/shard_map/state/all_to_all | solution.py:665
  41.4 2.0 collective-permute-start.3
  41.4 2.6 collective-permute-start.5
  63.3 31.1 %collective-permute-start.10 = (bf16[2,128,1024]{2,1,0:T(8,128)(2,1)}, bf16[2,128,1024]{2,1,0:T(8,128)(2,1)S(1)}, u32[]{:S(2)}, u32[]{:S(2)}) collective-permute-start(bf16[2,128,1024]{2,1,0:T(8,128)(2,1)} %get-tuple-element.121), channel_id=1, source_target_pairs={{0,4},{4,0},{8,12},{12,8},{16,20},{20,16},{24,28},{28,24},{1,5},{5... | collective-permute-start | bytes 1572872 | tf_op jit(solution)/shard_map/reduce_down/ppermute | solution.py:571
  64.8 32.7 %collective-permute-start.11 = (bf16[2,128,1024]{2,1,0:T(8,128)(2,1)}, bf16[2,128,1024]{2,1,0:T(8,128)(2,1)S(1)}, u32[]{:S(2)}, u32[]{:S(2)}) collective-permute-start(bf16[2,128,1024]{2,1,0:T(8,128)(2,1)} %get-tuple-element.122), channel_id=1, source_target_pairs={{0,8},{4,12},{8,0},{12,4},{16,24},{20,28},{24,16},{28,20},{1,9},{5... | collective-permute-start | bytes 1572872 | tf_op jit(solution)/shard_map/reduce_down/ppermute | solution.py:571
  65.4 32.1 %collective-permute-start.12 = (bf16[2,128,1024]{2,1,0:T(8,128)(2,1)}, bf16[2,128,1024]{2,1,0:T(8,128)(2,1)S(1)}, u32[]{:S(2)}, u32[]{:S(2)}) collective-permute-start(bf16[2,128,1024]{2,1,0:T(8,128)(2,1)} %get-tuple-element.123), channel_id=1, source_target_pairs={{0,12},{4,8},{8,4},{12,0},{16,28},{20,24},{24,20},{28,16},{1,13},{... | collective-permute-start | bytes 1572872 | tf_op jit(solution)/shard_map/reduce_down/ppermute | solution.py:571
  68.4 15.6 %copy-start.16 = (f32[1024,1]{1,0:T(8,128)S(1)}, f32[1024,1]{1,0:T(8,128)}, u32[]{:S(2)}) copy-start(f32[1024,1]{1,0:T(8,128)} %get-tuple-element.147) | copy-start | bytes 12292
  68.4 16.3 %copy-start.30 = (f32[1,1024]{1,0:T(1,128)S(1)}, f32[1,1024]{1,0:T(1,128)}, u32[]{:S(2)}) copy-start(f32[1,1024]{1,0:T(1,128)} %get-tuple-element.152) | copy-start | bytes 12292
  68.4 29.1 %copy-start.18 = (bf16[2,128,1024]{2,1,0:T(8,128)(2,1)S(1)}, bf16[2,128,1024]{2,1,0:T(8,128)(2,1)}, u32[]{:S(2)}) copy-start(bf16[2,128,1024]{2,1,0:T(8,128)(2,1)} %get-tuple-element.120) | copy-start | bytes 1572868
  82.5 9.1 %collective-permute-start.6 = (f32[72,256]{1,0:T(8,128)}, f32[72,256]{1,0:T(8,128)S(1)}, u32[]{:S(2)}, u32[]{:S(2)}) collective-permute-start(f32[72,256]{1,0:T(8,128)} %get-tuple-element.118), channel_id=1, source_target_pairs={{0,4},{4,0},{8,12},{12,8},{16,20},{20,16},{24,28},{28,24},{1,5},{5... | collective-permute-start | bytes 221192 | tf_op jit(solution)/shard_map/grad_state/ppermute | solution.py:684
  92.5 10.6 %collective-permute-start.9 = (f32[72,256]{1,0:T(8,128)S(1)}, f32[72,256]{1,0:T(8,128)S(1)}, u32[]{:S(2)}, u32[]{:S(2)}) collective-permute-start(f32[72,256]{1,0:T(8,128)S(1)} %add.180), channel_id=1, source_target_pairs={{24,0},{28,4},{25,1},{29,5},{26,2},{30,6},{27,3},{31,7}} | collective-permute-start | bytes 221192 | tf_op jit(solution)/shard_map/grad_state/ppermute | solution.py:692
  93.1 9.9 %collective-permute-start.8 = (f32[72,256]{1,0:T(8,128)S(1)}, f32[72,256]{1,0:T(8,128)S(1)}, u32[]{:S(2)}, u32[]{:S(2)}) collective-permute-start(f32[72,256]{1,0:T(8,128)S(1)} %add.180), channel_id=1, source_target_pairs={{16,0},{20,4},{24,8},{28,12},{17,1},{21,5},{25,9},{29,13},{18,2},{... | collective-permute-start | bytes 221192 | tf_op jit(solution)/shard_map/grad_state/ppermute | solution.py:692
  94.4 15.3 %collective-permute-start.7 = (f32[72,256]{1,0:T(8,128)S(1)}, f32[72,256]{1,0:T(8,128)S(1)}, u32[]{:S(2)}, u32[]{:S(2)}) collective-permute-start(f32[72,256]{1,0:T(8,128)S(1)} %add.180), channel_id=1, source_target_pairs={{8,0},{12,4},{16,8},{20,12},{24,16},{28,20},{9,1},{13,5},{17,9},{2... | collective-permute-start | bytes 221192 | tf_op jit(solution)/shard_map/grad_state/ppermute | solution.py:692
  97.7 27.4 %collective-permute-start.16 = (bf16[1,128,1024]{2,1,0:T(8,128)(2,1)S(1)}, bf16[1,128,1024]{2,1,0:T(8,128)(2,1)S(1)}, u32[]{:S(2)}, u32[]{:S(2)}) collective-permute-start(bf16[1,128,1024]{2,1,0:T(8,128)(2,1)S(1)} %add_convert_fusion.12), channel_id=1, source_target_pairs={{0,16},{4,20},{8,24},{12,28},{16,0},{20,4},{24,8},{28,12},{1,17},{... | collective-permute-start | bytes 786440 | tf_op jit(solution)/shard_map/reduce_down/ppermute | solution.py:571
  101.3 23.8 %collective-permute-start.13 = (bf16[2,128,1024]{2,1,0:T(8,128)(2,1)}, bf16[2,128,1024]{2,1,0:T(8,128)(2,1)S(1)}, u32[]{:S(2)}, u32[]{:S(2)}) collective-permute-start(bf16[2,128,1024]{2,1,0:T(8,128)(2,1)} %get-tuple-element.135), channel_id=1, source_target_pairs={{0,4},{4,0},{8,12},{12,8},{16,20},{20,16},{24,28},{28,24},{1,5},{5... | collective-permute-start | bytes 1572872 | tf_op jit(solution)/shard_map/reduce_in/ppermute | solution.py:571
  103.0 24.2 %collective-permute-start.14 = (bf16[2,128,1024]{2,1,0:T(8,128)(2,1)}, bf16[2,128,1024]{2,1,0:T(8,128)(2,1)S(1)}, u32[]{:S(2)}, u32[]{:S(2)}) collective-permute-start(bf16[2,128,1024]{2,1,0:T(8,128)(2,1)} %get-tuple-element.136), channel_id=1, source_target_pairs={{0,8},{4,12},{8,0},{12,4},{16,24},{20,28},{24,16},{28,20},{1,9},{5... | collective-permute-start | bytes 1572872 | tf_op jit(solution)/shard_map/reduce_in/ppermute | solution.py:571
  103.0 35.2 %collective-permute-start.15 = (bf16[2,128,1024]{2,1,0:T(8,128)(2,1)}, bf16[2,128,1024]{2,1,0:T(8,128)(2,1)S(1)}, u32[]{:S(2)}, u32[]{:S(2)}) collective-permute-start(bf16[2,128,1024]{2,1,0:T(8,128)(2,1)} %get-tuple-element.137), channel_id=1, source_target_pairs={{0,12},{4,8},{8,4},{12,0},{16,28},{20,24},{24,20},{28,16},{1,13},{... | collective-permute-start | bytes 1572872 | tf_op jit(solution)/shard_map/reduce_in/ppermute | solution.py:571
  110.4 27.9 %copy-start.17 = (bf16[2,128,1024]{2,1,0:T(8,128)(2,1)S(1)}, bf16[2,128,1024]{2,1,0:T(8,128)(2,1)}, u32[]{:S(2)}) copy-start(bf16[2,128,1024]{2,1,0:T(8,128)(2,1)} %get-tuple-element.131) | copy-start | bytes 1572868
  123.4 39.3 %collective-permute-start.24 = (bf16[2,4,128,256]{3,2,1,0:T(8,128)(2,1)}, bf16[2,4,128,256]{3,2,1,0:T(8,128)(2,1)}, u32[]{:S(2)}, u32[]{:S(2)}) collective-permute-start(bf16[2,4,128,256]{3,2,1,0:T(8,128)(2,1)} %get-tuple-element.154), channel_id=1, source_target_pairs={{0,4},{4,0},{8,12},{12,8},{16,20},{20,16},{24,28},{28,24},{1,5},{5... | collective-permute-start | bytes 1572872 | tf_op jit(solution)/shard_map/reduce_attn/ppermute | solution.py:571
  125.1 40.7 %collective-permute-start.25 = (bf16[2,4,128,256]{3,2,1,0:T(8,128)(2,1)}, bf16[2,4,128,256]{3,2,1,0:T(8,128)(2,1)}, u32[]{:S(2)}, u32[]{:S(2)}) collective-permute-start(bf16[2,4,128,256]{3,2,1,0:T(8,128)(2,1)} %get-tuple-element.155), channel_id=1, source_target_pairs={{0,8},{4,12},{8,0},{12,4},{16,24},{20,28},{24,16},{28,20},{1,9},{5... | collective-permute-start | bytes 1572872 | tf_op jit(solution)/shard_map/reduce_attn/ppermute | solution.py:571
  125.2 31.5 %copy-start.20 = (bf16[2,128,1024]{2,1,0:T(8,128)(2,1)}, bf16[2,128,1024]{2,1,0:T(8,128)(2,1)S(1)}, u32[]{:S(2)}) copy-start(bf16[2,128,1024]{2,1,0:T(8,128)(2,1)S(1)} %collective-permute-done.13) | copy-start | bytes 1572868
  125.2 41.2 %collective-permute-start.26 = (bf16[2,4,128,256]{3,2,1,0:T(8,128)(2,1)}, bf16[2,4,128,256]{3,2,1,0:T(8,128)(2,1)}, u32[]{:S(2)}, u32[]{:S(2)}) collective-permute-start(bf16[2,4,128,256]{3,2,1,0:T(8,128)(2,1)} %get-tuple-element.156), channel_id=1, source_target_pairs={{0,12},{4,8},{8,4},{12,0},{16,28},{20,24},{24,20},{28,16},{1,13},{... | collective-permute-start | bytes 1572872 | tf_op jit(solution)/shard_map/reduce_attn/ppermute | solution.py:571
  127.2 29.5 %copy-start.22 = (bf16[2,128,1024]{2,1,0:T(8,128)(2,1)}, bf16[2,128,1024]{2,1,0:T(8,128)(2,1)S(1)}, u32[]{:S(2)}) copy-start(bf16[2,128,1024]{2,1,0:T(8,128)(2,1)S(1)} %collective-permute-done.14) | copy-start | bytes 1572868
  127.2 33.0 %collective-permute-start.27 = (bf16[1,128,1024]{2,1,0:T(8,128)(2,1)S(1)}, bf16[1,128,1024]{2,1,0:T(8,128)(2,1)S(1)}, u32[]{:S(2)}, u32[]{:S(2)}) collective-permute-start(bf16[1,128,1024]{2,1,0:T(8,128)(2,1)S(1)} %add_convert_fusion.10), channel_id=1, source_target_pairs={{0,16},{4,20},{8,24},{12,28},{16,0},{20,4},{24,8},{28,12},{1,17},{... | collective-permute-start | bytes 786440 | tf_op jit(solution)/shard_map/reduce_down/ppermute | solution.py:571
  138.3 18.4 %copy-start.23 = (bf16[2,128,1024]{2,1,0:T(8,128)(2,1)}, bf16[2,128,1024]{2,1,0:T(8,128)(2,1)S(1)}, u32[]{:S(2)}) copy-start(bf16[2,128,1024]{2,1,0:T(8,128)(2,1)S(1)} %collective-permute-done.15) | copy-start | bytes 1572868
  138.5 29.2 %collective-permute-start.23 = (bf16[1,128,1024]{2,1,0:T(8,128)(2,1)S(1)}, bf16[1,128,1024]{2,1,0:T(8,128)(2,1)}, u32[]{:S(2)}, u32[]{:S(2)}) collective-permute-start(bf16[1,128,1024]{2,1,0:T(8,128)(2,1)S(1)} %add_convert_fusion.9), channel_id=1, source_target_pairs={{0,16},{4,20},{8,24},{12,28},{16,0},{20,4},{24,8},{28,12},{1,17},{... | collective-permute-start | bytes 786440 | tf_op jit(solution)/shard_map/reduce_in/ppermute | solution.py:571
  140.6 25.8 %copy-start.19 = (bf16[2,4,128,256]{3,2,1,0:T(8,128)(2,1)S(1)}, bf16[2,4,128,256]{3,2,1,0:T(8,128)(2,1)}, u32[]{:S(2)}) copy-start(bf16[2,4,128,256]{3,2,1,0:T(8,128)(2,1)} %get-tuple-element.153) | copy-start | bytes 1572868
  160.2 7.4 %copy-start.21 = (bf16[2,128,1024]{2,1,0:T(8,128)(2,1)S(1)}, bf16[2,128,1024]{2,1,0:T(8,128)(2,1)}, u32[]{:S(2)}) copy-start(bf16[2,128,1024]{2,1,0:T(8,128)(2,1)} %copy-done.20) | copy-start | bytes 1572868
  160.2 11.8 %copy-start.27 = (f32[16,1024]{1,0:T(8,128)S(1)}, f32[16,1024]{1,0:T(8,128)}, u32[]{:S(2)}) copy-start(f32[16,1024]{1,0:T(8,128)} %get-tuple-element.150) | copy-start | bytes 196612
  160.3 38.0 %copy-start.2 = (bf16[2,128,1024]{2,1,0:T(8,128)(2,1)}, bf16[2,128,1024]{2,1,0:T(8,128)(2,1)S(1)}, u32[]{:S(2)}) copy-start(bf16[2,128,1024]{2,1,0:T(8,128)(2,1)S(1)} %pad_maximum_fusion.refs_0_) | copy-start | bytes 1572868
  162.6 38.6 %collective-permute-start.33 = (bf16[2,128,1024]{2,1,0:T(8,128)(2,1)S(1)}, bf16[2,128,1024]{2,1,0:T(8,128)(2,1)S(1)}, u32[]{:S(2)}, u32[]{:S(2)}) collective-permute-start(bf16[2,128,1024]{2,1,0:T(8,128)(2,1)S(1)} %pad_maximum_fusion.refs_0_), channel_id=1, source_target_pairs={{0,12},{4,8},{8,4},{12,0},{16,28},{20,24},{24,20},{28,16},{1,13},{... | collective-permute-start | bytes 1572872 | tf_op jit(solution)/shard_map/reduce_down/ppermute | solution.py:571
  162.7 44.0 %collective-permute-start.32 = (bf16[2,128,1024]{2,1,0:T(8,128)(2,1)S(1)}, bf16[2,128,1024]{2,1,0:T(8,128)(2,1)S(1)}, u32[]{:S(2)}, u32[]{:S(2)}) collective-permute-start(bf16[2,128,1024]{2,1,0:T(8,128)(2,1)S(1)} %pad_maximum_fusion.refs_0_), channel_id=1, source_target_pairs={{0,8},{4,12},{8,0},{12,4},{16,24},{20,28},{24,16},{28,20},{1,9},{5... | collective-permute-start | bytes 1572872 | tf_op jit(solution)/shard_map/reduce_down/ppermute | solution.py:571
  165.8 5.4 %collective-permute-start.21 = (f32[8,1024]{1,0:T(8,128)}, f32[8,1024]{1,0:T(8,128)S(1)}, u32[]{:S(2)}, u32[]{:S(2)}) collective-permute-start(f32[8,1024]{1,0:T(8,128)} %slice.178), channel_id=1, source_target_pairs={{0,1},{1,0},{2,3},{3,2},{4,5},{5,4},{6,7},{7,6},{8,9},{9,8},{10,11... | collective-permute-start | bytes 98312 | tf_op jit(solution)/shard_map/stats_sum/ppermute | solution.py:571
  166.4 53.3 %collective-permute-start.17 = (bf16[2,1024,256]{2,1,0:T(8,128)(2,1)}, bf16[2,1024,256]{2,1,0:T(8,128)(2,1)}, u32[]{:S(2)}, u32[]{:S(2)}) collective-permute-start(bf16[2,1024,256]{2,1,0:T(8,128)(2,1)} %get-tuple-element.146), channel_id=1, source_target_pairs={{0,1},{1,0},{2,3},{3,2},{4,5},{5,4},{6,7},{7,6},{8,9},{9,8},{10,11... | collective-permute-start | bytes 3145736 | tf_op jit(solution)/shard_map/mixed_sum/ppermute | solution.py:571
  169.0 26.4 %collective-permute-start.28 = (bf16[1,128,1024]{2,1,0:T(8,128)(2,1)S(1)}, bf16[1,128,1024]{2,1,0:T(8,128)(2,1)S(1)}, u32[]{:S(2)}, u32[]{:S(2)}) collective-permute-start(bf16[1,128,1024]{2,1,0:T(8,128)(2,1)S(1)} %add_convert_fusion.6), channel_id=1, source_target_pairs={{0,16},{4,20},{8,24},{12,28},{16,0},{20,4},{24,8},{28,12},{1,17},{... | collective-permute-start | bytes 786440 | tf_op jit(solution)/shard_map/reduce_in/ppermute | solution.py:571
  171.3 27.0 %collective-permute-start.29 = (bf16[1,4,128,256]{3,2,1,0:T(8,128)(2,1)S(1)}, bf16[1,4,128,256]{3,2,1,0:T(8,128)(2,1)S(1)}, u32[]{:S(2)}, u32[]{:S(2)}) collective-permute-start(bf16[1,4,128,256]{3,2,1,0:T(8,128)(2,1)S(1)} %add_convert_fusion.7), channel_id=1, source_target_pairs={{0,16},{4,20},{8,24},{12,28},{16,0},{20,4},{24,8},{28,12},{1,17},{... | collective-permute-start | bytes 786440 | tf_op jit(solution)/shard_map/reduce_attn/ppermute | solution.py:571
  195.4 4.6 %collective-permute-start.22 = (f32[8,1024]{1,0:T(8,128)S(1)}, f32[8,1024]{1,0:T(8,128)S(1)}, u32[]{:S(2)}, u32[]{:S(2)}) collective-permute-start(f32[8,1024]{1,0:T(8,128)S(1)} %slice_add_fusion.1), channel_id=1, source_target_pairs={{0,2},{1,3},{2,0},{3,1},{4,6},{5,7},{6,4},{7,5},{8,10},{9,11},{10,... | collective-permute-start | bytes 98312 | tf_op jit(solution)/shard_map/stats_sum/ppermute | solution.py:571
  195.9 23.3 %copy-start.3 = (bf16[2,128,1024]{2,1,0:T(8,128)(2,1)}, bf16[2,128,1024]{2,1,0:T(8,128)(2,1)S(1)}, u32[]{:S(2)}) copy-start(bf16[2,128,1024]{2,1,0:T(8,128)(2,1)S(1)} %pad_maximum_fusion.1.refs_0_) | copy-start | bytes 1572868
  198.3 14.0 %collective-permute-start.31 = (bf16[2,128,1024]{2,1,0:T(8,128)(2,1)S(1)}, bf16[2,128,1024]{2,1,0:T(8,128)(2,1)}, u32[]{:S(2)}, u32[]{:S(2)}) collective-permute-start(bf16[2,128,1024]{2,1,0:T(8,128)(2,1)S(1)} %pad_maximum_fusion.refs_0_), channel_id=1, source_target_pairs={{0,4},{4,0},{8,12},{12,8},{16,20},{20,16},{24,28},{28,24},{1,5},{5... | collective-permute-start | bytes 1572872 | tf_op jit(solution)/shard_map/reduce_down/ppermute | solution.py:571
  200.0 25.2 %collective-permute-start.19 = (bf16[2,1024,256]{2,1,0:T(8,128)(2,1)}, bf16[2,1024,256]{2,1,0:T(8,128)(2,1)}, u32[]{:S(2)}, u32[]{:S(2)}) collective-permute-start(bf16[2,1024,256]{2,1,0:T(8,128)(2,1)} %get-tuple-element.149), channel_id=1, source_target_pairs={{0,1},{1,0},{2,3},{3,2},{4,5},{5,4},{6,7},{7,6},{8,9},{9,8},{10,11... | collective-permute-start | bytes 3145736 | tf_op jit(solution)/shard_map/e_sum/ppermute | solution.py:571
  201.3 11.0 %copy-start.8 = (bf16[2,128,1024]{2,1,0:T(8,128)(2,1)}, bf16[2,128,1024]{2,1,0:T(8,128)(2,1)S(1)}, u32[]{:S(2)}) copy-start(bf16[2,128,1024]{2,1,0:T(8,128)(2,1)S(1)} %collective-permute-done.33.refs_3_) | copy-start | bytes 1572868
  201.3 18.0 %collective-permute-start.30 = (bf16[1,4,128,256]{3,2,1,0:T(8,128)(2,1)S(1)}, bf16[1,4,128,256]{3,2,1,0:T(8,128)(2,1)S(1)}, u32[]{:S(2)}, u32[]{:S(2)}) collective-permute-start(bf16[1,4,128,256]{3,2,1,0:T(8,128)(2,1)S(1)} %add_convert_fusion.4), channel_id=1, source_target_pairs={{0,16},{4,20},{8,24},{12,28},{16,0},{20,4},{24,8},{28,12},{1,17},{... | collective-permute-start | bytes 786440 | tf_op jit(solution)/shard_map/reduce_attn/ppermute | solution.py:571
  202.2 46.6 %all-to-all-start.1 = ((f32[32,13,256]{2,1,0:T(8,128)}), f32[32,13,256]{2,1,0:T(8,128)S(1)}, u32[]{:S(2)}, u32[]{:S(2)}) async-start(f32[32,13,256]{2,1,0:T(8,128)} %bitcast.22), calls=%async_computation.1 | async-start | bytes 1048576 | tf_op jit(solution)/shard_map/small_sum/all_to_all | solution.py:1034
  206.7 16.5 %copy-start.7 = (bf16[2,1024,256]{2,1,0:T(8,128)(2,1)S(1)}, bf16[2,1024,256]{2,1,0:T(8,128)(2,1)}, u32[]{:S(2)}) copy-start(bf16[2,1024,256]{2,1,0:T(8,128)(2,1)} %get-tuple-element.144) | copy-start | bytes 3145732
  206.8 25.0 %collective-permute-start.39 = (bf16[2,128,1024]{2,1,0:T(8,128)(2,1)S(1)}, bf16[2,128,1024]{2,1,0:T(8,128)(2,1)S(1)}, u32[]{:S(2)}, u32[]{:S(2)}) collective-permute-start(bf16[2,128,1024]{2,1,0:T(8,128)(2,1)S(1)} %pad_maximum_fusion.1.refs_0_), channel_id=1, source_target_pairs={{0,12},{4,8},{8,4},{12,0},{16,28},{20,24},{24,20},{28,16},{1,13},{... | collective-permute-start | bytes 1572872 | tf_op jit(solution)/shard_map/reduce_in/ppermute | solution.py:571
  212.3 30.6 %collective-permute-start.38 = (bf16[2,128,1024]{2,1,0:T(8,128)(2,1)S(1)}, bf16[2,128,1024]{2,1,0:T(8,128)(2,1)S(1)}, u32[]{:S(2)}, u32[]{:S(2)}) collective-permute-start(bf16[2,128,1024]{2,1,0:T(8,128)(2,1)S(1)} %pad_maximum_fusion.1.refs_0_), channel_id=1, source_target_pairs={{0,8},{4,12},{8,0},{12,4},{16,24},{20,28},{24,16},{28,20},{1,9},{5... | collective-permute-start | bytes 1572872 | tf_op jit(solution)/shard_map/reduce_in/ppermute | solution.py:571
  215.7 10.0 %copy-start.6 = (bf16[2,1024,256]{2,1,0:T(8,128)(2,1)S(1)}, bf16[2,1024,256]{2,1,0:T(8,128)(2,1)}, u32[]{:S(2)}) copy-start(bf16[2,1024,256]{2,1,0:T(8,128)(2,1)} %get-tuple-element.148) | copy-start | bytes 3145732
  219.3 24.7 %collective-permute-start.37 = (bf16[2,128,1024]{2,1,0:T(8,128)(2,1)S(1)}, bf16[2,128,1024]{2,1,0:T(8,128)(2,1)S(1)}, u32[]{:S(2)}, u32[]{:S(2)}) collective-permute-start(bf16[2,128,1024]{2,1,0:T(8,128)(2,1)S(1)} %pad_maximum_fusion.1.refs_0_), channel_id=1, source_target_pairs={{0,4},{4,0},{8,12},{12,8},{16,20},{20,16},{24,28},{28,24},{1,5},{5... | collective-permute-start | bytes 1572872 | tf_op jit(solution)/shard_map/reduce_in/ppermute | solution.py:571
  219.7 29.2 %copy-start.4 = (bf16[2,4,128,256]{3,2,1,0:T(8,128)(2,1)}, bf16[2,4,128,256]{3,2,1,0:T(8,128)(2,1)S(1)}, u32[]{:S(2)}) copy-start(bf16[2,4,128,256]{3,2,1,0:T(8,128)(2,1)S(1)} %pad_maximum_fusion.2.refs_0_) | copy-start | bytes 1572868
  219.7 40.1 %collective-permute-start.36 = (bf16[2,4,128,256]{3,2,1,0:T(8,128)(2,1)S(1)}, bf16[2,4,128,256]{3,2,1,0:T(8,128)(2,1)}, u32[]{:S(2)}, u32[]{:S(2)}) collective-permute-start(bf16[2,4,128,256]{3,2,1,0:T(8,128)(2,1)S(1)} %pad_maximum_fusion.2.refs_0_), channel_id=1, source_target_pairs={{0,12},{4,8},{8,4},{12,0},{16,28},{20,24},{24,20},{28,16},{1,13},{... | collective-permute-start | bytes 1572872 | tf_op jit(solution)/shard_map/reduce_attn/ppermute | solution.py:571
  225.2 26.2 %collective-permute-start.18 = (bf16[1,1024,256]{2,1,0:T(8,128)(2,1)}, bf16[1,1024,256]{2,1,0:T(8,128)(2,1)}, u32[]{:S(2)}, u32[]{:S(2)}) collective-permute-start(bf16[1,1024,256]{2,1,0:T(8,128)(2,1)} %add_convert_fusion.2), channel_id=1, source_target_pairs={{0,2},{1,3},{2,0},{3,1},{4,6},{5,7},{6,4},{7,5},{8,10},{9,11},{10,... | collective-permute-start | bytes 1572872 | tf_op jit(solution)/shard_map/mixed_sum/ppermute | solution.py:571
  227.7 23.7 %copy-start.5 = (bf16[1024,256]{1,0:T(8,128)(2,1)S(1)}, bf16[1024,256]{1,0:T(8,128)(2,1)}, u32[]{:S(2)}) copy-start(bf16[1024,256]{1,0:T(8,128)(2,1)} %refs_0_.1) | copy-start | bytes 1572868
  231.7 13.7 %copy-start.11 = (bf16[2,128,1024]{2,1,0:T(8,128)(2,1)}, bf16[2,128,1024]{2,1,0:T(8,128)(2,1)S(1)}, u32[]{:S(2)}) copy-start(bf16[2,128,1024]{2,1,0:T(8,128)(2,1)S(1)} %collective-permute-done.39.refs_3_) | copy-start | bytes 1572868
  231.7 33.3 %collective-permute-start.35 = (bf16[2,4,128,256]{3,2,1,0:T(8,128)(2,1)S(1)}, bf16[2,4,128,256]{3,2,1,0:T(8,128)(2,1)}, u32[]{:S(2)}, u32[]{:S(2)}) collective-permute-start(bf16[2,4,128,256]{3,2,1,0:T(8,128)(2,1)S(1)} %pad_maximum_fusion.2.refs_0_), channel_id=1, source_target_pairs={{0,8},{4,12},{8,0},{12,4},{16,24},{20,28},{24,16},{28,20},{1,9},{5... | collective-permute-start | bytes 1572872 | tf_op jit(solution)/shard_map/reduce_attn/ppermute | solution.py:571
  242.9 22.3 %collective-permute-start.34 = (bf16[2,4,128,256]{3,2,1,0:T(8,128)(2,1)S(1)}, bf16[2,4,128,256]{3,2,1,0:T(8,128)(2,1)}, u32[]{:S(2)}, u32[]{:S(2)}) collective-permute-start(bf16[2,4,128,256]{3,2,1,0:T(8,128)(2,1)S(1)} %pad_maximum_fusion.2.refs_0_), channel_id=1, source_target_pairs={{0,4},{4,0},{8,12},{12,8},{16,20},{20,16},{24,28},{28,24},{1,5},{5... | collective-permute-start | bytes 1572872 | tf_op jit(solution)/shard_map/reduce_attn/ppermute | solution.py:571
  244.0 13.0 %collective-permute-start.20 = (bf16[1,1024,256]{2,1,0:T(8,128)(2,1)}, bf16[1,1024,256]{2,1,0:T(8,128)(2,1)}, u32[]{:S(2)}, u32[]{:S(2)}) collective-permute-start(bf16[1,1024,256]{2,1,0:T(8,128)(2,1)} %add_convert_fusion), channel_id=1, source_target_pairs={{0,2},{1,3},{2,0},{3,1},{4,6},{5,7},{6,4},{7,5},{8,10},{9,11},{10,... | collective-permute-start | bytes 1572872 | tf_op jit(solution)/shard_map/e_sum/ppermute | solution.py:571
  248.9 8.1 %copy-start.1 = (bf16[1024,256]{1,0:T(8,128)(2,1)S(1)}, bf16[1024,256]{1,0:T(8,128)(2,1)}, u32[]{:S(2)}) copy-start(bf16[1024,256]{1,0:T(8,128)(2,1)} %refs_0_.2) | copy-start | bytes 1572868
  250.7 19.5 %copy-start.29 = (f32[1,256]{1,0:T(1,128)}, f32[1,256]{1,0:T(1,128)S(1)}, u32[]{:S(2)}) copy-start(f32[1,256]{1,0:T(1,128)S(1)} %get-tuple-element.179) | copy-start | bytes 3076
  (9 other events, 19.3 us)

commit v4 on v3

--- a/solution.py
+++ b/solution.py
@@ -18,10 +18,10 @@
 LANES = 128
 bf16 = jnp.bfloat16
 f32 = jnp.float32
-COST_SCALE = 0.02
+COST_SCALE = 1.0
 END_COST = 12
 BEFORE = "DI"
-AFTER = "DCIICDCIC"
+AFTER = "DCICIDCIC"
 PINNED = "C"
 LATE = 3
 VMEM_LIMIT = 56 * 1024 * 1024
@@ -176,8 +176,9 @@
     @pl.when(step == pl.num_programs(0) - 1)
     def _():
         packed, norm = pack_state(state_ref[...], norm_ref[...], head_size)
-        pk_ref[:head_size] = packed
-        pk_ref[head_size:] = norm
+        for i in range(pk_ref.shape[0]):
+            pk_ref[i, :head_size] = packed
+            pk_ref[i, head_size:] = norm
 
 
 def slot_of(relative, count):
@@ -659,9 +660,8 @@
     )(me_seq, *chunk.arrays)
 
 
-def sum_before(packet):
+def sum_before(copies):
     count = lax.axis_size("seq")
-    copies = jnp.broadcast_to(packet[None], (count,) + packet.shape)
     packets = lax.all_to_all(copies, "seq", 0, 0, tiled=True)
     wanted = (jnp.arange(count) < lax.axis_index("seq")).astype(f32)
     return jnp.sum(packets * wanted[:, None, None], 0)
@@ -792,7 +792,7 @@
             rows_of(BT, width),
             rows_of(BT, width),
             rows_of(BT, width),
-            whole(*packet_shape),
+            whole(n_seq, *packet_shape),
         ],
         [
             sds((model, rows), bf16),
@@ -805,7 +805,7 @@
             sds((rows, width), bf16),
             sds((rows, width), bf16),
             sds((rows, width), bf16),
-            sds(packet_shape, f32),
+            sds((n_seq,) + packet_shape, f32),
         ],
         [pltpu.VMEM((BT, model), bf16), pltpu.VMEM((width, width), f32), pltpu.VMEM((8, width), f32)],
         2 * rows * model * 3 * width + 16 * rows * width * width,

time: 276 us -> 267 us (0.967)
  waiting for transfers between devices: 81.6 us -> 65.4 us
  starting transfers between devices: 58.6 us -> 67.2 us
    ppermute x36, waiting for transfers between devices: 71.9 us -> 55.3 us  [exchange(): return lax.ppermute(x, axis, [(i, i ^ mask) for i in range(count)])]
    ppermute x36, starting transfers between devices: 41.4 us -> 49.7 us  [exchange(): return lax.ppermute(x, axis, [(i, i ^ mask) for i in range(count)])]
  transfers between devices with their start and end apart: 42 -> 42, of which waited for: 17 -> 14; matrix products, arithmetic and copies ran while one was open for 15% -> 15% of each run, Pallas kernels for 30% -> 31%
where the time goes in v4:
time: 267 us; the launch traced here: 263 us
  Pallas kernels  86.4 us (32%)
  starting transfers between devices  67.2 us (25%)
  waiting for transfers between devices  65.4 us (24%)
  other arithmetic  28.1 us (11%)
  local copies, waits for them, and re-layouts  15 us (6%)
    ppermute x36, waiting for transfers between devices, exchange(): return lax.ppermute(x, axis, [(i, i ^ mask) for i in range(count)])  55.3 us
    ppermute x36, starting transfers between devices, exchange(): return lax.ppermute(x, axis, [(i, i ^ mask) for i in range(count)])  49.7 us
    pallas_call x1, Pallas kernels, body(): call(functools.partial(ff_kernel, n_head), hidden // fb, [smem(), smem(),...  18.4 us
    pallas_call x1, Pallas kernels, body(): call(finish_kernel, blocks, [smem(), rows_of(BT, hidden), whole(hidden, m...  16.1 us
    pallas_call x1, Pallas kernels, body(): call(functools.partial(attn_kernel, head_size), blocks, [smem(), rows_of(...  14.1 us
    pallas_call x1, Pallas kernels, body(): call(functools.partial(pre_kernel, head_size, n_head), blocks, [smem(), s...  13.7 us
    pallas_call x1, Pallas kernels, body(): call(functools.partial(tail_kernel, head_size), blocks, [smem(), *[back_r...  12.3 us
    pallas_call x2, Pallas kernels, block_out(): pl.pallas_call(block_out_kernel, grid_spec=pltpu.PrefetchScalarGridSpec(n...  6.69 us
  transfers between devices with their start and end apart: 42, of which 14 were waited for; matrix products, arithmetic and copies ran while one was open for 15% of the time, Pallas kernels for 31%

profile of v4, /device:TPU:8, one launch (start us, length us, event | category | flops | bytes accessed | tf_op | source)
XLA Modules:
  0.0 263.2 jit_solution(7545958803588207927)
XLA Ops:
  0.7 1.6 collective-permute-start.1
  2.3 0.8 reduce-window.8
  3.8 1.2 convert_reduce_fusion
  7.4 1.4 pad_maximum_fusion.4.refs_4_.gains_ref
  8.8 1.3 reshape.121.refs_7_.fw_ref
  10.8 3.8 %fusion.4 = (f32[1024,128]{1,0:T(8,128)}, f32[1024,128]{1,0:T(8,128)}) fusion(f32[128]{0:T(128)} %constant.54.clone, f32[128]{0:T(128)} %constant.53.clone, f32[1024]{0:T(1024)S(1)} %subtract_convert_fusion), kind=kLoop, calls=%fused_computation.15 | loop fusion | flops 262144 | bytes 1053696 | tf_op jit(solution)/shard_map/mul | solution.py:751
  15.3 1.5 collective-permute-start.4
  16.8 1.0 copy.54.refs_12_.segc_ref
  17.8 1.0 copy.53.refs_11_
  18.9 0.8 copy-done.27
  19.8 13.7 %pre_kernel.1 = (bf16[1024,1024]{1,0:T(8,128)(2,1)}, bf16[1024,1024]{1,0:T(8,128)(2,1)}, bf16[1024,1024]{1,0:T(8,128)(2,1)}, bf16[1024,1024]{1,0:T(8,128)(2,1)},...) custom-call(s32[4,3]{1,0:T(4,128)} %add_add_fusion.1.labels_ref, ...), custom_call_target="tpu_custom_call" | custom-call | flops 2684354560 | bytes 12058624 | tf_op jit(solution)/shard_map/pre_kernel/pallas_call | solution.py:767
  34.2 6.3 %all-to-all-start = ((f32[8,72,256]{2,1,0:T(8,128)}), f32[8,72,256]{2,1,0:T(8,128)S(1)}, u32[]{:S(2)}, u32[]{:S(2)}) async-start(f32[8,72,256]{2,1,0:T(8,128)} %get-tuple-element.98), calls=%async_computation | async-start | bytes 1179648 | tf_op jit(solution)/shard_map/state/all_to_all | solution.py:665
  40.4 0.8 dynamic-slice_add_fusion
  41.2 0.8 copy-done.28
  42.2 18.4 %ff_kernel.1 = (bf16[1024,1024]{1,0:T(8,128)(2,1)}, bf16[1024,1024]{1,0:T(8,128)(2,1)}, bf16[1024,1024]{1,0:T(8,128)(2,1)}, bf16[2,128,1024]{2,1,0:T(8,128)(2,1)...) custom-call(s32[1]{0:T(128)} %bitcast.me_ref, ...), custom_call_target="tpu_custom_call" | custom-call | flops 8589934592 | bytes 14680064 | tf_op jit(solution)/shard_map/ff_kernel/pallas_call | solution.py:822
  60.6 1.5 collective-permute-start.10
  62.7 1.5 collective-permute-start.12
  64.9 14.1 %attn_kernel.1 = (bf16[1024,256]{1,0:T(8,128)(2,1)}, f32[1024,256]{1,0:T(8,128)}, f32[1024,256]{1,0:T(8,128)}, f32[1024,256]{1,0:T(8,128)}, f32[4,256,256]{2,1,0...) custom-call(s32[4,3]{1,0:T(4,128)} %add_add_fusion.1.labels_ref, ...), custom_call_target="tpu_custom_call" | custom-call | flops 6442450944 | bytes 7340032 | tf_op jit(solution)/shard_map/attn_kernel/pallas_call | solution.py:858
  79.0 1.5 collective-permute-start.6
  82.0 6.5 %collective-permute-done.6 = f32[72,256]{1,0:T(8,128)S(1)} collective-permute-done((f32[72,256]{1,0:T(8,128)}, f32[72,256]{1,0:T(8,128)S(1)}, u32[]{:S(2)}, u32[]{:S(2)}) %collective-permute-start.6) | collective-permute-done | bytes 73760 | tf_op jit(solution)/shard_map/grad_state/ppermute | solution.py:684
  88.4 0.9 add.180
  90.0 1.3 collective-permute-start.8
  91.3 3.1 %collective-permute-start.7 = (f32[72,256]{1,0:T(8,128)S(1)}, f32[72,256]{1,0:T(8,128)S(1)}, u32[]{:S(2)}, u32[]{:S(2)}) collective-permute-start(f32[72,256]{1,0:T(8,128)S(1)} %add.180), channel_id=1, source_target_pairs={{8,0},{12,4},{16,8},{20,12},{24,16},{28,20},{9,1},{13,5},{17,9},{2... | collective-permute-start | bytes 221192 | tf_op jit(solution)/shard_map/grad_state/ppermute | solution.py:692
  94.6 3.6 %collective-permute-start.16 = (bf16[1,128,1024]{2,1,0:T(8,128)(2,1)S(1)}, bf16[1,128,1024]{2,1,0:T(8,128)(2,1)S(1)}, u32[]{:S(2)}, u32[]{:S(2)}) collective-permute-start(bf16[1,128,1024]{2,1,0:T(8,128)(2,1)S(1)} %add_convert_fusion.12), channel_id=1, source_target_pairs={{0,16},{4,20},{8,24},{12,28},{16,0},{20,4},{24,8},{28,12},{1,17},{... | collective-permute-start | bytes 786440 | tf_op jit(solution)/shard_map/reduce_down/ppermute | solution.py:572
  98.2 1.7 collective-permute-start.13
  99.9 3.2 %collective-permute-start.15 = (bf16[2,128,1024]{2,1,0:T(8,128)(2,1)}, bf16[2,128,1024]{2,1,0:T(8,128)(2,1)S(1)}, u32[]{:S(2)}, u32[]{:S(2)}) collective-permute-start(bf16[2,128,1024]{2,1,0:T(8,128)(2,1)} %get-tuple-element.137), channel_id=1, source_target_pairs={{0,12},{4,8},{8,4},{12,0},{16,28},{20,24},{24,20},{28,16},{1,13},{... | collective-permute-start | bytes 1572872 | tf_op jit(solution)/shard_map/reduce_in/ppermute | solution.py:572
  103.1 3.6 %collective-permute-done.7 = f32[72,256]{1,0:T(8,128)S(1)} collective-permute-done((f32[72,256]{1,0:T(8,128)S(1)}, f32[72,256]{1,0:T(8,128)S(1)}, u32[]{:S(2)}, u32[]{:S(2)}) %collective-permute-start.7) | collective-permute-done | bytes 73760 | tf_op jit(solution)/shard_map/grad_state/ppermute | solution.py:692
  107.3 12.3 %tail_kernel.1 = (bf16[3,1024,256]{2,1,0:T(8,128)(2,1)}, f32[8,256]{1,0:T(8,128)}, bf16[2,4,128,256]{3,2,1,0:T(8,128)(2,1)}, bf16[2,4,128,256]{3,2,1,0:T(8,128)(...) custom-call(s32[4,3]{1,0:T(4,128)} %add_add_fusion.1.labels_ref, ...), custom_call_target="tpu_custom_call" | custom-call | flops 1610612736 | bytes 11534336 | tf_op jit(solution)/shard_map/tail_kernel/pallas_call | solution.py:915
  120.3 1.7 collective-permute-start.24
  122.3 1.9 collective-permute-start.26
  124.2 11.0 %collective-permute-done.15 = bf16[2,128,1024]{2,1,0:T(8,128)(2,1)S(1)} collective-permute-done((bf16[2,128,1024]{2,1,0:T(8,128)(2,1)}, bf16[2,128,1024]{2,1,0:T(8,128)(2,1)S(1)}, u32[]{:S(2)}, u32[]{:S(2)}) %collective-permute-start.15) | collective-permute-done | bytes 524320 | tf_op jit(solution)/shard_map/reduce_in/ppermute | solution.py:572
  135.3 2.2 collective-permute-start.23
  137.5 16.1 %finish_kernel.1 = (bf16[2,1024,256]{2,1,0:T(8,128)(2,1)}, bf16[2,1024,256]{2,1,0:T(8,128)(2,1)}, bf16[2,1024,256]{2,1,0:T(8,128)(2,1)}, bf16[2,1024,256]{2,1,0:T(8,128)(2,1)}, f32[16,1024]{1,0:T(8,128)}) custom-call(s32[1]{0:T(128)} %bitcast.me_ref, bf16[1024,1024]{1,0:T(8,128)(2,1)} %get-tuple-element.103.hid_ref, bf16[1024,1024]{1,0:T(8,128)(2,1)} %wdown_ref.1, ...), custom_call_target="tpu_custom_call" | custom-call | flops 3758096384 | bytes 12058624 | tf_op jit(solution)/shard_map/finish_kernel/pallas_call | solution.py:959
  153.6 3.5 %collective-permute-done.27 = bf16[1,128,1024]{2,1,0:T(8,128)(2,1)S(1)} collective-permute-done((bf16[1,128,1024]{2,1,0:T(8,128)(2,1)S(1)}, bf16[1,128,1024]{2,1,0:T(8,128)(2,1)S(1)}, u32[]{:S(2)}, u32[]{:S(2)}) %collective-permute-start.27) | collective-permute-done | bytes 262176 | tf_op jit(solution)/shard_map/reduce_down/ppermute | solution.py:572
  157.9 0.8 slice.182
  159.1 0.8 slice_add_fusion.1
  160.7 2.2 collective-permute-done.26
  162.9 1.9 add_convert_fusion.7
  164.9 1.1 collective-permute-start.28
  166.0 1.4 add_convert_fusion.6
  167.4 1.9 collective-permute-start.33
  169.4 0.9 broadcast_in_dim.61
  170.2 4.6 %all-to-all-start.1 = ((f32[32,13,256]{2,1,0:T(8,128)}), f32[32,13,256]{2,1,0:T(8,128)S(1)}, u32[]{:S(2)}, u32[]{:S(2)}) async-start(f32[32,13,256]{2,1,0:T(8,128)} %bitcast.22), calls=%async_computation.1 | async-start | bytes 1048576 | tf_op jit(solution)/shard_map/small_sum/all_to_all | solution.py:1034
  174.9 5.6 %collective-permute-done.28 = bf16[1,4,128,256]{3,2,1,0:T(8,128)(2,1)S(1)} collective-permute-done((bf16[1,4,128,256]{3,2,1,0:T(8,128)(2,1)}, bf16[1,4,128,256]{3,2,1,0:T(8,128)(2,1)S(1)}, u32[]{:S(2)}, u32[]{:S(2)}) %collective-permute-start.28) | collective-permute-done | bytes 262176 | tf_op jit(solution)/shard_map/reduce_attn/ppermute | solution.py:572
  180.5 9.1 %collective-permute-start.31 = (bf16[2,128,1024]{2,1,0:T(8,128)(2,1)S(1)}, bf16[2,128,1024]{2,1,0:T(8,128)(2,1)S(1)}, u32[]{:S(2)}, u32[]{:S(2)}) collective-permute-start(bf16[2,128,1024]{2,1,0:T(8,128)(2,1)S(1)} %pad_maximum_fusion.refs_0_), channel_id=1, source_target_pairs={{0,8},{4,12},{8,0},{12,4},{16,24},{20,28},{24,16},{28,20},{1,9},{5... | collective-permute-start | bytes 1572872 | tf_op jit(solution)/shard_map/reduce_down/ppermute | solution.py:572
  189.6 5.8 %collective-permute-done.33 = bf16[1,128,1024]{2,1,0:T(8,128)(2,1)S(1)} collective-permute-done((bf16[1,128,1024]{2,1,0:T(8,128)(2,1)S(1)}, bf16[1,128,1024]{2,1,0:T(8,128)(2,1)S(1)}, u32[]{:S(2)}, u32[]{:S(2)}) %collective-permute-start.33) | collective-permute-done | bytes 262176 | tf_op jit(solution)/shard_map/reduce_in/ppermute | solution.py:572
  195.4 1.8 collective-permute-start.30
  197.2 1.4 add_convert_fusion.4
  198.6 3.5 %collective-permute-start.29 = (bf16[1,4,128,256]{3,2,1,0:T(8,128)(2,1)S(1)}, bf16[1,4,128,256]{3,2,1,0:T(8,128)(2,1)S(1)}, u32[]{:S(2)}, u32[]{:S(2)}) collective-permute-start(bf16[1,4,128,256]{3,2,1,0:T(8,128)(2,1)S(1)} %add_convert_fusion.4), channel_id=1, source_target_pairs={{0,16},{4,20},{8,24},{12,28},{16,0},{20,4},{24,8},{28,12},{1,17},{... | collective-permute-start | bytes 786440 | tf_op jit(solution)/shard_map/reduce_attn/ppermute | solution.py:572
  202.2 6.6 %collective-permute-done.31.refs_2_ = bf16[2,128,1024]{2,1,0:T(8,128)(2,1)S(1)} collective-permute-done((bf16[2,128,1024]{2,1,0:T(8,128)(2,1)S(1)}, bf16[2,128,1024]{2,1,0:T(8,128)(2,1)S(1)}, u32[]{:S(2)}, u32[]{:S(2)}) %collective-permute-start.31) | collective-permute-done | bytes 524320 | tf_op jit(solution)/shard_map/reduce_down/ppermute | solution.py:572
  208.8 6.0 %collective-permute-start.39 = (bf16[2,128,1024]{2,1,0:T(8,128)(2,1)S(1)}, bf16[2,128,1024]{2,1,0:T(8,128)(2,1)S(1)}, u32[]{:S(2)}, u32[]{:S(2)}) collective-permute-start(bf16[2,128,1024]{2,1,0:T(8,128)(2,1)S(1)} %pad_maximum_fusion.1.refs_0_), channel_id=1, source_target_pairs={{0,12},{4,8},{8,4},{12,0},{16,28},{20,24},{24,20},{28,16},{1,13},{... | collective-permute-start | bytes 1572872 | tf_op jit(solution)/shard_map/reduce_in/ppermute | solution.py:572
  215.7 3.3 %block_out_kernel.3 = f32[1024,1024]{1,0:T(8,128)} custom-call(s32[1]{0:T(128)} %bitcast.1.rank_ref, bf16[2,128,1024]{2,1,0:T(8,128)(2,1)} %copy-done.2, bf16[2,128,1024]{2,1,0:T(8,128)(2,1)} %copy-done.13, bf16[2,128,1024]{2,1,0:T(8,128)(2,1)} %copy-done.12, bf16[2,128,1024]{2,1,0:T(8,128)(2,1)} %copy-done.8), custom_call_target="tpu_custom_call" | custom-call | bytes 6291456 | tf_op jit(solution)/shard_map/block_out_kernel/pallas_call | solution.py:648
  219.2 2.8 %collective-permute-start.36 = (bf16[2,4,128,256]{3,2,1,0:T(8,128)(2,1)S(1)}, bf16[2,4,128,256]{3,2,1,0:T(8,128)(2,1)}, u32[]{:S(2)}, u32[]{:S(2)}) collective-permute-start(bf16[2,4,128,256]{3,2,1,0:T(8,128)(2,1)S(1)} %pad_maximum_fusion.2.refs_0_), channel_id=1, source_target_pairs={{0,12},{4,8},{8,4},{12,0},{16,28},{20,24},{24,20},{28,16},{1,13},{... | collective-permute-start | bytes 1572872 | tf_op jit(solution)/shard_map/reduce_attn/ppermute | solution.py:572
  222.0 0.9 add_convert_fusion.2
  223.0 2.0 add_convert_fusion
  224.9 2.8 %collective-permute-done.39.refs_3_ = bf16[2,128,1024]{2,1,0:T(8,128)(2,1)S(1)} collective-permute-done((bf16[2,128,1024]{2,1,0:T(8,128)(2,1)S(1)}, bf16[2,128,1024]{2,1,0:T(8,128)(2,1)S(1)}, u32[]{:S(2)}, u32[]{:S(2)}) %collective-permute-start.39) | collective-permute-done | bytes 524320 | tf_op jit(solution)/shard_map/reduce_in/ppermute | solution.py:572
  227.7 10.8 %collective-permute-done.38.refs_2_ = bf16[2,128,1024]{2,1,0:T(8,128)(2,1)S(1)} collective-permute-done((bf16[2,128,1024]{2,1,0:T(8,128)(2,1)S(1)}, bf16[2,128,1024]{2,1,0:T(8,128)(2,1)S(1)}, u32[]{:S(2)}, u32[]{:S(2)}) %collective-permute-start.38) | collective-permute-done | bytes 524320 | tf_op jit(solution)/shard_map/reduce_in/ppermute | solution.py:572
  238.5 1.0 collective-permute-start.34
  239.5 5.7 %collective-permute-done.37.refs_1_ = bf16[2,128,1024]{2,1,0:T(8,128)(2,1)S(1)} collective-permute-done((bf16[2,128,1024]{2,1,0:T(8,128)(2,1)S(1)}, bf16[2,128,1024]{2,1,0:T(8,128)(2,1)S(1)}, u32[]{:S(2)}, u32[]{:S(2)}) %collective-permute-start.37) | collective-permute-done | bytes 524320 | tf_op jit(solution)/shard_map/reduce_in/ppermute | solution.py:572
  245.3 0.8 copy-done.11
  246.0 3.3 %block_out_kernel.2 = f32[1024,1024]{1,0:T(8,128)} custom-call(s32[1]{0:T(128)} %bitcast.1.rank_ref, bf16[2,128,1024]{2,1,0:T(8,128)(2,1)} %copy-done.4, bf16[2,128,1024]{2,1,0:T(8,128)(2,1)} %copy-done.11, bf16[2,128,1024]{2,1,0:T(8,128)(2,1)} %copy-done.10, bf16[2,128,1024]{2,1,0:T(8,128)(2,1)} %copy-done.9), custom_call_target="tpu_custom_call" | custom-call | bytes 6291456 | tf_op jit(solution)/shard_map/block_out_kernel/pallas_call | solution.py:648
  251.9 2.6 fusion.3
  254.7 2.8 %convert_add_fusion = f32[1024,256]{1,0:T(8,128)} fusion(bf16[1024,256]{1,0:T(8,128)(2,1)S(1)} %copy-done.1, bf16[1,1024,256]{2,1,0:T(8,128)(2,1)} %collective-permute-done.20, bf16[2,1024,256]{2,1,0:T(8,128)(2,1)} %collective-permute-done.19, f32[1024]{0:T(1024)S(1)} %bitcast.50, bf16[1024,1024]{1,0:T(8,128)(2,1)} %get-tuple-element.143.xhat_ref, ...), kind=kLoop, calls=%fused_computation | loop fusion | flops 3670016 | bytes 3682308 | tf_op jit(solution)/shard_map/add | solution.py:999
  257.6 5.1 %widen_kernel.1 = (f32[3,1024,256]{2,1,0:T(8,128)}, f32[256,1024]{1,0:T(8,128)}) custom-call(s32[1]{0:T(128)} %bitcast.1.rank_ref, bf16[2,4,128,256]{3,2,1,0:T(8,128)(2,1)} %copy-done.3, bf16[2,4,128,256]{3,2,1,0:T(8,128)(2,1)} %collective-permute-done.34.refs_1_, bf16[2,4,128,256]{3,2,1,0:T(8,128)(2,1)} %collective-permute-done.35.refs_2_, ...), custom_call_target="tpu_custom_call" | custom-call | bytes 3145728 | tf_op jit(solution)/shard_map/widen_kernel/pallas_call | solution.py:1014
  (154 shorter events, 17.5 us)
Async XLA Ops:
  0.6 18.2 %collective-permute-start = (bf16[1024,256]{1,0:T(8,128)(2,1)}, bf16[1024,256]{1,0:T(8,128)(2,1)S(1)}, u32[]{:S(2)}, u32[]{:S(2)}) collective-permute-start(bf16[1024,256]{1,0:T(8,128)(2,1)} %refs_0_.1), channel_id=1, source_target_pairs={{0,1},{1,0},{2,3},{3,2},{4,5},{5,4},{6,7},{7,6},{8,9},{9,8},{10,11... | collective-permute-start | bytes 1572872 | tf_op jit(solution)/shard_map/gather_tokens/ppermute | solution.py:572
  0.7 14.5 %collective-permute-start.1 = (bf16[1024,256]{1,0:T(8,128)(2,1)}, bf16[1024,256]{1,0:T(8,128)(2,1)S(1)}, u32[]{:S(2)}, u32[]{:S(2)}) collective-permute-start(bf16[1024,256]{1,0:T(8,128)(2,1)} %refs_0_.1), channel_id=1, source_target_pairs={{0,2},{1,3},{2,0},{3,1},{4,6},{5,7},{6,4},{7,5},{8,10},{9,11},{10,... | collective-permute-start | bytes 1572872 | tf_op jit(solution)/shard_map/gather_tokens/ppermute | solution.py:572
  5.5 28.1 %copy-start.23 = (s32[1024]{0:T(1024)}, s32[1024]{0:T(1024)S(1)}, u32[]{:S(2)}) copy-start(s32[1024]{0:T(1024)S(1)} %convert_reduce_fusion.1) | copy-start | bytes 12292
  15.3 3.6 %collective-permute-start.2 = (bf16[1024,256]{1,0:T(8,128)(2,1)S(1)}, bf16[1024,256]{1,0:T(8,128)(2,1)S(1)}, u32[]{:S(2)}, u32[]{:S(2)}) collective-permute-start(bf16[1024,256]{1,0:T(8,128)(2,1)S(1)} %collective-permute-done.1.refs_2_), channel_id=1, source_target_pairs={{0,1},{1,0},{2,3},{3,2},{4,5},{5,4},{6,7},{7,6},{8,9},{9,8},{10,11... | collective-permute-start | bytes 1572872 | tf_op jit(solution)/shard_map/gather_tokens/ppermute | solution.py:572
  15.3 18.3 %collective-permute-start.4 = (bf16[1024,256]{1,0:T(8,128)(2,1)}, bf16[1024,256]{1,0:T(8,128)(2,1)S(1)}, u32[]{:S(2)}, u32[]{:S(2)}) collective-permute-start(bf16[1024,256]{1,0:T(8,128)(2,1)} %refs_0_.2), channel_id=1, source_target_pairs={{0,2},{1,3},{2,0},{3,1},{4,6},{5,7},{6,4},{7,5},{8,10},{9,11},{10,... | collective-permute-start | bytes 1572872 | tf_op jit(solution)/shard_map/gather_grads/ppermute | solution.py:572
  19.8 13.7 %copy-start = (bf16[1024,256]{1,0:T(8,128)(2,1)S(1)}, bf16[1024,256]{1,0:T(8,128)(2,1)}, u32[]{:S(2)}) copy-start(bf16[1024,256]{1,0:T(8,128)(2,1)} %refs_0_.2) | copy-start | bytes 1572868
  33.6 7.7 %copy-start.26 = (bf16[1024,256]{1,0:T(8,128)(2,1)}, bf16[1024,256]{1,0:T(8,128)(2,1)S(1)}, u32[]{:S(2)}) copy-start(bf16[1024,256]{1,0:T(8,128)(2,1)S(1)} %collective-permute-done.4.refs_2_) | copy-start | bytes 1572868
  33.6 7.6 %collective-permute-start.3 = (bf16[1024,256]{1,0:T(8,128)(2,1)S(1)}, bf16[1024,256]{1,0:T(8,128)(2,1)S(1)}, u32[]{:S(2)}, u32[]{:S(2)}) collective-permute-start(bf16[1024,256]{1,0:T(8,128)(2,1)S(1)} %copy-done), channel_id=1, source_target_pairs={{0,1},{1,0},{2,3},{3,2},{4,5},{5,4},{6,7},{7,6},{8,9},{9,8},{10,11... | collective-permute-start | bytes 1572872 | tf_op jit(solution)/shard_map/gather_grads/ppermute | solution.py:572
  33.9 7.3 %collective-permute-start.5 = (bf16[1024,256]{1,0:T(8,128)(2,1)S(1)}, bf16[1024,256]{1,0:T(8,128)(2,1)S(1)}, u32[]{:S(2)}, u32[]{:S(2)}) collective-permute-start(bf16[1024,256]{1,0:T(8,128)(2,1)S(1)} %collective-permute-done.4.refs_2_), channel_id=1, source_target_pairs={{0,1},{1,0},{2,3},{3,2},{4,5},{5,4},{6,7},{7,6},{8,9},{9,8},{10,11... | collective-permute-start | bytes 1572872 | tf_op jit(solution)/shard_map/gather_grads/ppermute | solution.py:572
  34.2 30.0 %all-to-all-start = ((f32[8,72,256]{2,1,0:T(8,128)}), f32[8,72,256]{2,1,0:T(8,128)S(1)}, u32[]{:S(2)}, u32[]{:S(2)}) async-start(f32[8,72,256]{2,1,0:T(8,128)} %get-tuple-element.98), calls=%async_computation | async-start | bytes 1179648 | tf_op jit(solution)/shard_map/state/all_to_all | solution.py:665
  60.6 30.7 %collective-permute-start.10 = (bf16[2,128,1024]{2,1,0:T(8,128)(2,1)}, bf16[2,128,1024]{2,1,0:T(8,128)(2,1)S(1)}, u32[]{:S(2)}, u32[]{:S(2)}) collective-permute-start(bf16[2,128,1024]{2,1,0:T(8,128)(2,1)} %get-tuple-element.121), channel_id=1, source_target_pairs={{0,4},{4,0},{8,12},{12,8},{16,20},{20,16},{24,28},{28,24},{1,5},{5... | collective-permute-start | bytes 1572872 | tf_op jit(solution)/shard_map/reduce_down/ppermute | solution.py:572
  62.2 32.2 %collective-permute-start.11 = (bf16[2,128,1024]{2,1,0:T(8,128)(2,1)}, bf16[2,128,1024]{2,1,0:T(8,128)(2,1)S(1)}, u32[]{:S(2)}, u32[]{:S(2)}) collective-permute-start(bf16[2,128,1024]{2,1,0:T(8,128)(2,1)} %get-tuple-element.122), channel_id=1, source_target_pairs={{0,8},{4,12},{8,0},{12,4},{16,24},{20,28},{24,16},{28,20},{1,9},{5... | collective-permute-start | bytes 1572872 | tf_op jit(solution)/shard_map/reduce_down/ppermute | solution.py:572
  62.7 31.7 %collective-permute-start.12 = (bf16[2,128,1024]{2,1,0:T(8,128)(2,1)}, bf16[2,128,1024]{2,1,0:T(8,128)(2,1)S(1)}, u32[]{:S(2)}, u32[]{:S(2)}) collective-permute-start(bf16[2,128,1024]{2,1,0:T(8,128)(2,1)} %get-tuple-element.123), channel_id=1, source_target_pairs={{0,12},{4,8},{8,4},{12,0},{16,28},{20,24},{24,20},{28,16},{1,13},{... | collective-permute-start | bytes 1572872 | tf_op jit(solution)/shard_map/reduce_down/ppermute | solution.py:572
  64.9 15.6 %copy-start.14 = (f32[1024,1]{1,0:T(8,128)S(1)}, f32[1024,1]{1,0:T(8,128)}, u32[]{:S(2)}) copy-start(f32[1024,1]{1,0:T(8,128)} %get-tuple-element.147) | copy-start | bytes 12292
  64.9 16.3 %copy-start.25 = (f32[1,1024]{1,0:T(1,128)S(1)}, f32[1,1024]{1,0:T(1,128)}, u32[]{:S(2)}) copy-start(f32[1,1024]{1,0:T(1,128)} %get-tuple-element.152) | copy-start | bytes 12292
  64.9 29.5 %copy-start.19 = (bf16[2,128,1024]{2,1,0:T(8,128)(2,1)S(1)}, bf16[2,128,1024]{2,1,0:T(8,128)(2,1)}, u32[]{:S(2)}) copy-start(bf16[2,128,1024]{2,1,0:T(8,128)(2,1)} %get-tuple-element.120) | copy-start | bytes 1572868
  79.0 9.4 %collective-permute-start.6 = (f32[72,256]{1,0:T(8,128)}, f32[72,256]{1,0:T(8,128)S(1)}, u32[]{:S(2)}, u32[]{:S(2)}) collective-permute-start(f32[72,256]{1,0:T(8,128)} %get-tuple-element.118), channel_id=1, source_target_pairs={{0,4},{4,0},{8,12},{12,8},{16,20},{20,16},{24,28},{28,24},{1,5},{5... | collective-permute-start | bytes 221192 | tf_op jit(solution)/shard_map/grad_state/ppermute | solution.py:684
  89.3 10.6 %collective-permute-start.9 = (f32[72,256]{1,0:T(8,128)S(1)}, f32[72,256]{1,0:T(8,128)S(1)}, u32[]{:S(2)}, u32[]{:S(2)}) collective-permute-start(f32[72,256]{1,0:T(8,128)S(1)} %add.180), channel_id=1, source_target_pairs={{24,0},{28,4},{25,1},{29,5},{26,2},{30,6},{27,3},{31,7}} | collective-permute-start | bytes 221192 | tf_op jit(solution)/shard_map/grad_state/ppermute | solution.py:692
  90.0 9.9 %collective-permute-start.8 = (f32[72,256]{1,0:T(8,128)S(1)}, f32[72,256]{1,0:T(8,128)S(1)}, u32[]{:S(2)}, u32[]{:S(2)}) collective-permute-start(f32[72,256]{1,0:T(8,128)S(1)} %add.180), channel_id=1, source_target_pairs={{16,0},{20,4},{24,8},{28,12},{17,1},{21,5},{25,9},{29,13},{18,2},{... | collective-permute-start | bytes 221192 | tf_op jit(solution)/shard_map/grad_state/ppermute | solution.py:692
  91.3 15.3 %collective-permute-start.7 = (f32[72,256]{1,0:T(8,128)S(1)}, f32[72,256]{1,0:T(8,128)S(1)}, u32[]{:S(2)}, u32[]{:S(2)}) collective-permute-start(f32[72,256]{1,0:T(8,128)S(1)} %add.180), channel_id=1, source_target_pairs={{8,0},{12,4},{16,8},{20,12},{24,16},{28,20},{9,1},{13,5},{17,9},{2... | collective-permute-start | bytes 221192 | tf_op jit(solution)/shard_map/grad_state/ppermute | solution.py:692
  94.6 27.4 %collective-permute-start.16 = (bf16[1,128,1024]{2,1,0:T(8,128)(2,1)S(1)}, bf16[1,128,1024]{2,1,0:T(8,128)(2,1)S(1)}, u32[]{:S(2)}, u32[]{:S(2)}) collective-permute-start(bf16[1,128,1024]{2,1,0:T(8,128)(2,1)S(1)} %add_convert_fusion.12), channel_id=1, source_target_pairs={{0,16},{4,20},{8,24},{12,28},{16,0},{20,4},{24,8},{28,12},{1,17},{... | collective-permute-start | bytes 786440 | tf_op jit(solution)/shard_map/reduce_down/ppermute | solution.py:572
  98.2 24.1 %collective-permute-start.13 = (bf16[2,128,1024]{2,1,0:T(8,128)(2,1)}, bf16[2,128,1024]{2,1,0:T(8,128)(2,1)S(1)}, u32[]{:S(2)}, u32[]{:S(2)}) collective-permute-start(bf16[2,128,1024]{2,1,0:T(8,128)(2,1)} %get-tuple-element.135), channel_id=1, source_target_pairs={{0,4},{4,0},{8,12},{12,8},{16,20},{20,16},{24,28},{28,24},{1,5},{5... | collective-permute-start | bytes 1572872 | tf_op jit(solution)/shard_map/reduce_in/ppermute | solution.py:572
  99.9 24.3 %collective-permute-start.14 = (bf16[2,128,1024]{2,1,0:T(8,128)(2,1)}, bf16[2,128,1024]{2,1,0:T(8,128)(2,1)S(1)}, u32[]{:S(2)}, u32[]{:S(2)}) collective-permute-start(bf16[2,128,1024]{2,1,0:T(8,128)(2,1)} %get-tuple-element.136), channel_id=1, source_target_pairs={{0,8},{4,12},{8,0},{12,4},{16,24},{20,28},{24,16},{28,20},{1,9},{5... | collective-permute-start | bytes 1572872 | tf_op jit(solution)/shard_map/reduce_in/ppermute | solution.py:572
  99.9 35.2 %collective-permute-start.15 = (bf16[2,128,1024]{2,1,0:T(8,128)(2,1)}, bf16[2,128,1024]{2,1,0:T(8,128)(2,1)S(1)}, u32[]{:S(2)}, u32[]{:S(2)}) collective-permute-start(bf16[2,128,1024]{2,1,0:T(8,128)(2,1)} %get-tuple-element.137), channel_id=1, source_target_pairs={{0,12},{4,8},{8,4},{12,0},{16,28},{20,24},{24,20},{28,16},{1,13},{... | collective-permute-start | bytes 1572872 | tf_op jit(solution)/shard_map/reduce_in/ppermute | solution.py:572
  107.3 14.8 %copy-start.22 = (bf16[2,128,1024]{2,1,0:T(8,128)(2,1)S(1)}, bf16[2,128,1024]{2,1,0:T(8,128)(2,1)}, u32[]{:S(2)}) copy-start(bf16[2,128,1024]{2,1,0:T(8,128)(2,1)} %copy-done.21) | copy-start | bytes 1572868
  107.3 27.9 %copy-start.15 = (bf16[2,128,1024]{2,1,0:T(8,128)(2,1)S(1)}, bf16[2,128,1024]{2,1,0:T(8,128)(2,1)}, u32[]{:S(2)}) copy-start(bf16[2,128,1024]{2,1,0:T(8,128)(2,1)} %get-tuple-element.131) | copy-start | bytes 1572868
  120.3 39.6 %collective-permute-start.24 = (bf16[2,4,128,256]{3,2,1,0:T(8,128)(2,1)}, bf16[2,4,128,256]{3,2,1,0:T(8,128)(2,1)}, u32[]{:S(2)}, u32[]{:S(2)}) collective-permute-start(bf16[2,4,128,256]{3,2,1,0:T(8,128)(2,1)} %get-tuple-element.154), channel_id=1, source_target_pairs={{0,4},{4,0},{8,12},{12,8},{16,20},{20,16},{24,28},{28,24},{1,5},{5... | collective-permute-start | bytes 1572872 | tf_op jit(solution)/shard_map/reduce_attn/ppermute | solution.py:572
  122.0 38.2 %collective-permute-start.25 = (bf16[2,4,128,256]{3,2,1,0:T(8,128)(2,1)}, bf16[2,4,128,256]{3,2,1,0:T(8,128)(2,1)}, u32[]{:S(2)}, u32[]{:S(2)}) collective-permute-start(bf16[2,4,128,256]{3,2,1,0:T(8,128)(2,1)} %get-tuple-element.155), channel_id=1, source_target_pairs={{0,8},{4,12},{8,0},{12,4},{16,24},{20,28},{24,16},{28,20},{1,9},{5... | collective-permute-start | bytes 1572872 | tf_op jit(solution)/shard_map/reduce_attn/ppermute | solution.py:572
  122.3 31.3 %copy-start.17 = (bf16[2,128,1024]{2,1,0:T(8,128)(2,1)}, bf16[2,128,1024]{2,1,0:T(8,128)(2,1)S(1)}, u32[]{:S(2)}) copy-start(bf16[2,128,1024]{2,1,0:T(8,128)(2,1)S(1)} %collective-permute-done.13) | copy-start | bytes 1572868
  122.3 40.6 %collective-permute-start.26 = (bf16[2,4,128,256]{3,2,1,0:T(8,128)(2,1)}, bf16[2,4,128,256]{3,2,1,0:T(8,128)(2,1)}, u32[]{:S(2)}, u32[]{:S(2)}) collective-permute-start(bf16[2,4,128,256]{3,2,1,0:T(8,128)(2,1)} %get-tuple-element.156), channel_id=1, source_target_pairs={{0,12},{4,8},{8,4},{12,0},{16,28},{20,24},{24,20},{28,16},{1,13},{... | collective-permute-start | bytes 1572872 | tf_op jit(solution)/shard_map/reduce_attn/ppermute | solution.py:572
  124.2 29.4 %copy-start.18 = (bf16[2,128,1024]{2,1,0:T(8,128)(2,1)}, bf16[2,128,1024]{2,1,0:T(8,128)(2,1)S(1)}, u32[]{:S(2)}) copy-start(bf16[2,128,1024]{2,1,0:T(8,128)(2,1)S(1)} %collective-permute-done.14) | copy-start | bytes 1572868
  124.2 32.9 %collective-permute-start.27 = (bf16[1,128,1024]{2,1,0:T(8,128)(2,1)S(1)}, bf16[1,128,1024]{2,1,0:T(8,128)(2,1)S(1)}, u32[]{:S(2)}, u32[]{:S(2)}) collective-permute-start(bf16[1,128,1024]{2,1,0:T(8,128)(2,1)S(1)} %add_convert_fusion.10), channel_id=1, source_target_pairs={{0,16},{4,20},{8,24},{12,28},{16,0},{20,4},{24,8},{28,12},{1,17},{... | collective-permute-start | bytes 786440 | tf_op jit(solution)/shard_map/reduce_down/ppermute | solution.py:572
  135.2 18.5 %copy-start.20 = (bf16[2,128,1024]{2,1,0:T(8,128)(2,1)}, bf16[2,128,1024]{2,1,0:T(8,128)(2,1)S(1)}, u32[]{:S(2)}) copy-start(bf16[2,128,1024]{2,1,0:T(8,128)(2,1)S(1)} %collective-permute-done.15) | copy-start | bytes 1572868
  135.3 30.7 %collective-permute-start.23 = (bf16[1,128,1024]{2,1,0:T(8,128)(2,1)S(1)}, bf16[1,128,1024]{2,1,0:T(8,128)(2,1)}, u32[]{:S(2)}, u32[]{:S(2)}) collective-permute-start(bf16[1,128,1024]{2,1,0:T(8,128)(2,1)S(1)} %add_convert_fusion.9), channel_id=1, source_target_pairs={{0,16},{4,20},{8,24},{12,28},{16,0},{20,4},{24,8},{28,12},{1,17},{... | collective-permute-start | bytes 786440 | tf_op jit(solution)/shard_map/reduce_in/ppermute | solution.py:572
  137.5 25.4 %copy-start.16 = (bf16[2,4,128,256]{3,2,1,0:T(8,128)(2,1)S(1)}, bf16[2,4,128,256]{3,2,1,0:T(8,128)(2,1)}, u32[]{:S(2)}) copy-start(bf16[2,4,128,256]{3,2,1,0:T(8,128)(2,1)} %get-tuple-element.153) | copy-start | bytes 1572868
  157.9 1.2 collective-permute-start.21
  157.9 37.5 %copy-start.2 = (bf16[2,128,1024]{2,1,0:T(8,128)(2,1)}, bf16[2,128,1024]{2,1,0:T(8,128)(2,1)S(1)}, u32[]{:S(2)}) copy-start(bf16[2,128,1024]{2,1,0:T(8,128)(2,1)S(1)} %pad_maximum_fusion.refs_0_) | copy-start | bytes 1572868
  159.1 39.5 %collective-permute-start.32 = (bf16[2,128,1024]{2,1,0:T(8,128)(2,1)S(1)}, bf16[2,128,1024]{2,1,0:T(8,128)(2,1)S(1)}, u32[]{:S(2)}, u32[]{:S(2)}) collective-permute-start(bf16[2,128,1024]{2,1,0:T(8,128)(2,1)S(1)} %pad_maximum_fusion.refs_0_), channel_id=1, source_target_pairs={{0,12},{4,8},{8,4},{12,0},{16,28},{20,24},{24,20},{28,16},{1,13},{... | collective-permute-start | bytes 1572872 | tf_op jit(solution)/shard_map/reduce_down/ppermute | solution.py:572
  159.8 59.3 %collective-permute-start.17 = (bf16[2,1024,256]{2,1,0:T(8,128)(2,1)}, bf16[2,1024,256]{2,1,0:T(8,128)(2,1)S(1)}, u32[]{:S(2)}, u32[]{:S(2)}) collective-permute-start(bf16[2,1024,256]{2,1,0:T(8,128)(2,1)} %get-tuple-element.146), channel_id=1, source_target_pairs={{0,1},{1,0},{2,3},{3,2},{4,5},{5,4},{6,7},{7,6},{8,9},{9,8},{10,11... | collective-permute-start | bytes 3145736 | tf_op jit(solution)/shard_map/mixed_sum/ppermute | solution.py:572
  160.2 9.1 %collective-permute-start.22 = (f32[8,1024]{1,0:T(8,128)S(1)}, f32[8,1024]{1,0:T(8,128)S(1)}, u32[]{:S(2)}, u32[]{:S(2)}) collective-permute-start(f32[8,1024]{1,0:T(8,128)S(1)} %slice_add_fusion.1), channel_id=1, source_target_pairs={{0,2},{1,3},{2,0},{3,1},{4,6},{5,7},{6,4},{7,5},{8,10},{9,11},{10,... | collective-permute-start | bytes 98312 | tf_op jit(solution)/shard_map/stats_sum/ppermute | solution.py:572
  164.9 15.6 %collective-permute-start.28 = (bf16[1,4,128,256]{3,2,1,0:T(8,128)(2,1)}, bf16[1,4,128,256]{3,2,1,0:T(8,128)(2,1)S(1)}, u32[]{:S(2)}, u32[]{:S(2)}) collective-permute-start(bf16[1,4,128,256]{3,2,1,0:T(8,128)(2,1)} %add_convert_fusion.7), channel_id=1, source_target_pairs={{0,16},{4,20},{8,24},{12,28},{16,0},{20,4},{24,8},{28,12},{1,17},{... | collective-permute-start | bytes 786440 | tf_op jit(solution)/shard_map/reduce_attn/ppermute | solution.py:572
  167.4 28.1 %collective-permute-start.33 = (bf16[1,128,1024]{2,1,0:T(8,128)(2,1)S(1)}, bf16[1,128,1024]{2,1,0:T(8,128)(2,1)S(1)}, u32[]{:S(2)}, u32[]{:S(2)}) collective-permute-start(bf16[1,128,1024]{2,1,0:T(8,128)(2,1)S(1)} %add_convert_fusion.6), channel_id=1, source_target_pairs={{0,16},{4,20},{8,24},{12,28},{16,0},{20,4},{24,8},{28,12},{1,17},{... | collective-permute-start | bytes 786440 | tf_op jit(solution)/shard_map/reduce_in/ppermute | solution.py:572
  169.3 53.7 %collective-permute-start.19 = (bf16[2,1024,256]{2,1,0:T(8,128)(2,1)}, bf16[2,1024,256]{2,1,0:T(8,128)(2,1)}, u32[]{:S(2)}, u32[]{:S(2)}) collective-permute-start(bf16[2,1024,256]{2,1,0:T(8,128)(2,1)} %get-tuple-element.149), channel_id=1, source_target_pairs={{0,1},{1,0},{2,3},{3,2},{4,5},{5,4},{6,7},{7,6},{8,9},{9,8},{10,11... | collective-permute-start | bytes 3145736 | tf_op jit(solution)/shard_map/e_sum/ppermute | solution.py:572
  170.2 79.2 %all-to-all-start.1 = ((f32[32,13,256]{2,1,0:T(8,128)}), f32[32,13,256]{2,1,0:T(8,128)S(1)}, u32[]{:S(2)}, u32[]{:S(2)}) async-start(f32[32,13,256]{2,1,0:T(8,128)} %bitcast.22), calls=%async_computation.1 | async-start | bytes 1048576 | tf_op jit(solution)/shard_map/small_sum/all_to_all | solution.py:1034
  180.5 28.3 %collective-permute-start.31 = (bf16[2,128,1024]{2,1,0:T(8,128)(2,1)S(1)}, bf16[2,128,1024]{2,1,0:T(8,128)(2,1)S(1)}, u32[]{:S(2)}, u32[]{:S(2)}) collective-permute-start(bf16[2,128,1024]{2,1,0:T(8,128)(2,1)S(1)} %pad_maximum_fusion.refs_0_), channel_id=1, source_target_pairs={{0,8},{4,12},{8,0},{12,4},{16,24},{20,28},{24,16},{28,20},{1,9},{5... | collective-permute-start | bytes 1572872 | tf_op jit(solution)/shard_map/reduce_down/ppermute | solution.py:572
  195.4 19.4 %collective-permute-start.30 = (bf16[2,128,1024]{2,1,0:T(8,128)(2,1)S(1)}, bf16[2,128,1024]{2,1,0:T(8,128)(2,1)S(1)}, u32[]{:S(2)}, u32[]{:S(2)}) collective-permute-start(bf16[2,128,1024]{2,1,0:T(8,128)(2,1)S(1)} %pad_maximum_fusion.refs_0_), channel_id=1, source_target_pairs={{0,4},{4,0},{8,12},{12,8},{16,20},{20,16},{24,28},{28,24},{1,5},{5... | collective-permute-start | bytes 1572872 | tf_op jit(solution)/shard_map/reduce_down/ppermute | solution.py:572
  198.6 16.3 %copy-start.8 = (bf16[2,128,1024]{2,1,0:T(8,128)(2,1)}, bf16[2,128,1024]{2,1,0:T(8,128)(2,1)S(1)}, u32[]{:S(2)}) copy-start(bf16[2,128,1024]{2,1,0:T(8,128)(2,1)S(1)} %collective-permute-done.32.refs_3_) | copy-start | bytes 1572868
  198.6 20.4 %collective-permute-start.29 = (bf16[1,4,128,256]{3,2,1,0:T(8,128)(2,1)S(1)}, bf16[1,4,128,256]{3,2,1,0:T(8,128)(2,1)S(1)}, u32[]{:S(2)}, u32[]{:S(2)}) collective-permute-start(bf16[1,4,128,256]{3,2,1,0:T(8,128)(2,1)S(1)} %add_convert_fusion.4), channel_id=1, source_target_pairs={{0,16},{4,20},{8,24},{12,28},{16,0},{20,4},{24,8},{28,12},{1,17},{... | collective-permute-start | bytes 786440 | tf_op jit(solution)/shard_map/reduce_attn/ppermute | solution.py:572
  202.2 16.8 %copy-start.4 = (bf16[2,128,1024]{2,1,0:T(8,128)(2,1)}, bf16[2,128,1024]{2,1,0:T(8,128)(2,1)S(1)}, u32[]{:S(2)}) copy-start(bf16[2,128,1024]{2,1,0:T(8,128)(2,1)S(1)} %pad_maximum_fusion.1.refs_0_) | copy-start | bytes 1572868
  202.2 19.8 %copy-start.6 = (bf16[2,1024,256]{2,1,0:T(8,128)(2,1)S(1)}, bf16[2,1024,256]{2,1,0:T(8,128)(2,1)}, u32[]{:S(2)}) copy-start(bf16[2,1024,256]{2,1,0:T(8,128)(2,1)} %get-tuple-element.144) | copy-start | bytes 3145732
  208.8 6.0 %copy-start.12 = (bf16[2,128,1024]{2,1,0:T(8,128)(2,1)}, bf16[2,128,1024]{2,1,0:T(8,128)(2,1)S(1)}, u32[]{:S(2)}) copy-start(bf16[2,128,1024]{2,1,0:T(8,128)(2,1)S(1)} %collective-permute-done.31.refs_2_) | copy-start | bytes 1572868
  208.8 18.9 %collective-permute-start.39 = (bf16[2,128,1024]{2,1,0:T(8,128)(2,1)S(1)}, bf16[2,128,1024]{2,1,0:T(8,128)(2,1)S(1)}, u32[]{:S(2)}, u32[]{:S(2)}) collective-permute-start(bf16[2,128,1024]{2,1,0:T(8,128)(2,1)S(1)} %pad_maximum_fusion.1.refs_0_), channel_id=1, source_target_pairs={{0,12},{4,8},{8,4},{12,0},{16,28},{20,24},{24,20},{28,16},{1,13},{... | collective-permute-start | bytes 1572872 | tf_op jit(solution)/shard_map/reduce_in/ppermute | solution.py:572
  214.9 23.7 %collective-permute-start.38 = (bf16[2,128,1024]{2,1,0:T(8,128)(2,1)S(1)}, bf16[2,128,1024]{2,1,0:T(8,128)(2,1)S(1)}, u32[]{:S(2)}, u32[]{:S(2)}) collective-permute-start(bf16[2,128,1024]{2,1,0:T(8,128)(2,1)S(1)} %pad_maximum_fusion.1.refs_0_), channel_id=1, source_target_pairs={{0,8},{4,12},{8,0},{12,4},{16,24},{20,28},{24,16},{28,20},{1,9},{5... | collective-permute-start | bytes 1572872 | tf_op jit(solution)/shard_map/reduce_in/ppermute | solution.py:572
  219.0 26.2 %collective-permute-start.37 = (bf16[2,128,1024]{2,1,0:T(8,128)(2,1)S(1)}, bf16[2,128,1024]{2,1,0:T(8,128)(2,1)S(1)}, u32[]{:S(2)}, u32[]{:S(2)}) collective-permute-start(bf16[2,128,1024]{2,1,0:T(8,128)(2,1)S(1)} %pad_maximum_fusion.1.refs_0_), channel_id=1, source_target_pairs={{0,4},{4,0},{8,12},{12,8},{16,20},{20,16},{24,28},{28,24},{1,5},{5... | collective-permute-start | bytes 1572872 | tf_op jit(solution)/shard_map/reduce_in/ppermute | solution.py:572
  219.2 30.2 %copy-start.3 = (bf16[2,4,128,256]{3,2,1,0:T(8,128)(2,1)}, bf16[2,4,128,256]{3,2,1,0:T(8,128)(2,1)S(1)}, u32[]{:S(2)}) copy-start(bf16[2,4,128,256]{3,2,1,0:T(8,128)(2,1)S(1)} %pad_maximum_fusion.2.refs_0_) | copy-start | bytes 1572868
  219.2 26.1 %copy-start.7 = (bf16[2,1024,256]{2,1,0:T(8,128)(2,1)}, bf16[2,1024,256]{2,1,0:T(8,128)(2,1)S(1)}, u32[]{:S(2)}) copy-start(bf16[2,1024,256]{2,1,0:T(8,128)(2,1)S(1)} %collective-permute-done.17) | copy-start | bytes 3145732
  219.2 38.4 %collective-permute-start.36 = (bf16[2,4,128,256]{3,2,1,0:T(8,128)(2,1)S(1)}, bf16[2,4,128,256]{3,2,1,0:T(8,128)(2,1)}, u32[]{:S(2)}, u32[]{:S(2)}) collective-permute-start(bf16[2,4,128,256]{3,2,1,0:T(8,128)(2,1)S(1)} %pad_maximum_fusion.2.refs_0_), channel_id=1, source_target_pairs={{0,12},{4,8},{8,4},{12,0},{16,28},{20,24},{24,20},{28,16},{1,13},{... | collective-permute-start | bytes 1572872 | tf_op jit(solution)/shard_map/reduce_attn/ppermute | solution.py:572
  223.0 28.9 %collective-permute-start.18 = (bf16[1,1024,256]{2,1,0:T(8,128)(2,1)}, bf16[1,1024,256]{2,1,0:T(8,128)(2,1)}, u32[]{:S(2)}, u32[]{:S(2)}) collective-permute-start(bf16[1,1024,256]{2,1,0:T(8,128)(2,1)} %add_convert_fusion.2), channel_id=1, source_target_pairs={{0,2},{1,3},{2,0},{3,1},{4,6},{5,7},{6,4},{7,5},{8,10},{9,11},{10,... | collective-permute-start | bytes 1572872 | tf_op jit(solution)/shard_map/mixed_sum/ppermute | solution.py:572
  227.7 17.5 %copy-start.9 = (bf16[2,128,1024]{2,1,0:T(8,128)(2,1)}, bf16[2,128,1024]{2,1,0:T(8,128)(2,1)S(1)}, u32[]{:S(2)}) copy-start(bf16[2,128,1024]{2,1,0:T(8,128)(2,1)S(1)} %collective-permute-done.39.refs_3_) | copy-start | bytes 1572868
  227.7 29.8 %collective-permute-start.35 = (bf16[2,4,128,256]{3,2,1,0:T(8,128)(2,1)S(1)}, bf16[2,4,128,256]{3,2,1,0:T(8,128)(2,1)}, u32[]{:S(2)}, u32[]{:S(2)}) collective-permute-start(bf16[2,4,128,256]{3,2,1,0:T(8,128)(2,1)S(1)} %pad_maximum_fusion.2.refs_0_), channel_id=1, source_target_pairs={{0,8},{4,12},{8,0},{12,4},{16,24},{20,28},{24,16},{28,20},{1,9},{5... | collective-permute-start | bytes 1572872 | tf_op jit(solution)/shard_map/reduce_attn/ppermute | solution.py:572
  238.5 6.7 %copy-start.10 = (bf16[2,128,1024]{2,1,0:T(8,128)(2,1)}, bf16[2,128,1024]{2,1,0:T(8,128)(2,1)S(1)}, u32[]{:S(2)}) copy-start(bf16[2,128,1024]{2,1,0:T(8,128)(2,1)S(1)} %collective-permute-done.38.refs_2_) | copy-start | bytes 1572868
  238.5 19.0 %collective-permute-start.34 = (bf16[2,4,128,256]{3,2,1,0:T(8,128)(2,1)S(1)}, bf16[2,4,128,256]{3,2,1,0:T(8,128)(2,1)}, u32[]{:S(2)}, u32[]{:S(2)}) collective-permute-start(bf16[2,4,128,256]{3,2,1,0:T(8,128)(2,1)S(1)} %pad_maximum_fusion.2.refs_0_), channel_id=1, source_target_pairs={{0,4},{4,0},{8,12},{12,8},{16,20},{20,16},{24,28},{28,24},{1,5},{5... | collective-permute-start | bytes 1572872 | tf_op jit(solution)/shard_map/reduce_attn/ppermute | solution.py:572
  245.2 9.5 %collective-permute-start.20 = (bf16[1,1024,256]{2,1,0:T(8,128)(2,1)}, bf16[1,1024,256]{2,1,0:T(8,128)(2,1)}, u32[]{:S(2)}, u32[]{:S(2)}) collective-permute-start(bf16[1,1024,256]{2,1,0:T(8,128)(2,1)} %add_convert_fusion), channel_id=1, source_target_pairs={{0,2},{1,3},{2,0},{3,1},{4,6},{5,7},{6,4},{7,5},{8,10},{9,11},{10,... | collective-permute-start | bytes 1572872 | tf_op jit(solution)/shard_map/e_sum/ppermute | solution.py:572
  251.2 11.4 %copy-start.24 = (f32[1,256]{1,0:T(1,128)}, f32[1,256]{1,0:T(1,128)S(1)}, u32[]{:S(2)}) copy-start(f32[1,256]{1,0:T(1,128)S(1)} %get-tuple-element.179) | copy-start | bytes 3076
  (10 other events, 23.5 us)

commit v5 on v4

--- a/solution.py
+++ b/solution.py
@@ -14,7 +14,7 @@
 eps_norm = 1e-05
 rope_base = 10000.0
 feature_scale = 0.5
-BT = 256
+BT = 512
 LANES = 128
 bf16 = jnp.bfloat16
 f32 = jnp.float32
@@ -817,7 +817,7 @@
     with jax.named_scope("state"):
         s_in = sum_before(s_own)
 
-    fb = 256
+    fb = 512
     quarter = n_seq // 4
     full_grad, hid, dpre, *ff_sums, gb_in = call(
         functools.partial(ff_kernel, n_head),

time: 267 us -> 266 us (level)
  waiting for transfers between devices: 65.4 us -> 62.5 us
    ppermute x1, waiting for transfers between devices: 6.47 us -> 3.33 us  [neighbour_sum(): got = after(lax.ppermute(packet, 'seq', route), pin)]
    pallas_call x1, Pallas kernels: 14.1 us -> 17.2 us  [body(): call(functools.partial(attn_kernel, head_size), blocks, [smem(), rows_of(...]
  transfers between devices with their start and end apart: 42 -> 42, of which waited for: 14 -> 14; matrix products, arithmetic and copies ran while one was open for 15% -> 15% of each run, Pallas kernels for 31% -> 32%
where the time goes in v5:
time: 266 us; the launch traced here: 262 us
  Pallas kernels  88.6 us (33%)
  starting transfers between devices  66.8 us (25%)
  waiting for transfers between devices  62.5 us (23%)
  other arithmetic  28 us (11%)
  local copies, waits for them, and re-layouts  15.1 us (6%)
    ppermute x36, waiting for transfers between devices, exchange(): return lax.ppermute(x, axis, [(i, i ^ mask) for i in range(count)])  55.6 us
    ppermute x36, starting transfers between devices, exchange(): return lax.ppermute(x, axis, [(i, i ^ mask) for i in range(count)])  49.6 us
    pallas_call x1, Pallas kernels, body(): call(functools.partial(ff_kernel, n_head), hidden // fb, [smem(), smem(),...  18.4 us
    pallas_call x1, Pallas kernels, body(): call(functools.partial(attn_kernel, head_size), blocks, [smem(), rows_of(...  17.2 us
    pallas_call x1, Pallas kernels, body(): call(finish_kernel, blocks, [smem(), rows_of(BT, hidden), whole(hidden, m...  15.9 us
    pallas_call x1, Pallas kernels, body(): call(functools.partial(pre_kernel, head_size, n_head), blocks, [smem(), s...  13.2 us
    pallas_call x1, Pallas kernels, body(): call(functools.partial(tail_kernel, head_size), blocks, [smem(), *[back_r...  12.1 us
    pallas_call x2, Pallas kernels, block_out(): pl.pallas_call(block_out_kernel, grid_spec=pltpu.PrefetchScalarGridSpec(n...  6.69 us
  transfers between devices with their start and end apart: 42, of which 14 were waited for; matrix products, arithmetic and copies ran while one was open for 15% of the time, Pallas kernels for 32%

profile of v5, /device:TPU:8, one launch (start us, length us, event | category | flops | bytes accessed | tf_op | source)
XLA Modules:
  0.0 262.2 jit_solution(614112404232276534)
XLA Ops:
  0.7 1.6 collective-permute-start.1
  2.3 0.8 reduce-window.8
  3.8 1.2 convert_reduce_fusion
  7.4 1.3 pad_maximum_fusion.4.refs_4_.gains_ref
  8.8 1.3 reshape.121.refs_7_.fw_ref
  10.8 3.8 %fusion.4 = (f32[1024,128]{1,0:T(8,128)}, f32[1024,128]{1,0:T(8,128)}) fusion(f32[128]{0:T(128)} %constant.55.clone, f32[128]{0:T(128)} %constant.54.clone, f32[1024]{0:T(1024)S(1)} %subtract_convert_fusion), kind=kLoop, calls=%fused_computation.15 | loop fusion | flops 262144 | bytes 1053696 | tf_op jit(solution)/shard_map/mul | solution.py:751
  15.3 1.5 collective-permute-start.4
  16.8 1.1 copy.54.refs_12_.segc_ref
  17.8 1.1 copy.53.refs_11_
  18.9 0.8 copy-done.27
  19.9 13.2 %pre_kernel.1 = (bf16[1024,1024]{1,0:T(8,128)(2,1)}, bf16[1024,1024]{1,0:T(8,128)(2,1)}, bf16[1024,1024]{1,0:T(8,128)(2,1)}, bf16[1024,1024]{1,0:T(8,128)(2,1)},...) custom-call(s32[2,3]{1,0:T(2,128)} %add_add_fusion.1.labels_ref, ...), custom_call_target="tpu_custom_call" | custom-call | flops 2684354560 | bytes 12058624 | tf_op jit(solution)/shard_map/pre_kernel/pallas_call | solution.py:767
  33.7 6.3 %all-to-all-start = ((f32[8,72,256]{2,1,0:T(8,128)}), f32[8,72,256]{2,1,0:T(8,128)S(1)}, u32[]{:S(2)}, u32[]{:S(2)}) async-start(f32[8,72,256]{2,1,0:T(8,128)} %get-tuple-element.98), calls=%async_computation | async-start | bytes 1179648 | tf_op jit(solution)/shard_map/state/all_to_all | solution.py:665
  40.0 0.8 dynamic-slice_add_fusion
  40.8 0.8 copy-done.28
  41.7 18.4 %ff_kernel.1 = (bf16[1024,1024]{1,0:T(8,128)(2,1)}, bf16[1024,1024]{1,0:T(8,128)(2,1)}, bf16[1024,1024]{1,0:T(8,128)(2,1)}, bf16[2,128,1024]{2,1,0:T(8,128)(2,1)...) custom-call(s32[1]{0:T(128)} %bitcast.me_ref, ...), custom_call_target="tpu_custom_call" | custom-call | flops 8589934592 | bytes 14680064 | tf_op jit(solution)/shard_map/ff_kernel/pallas_call | solution.py:822
  60.2 1.5 collective-permute-start.10
  62.3 1.4 collective-permute-start.12
  64.5 17.2 %attn_kernel.1 = (bf16[1024,256]{1,0:T(8,128)(2,1)}, f32[1024,256]{1,0:T(8,128)}, f32[1024,256]{1,0:T(8,128)}, f32[1024,256]{1,0:T(8,128)}, f32[2,256,256]{2,1,0...) custom-call(s32[2,3]{1,0:T(2,128)} %add_add_fusion.1.labels_ref, ...), custom_call_target="tpu_custom_call" | custom-call | flops 12884901888 | bytes 7340032 | tf_op jit(solution)/shard_map/attn_kernel/pallas_call | solution.py:858
  81.6 1.5 collective-permute-start.6
  84.6 3.3 %collective-permute-done.6 = f32[72,256]{1,0:T(8,128)S(1)} collective-permute-done((f32[72,256]{1,0:T(8,128)}, f32[72,256]{1,0:T(8,128)S(1)}, u32[]{:S(2)}, u32[]{:S(2)}) %collective-permute-start.6) | collective-permute-done | bytes 73760 | tf_op jit(solution)/shard_map/grad_state/ppermute | solution.py:684
  87.9 0.9 add.180
  89.5 1.3 collective-permute-start.8
  90.8 2.9 %collective-permute-start.7 = (f32[72,256]{1,0:T(8,128)S(1)}, f32[72,256]{1,0:T(8,128)S(1)}, u32[]{:S(2)}, u32[]{:S(2)}) collective-permute-start(f32[72,256]{1,0:T(8,128)S(1)} %add.180), channel_id=1, source_target_pairs={{8,0},{12,4},{16,8},{20,12},{24,16},{28,20},{9,1},{13,5},{17,9},{2... | collective-permute-start | bytes 221192 | tf_op jit(solution)/shard_map/grad_state/ppermute | solution.py:692
  93.9 3.6 %collective-permute-start.16 = (bf16[1,128,1024]{2,1,0:T(8,128)(2,1)S(1)}, bf16[1,128,1024]{2,1,0:T(8,128)(2,1)S(1)}, u32[]{:S(2)}, u32[]{:S(2)}) collective-permute-start(bf16[1,128,1024]{2,1,0:T(8,128)(2,1)S(1)} %add_convert_fusion.12), channel_id=1, source_target_pairs={{0,16},{4,20},{8,24},{12,28},{16,0},{20,4},{24,8},{28,12},{1,17},{... | collective-permute-start | bytes 786440 | tf_op jit(solution)/shard_map/reduce_down/ppermute | solution.py:572
  97.5 1.7 collective-permute-start.13
  99.2 3.3 %collective-permute-start.15 = (bf16[2,128,1024]{2,1,0:T(8,128)(2,1)}, bf16[2,128,1024]{2,1,0:T(8,128)(2,1)S(1)}, u32[]{:S(2)}, u32[]{:S(2)}) collective-permute-start(bf16[2,128,1024]{2,1,0:T(8,128)(2,1)} %get-tuple-element.137), channel_id=1, source_target_pairs={{0,12},{4,8},{8,4},{12,0},{16,28},{20,24},{24,20},{28,16},{1,13},{... | collective-permute-start | bytes 1572872 | tf_op jit(solution)/shard_map/reduce_in/ppermute | solution.py:572
  102.6 3.6 %collective-permute-done.7 = f32[72,256]{1,0:T(8,128)S(1)} collective-permute-done((f32[72,256]{1,0:T(8,128)S(1)}, f32[72,256]{1,0:T(8,128)S(1)}, u32[]{:S(2)}, u32[]{:S(2)}) %collective-permute-start.7) | collective-permute-done | bytes 73760 | tf_op jit(solution)/shard_map/grad_state/ppermute | solution.py:692
  106.8 12.1 %tail_kernel.1 = (bf16[3,1024,256]{2,1,0:T(8,128)(2,1)}, f32[8,256]{1,0:T(8,128)}, bf16[2,4,128,256]{3,2,1,0:T(8,128)(2,1)}, bf16[2,4,128,256]{3,2,1,0:T(8,128)(...) custom-call(s32[2,3]{1,0:T(2,128)} %add_add_fusion.1.labels_ref, ...), custom_call_target="tpu_custom_call" | custom-call | flops 1610612736 | bytes 11534336 | tf_op jit(solution)/shard_map/tail_kernel/pallas_call | solution.py:915
  119.6 1.7 collective-permute-start.24
  121.6 1.9 collective-permute-start.26
  123.5 11.0 %collective-permute-done.15 = bf16[2,128,1024]{2,1,0:T(8,128)(2,1)S(1)} collective-permute-done((bf16[2,128,1024]{2,1,0:T(8,128)(2,1)}, bf16[2,128,1024]{2,1,0:T(8,128)(2,1)S(1)}, u32[]{:S(2)}, u32[]{:S(2)}) %collective-permute-start.15) | collective-permute-done | bytes 524320 | tf_op jit(solution)/shard_map/reduce_in/ppermute | solution.py:572
  134.6 2.2 collective-permute-start.23
  136.8 15.9 %finish_kernel.1 = (bf16[2,1024,256]{2,1,0:T(8,128)(2,1)}, bf16[2,1024,256]{2,1,0:T(8,128)(2,1)}, bf16[2,1024,256]{2,1,0:T(8,128)(2,1)}, bf16[2,1024,256]{2,1,0:T(8,128)(2,1)}, f32[16,1024]{1,0:T(8,128)}) custom-call(s32[1]{0:T(128)} %bitcast.me_ref, bf16[1024,1024]{1,0:T(8,128)(2,1)} %get-tuple-element.103.hid_ref, bf16[1024,1024]{1,0:T(8,128)(2,1)} %wdown_ref.1, ...), custom_call_target="tpu_custom_call" | custom-call | flops 3758096384 | bytes 12058624 | tf_op jit(solution)/shard_map/finish_kernel/pallas_call | solution.py:959
  152.7 3.9 %collective-permute-done.27 = bf16[1,128,1024]{2,1,0:T(8,128)(2,1)S(1)} collective-permute-done((bf16[1,128,1024]{2,1,0:T(8,128)(2,1)S(1)}, bf16[1,128,1024]{2,1,0:T(8,128)(2,1)S(1)}, u32[]{:S(2)}, u32[]{:S(2)}) %collective-permute-start.27) | collective-permute-done | bytes 262176 | tf_op jit(solution)/shard_map/reduce_down/ppermute | solution.py:572
  157.4 0.8 slice.182
  158.6 0.8 slice_add_fusion.1
  160.2 1.9 collective-permute-done.26
  162.1 1.9 add_convert_fusion.7
  164.1 1.2 collective-permute-start.28
  165.3 1.4 add_convert_fusion.6
  166.7 1.8 collective-permute-start.33
  168.6 0.9 broadcast_in_dim.61
  169.5 4.6 %all-to-all-start.1 = ((f32[32,13,256]{2,1,0:T(8,128)}), f32[32,13,256]{2,1,0:T(8,128)S(1)}, u32[]{:S(2)}, u32[]{:S(2)}) async-start(f32[32,13,256]{2,1,0:T(8,128)} %bitcast.22), calls=%async_computation.1 | async-start | bytes 1048576 | tf_op jit(solution)/shard_map/small_sum/all_to_all | solution.py:1034
  174.0 5.8 %collective-permute-done.28 = bf16[1,4,128,256]{3,2,1,0:T(8,128)(2,1)S(1)} collective-permute-done((bf16[1,4,128,256]{3,2,1,0:T(8,128)(2,1)}, bf16[1,4,128,256]{3,2,1,0:T(8,128)(2,1)S(1)}, u32[]{:S(2)}, u32[]{:S(2)}) %collective-permute-start.28) | collective-permute-done | bytes 262176 | tf_op jit(solution)/shard_map/reduce_attn/ppermute | solution.py:572
  179.8 8.9 %collective-permute-start.31 = (bf16[2,128,1024]{2,1,0:T(8,128)(2,1)S(1)}, bf16[2,128,1024]{2,1,0:T(8,128)(2,1)S(1)}, u32[]{:S(2)}, u32[]{:S(2)}) collective-permute-start(bf16[2,128,1024]{2,1,0:T(8,128)(2,1)S(1)} %pad_maximum_fusion.refs_0_), channel_id=1, source_target_pairs={{0,8},{4,12},{8,0},{12,4},{16,24},{20,28},{24,16},{28,20},{1,9},{5... | collective-permute-start | bytes 1572872 | tf_op jit(solution)/shard_map/reduce_down/ppermute | solution.py:572
  188.7 6.1 %collective-permute-done.33 = bf16[1,128,1024]{2,1,0:T(8,128)(2,1)S(1)} collective-permute-done((bf16[1,128,1024]{2,1,0:T(8,128)(2,1)S(1)}, bf16[1,128,1024]{2,1,0:T(8,128)(2,1)S(1)}, u32[]{:S(2)}, u32[]{:S(2)}) %collective-permute-start.33) | collective-permute-done | bytes 262176 | tf_op jit(solution)/shard_map/reduce_in/ppermute | solution.py:572
  194.8 1.8 collective-permute-start.30
  196.6 1.4 add_convert_fusion.4
  197.9 3.5 %collective-permute-start.29 = (bf16[1,4,128,256]{3,2,1,0:T(8,128)(2,1)S(1)}, bf16[1,4,128,256]{3,2,1,0:T(8,128)(2,1)S(1)}, u32[]{:S(2)}, u32[]{:S(2)}) collective-permute-start(bf16[1,4,128,256]{3,2,1,0:T(8,128)(2,1)S(1)} %add_convert_fusion.4), channel_id=1, source_target_pairs={{0,16},{4,20},{8,24},{12,28},{16,0},{20,4},{24,8},{28,12},{1,17},{... | collective-permute-start | bytes 786440 | tf_op jit(solution)/shard_map/reduce_attn/ppermute | solution.py:572
  201.5 6.5 %collective-permute-done.31.refs_2_ = bf16[2,128,1024]{2,1,0:T(8,128)(2,1)S(1)} collective-permute-done((bf16[2,128,1024]{2,1,0:T(8,128)(2,1)S(1)}, bf16[2,128,1024]{2,1,0:T(8,128)(2,1)S(1)}, u32[]{:S(2)}, u32[]{:S(2)}) %collective-permute-start.31) | collective-permute-done | bytes 524320 | tf_op jit(solution)/shard_map/reduce_down/ppermute | solution.py:572
  208.0 5.8 %collective-permute-start.39 = (bf16[2,128,1024]{2,1,0:T(8,128)(2,1)S(1)}, bf16[2,128,1024]{2,1,0:T(8,128)(2,1)S(1)}, u32[]{:S(2)}, u32[]{:S(2)}) collective-permute-start(bf16[2,128,1024]{2,1,0:T(8,128)(2,1)S(1)} %pad_maximum_fusion.1.refs_0_), channel_id=1, source_target_pairs={{0,12},{4,8},{8,4},{12,0},{16,28},{20,24},{24,20},{28,16},{1,13},{... | collective-permute-start | bytes 1572872 | tf_op jit(solution)/shard_map/reduce_in/ppermute | solution.py:572
  214.6 3.3 %block_out_kernel.3 = f32[1024,1024]{1,0:T(8,128)} custom-call(s32[1]{0:T(128)} %bitcast.1.rank_ref, bf16[2,128,1024]{2,1,0:T(8,128)(2,1)} %copy-done.2, bf16[2,128,1024]{2,1,0:T(8,128)(2,1)} %copy-done.13, bf16[2,128,1024]{2,1,0:T(8,128)(2,1)} %copy-done.12, bf16[2,128,1024]{2,1,0:T(8,128)(2,1)} %copy-done.8), custom_call_target="tpu_custom_call" | custom-call | bytes 6291456 | tf_op jit(solution)/shard_map/block_out_kernel/pallas_call | solution.py:648
  218.2 2.8 %collective-permute-start.36 = (bf16[2,4,128,256]{3,2,1,0:T(8,128)(2,1)S(1)}, bf16[2,4,128,256]{3,2,1,0:T(8,128)(2,1)}, u32[]{:S(2)}, u32[]{:S(2)}) collective-permute-start(bf16[2,4,128,256]{3,2,1,0:T(8,128)(2,1)S(1)} %pad_maximum_fusion.2.refs_0_), channel_id=1, source_target_pairs={{0,12},{4,8},{8,4},{12,0},{16,28},{20,24},{24,20},{28,16},{1,13},{... | collective-permute-start | bytes 1572872 | tf_op jit(solution)/shard_map/reduce_attn/ppermute | solution.py:572
  221.0 0.9 add_convert_fusion.2
  222.0 2.0 add_convert_fusion
  223.9 2.8 %collective-permute-done.39.refs_3_ = bf16[2,128,1024]{2,1,0:T(8,128)(2,1)S(1)} collective-permute-done((bf16[2,128,1024]{2,1,0:T(8,128)(2,1)S(1)}, bf16[2,128,1024]{2,1,0:T(8,128)(2,1)S(1)}, u32[]{:S(2)}, u32[]{:S(2)}) %collective-permute-start.39) | collective-permute-done | bytes 524320 | tf_op jit(solution)/shard_map/reduce_in/ppermute | solution.py:572
  226.7 10.7 %collective-permute-done.38.refs_2_ = bf16[2,128,1024]{2,1,0:T(8,128)(2,1)S(1)} collective-permute-done((bf16[2,128,1024]{2,1,0:T(8,128)(2,1)S(1)}, bf16[2,128,1024]{2,1,0:T(8,128)(2,1)S(1)}, u32[]{:S(2)}, u32[]{:S(2)}) %collective-permute-start.38) | collective-permute-done | bytes 524320 | tf_op jit(solution)/shard_map/reduce_in/ppermute | solution.py:572
  237.5 1.1 collective-permute-start.34
  238.5 5.7 %collective-permute-done.37.refs_1_ = bf16[2,128,1024]{2,1,0:T(8,128)(2,1)S(1)} collective-permute-done((bf16[2,128,1024]{2,1,0:T(8,128)(2,1)S(1)}, bf16[2,128,1024]{2,1,0:T(8,128)(2,1)S(1)}, u32[]{:S(2)}, u32[]{:S(2)}) %collective-permute-start.37) | collective-permute-done | bytes 524320 | tf_op jit(solution)/shard_map/reduce_in/ppermute | solution.py:572
  244.3 0.8 copy-done.11
  245.0 3.3 %block_out_kernel.2 = f32[1024,1024]{1,0:T(8,128)} custom-call(s32[1]{0:T(128)} %bitcast.1.rank_ref, bf16[2,128,1024]{2,1,0:T(8,128)(2,1)} %copy-done.4, bf16[2,128,1024]{2,1,0:T(8,128)(2,1)} %copy-done.11, bf16[2,128,1024]{2,1,0:T(8,128)(2,1)} %copy-done.10, bf16[2,128,1024]{2,1,0:T(8,128)(2,1)} %copy-done.9), custom_call_target="tpu_custom_call" | custom-call | bytes 6291456 | tf_op jit(solution)/shard_map/block_out_kernel/pallas_call | solution.py:648
  250.9 2.6 fusion.3
  253.7 2.8 %convert_add_fusion = f32[1024,256]{1,0:T(8,128)} fusion(bf16[1024,256]{1,0:T(8,128)(2,1)S(1)} %copy-done.1, bf16[1,1024,256]{2,1,0:T(8,128)(2,1)} %collective-permute-done.20, bf16[2,1024,256]{2,1,0:T(8,128)(2,1)} %collective-permute-done.19, f32[1024]{0:T(1024)S(1)} %bitcast.50, bf16[1024,1024]{1,0:T(8,128)(2,1)} %get-tuple-element.143.xhat_ref, ...), kind=kLoop, calls=%fused_computation | loop fusion | flops 3670016 | bytes 3682308 | tf_op jit(solution)/shard_map/add | solution.py:999
  256.5 5.1 %widen_kernel.1 = (f32[3,1024,256]{2,1,0:T(8,128)}, f32[256,1024]{1,0:T(8,128)}) custom-call(s32[1]{0:T(128)} %bitcast.1.rank_ref, bf16[2,4,128,256]{3,2,1,0:T(8,128)(2,1)} %copy-done.3, bf16[2,4,128,256]{3,2,1,0:T(8,128)(2,1)} %collective-permute-done.34.refs_1_, bf16[2,4,128,256]{3,2,1,0:T(8,128)(2,1)} %collective-permute-done.35.refs_2_, ...), custom_call_target="tpu_custom_call" | custom-call | bytes 3145728 | tf_op jit(solution)/shard_map/widen_kernel/pallas_call | solution.py:1014
  (154 shorter events, 17.5 us)
Async XLA Ops:
  0.6 18.3 %collective-permute-start = (bf16[1024,256]{1,0:T(8,128)(2,1)}, bf16[1024,256]{1,0:T(8,128)(2,1)S(1)}, u32[]{:S(2)}, u32[]{:S(2)}) collective-permute-start(bf16[1024,256]{1,0:T(8,128)(2,1)} %refs_0_.1), channel_id=1, source_target_pairs={{0,1},{1,0},{2,3},{3,2},{4,5},{5,4},{6,7},{7,6},{8,9},{9,8},{10,11... | collective-permute-start | bytes 1572872 | tf_op jit(solution)/shard_map/gather_tokens/ppermute | solution.py:572
  0.7 14.5 %collective-permute-start.1 = (bf16[1024,256]{1,0:T(8,128)(2,1)}, bf16[1024,256]{1,0:T(8,128)(2,1)S(1)}, u32[]{:S(2)}, u32[]{:S(2)}) collective-permute-start(bf16[1024,256]{1,0:T(8,128)(2,1)} %refs_0_.1), channel_id=1, source_target_pairs={{0,2},{1,3},{2,0},{3,1},{4,6},{5,7},{6,4},{7,5},{8,10},{9,11},{10,... | collective-permute-start | bytes 1572872 | tf_op jit(solution)/shard_map/gather_tokens/ppermute | solution.py:572
  5.5 27.6 %copy-start.23 = (s32[1024]{0:T(1024)}, s32[1024]{0:T(1024)S(1)}, u32[]{:S(2)}) copy-start(s32[1024]{0:T(1024)S(1)} %convert_reduce_fusion.1) | copy-start | bytes 12292
  15.3 3.6 %collective-permute-start.2 = (bf16[1024,256]{1,0:T(8,128)(2,1)S(1)}, bf16[1024,256]{1,0:T(8,128)(2,1)S(1)}, u32[]{:S(2)}, u32[]{:S(2)}) collective-permute-start(bf16[1024,256]{1,0:T(8,128)(2,1)S(1)} %collective-permute-done.1.refs_2_), channel_id=1, source_target_pairs={{0,1},{1,0},{2,3},{3,2},{4,5},{5,4},{6,7},{7,6},{8,9},{9,8},{10,11... | collective-permute-start | bytes 1572872 | tf_op jit(solution)/shard_map/gather_tokens/ppermute | solution.py:572
  15.3 17.8 %collective-permute-start.4 = (bf16[1024,256]{1,0:T(8,128)(2,1)}, bf16[1024,256]{1,0:T(8,128)(2,1)S(1)}, u32[]{:S(2)}, u32[]{:S(2)}) collective-permute-start(bf16[1024,256]{1,0:T(8,128)(2,1)} %refs_0_.2), channel_id=1, source_target_pairs={{0,2},{1,3},{2,0},{3,1},{4,6},{5,7},{6,4},{7,5},{8,10},{9,11},{10,... | collective-permute-start | bytes 1572872 | tf_op jit(solution)/shard_map/gather_grads/ppermute | solution.py:572
  19.9 13.2 %copy-start = (bf16[1024,256]{1,0:T(8,128)(2,1)S(1)}, bf16[1024,256]{1,0:T(8,128)(2,1)}, u32[]{:S(2)}) copy-start(bf16[1024,256]{1,0:T(8,128)(2,1)} %refs_0_.2) | copy-start | bytes 1572868
  33.1 7.7 %copy-start.26 = (bf16[1024,256]{1,0:T(8,128)(2,1)}, bf16[1024,256]{1,0:T(8,128)(2,1)S(1)}, u32[]{:S(2)}) copy-start(bf16[1024,256]{1,0:T(8,128)(2,1)S(1)} %collective-permute-done.4.refs_2_) | copy-start | bytes 1572868
  33.1 7.6 %collective-permute-start.3 = (bf16[1024,256]{1,0:T(8,128)(2,1)S(1)}, bf16[1024,256]{1,0:T(8,128)(2,1)S(1)}, u32[]{:S(2)}, u32[]{:S(2)}) collective-permute-start(bf16[1024,256]{1,0:T(8,128)(2,1)S(1)} %copy-done), channel_id=1, source_target_pairs={{0,1},{1,0},{2,3},{3,2},{4,5},{5,4},{6,7},{7,6},{8,9},{9,8},{10,11... | collective-permute-start | bytes 1572872 | tf_op jit(solution)/shard_map/gather_grads/ppermute | solution.py:572
  33.4 7.3 %collective-permute-start.5 = (bf16[1024,256]{1,0:T(8,128)(2,1)S(1)}, bf16[1024,256]{1,0:T(8,128)(2,1)S(1)}, u32[]{:S(2)}, u32[]{:S(2)}) collective-permute-start(bf16[1024,256]{1,0:T(8,128)(2,1)S(1)} %collective-permute-done.4.refs_2_), channel_id=1, source_target_pairs={{0,1},{1,0},{2,3},{3,2},{4,5},{5,4},{6,7},{7,6},{8,9},{9,8},{10,11... | collective-permute-start | bytes 1572872 | tf_op jit(solution)/shard_map/gather_grads/ppermute | solution.py:572
  33.7 30.0 %all-to-all-start = ((f32[8,72,256]{2,1,0:T(8,128)}), f32[8,72,256]{2,1,0:T(8,128)S(1)}, u32[]{:S(2)}, u32[]{:S(2)}) async-start(f32[8,72,256]{2,1,0:T(8,128)} %get-tuple-element.98), calls=%async_computation | async-start | bytes 1179648 | tf_op jit(solution)/shard_map/state/all_to_all | solution.py:665
  60.2 30.6 %collective-permute-start.10 = (bf16[2,128,1024]{2,1,0:T(8,128)(2,1)}, bf16[2,128,1024]{2,1,0:T(8,128)(2,1)S(1)}, u32[]{:S(2)}, u32[]{:S(2)}) collective-permute-start(bf16[2,128,1024]{2,1,0:T(8,128)(2,1)} %get-tuple-element.121), channel_id=1, source_target_pairs={{0,4},{4,0},{8,12},{12,8},{16,20},{20,16},{24,28},{28,24},{1,5},{5... | collective-permute-start | bytes 1572872 | tf_op jit(solution)/shard_map/reduce_down/ppermute | solution.py:572
  61.7 32.0 %collective-permute-start.11 = (bf16[2,128,1024]{2,1,0:T(8,128)(2,1)}, bf16[2,128,1024]{2,1,0:T(8,128)(2,1)S(1)}, u32[]{:S(2)}, u32[]{:S(2)}) collective-permute-start(bf16[2,128,1024]{2,1,0:T(8,128)(2,1)} %get-tuple-element.122), channel_id=1, source_target_pairs={{0,8},{4,12},{8,0},{12,4},{16,24},{20,28},{24,16},{28,20},{1,9},{5... | collective-permute-start | bytes 1572872 | tf_op jit(solution)/shard_map/reduce_down/ppermute | solution.py:572
  62.3 31.5 %collective-permute-start.12 = (bf16[2,128,1024]{2,1,0:T(8,128)(2,1)}, bf16[2,128,1024]{2,1,0:T(8,128)(2,1)S(1)}, u32[]{:S(2)}, u32[]{:S(2)}) collective-permute-start(bf16[2,128,1024]{2,1,0:T(8,128)(2,1)} %get-tuple-element.123), channel_id=1, source_target_pairs={{0,12},{4,8},{8,4},{12,0},{16,28},{20,24},{24,20},{28,16},{1,13},{... | collective-permute-start | bytes 1572872 | tf_op jit(solution)/shard_map/reduce_down/ppermute | solution.py:572
  64.4 18.7 %copy-start.14 = (f32[1024,1]{1,0:T(8,128)S(1)}, f32[1024,1]{1,0:T(8,128)}, u32[]{:S(2)}) copy-start(f32[1024,1]{1,0:T(8,128)} %get-tuple-element.147) | copy-start | bytes 12292
  64.4 19.5 %copy-start.25 = (f32[1,1024]{1,0:T(1,128)S(1)}, f32[1,1024]{1,0:T(1,128)}, u32[]{:S(2)}) copy-start(f32[1,1024]{1,0:T(1,128)} %get-tuple-element.152) | copy-start | bytes 12292
  64.5 29.3 %copy-start.19 = (bf16[2,128,1024]{2,1,0:T(8,128)(2,1)S(1)}, bf16[2,128,1024]{2,1,0:T(8,128)(2,1)}, u32[]{:S(2)}) copy-start(bf16[2,128,1024]{2,1,0:T(8,128)(2,1)} %get-tuple-element.120) | copy-start | bytes 1572868
  81.6 6.3 %collective-permute-start.6 = (f32[72,256]{1,0:T(8,128)}, f32[72,256]{1,0:T(8,128)S(1)}, u32[]{:S(2)}, u32[]{:S(2)}) collective-permute-start(f32[72,256]{1,0:T(8,128)} %get-tuple-element.118), channel_id=1, source_target_pairs={{0,4},{4,0},{8,12},{12,8},{16,20},{20,16},{24,28},{28,24},{1,5},{5... | collective-permute-start | bytes 221192 | tf_op jit(solution)/shard_map/grad_state/ppermute | solution.py:684
  88.8 10.4 %collective-permute-start.9 = (f32[72,256]{1,0:T(8,128)S(1)}, f32[72,256]{1,0:T(8,128)S(1)}, u32[]{:S(2)}, u32[]{:S(2)}) collective-permute-start(f32[72,256]{1,0:T(8,128)S(1)} %add.180), channel_id=1, source_target_pairs={{24,0},{28,4},{25,1},{29,5},{26,2},{30,6},{27,3},{31,7}} | collective-permute-start | bytes 221192 | tf_op jit(solution)/shard_map/grad_state/ppermute | solution.py:692
  89.5 9.7 %collective-permute-start.8 = (f32[72,256]{1,0:T(8,128)S(1)}, f32[72,256]{1,0:T(8,128)S(1)}, u32[]{:S(2)}, u32[]{:S(2)}) collective-permute-start(f32[72,256]{1,0:T(8,128)S(1)} %add.180), channel_id=1, source_target_pairs={{16,0},{20,4},{24,8},{28,12},{17,1},{21,5},{25,9},{29,13},{18,2},{... | collective-permute-start | bytes 221192 | tf_op jit(solution)/shard_map/grad_state/ppermute | solution.py:692
  90.8 15.3 %collective-permute-start.7 = (f32[72,256]{1,0:T(8,128)S(1)}, f32[72,256]{1,0:T(8,128)S(1)}, u32[]{:S(2)}, u32[]{:S(2)}) collective-permute-start(f32[72,256]{1,0:T(8,128)S(1)} %add.180), channel_id=1, source_target_pairs={{8,0},{12,4},{16,8},{20,12},{24,16},{28,20},{9,1},{13,5},{17,9},{2... | collective-permute-start | bytes 221192 | tf_op jit(solution)/shard_map/grad_state/ppermute | solution.py:692
  93.9 27.4 %collective-permute-start.16 = (bf16[1,128,1024]{2,1,0:T(8,128)(2,1)S(1)}, bf16[1,128,1024]{2,1,0:T(8,128)(2,1)S(1)}, u32[]{:S(2)}, u32[]{:S(2)}) collective-permute-start(bf16[1,128,1024]{2,1,0:T(8,128)(2,1)S(1)} %add_convert_fusion.12), channel_id=1, source_target_pairs={{0,16},{4,20},{8,24},{12,28},{16,0},{20,4},{24,8},{28,12},{1,17},{... | collective-permute-start | bytes 786440 | tf_op jit(solution)/shard_map/reduce_down/ppermute | solution.py:572
  97.5 24.1 %collective-permute-start.13 = (bf16[2,128,1024]{2,1,0:T(8,128)(2,1)}, bf16[2,128,1024]{2,1,0:T(8,128)(2,1)S(1)}, u32[]{:S(2)}, u32[]{:S(2)}) collective-permute-start(bf16[2,128,1024]{2,1,0:T(8,128)(2,1)} %get-tuple-element.135), channel_id=1, source_target_pairs={{0,4},{4,0},{8,12},{12,8},{16,20},{20,16},{24,28},{28,24},{1,5},{5... | collective-permute-start | bytes 1572872 | tf_op jit(solution)/shard_map/reduce_in/ppermute | solution.py:572
  99.2 24.3 %collective-permute-start.14 = (bf16[2,128,1024]{2,1,0:T(8,128)(2,1)}, bf16[2,128,1024]{2,1,0:T(8,128)(2,1)S(1)}, u32[]{:S(2)}, u32[]{:S(2)}) collective-permute-start(bf16[2,128,1024]{2,1,0:T(8,128)(2,1)} %get-tuple-element.136), channel_id=1, source_target_pairs={{0,8},{4,12},{8,0},{12,4},{16,24},{20,28},{24,16},{28,20},{1,9},{5... | collective-permute-start | bytes 1572872 | tf_op jit(solution)/shard_map/reduce_in/ppermute | solution.py:572
  99.2 35.2 %collective-permute-start.15 = (bf16[2,128,1024]{2,1,0:T(8,128)(2,1)}, bf16[2,128,1024]{2,1,0:T(8,128)(2,1)S(1)}, u32[]{:S(2)}, u32[]{:S(2)}) collective-permute-start(bf16[2,128,1024]{2,1,0:T(8,128)(2,1)} %get-tuple-element.137), channel_id=1, source_target_pairs={{0,12},{4,8},{8,4},{12,0},{16,28},{20,24},{24,20},{28,16},{1,13},{... | collective-permute-start | bytes 1572872 | tf_op jit(solution)/shard_map/reduce_in/ppermute | solution.py:572
  106.8 14.6 %copy-start.22 = (bf16[2,128,1024]{2,1,0:T(8,128)(2,1)S(1)}, bf16[2,128,1024]{2,1,0:T(8,128)(2,1)}, u32[]{:S(2)}) copy-start(bf16[2,128,1024]{2,1,0:T(8,128)(2,1)} %copy-done.21) | copy-start | bytes 1572868
  106.8 27.7 %copy-start.15 = (bf16[2,128,1024]{2,1,0:T(8,128)(2,1)S(1)}, bf16[2,128,1024]{2,1,0:T(8,128)(2,1)}, u32[]{:S(2)}) copy-start(bf16[2,128,1024]{2,1,0:T(8,128)(2,1)} %get-tuple-element.131) | copy-start | bytes 1572868
  119.6 39.8 %collective-permute-start.24 = (bf16[2,4,128,256]{3,2,1,0:T(8,128)(2,1)}, bf16[2,4,128,256]{3,2,1,0:T(8,128)(2,1)}, u32[]{:S(2)}, u32[]{:S(2)}) collective-permute-start(bf16[2,4,128,256]{3,2,1,0:T(8,128)(2,1)} %get-tuple-element.154), channel_id=1, source_target_pairs={{0,4},{4,0},{8,12},{12,8},{16,20},{20,16},{24,28},{28,24},{1,5},{5... | collective-permute-start | bytes 1572872 | tf_op jit(solution)/shard_map/reduce_attn/ppermute | solution.py:572
  121.3 38.4 %collective-permute-start.25 = (bf16[2,4,128,256]{3,2,1,0:T(8,128)(2,1)}, bf16[2,4,128,256]{3,2,1,0:T(8,128)(2,1)}, u32[]{:S(2)}, u32[]{:S(2)}) collective-permute-start(bf16[2,4,128,256]{3,2,1,0:T(8,128)(2,1)} %get-tuple-element.155), channel_id=1, source_target_pairs={{0,8},{4,12},{8,0},{12,4},{16,24},{20,28},{24,16},{28,20},{1,9},{5... | collective-permute-start | bytes 1572872 | tf_op jit(solution)/shard_map/reduce_attn/ppermute | solution.py:572
  121.6 31.1 %copy-start.17 = (bf16[2,128,1024]{2,1,0:T(8,128)(2,1)}, bf16[2,128,1024]{2,1,0:T(8,128)(2,1)S(1)}, u32[]{:S(2)}) copy-start(bf16[2,128,1024]{2,1,0:T(8,128)(2,1)S(1)} %collective-permute-done.13) | copy-start | bytes 1572868
  121.6 40.5 %collective-permute-start.26 = (bf16[2,4,128,256]{3,2,1,0:T(8,128)(2,1)}, bf16[2,4,128,256]{3,2,1,0:T(8,128)(2,1)}, u32[]{:S(2)}, u32[]{:S(2)}) collective-permute-start(bf16[2,4,128,256]{3,2,1,0:T(8,128)(2,1)} %get-tuple-element.156), channel_id=1, source_target_pairs={{0,12},{4,8},{8,4},{12,0},{16,28},{20,24},{24,20},{28,16},{1,13},{... | collective-permute-start | bytes 1572872 | tf_op jit(solution)/shard_map/reduce_attn/ppermute | solution.py:572
  123.5 29.2 %copy-start.18 = (bf16[2,128,1024]{2,1,0:T(8,128)(2,1)}, bf16[2,128,1024]{2,1,0:T(8,128)(2,1)S(1)}, u32[]{:S(2)}) copy-start(bf16[2,128,1024]{2,1,0:T(8,128)(2,1)S(1)} %collective-permute-done.14) | copy-start | bytes 1572868
  123.5 33.1 %collective-permute-start.27 = (bf16[1,128,1024]{2,1,0:T(8,128)(2,1)S(1)}, bf16[1,128,1024]{2,1,0:T(8,128)(2,1)S(1)}, u32[]{:S(2)}, u32[]{:S(2)}) collective-permute-start(bf16[1,128,1024]{2,1,0:T(8,128)(2,1)S(1)} %add_convert_fusion.10), channel_id=1, source_target_pairs={{0,16},{4,20},{8,24},{12,28},{16,0},{20,4},{24,8},{28,12},{1,17},{... | collective-permute-start | bytes 786440 | tf_op jit(solution)/shard_map/reduce_down/ppermute | solution.py:572
  134.5 18.2 %copy-start.20 = (bf16[2,128,1024]{2,1,0:T(8,128)(2,1)}, bf16[2,128,1024]{2,1,0:T(8,128)(2,1)S(1)}, u32[]{:S(2)}) copy-start(bf16[2,128,1024]{2,1,0:T(8,128)(2,1)S(1)} %collective-permute-done.15) | copy-start | bytes 1572868
  134.6 30.7 %collective-permute-start.23 = (bf16[1,128,1024]{2,1,0:T(8,128)(2,1)S(1)}, bf16[1,128,1024]{2,1,0:T(8,128)(2,1)}, u32[]{:S(2)}, u32[]{:S(2)}) collective-permute-start(bf16[1,128,1024]{2,1,0:T(8,128)(2,1)S(1)} %add_convert_fusion.9), channel_id=1, source_target_pairs={{0,16},{4,20},{8,24},{12,28},{16,0},{20,4},{24,8},{28,12},{1,17},{... | collective-permute-start | bytes 786440 | tf_op jit(solution)/shard_map/reduce_in/ppermute | solution.py:572
  136.8 25.3 %copy-start.16 = (bf16[2,4,128,256]{3,2,1,0:T(8,128)(2,1)S(1)}, bf16[2,4,128,256]{3,2,1,0:T(8,128)(2,1)}, u32[]{:S(2)}) copy-start(bf16[2,4,128,256]{3,2,1,0:T(8,128)(2,1)} %get-tuple-element.153) | copy-start | bytes 1572868
  157.4 1.2 collective-permute-start.21
  157.4 37.4 %copy-start.2 = (bf16[2,128,1024]{2,1,0:T(8,128)(2,1)}, bf16[2,128,1024]{2,1,0:T(8,128)(2,1)S(1)}, u32[]{:S(2)}) copy-start(bf16[2,128,1024]{2,1,0:T(8,128)(2,1)S(1)} %pad_maximum_fusion.refs_0_) | copy-start | bytes 1572868
  158.6 39.4 %collective-permute-start.32 = (bf16[2,128,1024]{2,1,0:T(8,128)(2,1)S(1)}, bf16[2,128,1024]{2,1,0:T(8,128)(2,1)S(1)}, u32[]{:S(2)}, u32[]{:S(2)}) collective-permute-start(bf16[2,128,1024]{2,1,0:T(8,128)(2,1)S(1)} %pad_maximum_fusion.refs_0_), channel_id=1, source_target_pairs={{0,12},{4,8},{8,4},{12,0},{16,28},{20,24},{24,20},{28,16},{1,13},{... | collective-permute-start | bytes 1572872 | tf_op jit(solution)/shard_map/reduce_down/ppermute | solution.py:572
  159.3 58.8 %collective-permute-start.17 = (bf16[2,1024,256]{2,1,0:T(8,128)(2,1)}, bf16[2,1024,256]{2,1,0:T(8,128)(2,1)S(1)}, u32[]{:S(2)}, u32[]{:S(2)}) collective-permute-start(bf16[2,1024,256]{2,1,0:T(8,128)(2,1)} %get-tuple-element.146), channel_id=1, source_target_pairs={{0,1},{1,0},{2,3},{3,2},{4,5},{5,4},{6,7},{7,6},{8,9},{9,8},{10,11... | collective-permute-start | bytes 3145736 | tf_op jit(solution)/shard_map/mixed_sum/ppermute | solution.py:572
  159.7 8.8 %collective-permute-start.22 = (f32[8,1024]{1,0:T(8,128)S(1)}, f32[8,1024]{1,0:T(8,128)S(1)}, u32[]{:S(2)}, u32[]{:S(2)}) collective-permute-start(f32[8,1024]{1,0:T(8,128)S(1)} %slice_add_fusion.1), channel_id=1, source_target_pairs={{0,2},{1,3},{2,0},{3,1},{4,6},{5,7},{6,4},{7,5},{8,10},{9,11},{10,... | collective-permute-start | bytes 98312 | tf_op jit(solution)/shard_map/stats_sum/ppermute | solution.py:572
  164.1 15.7 %collective-permute-start.28 = (bf16[1,4,128,256]{3,2,1,0:T(8,128)(2,1)}, bf16[1,4,128,256]{3,2,1,0:T(8,128)(2,1)S(1)}, u32[]{:S(2)}, u32[]{:S(2)}) collective-permute-start(bf16[1,4,128,256]{3,2,1,0:T(8,128)(2,1)} %add_convert_fusion.7), channel_id=1, source_target_pairs={{0,16},{4,20},{8,24},{12,28},{16,0},{20,4},{24,8},{28,12},{1,17},{... | collective-permute-start | bytes 786440 | tf_op jit(solution)/shard_map/reduce_attn/ppermute | solution.py:572
  166.7 28.1 %collective-permute-start.33 = (bf16[1,128,1024]{2,1,0:T(8,128)(2,1)S(1)}, bf16[1,128,1024]{2,1,0:T(8,128)(2,1)S(1)}, u32[]{:S(2)}, u32[]{:S(2)}) collective-permute-start(bf16[1,128,1024]{2,1,0:T(8,128)(2,1)S(1)} %add_convert_fusion.6), channel_id=1, source_target_pairs={{0,16},{4,20},{8,24},{12,28},{16,0},{20,4},{24,8},{28,12},{1,17},{... | collective-permute-start | bytes 786440 | tf_op jit(solution)/shard_map/reduce_in/ppermute | solution.py:572
  168.5 53.4 %collective-permute-start.19 = (bf16[2,1024,256]{2,1,0:T(8,128)(2,1)}, bf16[2,1024,256]{2,1,0:T(8,128)(2,1)}, u32[]{:S(2)}, u32[]{:S(2)}) collective-permute-start(bf16[2,1024,256]{2,1,0:T(8,128)(2,1)} %get-tuple-element.149), channel_id=1, source_target_pairs={{0,1},{1,0},{2,3},{3,2},{4,5},{5,4},{6,7},{7,6},{8,9},{9,8},{10,11... | collective-permute-start | bytes 3145736 | tf_op jit(solution)/shard_map/e_sum/ppermute | solution.py:572
  169.5 78.9 %all-to-all-start.1 = ((f32[32,13,256]{2,1,0:T(8,128)}), f32[32,13,256]{2,1,0:T(8,128)S(1)}, u32[]{:S(2)}, u32[]{:S(2)}) async-start(f32[32,13,256]{2,1,0:T(8,128)} %bitcast.22), calls=%async_computation.1 | async-start | bytes 1048576 | tf_op jit(solution)/shard_map/small_sum/all_to_all | solution.py:1034
  179.8 28.2 %collective-permute-start.31 = (bf16[2,128,1024]{2,1,0:T(8,128)(2,1)S(1)}, bf16[2,128,1024]{2,1,0:T(8,128)(2,1)S(1)}, u32[]{:S(2)}, u32[]{:S(2)}) collective-permute-start(bf16[2,128,1024]{2,1,0:T(8,128)(2,1)S(1)} %pad_maximum_fusion.refs_0_), channel_id=1, source_target_pairs={{0,8},{4,12},{8,0},{12,4},{16,24},{20,28},{24,16},{28,20},{1,9},{5... | collective-permute-start | bytes 1572872 | tf_op jit(solution)/shard_map/reduce_down/ppermute | solution.py:572
  194.8 19.1 %collective-permute-start.30 = (bf16[2,128,1024]{2,1,0:T(8,128)(2,1)S(1)}, bf16[2,128,1024]{2,1,0:T(8,128)(2,1)S(1)}, u32[]{:S(2)}, u32[]{:S(2)}) collective-permute-start(bf16[2,128,1024]{2,1,0:T(8,128)(2,1)S(1)} %pad_maximum_fusion.refs_0_), channel_id=1, source_target_pairs={{0,4},{4,0},{8,12},{12,8},{16,20},{20,16},{24,28},{28,24},{1,5},{5... | collective-permute-start | bytes 1572872 | tf_op jit(solution)/shard_map/reduce_down/ppermute | solution.py:572
  197.9 15.9 %copy-start.8 = (bf16[2,128,1024]{2,1,0:T(8,128)(2,1)}, bf16[2,128,1024]{2,1,0:T(8,128)(2,1)S(1)}, u32[]{:S(2)}) copy-start(bf16[2,128,1024]{2,1,0:T(8,128)(2,1)S(1)} %collective-permute-done.32.refs_3_) | copy-start | bytes 1572868
  197.9 20.1 %collective-permute-start.29 = (bf16[1,4,128,256]{3,2,1,0:T(8,128)(2,1)S(1)}, bf16[1,4,128,256]{3,2,1,0:T(8,128)(2,1)S(1)}, u32[]{:S(2)}, u32[]{:S(2)}) collective-permute-start(bf16[1,4,128,256]{3,2,1,0:T(8,128)(2,1)S(1)} %add_convert_fusion.4), channel_id=1, source_target_pairs={{0,16},{4,20},{8,24},{12,28},{16,0},{20,4},{24,8},{28,12},{1,17},{... | collective-permute-start | bytes 786440 | tf_op jit(solution)/shard_map/reduce_attn/ppermute | solution.py:572
  201.5 16.5 %copy-start.4 = (bf16[2,128,1024]{2,1,0:T(8,128)(2,1)}, bf16[2,128,1024]{2,1,0:T(8,128)(2,1)S(1)}, u32[]{:S(2)}) copy-start(bf16[2,128,1024]{2,1,0:T(8,128)(2,1)S(1)} %pad_maximum_fusion.1.refs_0_) | copy-start | bytes 1572868
  201.5 19.5 %copy-start.6 = (bf16[2,1024,256]{2,1,0:T(8,128)(2,1)S(1)}, bf16[2,1024,256]{2,1,0:T(8,128)(2,1)}, u32[]{:S(2)}) copy-start(bf16[2,1024,256]{2,1,0:T(8,128)(2,1)} %get-tuple-element.144) | copy-start | bytes 3145732
  208.0 5.9 %copy-start.12 = (bf16[2,128,1024]{2,1,0:T(8,128)(2,1)}, bf16[2,128,1024]{2,1,0:T(8,128)(2,1)S(1)}, u32[]{:S(2)}) copy-start(bf16[2,128,1024]{2,1,0:T(8,128)(2,1)S(1)} %collective-permute-done.31.refs_2_) | copy-start | bytes 1572868
  208.0 18.7 %collective-permute-start.39 = (bf16[2,128,1024]{2,1,0:T(8,128)(2,1)S(1)}, bf16[2,128,1024]{2,1,0:T(8,128)(2,1)S(1)}, u32[]{:S(2)}, u32[]{:S(2)}) collective-permute-start(bf16[2,128,1024]{2,1,0:T(8,128)(2,1)S(1)} %pad_maximum_fusion.1.refs_0_), channel_id=1, source_target_pairs={{0,12},{4,8},{8,4},{12,0},{16,28},{20,24},{24,20},{28,16},{1,13},{... | collective-permute-start | bytes 1572872 | tf_op jit(solution)/shard_map/reduce_in/ppermute | solution.py:572
  213.9 23.6 %collective-permute-start.38 = (bf16[2,128,1024]{2,1,0:T(8,128)(2,1)S(1)}, bf16[2,128,1024]{2,1,0:T(8,128)(2,1)S(1)}, u32[]{:S(2)}, u32[]{:S(2)}) collective-permute-start(bf16[2,128,1024]{2,1,0:T(8,128)(2,1)S(1)} %pad_maximum_fusion.1.refs_0_), channel_id=1, source_target_pairs={{0,8},{4,12},{8,0},{12,4},{16,24},{20,28},{24,16},{28,20},{1,9},{5... | collective-permute-start | bytes 1572872 | tf_op jit(solution)/shard_map/reduce_in/ppermute | solution.py:572
  218.0 26.2 %collective-permute-start.37 = (bf16[2,128,1024]{2,1,0:T(8,128)(2,1)S(1)}, bf16[2,128,1024]{2,1,0:T(8,128)(2,1)S(1)}, u32[]{:S(2)}, u32[]{:S(2)}) collective-permute-start(bf16[2,128,1024]{2,1,0:T(8,128)(2,1)S(1)} %pad_maximum_fusion.1.refs_0_), channel_id=1, source_target_pairs={{0,4},{4,0},{8,12},{12,8},{16,20},{20,16},{24,28},{28,24},{1,5},{5... | collective-permute-start | bytes 1572872 | tf_op jit(solution)/shard_map/reduce_in/ppermute | solution.py:572
  218.1 30.2 %copy-start.3 = (bf16[2,4,128,256]{3,2,1,0:T(8,128)(2,1)}, bf16[2,4,128,256]{3,2,1,0:T(8,128)(2,1)S(1)}, u32[]{:S(2)}) copy-start(bf16[2,4,128,256]{3,2,1,0:T(8,128)(2,1)S(1)} %pad_maximum_fusion.2.refs_0_) | copy-start | bytes 1572868
  218.2 26.1 %copy-start.7 = (bf16[2,1024,256]{2,1,0:T(8,128)(2,1)}, bf16[2,1024,256]{2,1,0:T(8,128)(2,1)S(1)}, u32[]{:S(2)}) copy-start(bf16[2,1024,256]{2,1,0:T(8,128)(2,1)S(1)} %collective-permute-done.17) | copy-start | bytes 3145732
  218.2 38.4 %collective-permute-start.36 = (bf16[2,4,128,256]{3,2,1,0:T(8,128)(2,1)S(1)}, bf16[2,4,128,256]{3,2,1,0:T(8,128)(2,1)}, u32[]{:S(2)}, u32[]{:S(2)}) collective-permute-start(bf16[2,4,128,256]{3,2,1,0:T(8,128)(2,1)S(1)} %pad_maximum_fusion.2.refs_0_), channel_id=1, source_target_pairs={{0,12},{4,8},{8,4},{12,0},{16,28},{20,24},{24,20},{28,16},{1,13},{... | collective-permute-start | bytes 1572872 | tf_op jit(solution)/shard_map/reduce_attn/ppermute | solution.py:572
  222.0 28.9 %collective-permute-start.18 = (bf16[1,1024,256]{2,1,0:T(8,128)(2,1)}, bf16[1,1024,256]{2,1,0:T(8,128)(2,1)}, u32[]{:S(2)}, u32[]{:S(2)}) collective-permute-start(bf16[1,1024,256]{2,1,0:T(8,128)(2,1)} %add_convert_fusion.2), channel_id=1, source_target_pairs={{0,2},{1,3},{2,0},{3,1},{4,6},{5,7},{6,4},{7,5},{8,10},{9,11},{10,... | collective-permute-start | bytes 1572872 | tf_op jit(solution)/shard_map/mixed_sum/ppermute | solution.py:572
  226.7 17.5 %copy-start.9 = (bf16[2,128,1024]{2,1,0:T(8,128)(2,1)}, bf16[2,128,1024]{2,1,0:T(8,128)(2,1)S(1)}, u32[]{:S(2)}) copy-start(bf16[2,128,1024]{2,1,0:T(8,128)(2,1)S(1)} %collective-permute-done.39.refs_3_) | copy-start | bytes 1572868
  226.7 29.8 %collective-permute-start.35 = (bf16[2,4,128,256]{3,2,1,0:T(8,128)(2,1)S(1)}, bf16[2,4,128,256]{3,2,1,0:T(8,128)(2,1)}, u32[]{:S(2)}, u32[]{:S(2)}) collective-permute-start(bf16[2,4,128,256]{3,2,1,0:T(8,128)(2,1)S(1)} %pad_maximum_fusion.2.refs_0_), channel_id=1, source_target_pairs={{0,8},{4,12},{8,0},{12,4},{16,24},{20,28},{24,16},{28,20},{1,9},{5... | collective-permute-start | bytes 1572872 | tf_op jit(solution)/shard_map/reduce_attn/ppermute | solution.py:572
  237.5 6.8 %copy-start.10 = (bf16[2,128,1024]{2,1,0:T(8,128)(2,1)}, bf16[2,128,1024]{2,1,0:T(8,128)(2,1)S(1)}, u32[]{:S(2)}) copy-start(bf16[2,128,1024]{2,1,0:T(8,128)(2,1)S(1)} %collective-permute-done.38.refs_2_) | copy-start | bytes 1572868
  237.5 19.1 %collective-permute-start.34 = (bf16[2,4,128,256]{3,2,1,0:T(8,128)(2,1)S(1)}, bf16[2,4,128,256]{3,2,1,0:T(8,128)(2,1)}, u32[]{:S(2)}, u32[]{:S(2)}) collective-permute-start(bf16[2,4,128,256]{3,2,1,0:T(8,128)(2,1)S(1)} %pad_maximum_fusion.2.refs_0_), channel_id=1, source_target_pairs={{0,4},{4,0},{8,12},{12,8},{16,20},{20,16},{24,28},{28,24},{1,5},{5... | collective-permute-start | bytes 1572872 | tf_op jit(solution)/shard_map/reduce_attn/ppermute | solution.py:572
  244.2 9.5 %collective-permute-start.20 = (bf16[1,1024,256]{2,1,0:T(8,128)(2,1)}, bf16[1,1024,256]{2,1,0:T(8,128)(2,1)}, u32[]{:S(2)}, u32[]{:S(2)}) collective-permute-start(bf16[1,1024,256]{2,1,0:T(8,128)(2,1)} %add_convert_fusion), channel_id=1, source_target_pairs={{0,2},{1,3},{2,0},{3,1},{4,6},{5,7},{6,4},{7,5},{8,10},{9,11},{10,... | collective-permute-start | bytes 1572872 | tf_op jit(solution)/shard_map/e_sum/ppermute | solution.py:572
  250.2 11.4 %copy-start.24 = (f32[1,256]{1,0:T(1,128)}, f32[1,256]{1,0:T(1,128)S(1)}, u32[]{:S(2)}) copy-start(f32[1,256]{1,0:T(1,128)S(1)} %get-tuple-element.179) | copy-start | bytes 3076
  (10 other events, 23.6 us)

commit v6 on v5

--- a/solution.py
+++ b/solution.py
@@ -631,7 +631,7 @@
         kind, mask = self.plan.pop(0)
         with jax.named_scope(self.name):
             if kind == "group":
-                got = after(tuple(exchange(self.arrays[g], "seq", g) for g in (1, 2, 3)), *pins)
+                got = after(tuple(exchange(self.arrays[g], "seq", g) for g in (3, 2, 1)), *pins)
                 return self.halves([self.arrays[0], *got])
             if kind == "reduce":
                 return self.halves([self.keep, after(exchange(self.send, "seq", mask), *pins)])

time: 266 us -> 265 us (level)
  starting transfers between devices: 66.8 us -> 74.4 us
  waiting for transfers between devices: 62.5 us -> 56.5 us
    ppermute x36, starting transfers between devices: 49.6 us -> 57.1 us  [exchange(): return lax.ppermute(x, axis, [(i, i ^ mask) for i in range(count)])]
    ppermute x36, waiting for transfers between devices: 55.6 us -> 48.4 us  [exchange(): return lax.ppermute(x, axis, [(i, i ^ mask) for i in range(count)])]
  transfers between devices with their start and end apart: 42 -> 42, of which waited for: 14 -> 12; matrix products, arithmetic and copies ran while one was open for 15% -> 15% of each run, Pallas kernels for 32% -> 32%
where the time goes in v6:
time: 265 us; the launch traced here: 262 us
  Pallas kernels  88.7 us (33%)
  starting transfers between devices  74.4 us (28%)
  waiting for transfers between devices  56.5 us (21%)
  other arithmetic  28 us (11%)
  local copies, waits for them, and re-layouts  13.5 us (5%)
    ppermute x36, starting transfers between devices, exchange(): return lax.ppermute(x, axis, [(i, i ^ mask) for i in range(count)])  57.1 us
    ppermute x36, waiting for transfers between devices, exchange(): return lax.ppermute(x, axis, [(i, i ^ mask) for i in range(count)])  48.4 us
    pallas_call x1, Pallas kernels, body(): call(functools.partial(ff_kernel, n_head), hidden // fb, [smem(), smem(),...  18.4 us
    pallas_call x1, Pallas kernels, body(): call(functools.partial(attn_kernel, head_size), blocks, [smem(), rows_of(...  17.2 us
    pallas_call x1, Pallas kernels, body(): call(finish_kernel, blocks, [smem(), rows_of(BT, hidden), whole(hidden, m...  15.9 us
    pallas_call x1, Pallas kernels, body(): call(functools.partial(pre_kernel, head_size, n_head), blocks, [smem(), s...  13.2 us
    pallas_call x1, Pallas kernels, body(): call(functools.partial(tail_kernel, head_size), blocks, [smem(), *[back_r...  12.1 us
    pallas_call x2, Pallas kernels, block_out(): pl.pallas_call(block_out_kernel, grid_spec=pltpu.PrefetchScalarGridSpec(n...  6.83 us
  transfers between devices with their start and end apart: 42, of which 12 were waited for; matrix products, arithmetic and copies ran while one was open for 15% of the time, Pallas kernels for 32%

profile of v6, /device:TPU:8, one launch (start us, length us, event | category | flops | bytes accessed | tf_op | source)
XLA Modules:
  0.0 262.4 jit_solution(3347140197809760144)
XLA Ops:
  0.7 1.6 collective-permute-start.1
  2.3 0.8 reduce-window.8
  3.8 1.2 convert_reduce_fusion
  7.4 1.3 pad_maximum_fusion.4.refs_4_.gains_ref
  8.8 1.3 reshape.121.refs_7_.fw_ref
  10.8 3.8 %fusion.4 = (f32[1024,128]{1,0:T(8,128)}, f32[1024,128]{1,0:T(8,128)}) fusion(f32[128]{0:T(128)} %constant.55.clone, f32[128]{0:T(128)} %constant.54.clone, f32[1024]{0:T(1024)S(1)} %subtract_convert_fusion), kind=kLoop, calls=%fused_computation.15 | loop fusion | flops 262144 | bytes 1053696 | tf_op jit(solution)/shard_map/mul | solution.py:751
  15.3 1.5 collective-permute-start.4
  16.8 1.1 copy.54.refs_12_.segc_ref
  17.8 1.1 copy.53.refs_11_
  18.9 0.8 copy-done.27
  19.9 13.2 %pre_kernel.1 = (bf16[1024,1024]{1,0:T(8,128)(2,1)}, bf16[1024,1024]{1,0:T(8,128)(2,1)}, bf16[1024,1024]{1,0:T(8,128)(2,1)}, bf16[1024,1024]{1,0:T(8,128)(2,1)},...) custom-call(s32[2,3]{1,0:T(2,128)} %add_add_fusion.1.labels_ref, ...), custom_call_target="tpu_custom_call" | custom-call | flops 2684354560 | bytes 12058624 | tf_op jit(solution)/shard_map/pre_kernel/pallas_call | solution.py:767
  33.7 6.3 %all-to-all-start = ((f32[8,72,256]{2,1,0:T(8,128)}), f32[8,72,256]{2,1,0:T(8,128)S(1)}, u32[]{:S(2)}, u32[]{:S(2)}) async-start(f32[8,72,256]{2,1,0:T(8,128)} %get-tuple-element.98), calls=%async_computation | async-start | bytes 1179648 | tf_op jit(solution)/shard_map/state/all_to_all | solution.py:665
  40.0 0.8 dynamic-slice_add_fusion
  40.8 0.8 copy-done.28
  41.7 18.4 %ff_kernel.1 = (bf16[1024,1024]{1,0:T(8,128)(2,1)}, bf16[1024,1024]{1,0:T(8,128)(2,1)}, bf16[1024,1024]{1,0:T(8,128)(2,1)}, bf16[2,128,1024]{2,1,0:T(8,128)(2,1)...) custom-call(s32[1]{0:T(128)} %bitcast.me_ref, ...), custom_call_target="tpu_custom_call" | custom-call | flops 8589934592 | bytes 14680064 | tf_op jit(solution)/shard_map/ff_kernel/pallas_call | solution.py:822
  60.2 1.5 collective-permute-start.10
  61.7 1.4 collective-permute-start.11
  64.5 17.2 %attn_kernel.1 = (bf16[1024,256]{1,0:T(8,128)(2,1)}, f32[1024,256]{1,0:T(8,128)}, f32[1024,256]{1,0:T(8,128)}, f32[1024,256]{1,0:T(8,128)}, f32[2,256,256]{2,1,0...) custom-call(s32[2,3]{1,0:T(2,128)} %add_add_fusion.1.labels_ref, ...), custom_call_target="tpu_custom_call" | custom-call | flops 12884901888 | bytes 7340032 | tf_op jit(solution)/shard_map/attn_kernel/pallas_call | solution.py:858
  81.6 1.5 collective-permute-start.6
  84.6 3.1 %collective-permute-done.6 = f32[72,256]{1,0:T(8,128)S(1)} collective-permute-done((f32[72,256]{1,0:T(8,128)}, f32[72,256]{1,0:T(8,128)S(1)}, u32[]{:S(2)}, u32[]{:S(2)}) %collective-permute-start.6) | collective-permute-done | bytes 73760 | tf_op jit(solution)/shard_map/grad_state/ppermute | solution.py:684
  87.6 0.9 add.180
  89.2 1.3 collective-permute-start.8
  90.5 2.8 %collective-permute-start.7 = (f32[72,256]{1,0:T(8,128)S(1)}, f32[72,256]{1,0:T(8,128)S(1)}, u32[]{:S(2)}, u32[]{:S(2)}) collective-permute-start(f32[72,256]{1,0:T(8,128)S(1)} %add.180), channel_id=1, source_target_pairs={{8,0},{12,4},{16,8},{20,12},{24,16},{28,20},{9,1},{13,5},{17,9},{2... | collective-permute-start | bytes 221192 | tf_op jit(solution)/shard_map/grad_state/ppermute | solution.py:692
  93.6 3.6 %collective-permute-start.16 = (bf16[1,128,1024]{2,1,0:T(8,128)(2,1)S(1)}, bf16[1,128,1024]{2,1,0:T(8,128)(2,1)S(1)}, u32[]{:S(2)}, u32[]{:S(2)}) collective-permute-start(bf16[1,128,1024]{2,1,0:T(8,128)(2,1)S(1)} %add_convert_fusion.12), channel_id=1, source_target_pairs={{0,16},{4,20},{8,24},{12,28},{16,0},{20,4},{24,8},{28,12},{1,17},{... | collective-permute-start | bytes 786440 | tf_op jit(solution)/shard_map/reduce_down/ppermute | solution.py:572
  97.2 1.2 collective-permute-start.13
  98.4 2.0 collective-permute-start.14
  100.7 5.1 %collective-permute-done.7 = f32[72,256]{1,0:T(8,128)S(1)} collective-permute-done((f32[72,256]{1,0:T(8,128)S(1)}, f32[72,256]{1,0:T(8,128)S(1)}, u32[]{:S(2)}, u32[]{:S(2)}) %collective-permute-start.7) | collective-permute-done | bytes 73760 | tf_op jit(solution)/shard_map/grad_state/ppermute | solution.py:692
  106.4 12.1 %tail_kernel.1 = (bf16[3,1024,256]{2,1,0:T(8,128)(2,1)}, f32[8,256]{1,0:T(8,128)}, bf16[2,4,128,256]{3,2,1,0:T(8,128)(2,1)}, bf16[2,4,128,256]{3,2,1,0:T(8,128)(...) custom-call(s32[2,3]{1,0:T(2,128)} %add_add_fusion.1.labels_ref, ...), custom_call_target="tpu_custom_call" | custom-call | flops 1610612736 | bytes 11534336 | tf_op jit(solution)/shard_map/tail_kernel/pallas_call | solution.py:915
  119.3 3.2 %collective-permute-start.25 = (bf16[2,4,128,256]{3,2,1,0:T(8,128)(2,1)}, bf16[2,4,128,256]{3,2,1,0:T(8,128)(2,1)}, u32[]{:S(2)}, u32[]{:S(2)}) collective-permute-start(bf16[2,4,128,256]{3,2,1,0:T(8,128)(2,1)} %get-tuple-element.155), channel_id=1, source_target_pairs={{0,8},{4,12},{8,0},{12,4},{16,24},{20,28},{24,16},{28,20},{1,9},{5... | collective-permute-start | bytes 1572872 | tf_op jit(solution)/shard_map/reduce_attn/ppermute | solution.py:572
  123.2 4.9 %collective-permute-done.14 = bf16[2,128,1024]{2,1,0:T(8,128)(2,1)S(1)} collective-permute-done((bf16[2,128,1024]{2,1,0:T(8,128)(2,1)}, bf16[2,128,1024]{2,1,0:T(8,128)(2,1)S(1)}, u32[]{:S(2)}, u32[]{:S(2)}) %collective-permute-start.14) | collective-permute-done | bytes 524320 | tf_op jit(solution)/shard_map/reduce_in/ppermute | solution.py:572
  128.0 2.3 collective-permute-start.27
  131.2 15.9 %finish_kernel.1 = (bf16[2,1024,256]{2,1,0:T(8,128)(2,1)}, bf16[2,1024,256]{2,1,0:T(8,128)(2,1)}, bf16[2,1024,256]{2,1,0:T(8,128)(2,1)}, bf16[2,1024,256]{2,1,0:T(8,128)(2,1)}, f32[16,1024]{1,0:T(8,128)}) custom-call(s32[1]{0:T(128)} %bitcast.me_ref, bf16[1024,1024]{1,0:T(8,128)(2,1)} %get-tuple-element.103.hid_ref, bf16[1024,1024]{1,0:T(8,128)(2,1)} %wdown_ref.1, ...), custom_call_target="tpu_custom_call" | custom-call | flops 3758096384 | bytes 12058624 | tf_op jit(solution)/shard_map/finish_kernel/pallas_call | solution.py:959
  147.1 9.2 %collective-permute-done.27 = bf16[1,128,1024]{2,1,0:T(8,128)(2,1)S(1)} collective-permute-done((bf16[1,128,1024]{2,1,0:T(8,128)(2,1)S(1)}, bf16[1,128,1024]{2,1,0:T(8,128)(2,1)S(1)}, u32[]{:S(2)}, u32[]{:S(2)}) %collective-permute-start.27) | collective-permute-done | bytes 262176 | tf_op jit(solution)/shard_map/reduce_down/ppermute | solution.py:572
  157.1 0.8 slice.182
  159.4 2.0 collective-permute-done.25
  162.0 1.9 add_convert_fusion.7
  163.9 1.8 collective-permute-start.28
  165.7 1.4 add_convert_fusion.6
  167.1 1.2 collective-permute-start.33
  168.4 0.9 broadcast_in_dim.61
  169.3 4.8 %all-to-all-start.1 = ((f32[32,13,256]{2,1,0:T(8,128)}), f32[32,13,256]{2,1,0:T(8,128)S(1)}, u32[]{:S(2)}, u32[]{:S(2)}) async-start(f32[32,13,256]{2,1,0:T(8,128)} %bitcast.22), calls=%async_computation.1 | async-start | bytes 1048576 | tf_op jit(solution)/shard_map/small_sum/all_to_all | solution.py:1034
  174.0 5.5 %collective-permute-done.28 = bf16[1,4,128,256]{3,2,1,0:T(8,128)(2,1)S(1)} collective-permute-done((bf16[1,4,128,256]{3,2,1,0:T(8,128)(2,1)}, bf16[1,4,128,256]{3,2,1,0:T(8,128)(2,1)S(1)}, u32[]{:S(2)}, u32[]{:S(2)}) %collective-permute-start.28) | collective-permute-done | bytes 262176 | tf_op jit(solution)/shard_map/reduce_attn/ppermute | solution.py:572
  179.6 12.0 %collective-permute-start.31 = (bf16[2,128,1024]{2,1,0:T(8,128)(2,1)S(1)}, bf16[2,128,1024]{2,1,0:T(8,128)(2,1)S(1)}, u32[]{:S(2)}, u32[]{:S(2)}) collective-permute-start(bf16[2,128,1024]{2,1,0:T(8,128)(2,1)S(1)} %pad_maximum_fusion.refs_0_), channel_id=1, source_target_pairs={{0,8},{4,12},{8,0},{12,4},{16,24},{20,28},{24,16},{28,20},{1,9},{5... | collective-permute-start | bytes 1572872 | tf_op jit(solution)/shard_map/reduce_down/ppermute | solution.py:572
  191.6 3.6 %collective-permute-done.33 = bf16[1,128,1024]{2,1,0:T(8,128)(2,1)S(1)} collective-permute-done((bf16[1,128,1024]{2,1,0:T(8,128)(2,1)S(1)}, bf16[1,128,1024]{2,1,0:T(8,128)(2,1)S(1)}, u32[]{:S(2)}, u32[]{:S(2)}) %collective-permute-start.33) | collective-permute-done | bytes 262176 | tf_op jit(solution)/shard_map/reduce_in/ppermute | solution.py:572
  195.2 1.4 add_convert_fusion.4
  196.6 3.5 %collective-permute-start.29 = (bf16[1,4,128,256]{3,2,1,0:T(8,128)(2,1)S(1)}, bf16[1,4,128,256]{3,2,1,0:T(8,128)(2,1)S(1)}, u32[]{:S(2)}, u32[]{:S(2)}) collective-permute-start(bf16[1,4,128,256]{3,2,1,0:T(8,128)(2,1)S(1)} %add_convert_fusion.4), channel_id=1, source_target_pairs={{0,16},{4,20},{8,24},{12,28},{16,0},{20,4},{24,8},{28,12},{1,17},{... | collective-permute-start | bytes 786440 | tf_op jit(solution)/shard_map/reduce_attn/ppermute | solution.py:572
  200.1 8.2 %collective-permute-done.31.refs_2_ = bf16[2,128,1024]{2,1,0:T(8,128)(2,1)S(1)} collective-permute-done((bf16[2,128,1024]{2,1,0:T(8,128)(2,1)S(1)}, bf16[2,128,1024]{2,1,0:T(8,128)(2,1)S(1)}, u32[]{:S(2)}, u32[]{:S(2)}) %collective-permute-start.31) | collective-permute-done | bytes 524320 | tf_op jit(solution)/shard_map/reduce_down/ppermute | solution.py:572
  208.3 1.8 collective-permute-start.39
  210.1 1.7 collective-permute-start.38
  211.8 3.4 %block_out_kernel.3 = f32[1024,1024]{1,0:T(8,128)} custom-call(s32[1]{0:T(128)} %bitcast.1.rank_ref, bf16[2,128,1024]{2,1,0:T(8,128)(2,1)} %copy-done.2, bf16[2,128,1024]{2,1,0:T(8,128)(2,1)} %copy-done.13, bf16[2,128,1024]{2,1,0:T(8,128)(2,1)} %copy-done.12, bf16[2,128,1024]{2,1,0:T(8,128)(2,1)} %copy-done.8), custom_call_target="tpu_custom_call" | custom-call | bytes 6291456 | tf_op jit(solution)/shard_map/block_out_kernel/pallas_call | solution.py:648
  215.2 1.2 collective-permute-start.37
  216.5 1.1 collective-permute-start.36
  217.7 0.9 add_convert_fusion.2
  218.6 4.8 %collective-permute-start.18 = (bf16[1,1024,256]{2,1,0:T(8,128)(2,1)}, bf16[1,1024,256]{2,1,0:T(8,128)(2,1)}, u32[]{:S(2)}, u32[]{:S(2)}) collective-permute-start(bf16[1,1024,256]{2,1,0:T(8,128)(2,1)} %add_convert_fusion.2), channel_id=1, source_target_pairs={{0,2},{1,3},{2,0},{3,1},{4,6},{5,7},{6,4},{7,5},{8,10},{9,11},{10,... | collective-permute-start | bytes 1572872 | tf_op jit(solution)/shard_map/mixed_sum/ppermute | solution.py:572
  223.4 2.0 add_convert_fusion
  225.3 1.2 collective-permute-start.35
  226.6 8.4 %collective-permute-done.38.refs_2_ = bf16[2,128,1024]{2,1,0:T(8,128)(2,1)S(1)} collective-permute-done((bf16[2,128,1024]{2,1,0:T(8,128)(2,1)S(1)}, bf16[2,128,1024]{2,1,0:T(8,128)(2,1)S(1)}, u32[]{:S(2)}, u32[]{:S(2)}) %collective-permute-start.38) | collective-permute-done | bytes 524320 | tf_op jit(solution)/shard_map/reduce_in/ppermute | solution.py:572
  234.9 1.0 collective-permute-start.34
  235.9 5.5 %collective-permute-done.37.refs_1_ = bf16[2,128,1024]{2,1,0:T(8,128)(2,1)S(1)} collective-permute-done((bf16[2,128,1024]{2,1,0:T(8,128)(2,1)S(1)}, bf16[2,128,1024]{2,1,0:T(8,128)(2,1)S(1)}, u32[]{:S(2)}, u32[]{:S(2)}) %collective-permute-start.37) | collective-permute-done | bytes 524320 | tf_op jit(solution)/shard_map/reduce_in/ppermute | solution.py:572
  241.4 4.0 %collective-permute-start.20 = (bf16[1,1024,256]{2,1,0:T(8,128)(2,1)}, bf16[1,1024,256]{2,1,0:T(8,128)(2,1)}, u32[]{:S(2)}, u32[]{:S(2)}) collective-permute-start(bf16[1,1024,256]{2,1,0:T(8,128)(2,1)} %add_convert_fusion), channel_id=1, source_target_pairs={{0,2},{1,3},{2,0},{3,1},{4,6},{5,7},{6,4},{7,5},{8,10},{9,11},{10,... | collective-permute-start | bytes 1572872 | tf_op jit(solution)/shard_map/e_sum/ppermute | solution.py:572
  245.4 3.4 %block_out_kernel.2 = f32[1024,1024]{1,0:T(8,128)} custom-call(s32[1]{0:T(128)} %bitcast.1.rank_ref, bf16[2,128,1024]{2,1,0:T(8,128)(2,1)} %copy-done.4, bf16[2,128,1024]{2,1,0:T(8,128)(2,1)} %copy-done.11, bf16[2,128,1024]{2,1,0:T(8,128)(2,1)} %copy-done.10, bf16[2,128,1024]{2,1,0:T(8,128)(2,1)} %copy-done.9), custom_call_target="tpu_custom_call" | custom-call | bytes 6291456 | tf_op jit(solution)/shard_map/block_out_kernel/pallas_call | solution.py:648
  251.3 2.6 fusion.3
  253.9 2.8 %convert_add_fusion = f32[1024,256]{1,0:T(8,128)} fusion(bf16[1024,256]{1,0:T(8,128)(2,1)S(1)} %copy-done.1, bf16[1,1024,256]{2,1,0:T(8,128)(2,1)} %collective-permute-done.20, bf16[2,1024,256]{2,1,0:T(8,128)(2,1)} %collective-permute-done.19, f32[1024]{0:T(1024)S(1)} %bitcast.50, bf16[1024,1024]{1,0:T(8,128)(2,1)} %get-tuple-element.143.xhat_ref, ...), kind=kLoop, calls=%fused_computation | loop fusion | flops 3670016 | bytes 3682308 | tf_op jit(solution)/shard_map/add | solution.py:999
  256.7 5.1 %widen_kernel.1 = (f32[3,1024,256]{2,1,0:T(8,128)}, f32[256,1024]{1,0:T(8,128)}) custom-call(s32[1]{0:T(128)} %bitcast.1.rank_ref, bf16[2,4,128,256]{3,2,1,0:T(8,128)(2,1)} %copy-done.3, bf16[2,4,128,256]{3,2,1,0:T(8,128)(2,1)} %collective-permute-done.34.refs_1_, bf16[2,4,128,256]{3,2,1,0:T(8,128)(2,1)} %collective-permute-done.35.refs_2_, ...), custom_call_target="tpu_custom_call" | custom-call | bytes 3145728 | tf_op jit(solution)/shard_map/widen_kernel/pallas_call | solution.py:1014
  (154 shorter events, 18.5 us)
Async XLA Ops:
  0.6 18.3 %collective-permute-start = (bf16[1024,256]{1,0:T(8,128)(2,1)}, bf16[1024,256]{1,0:T(8,128)(2,1)S(1)}, u32[]{:S(2)}, u32[]{:S(2)}) collective-permute-start(bf16[1024,256]{1,0:T(8,128)(2,1)} %refs_0_.1), channel_id=1, source_target_pairs={{0,1},{1,0},{2,3},{3,2},{4,5},{5,4},{6,7},{7,6},{8,9},{9,8},{10,11... | collective-permute-start | bytes 1572872 | tf_op jit(solution)/shard_map/gather_tokens/ppermute | solution.py:572
  0.7 14.5 %collective-permute-start.1 = (bf16[1024,256]{1,0:T(8,128)(2,1)}, bf16[1024,256]{1,0:T(8,128)(2,1)S(1)}, u32[]{:S(2)}, u32[]{:S(2)}) collective-permute-start(bf16[1024,256]{1,0:T(8,128)(2,1)} %refs_0_.1), channel_id=1, source_target_pairs={{0,2},{1,3},{2,0},{3,1},{4,6},{5,7},{6,4},{7,5},{8,10},{9,11},{10,... | collective-permute-start | bytes 1572872 | tf_op jit(solution)/shard_map/gather_tokens/ppermute | solution.py:572
  5.5 27.6 %copy-start.23 = (s32[1024]{0:T(1024)}, s32[1024]{0:T(1024)S(1)}, u32[]{:S(2)}) copy-start(s32[1024]{0:T(1024)S(1)} %convert_reduce_fusion.1) | copy-start | bytes 12292
  15.3 3.6 %collective-permute-start.2 = (bf16[1024,256]{1,0:T(8,128)(2,1)S(1)}, bf16[1024,256]{1,0:T(8,128)(2,1)S(1)}, u32[]{:S(2)}, u32[]{:S(2)}) collective-permute-start(bf16[1024,256]{1,0:T(8,128)(2,1)S(1)} %collective-permute-done.1.refs_2_), channel_id=1, source_target_pairs={{0,1},{1,0},{2,3},{3,2},{4,5},{5,4},{6,7},{7,6},{8,9},{9,8},{10,11... | collective-permute-start | bytes 1572872 | tf_op jit(solution)/shard_map/gather_tokens/ppermute | solution.py:572
  15.3 17.8 %collective-permute-start.4 = (bf16[1024,256]{1,0:T(8,128)(2,1)}, bf16[1024,256]{1,0:T(8,128)(2,1)S(1)}, u32[]{:S(2)}, u32[]{:S(2)}) collective-permute-start(bf16[1024,256]{1,0:T(8,128)(2,1)} %refs_0_.2), channel_id=1, source_target_pairs={{0,2},{1,3},{2,0},{3,1},{4,6},{5,7},{6,4},{7,5},{8,10},{9,11},{10,... | collective-permute-start | bytes 1572872 | tf_op jit(solution)/shard_map/gather_grads/ppermute | solution.py:572
  19.9 13.2 %copy-start = (bf16[1024,256]{1,0:T(8,128)(2,1)S(1)}, bf16[1024,256]{1,0:T(8,128)(2,1)}, u32[]{:S(2)}) copy-start(bf16[1024,256]{1,0:T(8,128)(2,1)} %refs_0_.2) | copy-start | bytes 1572868
  33.1 7.7 %copy-start.26 = (bf16[1024,256]{1,0:T(8,128)(2,1)}, bf16[1024,256]{1,0:T(8,128)(2,1)S(1)}, u32[]{:S(2)}) copy-start(bf16[1024,256]{1,0:T(8,128)(2,1)S(1)} %collective-permute-done.4.refs_2_) | copy-start | bytes 1572868
  33.1 7.6 %collective-permute-start.3 = (bf16[1024,256]{1,0:T(8,128)(2,1)S(1)}, bf16[1024,256]{1,0:T(8,128)(2,1)S(1)}, u32[]{:S(2)}, u32[]{:S(2)}) collective-permute-start(bf16[1024,256]{1,0:T(8,128)(2,1)S(1)} %copy-done), channel_id=1, source_target_pairs={{0,1},{1,0},{2,3},{3,2},{4,5},{5,4},{6,7},{7,6},{8,9},{9,8},{10,11... | collective-permute-start | bytes 1572872 | tf_op jit(solution)/shard_map/gather_grads/ppermute | solution.py:572
  33.4 7.3 %collective-permute-start.5 = (bf16[1024,256]{1,0:T(8,128)(2,1)S(1)}, bf16[1024,256]{1,0:T(8,128)(2,1)S(1)}, u32[]{:S(2)}, u32[]{:S(2)}) collective-permute-start(bf16[1024,256]{1,0:T(8,128)(2,1)S(1)} %collective-permute-done.4.refs_2_), channel_id=1, source_target_pairs={{0,1},{1,0},{2,3},{3,2},{4,5},{5,4},{6,7},{7,6},{8,9},{9,8},{10,11... | collective-permute-start | bytes 1572872 | tf_op jit(solution)/shard_map/gather_grads/ppermute | solution.py:572
  33.7 30.0 %all-to-all-start = ((f32[8,72,256]{2,1,0:T(8,128)}), f32[8,72,256]{2,1,0:T(8,128)S(1)}, u32[]{:S(2)}, u32[]{:S(2)}) async-start(f32[8,72,256]{2,1,0:T(8,128)} %get-tuple-element.98), calls=%async_computation | async-start | bytes 1179648 | tf_op jit(solution)/shard_map/state/all_to_all | solution.py:665
  60.2 30.4 %collective-permute-start.10 = (bf16[2,128,1024]{2,1,0:T(8,128)(2,1)}, bf16[2,128,1024]{2,1,0:T(8,128)(2,1)S(1)}, u32[]{:S(2)}, u32[]{:S(2)}) collective-permute-start(bf16[2,128,1024]{2,1,0:T(8,128)(2,1)} %get-tuple-element.121), channel_id=1, source_target_pairs={{0,12},{4,8},{8,4},{12,0},{16,28},{20,24},{24,20},{28,16},{1,13},{... | collective-permute-start | bytes 1572872 | tf_op jit(solution)/shard_map/reduce_down/ppermute | solution.py:572
  61.7 31.7 %collective-permute-start.11 = (bf16[2,128,1024]{2,1,0:T(8,128)(2,1)}, bf16[2,128,1024]{2,1,0:T(8,128)(2,1)S(1)}, u32[]{:S(2)}, u32[]{:S(2)}) collective-permute-start(bf16[2,128,1024]{2,1,0:T(8,128)(2,1)} %get-tuple-element.122), channel_id=1, source_target_pairs={{0,8},{4,12},{8,0},{12,4},{16,24},{20,28},{24,16},{28,20},{1,9},{5... | collective-permute-start | bytes 1572872 | tf_op jit(solution)/shard_map/reduce_down/ppermute | solution.py:572
  63.1 30.2 %collective-permute-start.12 = (bf16[2,128,1024]{2,1,0:T(8,128)(2,1)}, bf16[2,128,1024]{2,1,0:T(8,128)(2,1)S(1)}, u32[]{:S(2)}, u32[]{:S(2)}) collective-permute-start(bf16[2,128,1024]{2,1,0:T(8,128)(2,1)} %get-tuple-element.123), channel_id=1, source_target_pairs={{0,4},{4,0},{8,12},{12,8},{16,20},{20,16},{24,28},{28,24},{1,5},{5... | collective-permute-start | bytes 1572872 | tf_op jit(solution)/shard_map/reduce_down/ppermute | solution.py:572
  64.4 18.7 %copy-start.14 = (f32[1024,1]{1,0:T(8,128)S(1)}, f32[1024,1]{1,0:T(8,128)}, u32[]{:S(2)}) copy-start(f32[1024,1]{1,0:T(8,128)} %get-tuple-element.147) | copy-start | bytes 12292
  64.5 19.5 %copy-start.25 = (f32[1,1024]{1,0:T(1,128)S(1)}, f32[1,1024]{1,0:T(1,128)}, u32[]{:S(2)}) copy-start(f32[1,1024]{1,0:T(1,128)} %get-tuple-element.152) | copy-start | bytes 12292
  64.5 29.0 %copy-start.19 = (bf16[2,128,1024]{2,1,0:T(8,128)(2,1)S(1)}, bf16[2,128,1024]{2,1,0:T(8,128)(2,1)}, u32[]{:S(2)}) copy-start(bf16[2,128,1024]{2,1,0:T(8,128)(2,1)} %get-tuple-element.120) | copy-start | bytes 1572868
  81.6 6.0 %collective-permute-start.6 = (f32[72,256]{1,0:T(8,128)}, f32[72,256]{1,0:T(8,128)S(1)}, u32[]{:S(2)}, u32[]{:S(2)}) collective-permute-start(f32[72,256]{1,0:T(8,128)} %get-tuple-element.118), channel_id=1, source_target_pairs={{0,4},{4,0},{8,12},{12,8},{16,20},{20,16},{24,28},{28,24},{1,5},{5... | collective-permute-start | bytes 221192 | tf_op jit(solution)/shard_map/grad_state/ppermute | solution.py:684
  88.5 9.8 %collective-permute-start.9 = (f32[72,256]{1,0:T(8,128)S(1)}, f32[72,256]{1,0:T(8,128)S(1)}, u32[]{:S(2)}, u32[]{:S(2)}) collective-permute-start(f32[72,256]{1,0:T(8,128)S(1)} %add.180), channel_id=1, source_target_pairs={{24,0},{28,4},{25,1},{29,5},{26,2},{30,6},{27,3},{31,7}} | collective-permute-start | bytes 221192 | tf_op jit(solution)/shard_map/grad_state/ppermute | solution.py:692
  89.2 11.2 %collective-permute-start.8 = (f32[72,256]{1,0:T(8,128)S(1)}, f32[72,256]{1,0:T(8,128)S(1)}, u32[]{:S(2)}, u32[]{:S(2)}) collective-permute-start(f32[72,256]{1,0:T(8,128)S(1)} %add.180), channel_id=1, source_target_pairs={{16,0},{20,4},{24,8},{28,12},{17,1},{21,5},{25,9},{29,13},{18,2},{... | collective-permute-start | bytes 221192 | tf_op jit(solution)/shard_map/grad_state/ppermute | solution.py:692
  90.5 15.3 %collective-permute-start.7 = (f32[72,256]{1,0:T(8,128)S(1)}, f32[72,256]{1,0:T(8,128)S(1)}, u32[]{:S(2)}, u32[]{:S(2)}) collective-permute-start(f32[72,256]{1,0:T(8,128)S(1)} %add.180), channel_id=1, source_target_pairs={{8,0},{12,4},{16,8},{20,12},{24,16},{28,20},{9,1},{13,5},{17,9},{2... | collective-permute-start | bytes 221192 | tf_op jit(solution)/shard_map/grad_state/ppermute | solution.py:692
  93.6 25.7 %collective-permute-start.16 = (bf16[1,128,1024]{2,1,0:T(8,128)(2,1)S(1)}, bf16[1,128,1024]{2,1,0:T(8,128)(2,1)S(1)}, u32[]{:S(2)}, u32[]{:S(2)}) collective-permute-start(bf16[1,128,1024]{2,1,0:T(8,128)(2,1)S(1)} %add_convert_fusion.12), channel_id=1, source_target_pairs={{0,16},{4,20},{8,24},{12,28},{16,0},{20,4},{24,8},{28,12},{1,17},{... | collective-permute-start | bytes 786440 | tf_op jit(solution)/shard_map/reduce_down/ppermute | solution.py:572
  97.2 25.6 %collective-permute-start.13 = (bf16[2,128,1024]{2,1,0:T(8,128)(2,1)}, bf16[2,128,1024]{2,1,0:T(8,128)(2,1)S(1)}, u32[]{:S(2)}, u32[]{:S(2)}) collective-permute-start(bf16[2,128,1024]{2,1,0:T(8,128)(2,1)} %get-tuple-element.135), channel_id=1, source_target_pairs={{0,12},{4,8},{8,4},{12,0},{16,28},{20,24},{24,20},{28,16},{1,13},{... | collective-permute-start | bytes 1572872 | tf_op jit(solution)/shard_map/reduce_in/ppermute | solution.py:572
  98.4 29.6 %collective-permute-start.14 = (bf16[2,128,1024]{2,1,0:T(8,128)(2,1)}, bf16[2,128,1024]{2,1,0:T(8,128)(2,1)S(1)}, u32[]{:S(2)}, u32[]{:S(2)}) collective-permute-start(bf16[2,128,1024]{2,1,0:T(8,128)(2,1)} %get-tuple-element.136), channel_id=1, source_target_pairs={{0,8},{4,12},{8,0},{12,4},{16,24},{20,28},{24,16},{28,20},{1,9},{5... | collective-permute-start | bytes 1572872 | tf_op jit(solution)/shard_map/reduce_in/ppermute | solution.py:572
  100.4 29.9 %collective-permute-start.15 = (bf16[2,128,1024]{2,1,0:T(8,128)(2,1)}, bf16[2,128,1024]{2,1,0:T(8,128)(2,1)S(1)}, u32[]{:S(2)}, u32[]{:S(2)}) collective-permute-start(bf16[2,128,1024]{2,1,0:T(8,128)(2,1)} %get-tuple-element.137), channel_id=1, source_target_pairs={{0,4},{4,0},{8,12},{12,8},{16,20},{20,16},{24,28},{28,24},{1,5},{5... | collective-permute-start | bytes 1572872 | tf_op jit(solution)/shard_map/reduce_in/ppermute | solution.py:572
  106.4 16.1 %copy-start.22 = (bf16[2,128,1024]{2,1,0:T(8,128)(2,1)S(1)}, bf16[2,128,1024]{2,1,0:T(8,128)(2,1)}, u32[]{:S(2)}) copy-start(bf16[2,128,1024]{2,1,0:T(8,128)(2,1)} %copy-done.21) | copy-start | bytes 1572868
  106.4 23.9 %copy-start.15 = (bf16[2,128,1024]{2,1,0:T(8,128)(2,1)S(1)}, bf16[2,128,1024]{2,1,0:T(8,128)(2,1)}, u32[]{:S(2)}) copy-start(bf16[2,128,1024]{2,1,0:T(8,128)(2,1)} %get-tuple-element.131) | copy-start | bytes 1572868
  119.2 39.8 %collective-permute-start.24 = (bf16[2,4,128,256]{3,2,1,0:T(8,128)(2,1)}, bf16[2,4,128,256]{3,2,1,0:T(8,128)(2,1)}, u32[]{:S(2)}, u32[]{:S(2)}) collective-permute-start(bf16[2,4,128,256]{3,2,1,0:T(8,128)(2,1)} %get-tuple-element.154), channel_id=1, source_target_pairs={{0,12},{4,8},{8,4},{12,0},{16,28},{20,24},{24,20},{28,16},{1,13},{... | collective-permute-start | bytes 1572872 | tf_op jit(solution)/shard_map/reduce_attn/ppermute | solution.py:572
  119.3 42.1 %collective-permute-start.25 = (bf16[2,4,128,256]{3,2,1,0:T(8,128)(2,1)}, bf16[2,4,128,256]{3,2,1,0:T(8,128)(2,1)}, u32[]{:S(2)}, u32[]{:S(2)}) collective-permute-start(bf16[2,4,128,256]{3,2,1,0:T(8,128)(2,1)} %get-tuple-element.155), channel_id=1, source_target_pairs={{0,8},{4,12},{8,0},{12,4},{16,24},{20,28},{24,16},{28,20},{1,9},{5... | collective-permute-start | bytes 1572872 | tf_op jit(solution)/shard_map/reduce_attn/ppermute | solution.py:572
  122.8 24.3 %copy-start.17 = (bf16[2,128,1024]{2,1,0:T(8,128)(2,1)}, bf16[2,128,1024]{2,1,0:T(8,128)(2,1)S(1)}, u32[]{:S(2)}) copy-start(bf16[2,128,1024]{2,1,0:T(8,128)(2,1)S(1)} %collective-permute-done.13) | copy-start | bytes 1572868
  122.8 39.2 %collective-permute-start.26 = (bf16[2,4,128,256]{3,2,1,0:T(8,128)(2,1)}, bf16[2,4,128,256]{3,2,1,0:T(8,128)(2,1)}, u32[]{:S(2)}, u32[]{:S(2)}) collective-permute-start(bf16[2,4,128,256]{3,2,1,0:T(8,128)(2,1)} %get-tuple-element.156), channel_id=1, source_target_pairs={{0,4},{4,0},{8,12},{12,8},{16,20},{20,16},{24,28},{28,24},{1,5},{5... | collective-permute-start | bytes 1572872 | tf_op jit(solution)/shard_map/reduce_attn/ppermute | solution.py:572
  128.0 19.1 %copy-start.18 = (bf16[2,128,1024]{2,1,0:T(8,128)(2,1)}, bf16[2,128,1024]{2,1,0:T(8,128)(2,1)S(1)}, u32[]{:S(2)}) copy-start(bf16[2,128,1024]{2,1,0:T(8,128)(2,1)S(1)} %collective-permute-done.14) | copy-start | bytes 1572868
  128.0 28.3 %collective-permute-start.27 = (bf16[1,128,1024]{2,1,0:T(8,128)(2,1)S(1)}, bf16[1,128,1024]{2,1,0:T(8,128)(2,1)S(1)}, u32[]{:S(2)}, u32[]{:S(2)}) collective-permute-start(bf16[1,128,1024]{2,1,0:T(8,128)(2,1)S(1)} %add_convert_fusion.10), channel_id=1, source_target_pairs={{0,16},{4,20},{8,24},{12,28},{16,0},{20,4},{24,8},{28,12},{1,17},{... | collective-permute-start | bytes 786440 | tf_op jit(solution)/shard_map/reduce_down/ppermute | solution.py:572
  130.3 16.7 %copy-start.20 = (bf16[2,128,1024]{2,1,0:T(8,128)(2,1)}, bf16[2,128,1024]{2,1,0:T(8,128)(2,1)S(1)}, u32[]{:S(2)}) copy-start(bf16[2,128,1024]{2,1,0:T(8,128)(2,1)S(1)} %collective-permute-done.15) | copy-start | bytes 1572868
  130.5 35.2 %collective-permute-start.23 = (bf16[1,128,1024]{2,1,0:T(8,128)(2,1)S(1)}, bf16[1,128,1024]{2,1,0:T(8,128)(2,1)}, u32[]{:S(2)}, u32[]{:S(2)}) collective-permute-start(bf16[1,128,1024]{2,1,0:T(8,128)(2,1)S(1)} %add_convert_fusion.9), channel_id=1, source_target_pairs={{0,16},{4,20},{8,24},{12,28},{16,0},{20,4},{24,8},{28,12},{1,17},{... | collective-permute-start | bytes 786440 | tf_op jit(solution)/shard_map/reduce_in/ppermute | solution.py:572
  131.2 30.8 %copy-start.16 = (bf16[2,4,128,256]{3,2,1,0:T(8,128)(2,1)S(1)}, bf16[2,4,128,256]{3,2,1,0:T(8,128)(2,1)}, u32[]{:S(2)}) copy-start(bf16[2,4,128,256]{3,2,1,0:T(8,128)(2,1)} %get-tuple-element.153) | copy-start | bytes 1572868
  157.1 1.2 collective-permute-start.21
  157.1 38.1 %copy-start.2 = (bf16[2,128,1024]{2,1,0:T(8,128)(2,1)}, bf16[2,128,1024]{2,1,0:T(8,128)(2,1)S(1)}, u32[]{:S(2)}) copy-start(bf16[2,128,1024]{2,1,0:T(8,128)(2,1)S(1)} %pad_maximum_fusion.refs_0_) | copy-start | bytes 1572868
  158.3 38.3 %collective-permute-start.32 = (bf16[2,128,1024]{2,1,0:T(8,128)(2,1)S(1)}, bf16[2,128,1024]{2,1,0:T(8,128)(2,1)S(1)}, u32[]{:S(2)}, u32[]{:S(2)}) collective-permute-start(bf16[2,128,1024]{2,1,0:T(8,128)(2,1)S(1)} %pad_maximum_fusion.refs_0_), channel_id=1, source_target_pairs={{0,12},{4,8},{8,4},{12,0},{16,28},{20,24},{24,20},{28,16},{1,13},{... | collective-permute-start | bytes 1572872 | tf_op jit(solution)/shard_map/reduce_down/ppermute | solution.py:572
  159.0 57.5 %collective-permute-start.17 = (bf16[2,1024,256]{2,1,0:T(8,128)(2,1)}, bf16[2,1024,256]{2,1,0:T(8,128)(2,1)S(1)}, u32[]{:S(2)}, u32[]{:S(2)}) collective-permute-start(bf16[2,1024,256]{2,1,0:T(8,128)(2,1)} %get-tuple-element.146), channel_id=1, source_target_pairs={{0,1},{1,0},{2,3},{3,2},{4,5},{5,4},{6,7},{7,6},{8,9},{9,8},{10,11... | collective-permute-start | bytes 3145736 | tf_op jit(solution)/shard_map/mixed_sum/ppermute | solution.py:572
  161.4 6.9 %collective-permute-start.22 = (f32[8,1024]{1,0:T(8,128)S(1)}, f32[8,1024]{1,0:T(8,128)S(1)}, u32[]{:S(2)}, u32[]{:S(2)}) collective-permute-start(f32[8,1024]{1,0:T(8,128)S(1)} %slice_add_fusion.1), channel_id=1, source_target_pairs={{0,2},{1,3},{2,0},{3,1},{4,6},{5,7},{6,4},{7,5},{8,10},{9,11},{10,... | collective-permute-start | bytes 98312 | tf_op jit(solution)/shard_map/stats_sum/ppermute | solution.py:572
  163.9 15.7 %collective-permute-start.28 = (bf16[1,4,128,256]{3,2,1,0:T(8,128)(2,1)}, bf16[1,4,128,256]{3,2,1,0:T(8,128)(2,1)S(1)}, u32[]{:S(2)}, u32[]{:S(2)}) collective-permute-start(bf16[1,4,128,256]{3,2,1,0:T(8,128)(2,1)} %add_convert_fusion.7), channel_id=1, source_target_pairs={{0,16},{4,20},{8,24},{12,28},{16,0},{20,4},{24,8},{28,12},{1,17},{... | collective-permute-start | bytes 786440 | tf_op jit(solution)/shard_map/reduce_attn/ppermute | solution.py:572
  167.1 28.1 %collective-permute-start.33 = (bf16[1,128,1024]{2,1,0:T(8,128)(2,1)S(1)}, bf16[1,128,1024]{2,1,0:T(8,128)(2,1)S(1)}, u32[]{:S(2)}, u32[]{:S(2)}) collective-permute-start(bf16[1,128,1024]{2,1,0:T(8,128)(2,1)S(1)} %add_convert_fusion.6), channel_id=1, source_target_pairs={{0,16},{4,20},{8,24},{12,28},{16,0},{20,4},{24,8},{28,12},{1,17},{... | collective-permute-start | bytes 786440 | tf_op jit(solution)/shard_map/reduce_in/ppermute | solution.py:572
  168.3 50.3 %collective-permute-start.19 = (bf16[2,1024,256]{2,1,0:T(8,128)(2,1)}, bf16[2,1024,256]{2,1,0:T(8,128)(2,1)}, u32[]{:S(2)}, u32[]{:S(2)}) collective-permute-start(bf16[2,1024,256]{2,1,0:T(8,128)(2,1)} %get-tuple-element.149), channel_id=1, source_target_pairs={{0,1},{1,0},{2,3},{3,2},{4,5},{5,4},{6,7},{7,6},{8,9},{9,8},{10,11... | collective-permute-start | bytes 3145736 | tf_op jit(solution)/shard_map/e_sum/ppermute | solution.py:572
  169.3 79.5 %all-to-all-start.1 = ((f32[32,13,256]{2,1,0:T(8,128)}), f32[32,13,256]{2,1,0:T(8,128)S(1)}, u32[]{:S(2)}, u32[]{:S(2)}) async-start(f32[32,13,256]{2,1,0:T(8,128)} %bitcast.22), calls=%async_computation.1 | async-start | bytes 1048576 | tf_op jit(solution)/shard_map/small_sum/all_to_all | solution.py:1034
  179.6 28.7 %collective-permute-start.31 = (bf16[2,128,1024]{2,1,0:T(8,128)(2,1)S(1)}, bf16[2,128,1024]{2,1,0:T(8,128)(2,1)S(1)}, u32[]{:S(2)}, u32[]{:S(2)}) collective-permute-start(bf16[2,128,1024]{2,1,0:T(8,128)(2,1)S(1)} %pad_maximum_fusion.refs_0_), channel_id=1, source_target_pairs={{0,8},{4,12},{8,0},{12,4},{16,24},{20,28},{24,16},{28,20},{1,9},{5... | collective-permute-start | bytes 1572872 | tf_op jit(solution)/shard_map/reduce_down/ppermute | solution.py:572
  195.2 14.9 %collective-permute-start.30 = (bf16[2,128,1024]{2,1,0:T(8,128)(2,1)S(1)}, bf16[2,128,1024]{2,1,0:T(8,128)(2,1)S(1)}, u32[]{:S(2)}, u32[]{:S(2)}) collective-permute-start(bf16[2,128,1024]{2,1,0:T(8,128)(2,1)S(1)} %pad_maximum_fusion.refs_0_), channel_id=1, source_target_pairs={{0,4},{4,0},{8,12},{12,8},{16,20},{20,16},{24,28},{28,24},{1,5},{5... | collective-permute-start | bytes 1572872 | tf_op jit(solution)/shard_map/reduce_down/ppermute | solution.py:572
  196.6 15.2 %copy-start.8 = (bf16[2,128,1024]{2,1,0:T(8,128)(2,1)}, bf16[2,128,1024]{2,1,0:T(8,128)(2,1)S(1)}, u32[]{:S(2)}) copy-start(bf16[2,128,1024]{2,1,0:T(8,128)(2,1)S(1)} %collective-permute-done.32.refs_3_) | copy-start | bytes 1572868
  196.6 18.7 %collective-permute-start.29 = (bf16[1,4,128,256]{3,2,1,0:T(8,128)(2,1)S(1)}, bf16[1,4,128,256]{3,2,1,0:T(8,128)(2,1)S(1)}, u32[]{:S(2)}, u32[]{:S(2)}) collective-permute-start(bf16[1,4,128,256]{3,2,1,0:T(8,128)(2,1)S(1)} %add_convert_fusion.4), channel_id=1, source_target_pairs={{0,16},{4,20},{8,24},{12,28},{16,0},{20,4},{24,8},{28,12},{1,17},{... | collective-permute-start | bytes 786440 | tf_op jit(solution)/shard_map/reduce_attn/ppermute | solution.py:572
  200.1 15.1 %copy-start.4 = (bf16[2,128,1024]{2,1,0:T(8,128)(2,1)}, bf16[2,128,1024]{2,1,0:T(8,128)(2,1)S(1)}, u32[]{:S(2)}) copy-start(bf16[2,128,1024]{2,1,0:T(8,128)(2,1)S(1)} %pad_maximum_fusion.1.refs_0_) | copy-start | bytes 1572868
  200.1 17.6 %copy-start.6 = (bf16[2,1024,256]{2,1,0:T(8,128)(2,1)S(1)}, bf16[2,1024,256]{2,1,0:T(8,128)(2,1)}, u32[]{:S(2)}) copy-start(bf16[2,1024,256]{2,1,0:T(8,128)(2,1)} %get-tuple-element.144) | copy-start | bytes 3145732
  208.3 17.1 %collective-permute-start.39 = (bf16[2,128,1024]{2,1,0:T(8,128)(2,1)S(1)}, bf16[2,128,1024]{2,1,0:T(8,128)(2,1)S(1)}, u32[]{:S(2)}, u32[]{:S(2)}) collective-permute-start(bf16[2,128,1024]{2,1,0:T(8,128)(2,1)S(1)} %pad_maximum_fusion.1.refs_0_), channel_id=1, source_target_pairs={{0,12},{4,8},{8,4},{12,0},{16,28},{20,24},{24,20},{28,16},{1,13},{... | collective-permute-start | bytes 1572872 | tf_op jit(solution)/shard_map/reduce_in/ppermute | solution.py:572
  210.1 24.8 %collective-permute-start.38 = (bf16[2,128,1024]{2,1,0:T(8,128)(2,1)S(1)}, bf16[2,128,1024]{2,1,0:T(8,128)(2,1)S(1)}, u32[]{:S(2)}, u32[]{:S(2)}) collective-permute-start(bf16[2,128,1024]{2,1,0:T(8,128)(2,1)S(1)} %pad_maximum_fusion.1.refs_0_), channel_id=1, source_target_pairs={{0,8},{4,12},{8,0},{12,4},{16,24},{20,28},{24,16},{28,20},{1,9},{5... | collective-permute-start | bytes 1572872 | tf_op jit(solution)/shard_map/reduce_in/ppermute | solution.py:572
  215.2 8.2 %copy-start.5 = (bf16[2,1024,256]{2,1,0:T(8,128)(2,1)S(1)}, bf16[2,1024,256]{2,1,0:T(8,128)(2,1)}, u32[]{:S(2)}) copy-start(bf16[2,1024,256]{2,1,0:T(8,128)(2,1)} %get-tuple-element.148) | copy-start | bytes 3145732
  215.2 26.2 %collective-permute-start.37 = (bf16[2,128,1024]{2,1,0:T(8,128)(2,1)S(1)}, bf16[2,128,1024]{2,1,0:T(8,128)(2,1)S(1)}, u32[]{:S(2)}, u32[]{:S(2)}) collective-permute-start(bf16[2,128,1024]{2,1,0:T(8,128)(2,1)S(1)} %pad_maximum_fusion.1.refs_0_), channel_id=1, source_target_pairs={{0,4},{4,0},{8,12},{12,8},{16,20},{20,16},{24,28},{28,24},{1,5},{5... | collective-permute-start | bytes 1572872 | tf_op jit(solution)/shard_map/reduce_in/ppermute | solution.py:572
  216.5 32.3 %copy-start.3 = (bf16[2,4,128,256]{3,2,1,0:T(8,128)(2,1)}, bf16[2,4,128,256]{3,2,1,0:T(8,128)(2,1)S(1)}, u32[]{:S(2)}) copy-start(bf16[2,4,128,256]{3,2,1,0:T(8,128)(2,1)S(1)} %pad_maximum_fusion.2.refs_0_) | copy-start | bytes 1572868
  216.5 28.8 %copy-start.7 = (bf16[2,1024,256]{2,1,0:T(8,128)(2,1)}, bf16[2,1024,256]{2,1,0:T(8,128)(2,1)S(1)}, u32[]{:S(2)}) copy-start(bf16[2,1024,256]{2,1,0:T(8,128)(2,1)S(1)} %collective-permute-done.17) | copy-start | bytes 3145732
  216.5 40.2 %collective-permute-start.36 = (bf16[2,4,128,256]{3,2,1,0:T(8,128)(2,1)S(1)}, bf16[2,4,128,256]{3,2,1,0:T(8,128)(2,1)}, u32[]{:S(2)}, u32[]{:S(2)}) collective-permute-start(bf16[2,4,128,256]{3,2,1,0:T(8,128)(2,1)S(1)} %pad_maximum_fusion.2.refs_0_), channel_id=1, source_target_pairs={{0,12},{4,8},{8,4},{12,0},{16,28},{20,24},{24,20},{28,16},{1,13},{... | collective-permute-start | bytes 1572872 | tf_op jit(solution)/shard_map/reduce_attn/ppermute | solution.py:572
  218.6 32.7 %collective-permute-start.18 = (bf16[1,1024,256]{2,1,0:T(8,128)(2,1)}, bf16[1,1024,256]{2,1,0:T(8,128)(2,1)}, u32[]{:S(2)}, u32[]{:S(2)}) collective-permute-start(bf16[1,1024,256]{2,1,0:T(8,128)(2,1)} %add_convert_fusion.2), channel_id=1, source_target_pairs={{0,2},{1,3},{2,0},{3,1},{4,6},{5,7},{6,4},{7,5},{8,10},{9,11},{10,... | collective-permute-start | bytes 1572872 | tf_op jit(solution)/shard_map/mixed_sum/ppermute | solution.py:572
  225.3 20.0 %copy-start.9 = (bf16[2,128,1024]{2,1,0:T(8,128)(2,1)}, bf16[2,128,1024]{2,1,0:T(8,128)(2,1)S(1)}, u32[]{:S(2)}) copy-start(bf16[2,128,1024]{2,1,0:T(8,128)(2,1)S(1)} %collective-permute-done.39.refs_3_) | copy-start | bytes 1572868
  225.3 31.4 %collective-permute-start.35 = (bf16[2,4,128,256]{3,2,1,0:T(8,128)(2,1)S(1)}, bf16[2,4,128,256]{3,2,1,0:T(8,128)(2,1)}, u32[]{:S(2)}, u32[]{:S(2)}) collective-permute-start(bf16[2,4,128,256]{3,2,1,0:T(8,128)(2,1)S(1)} %pad_maximum_fusion.2.refs_0_), channel_id=1, source_target_pairs={{0,8},{4,12},{8,0},{12,4},{16,24},{20,28},{24,16},{28,20},{1,9},{5... | collective-permute-start | bytes 1572872 | tf_op jit(solution)/shard_map/reduce_attn/ppermute | solution.py:572
  234.9 10.5 %copy-start.10 = (bf16[2,128,1024]{2,1,0:T(8,128)(2,1)}, bf16[2,128,1024]{2,1,0:T(8,128)(2,1)S(1)}, u32[]{:S(2)}) copy-start(bf16[2,128,1024]{2,1,0:T(8,128)(2,1)S(1)} %collective-permute-done.38.refs_2_) | copy-start | bytes 1572868
  234.9 21.8 %collective-permute-start.34 = (bf16[2,4,128,256]{3,2,1,0:T(8,128)(2,1)S(1)}, bf16[2,4,128,256]{3,2,1,0:T(8,128)(2,1)}, u32[]{:S(2)}, u32[]{:S(2)}) collective-permute-start(bf16[2,4,128,256]{3,2,1,0:T(8,128)(2,1)S(1)} %pad_maximum_fusion.2.refs_0_), channel_id=1, source_target_pairs={{0,4},{4,0},{8,12},{12,8},{16,20},{20,16},{24,28},{28,24},{1,5},{5... | collective-permute-start | bytes 1572872 | tf_op jit(solution)/shard_map/reduce_attn/ppermute | solution.py:572
  241.4 12.5 %collective-permute-start.20 = (bf16[1,1024,256]{2,1,0:T(8,128)(2,1)}, bf16[1,1024,256]{2,1,0:T(8,128)(2,1)}, u32[]{:S(2)}, u32[]{:S(2)}) collective-permute-start(bf16[1,1024,256]{2,1,0:T(8,128)(2,1)} %add_convert_fusion), channel_id=1, source_target_pairs={{0,2},{1,3},{2,0},{3,1},{4,6},{5,7},{6,4},{7,5},{8,10},{9,11},{10,... | collective-permute-start | bytes 1572872 | tf_op jit(solution)/shard_map/e_sum/ppermute | solution.py:572
  250.6 11.2 %copy-start.24 = (f32[1,256]{1,0:T(1,128)}, f32[1,256]{1,0:T(1,128)S(1)}, u32[]{:S(2)}) copy-start(f32[1,256]{1,0:T(1,128)S(1)} %get-tuple-element.179) | copy-start | bytes 3076
  (10 other events, 28.5 us)
